TPU v7x, 32 devices: a whole 2x2x4 slice. The times are simulated.
32 devices in a mesh: row: 8 (over z, y), col: 4 (over x, core).
Axes of the slice: x: 2, y: 2, z: 4, core: 2. Of those that a mesh axis runs over, the one named last changes fastest.
Arguments:
- image_batch: bfloat16 [16, 64, 128, 2], P(None, 'row', 'col'), may hold values from -12 to 12
- valid_mask: int32 [16, 64, 128], P(None, 'row', 'col'), may hold values from 0 to 1, as said below
- flow_target: int32 [16, 64, 128, 2], P(None, 'row', 'col'), may hold values from -80 to 80
- cell_labels: int32 [16, 64, 128], P(None, 'row', 'col'), may hold values 0 or 1
- w_first: float32 [10, 2, 32], replicated, may hold values from -1.5 to 1.5
- w_convs: float32 [3, 9, 32, 32], replicated, may hold values from -0.375 to 0.375
- w_style: float32 [2, 32, 32], replicated, may hold values from -1 to 1
- w_head: float32 [33, 3], replicated, may hold values from -1 to 1
- batch_norm_table: float32 [2, 4, 32], replicated, may hold values from -0.6 to 1.5
- mom_first: float32 [10, 2, 32], replicated, may hold values from -0.022097087 to 0.022097087
- mom_convs: float32 [3, 9, 32, 32], replicated, may hold values from -0.022097087 to 0.022097087
- mom_style: float32 [2, 32, 32], replicated, may hold values from -0.022097087 to 0.022097087
- mom_head: float32 [33, 3], replicated, may hold values from -0.022097087 to 0.022097087
- mom_norms: float32 [2, 4, 32], replicated, may hold values from -0.022097087 to 0.022097087
- sqr_first: float32 [10, 2, 32], replicated, may hold values from 3.0517578e-05 to 0.00012207031
- sqr_convs: float32 [3, 9, 32, 32], replicated, may hold values from 3.0517578e-05 to 0.00012207031
- sqr_style: float32 [2, 32, 32], replicated, may hold values from 3.0517578e-05 to 0.00012207031
- sqr_head: float32 [33, 3], replicated, may hold values from 3.0517578e-05 to 0.00012207031
- sqr_norms: float32 [2, 4, 32], replicated, may hold values from 3.0517578e-05 to 0.00012207031
Outputs:
- loss_total: float32 [], replicated
- valid_count: float32 [], replicated
- first_master: float32 [10, 2, 32], replicated
- first_moment: float32 [10, 2, 32], replicated
- first_square: float32 [10, 2, 32], replicated
- first_copy: bfloat16 [10, 2, 32], replicated
- convs_master: float32 [3, 9, 32, 32], replicated
- convs_moment: float32 [3, 9, 32, 32], replicated
- convs_square: float32 [3, 9, 32, 32], replicated
- convs_copy: bfloat16 [3, 9, 32, 32], replicated
- style_master: float32 [2, 32, 32], replicated
- style_moment: float32 [2, 32, 32], replicated
- style_square: float32 [2, 32, 32], replicated
- head_master: float32 [33, 3], replicated
- head_moment: float32 [33, 3], replicated
- head_square: float32 [33, 3], replicated
- head_copy: bfloat16 [33, 3], replicated
- norms_master: float32 [2, 4, 32], replicated
- norms_moment: float32 [2, 4, 32], replicated
- norms_square: float32 [2, 4, 32], replicated
Inputs may be any that keep to these rules, and one draw needn't show every extreme that they name: `valid_mask`: each image's pixel at row 0, column 0 is 1.
All inputs are finite; a program needn't handle non-finite values. No bound on the sum of `cell_labels` on one device may be relied on, other than what follows from the above.
Results may differ from a plain program's by a relative error of at most 0.0087.
The roundings to bfloat16 on the way count: a program that leaves them out, or rounds other values in their place, can miss the bound.
Values may be sent and summed in bfloat16 or wider, within the bound.
No kernel may reach another device: no remote copies, remote signals or barrier semaphores. Data moves between devices by JAX's collectives and lax.ppermute only.
A program may use at most 128 MiB of HBM per device.

v0:
```python
import jax
import jax.numpy as jnp
from jax import lax
from jax.sharding import PartitionSpec as P

STEP = 5


highest = lax.Precision.HIGHEST
norm_eps = 1e-05
flow_scale = 32.0
adam_eps = 1e-08
weight_decay = 0.01
beta_one = 0.5
beta_two = 0.5
rate_table = (0.2, 0.05, 0.15, 0.15, 0.2)


def with_halo(block, sides, width):
    for axis, dim in sides:
        count = lax.axis_size(axis)
        forward = [(i, i + 1) for i in range(count - 1)]
        backward = [(target, source) for source, target in forward]
        low = lax.ppermute(
            lax.slice_in_dim(block, block.shape[dim] - width, None, axis=dim), axis, forward
        )
        high = lax.ppermute(lax.slice_in_dim(block, 0, width, axis=dim), axis, backward)
        block = jnp.concatenate([low, block, high], axis=dim)
    return block


def widen(tensor):
    return with_halo(tensor, (("row", 1), ("col", 2)), 1)


def conv_valid(padded, kernel):
    shaped = kernel.reshape(3, 3, kernel.shape[1], kernel.shape[2])
    return lax.conv_general_dilated(
        padded,
        shaped,
        (1, 1),
        ((0, 0), (0, 0)),
        dimension_numbers=("NHWC", "HWIO", "NHWC"),
        preferred_element_type=jnp.float32,
    )


def flipped(kernel):
    shaped = kernel.reshape(3, 3, kernel.shape[1], kernel.shape[2])[::-1, ::-1]
    return jnp.swapaxes(shaped, 2, 3).reshape(9, kernel.shape[2], kernel.shape[1])


def conv_input_grad(grad_low, kernel):
    spread_out = conv_valid(jnp.pad(grad_low, ((0, 0), (2, 2), (2, 2), (0, 0))), flipped(kernel))
    row_edges = jnp.concatenate([spread_out[:, :1], spread_out[:, -1:]], axis=1)
    row_parts = with_halo(row_edges.astype(jnp.bfloat16), (("row", 1),), 1).astype(row_edges.dtype)
    inner = spread_out[:, 1:-1]
    inner = inner.at[:, 0].add(row_parts[:, 0]).at[:, -1].add(row_parts[:, 3])
    col_edges = jnp.concatenate([inner[:, :, :1], inner[:, :, -1:]], axis=2)
    col_parts = with_halo(col_edges.astype(jnp.bfloat16), (("col", 2),), 1).astype(col_edges.dtype)
    result = inner[:, :, 1:-1]
    return result.at[:, :, 0].add(col_parts[:, :, 0]).at[:, :, -1].add(col_parts[:, :, 3])


def tap_grads(padded, grad_low):
    row_count = grad_low.shape[1]
    col_count = grad_low.shape[2]
    return jnp.stack(
        [
            jnp.einsum(
                "bhwc,bhwd->cd",
                padded[:, tap_row : tap_row + row_count, tap_col : tap_col + col_count],
                grad_low,
                preferred_element_type=jnp.float32,
            )
            for tap_row in range(3)
            for tap_col in range(3)
        ]
    )


def norm_stats(tensor, pixel_count):
    average = lax.psum(jnp.sum(tensor, axis=(0, 1, 2)), ("row", "col")) / pixel_count
    centred = tensor - average
    spread = lax.psum(jnp.sum(centred * centred, axis=(0, 1, 2)), ("row", "col")) / pixel_count
    inverse = lax.rsqrt(spread + norm_eps)
    return ((tensor - average) * inverse, inverse)


def norm_back(grad_norm, normal_form, inverse, scaling, pixel_count):
    shift_grad, scale_grad = lax.psum(
        (jnp.sum(grad_norm, axis=(0, 1, 2)), jnp.sum(grad_norm * normal_form, axis=(0, 1, 2))),
        ("row", "col"),
    )
    grad_input = (
        scaling * inverse * (grad_norm - (shift_grad + normal_form * scale_grad) / pixel_count)
    )
    return (grad_input, scale_grad, shift_grad)


def swish_derivative(tensor):
    logistic = jax.nn.sigmoid(tensor)
    return logistic * (1.0 + tensor * (1.0 - logistic))


def smooth_pool(tensor):
    images, row_count, col_count, chan_count = tensor.shape
    blocks = tensor.reshape(images, row_count // 2, 2, col_count // 2, 2, chan_count)
    block_top = jnp.max(blocks, axis=(2, 4), keepdims=True)
    expo_vals = jnp.exp(blocks - block_top)
    block_total = jnp.sum(expo_vals, axis=(2, 4), keepdims=True)
    pooled = (block_top + jnp.log(block_total))[:, :, 0, :, 0, :]
    shares = (expo_vals / block_total).reshape(tensor.shape)
    return (pooled, shares)


def expand(tensor):
    return jnp.repeat(jnp.repeat(tensor, 2, axis=1), 2, axis=2)


def block_sum(tensor):
    images, row_count, col_count, chan_count = tensor.shape
    return jnp.sum(
        tensor.reshape(images, row_count // 2, 2, col_count // 2, 2, chan_count), axis=(2, 4)
    )


def adamw(master, moment, square, grad, rate):
    new_moment = beta_one * moment + (1.0 - beta_one) * grad
    new_square = beta_two * square + (1.0 - beta_two) * grad * grad
    moment_hat = new_moment / (1.0 - beta_one**STEP)
    square_hat = new_square / (1.0 - beta_two**STEP)
    new_master = master - rate * (
        moment_hat / (jnp.sqrt(square_hat) + adam_eps) + weight_decay * master
    )
    return (new_master, new_moment, new_square)


def local(
    image_batch,
    valid_mask,
    flow_target,
    cell_labels,
    w_first,
    w_convs,
    w_style,
    w_head,
    batch_norm_table,
    mom_first,
    mom_convs,
    mom_style,
    mom_head,
    mom_norms,
    sqr_first,
    sqr_convs,
    sqr_style,
    sqr_head,
    sqr_norms,
):
    images, row_count, col_count, chan_in = image_batch.shape
    grid_total = lax.axis_size("row") * lax.axis_size("col")
    pixel_count = float(images * row_count * col_count * grid_total)
    pool_cells = float(row_count * col_count * grid_total // 4)
    first_low = w_first.astype(jnp.bfloat16)
    convs_low = w_convs.astype(jnp.bfloat16)
    head_low = w_head.astype(jnp.bfloat16)
    scale_factors = batch_norm_table[0]
    shift_values = batch_norm_table[1]
    padded_image = widen(image_batch)
    pre_first = conv_valid(padded_image, first_low[:9])
    skip_proj = jnp.einsum(
        "bhwc,cd->bhwd", image_batch, first_low[9], preferred_element_type=jnp.float32
    )
    first_preactivation, first_inverse_spread = norm_stats(pre_first, pixel_count)
    first_normalized = first_preactivation * scale_factors[0] + shift_values[0]
    hidden_one = jax.nn.silu(first_normalized).astype(jnp.bfloat16)
    padded_one = widen(hidden_one)
    summed_two = conv_valid(padded_one, convs_low[0]) + skip_proj
    second_preactivation, second_inverse_spread = norm_stats(summed_two, pixel_count)
    second_normalized = second_preactivation * scale_factors[1] + shift_values[1]
    encoded = jax.nn.silu(second_normalized)
    pooled, shares = smooth_pool(encoded)
    style = lax.psum(jnp.sum(pooled, axis=(1, 2)), ("row", "col")) / pool_cells
    merged = (expand(pooled) + encoded).astype(jnp.bfloat16)
    padded_merged = widen(merged)
    style_one = jnp.dot(style, w_style[0], precision=highest)[:, None, None, :]
    decode_one = conv_valid(padded_merged, convs_low[1]) + style_one
    third_preactivation, inverse_three = norm_stats(decode_one, pixel_count)
    third_normalized = third_preactivation * scale_factors[2] + shift_values[2]
    hidden_three = jax.nn.silu(third_normalized).astype(jnp.bfloat16)
    padded_three = widen(hidden_three)
    style_two = jnp.dot(style, w_style[1], precision=highest)[:, None, None, :]
    residual = conv_valid(padded_three, convs_low[2]) + style_two + merged.astype(jnp.float32)
    fourth_preactivation, fourth_inverse_spread = norm_stats(residual, pixel_count)
    fourth_normalized = fourth_preactivation * scale_factors[3] + shift_values[3]
    decoded = jax.nn.silu(fourth_normalized).astype(jnp.bfloat16)
    head_out = jnp.einsum(
        "bhwc,ck->bhwk", decoded, head_low[:-1], preferred_element_type=jnp.float32
    ) + head_low[-1].astype(jnp.float32)
    flows = head_out[..., :2]
    logits = head_out[..., 2]
    weights = valid_mask.astype(jnp.float32)
    targets = flow_target.astype(jnp.float32) / flow_scale
    labels = cell_labels.astype(jnp.float32)
    per_pixel = (
        jnp.sum(jnp.square(flows - targets), axis=-1) + jax.nn.softplus(logits) - labels * logits
    )
    loss_total, valid_count = lax.psum(
        (jnp.sum(weights * per_pixel), jnp.sum(weights)), ("row", "col")
    )
    flow_grad = 2.0 * weights[..., None] * (flows - targets) / valid_count
    logit_grad = weights * (jax.nn.sigmoid(logits) - labels) / valid_count
    grad_out = jnp.concatenate([flow_grad, logit_grad[..., None]], axis=-1).astype(jnp.bfloat16)
    head_grad = jnp.concatenate(
        [
            jnp.einsum("bhwc,bhwk->ck", decoded, grad_out, preferred_element_type=jnp.float32),
            jnp.sum(grad_out.astype(jnp.float32), axis=(0, 1, 2))[None],
        ],
        axis=0,
    )
    decoded_gradient = jnp.einsum(
        "bhwk,ck->bhwc", grad_out, head_low[:-1], preferred_element_type=jnp.float32
    )
    grad_resid, scale_four, shift_four = norm_back(
        decoded_gradient * swish_derivative(fourth_normalized),
        fourth_preactivation,
        fourth_inverse_spread,
        scale_factors[3],
        pixel_count,
    )
    grad_two_low = grad_resid.astype(jnp.bfloat16)
    conv_three = tap_grads(padded_three, grad_two_low)
    grad_hidden_three = conv_input_grad(grad_two_low, convs_low[2])
    grad_one_full, scale_three, shift_three = norm_back(
        grad_hidden_three * swish_derivative(third_normalized),
        third_preactivation,
        inverse_three,
        scale_factors[2],
        pixel_count,
    )
    grad_one_low = grad_one_full.astype(jnp.bfloat16)
    conv_two = tap_grads(padded_merged, grad_one_low)
    grad_merged = grad_resid + conv_input_grad(grad_one_low, convs_low[1])
    style_one_sum, style_two_sum = lax.psum(
        (
            jnp.sum(grad_one_low.astype(jnp.float32), axis=(1, 2)),
            jnp.sum(grad_two_low.astype(jnp.float32), axis=(1, 2)),
        ),
        ("row", "col"),
    )
    style_grad = jnp.stack(
        [
            jnp.dot(style.T, style_one_sum, precision=highest),
            jnp.dot(style.T, style_two_sum, precision=highest),
        ]
    )
    grad_style = jnp.dot(style_one_sum, w_style[0].T, precision=highest) + jnp.dot(
        style_two_sum, w_style[1].T, precision=highest
    )
    grad_pooled = block_sum(grad_merged) + grad_style[:, None, None, :] / pool_cells
    encoded_gradient = grad_merged + expand(grad_pooled) * shares
    grad_sum_full, scale_two, shift_two = norm_back(
        encoded_gradient * swish_derivative(second_normalized),
        second_preactivation,
        second_inverse_spread,
        scale_factors[1],
        pixel_count,
    )
    grad_sum_low = grad_sum_full.astype(jnp.bfloat16)
    conv_one = tap_grads(padded_one, grad_sum_low)
    proj_grad = jnp.einsum(
        "bhwc,bhwd->cd", image_batch, grad_sum_low, preferred_element_type=jnp.float32
    )
    first_hidden_gradient = conv_input_grad(grad_sum_low, convs_low[0])
    grad_first_full, scale_one, shift_one = norm_back(
        first_hidden_gradient * swish_derivative(first_normalized),
        first_preactivation,
        first_inverse_spread,
        scale_factors[0],
        pixel_count,
    )
    first_taps = tap_grads(padded_image, grad_first_full.astype(jnp.bfloat16))
    first_grad = jnp.concatenate([first_taps, proj_grad[None]], axis=0)
    first_sum, convs_sum, head_sum = lax.psum(
        (first_grad, jnp.stack([conv_one, conv_two, conv_three]), head_grad), ("row", "col")
    )
    norms_grad = jnp.stack(
        [
            jnp.stack([scale_one, scale_two, scale_three, scale_four]),
            jnp.stack([shift_one, shift_two, shift_three, shift_four]),
        ]
    )
    masters = (w_first, w_convs, w_style, w_head, batch_norm_table)
    moments = (mom_first, mom_convs, mom_style, mom_head, mom_norms)
    squares = (sqr_first, sqr_convs, sqr_style, sqr_head, sqr_norms)
    grads = (first_sum, convs_sum, style_grad, head_sum, norms_grad)
    updated = [
        adamw(masters[index], moments[index], squares[index], grads[index], rate_table[index])
        for index in range(5)
    ]
    return (
        loss_total,
        valid_count,
        updated[0][0],
        updated[0][1],
        updated[0][2],
        updated[0][0].astype(jnp.bfloat16),
        updated[1][0],
        updated[1][1],
        updated[1][2],
        updated[1][0].astype(jnp.bfloat16),
        updated[2][0],
        updated[2][1],
        updated[2][2],
        updated[3][0],
        updated[3][1],
        updated[3][2],
        updated[3][0].astype(jnp.bfloat16),
        updated[4][0],
        updated[4][1],
        updated[4][2],
    )


def solution(mesh):
    return jax.shard_map(
        local,
        mesh=mesh,
        in_specs=(
            P(None, "row", "col", None),
            P(None, "row", "col"),
            P(None, "row", "col", None),
            P(None, "row", "col"),
            P(),
            P(),
            P(),
            P(),
            P(),
            P(),
            P(),
            P(),
            P(),
            P(),
            P(),
            P(),
            P(),
            P(),
            P(),
        ),
        out_specs=(
            P(),
            P(),
            P(),
            P(),
            P(),
            P(),
            P(),
            P(),
            P(),
            P(),
            P(),
            P(),
            P(),
            P(),
            P(),
            P(),
            P(),
            P(),
            P(),
            P(),
        ),
        check_vma=False,
    )
```

profile of v0, /device:TPU:0, one launch (start us, length us, event | category | flops | bytes accessed | tf_op | source)
XLA Modules:
  0.0 939.3 jit_solution(15228334144341840181)
XLA Ops:
  8.0 4.9 collective-permute-start
  26.6 43.0 %psum.168 = f32[32]{0:T(128)S(1)} all-reduce(f32[32]{0:T(128)S(1)} %get-tuple-element.269), channel_id=1, replica_groups=mesh['row'=8,'col'=4] {'row','col'}, use_global_device_ids=true, to_apply=%region_1.0 | all-reduce | flops 32 | bytes 256 | tf_op jit(solution)/shard_map/psum | solution.py:83
  70.3 39.2 %psum.169 = f32[32]{0:T(128)S(1)} all-reduce(f32[32]{0:T(128)S(1)} %multiply_reduce_fusion.7), channel_id=1, replica_groups=mesh['row'=8,'col'=4] {'row','col'}, use_global_device_ids=true, to_apply=%region_3.0 | all-reduce | flops 32 | bytes 256 | tf_op jit(solution)/shard_map/psum | solution.py:85
  110.3 4.3 collective-permute-start.4
  130.6 41.9 %psum.170 = f32[32]{0:T(128)S(1)} all-reduce(f32[32]{0:T(128)S(1)} %get-tuple-element.271), channel_id=1, replica_groups=mesh['row'=8,'col'=4] {'row','col'}, use_global_device_ids=true, to_apply=%region_5.6 | all-reduce | flops 32 | bytes 256 | tf_op jit(solution)/shard_map/psum | solution.py:83
  173.1 38.7 %psum.171 = f32[32]{0:T(128)S(1)} all-reduce(f32[32]{0:T(128)S(1)} %multiply_reduce_fusion.6), channel_id=1, replica_groups=mesh['row'=8,'col'=4] {'row','col'}, use_global_device_ids=true, to_apply=%region_7.8 | all-reduce | flops 32 | bytes 256 | tf_op jit(solution)/shard_map/psum | solution.py:85
  220.4 4.8 collective-permute-start.8
  227.1 41.3 %psum.172 = f32[16,32]{1,0:T(8,128)S(1)} all-reduce(f32[16,32]{1,0:T(8,128)S(1)} %get-tuple-element.212), channel_id=1, replica_groups=mesh['row'=8,'col'=4] {'row','col'}, use_global_device_ids=true, to_apply=%region_11.12 | all-reduce | flops 512 | bytes 4096 | tf_op jit(solution)/shard_map/psum | solution.py:183
  280.3 40.0 %psum.173 = f32[32]{0:T(128)S(1)} all-reduce(f32[32]{0:T(128)S(1)} %get-tuple-element.273), channel_id=1, replica_groups=mesh['row'=8,'col'=4] {'row','col'}, use_global_device_ids=true, to_apply=%region_13.14 | all-reduce | flops 32 | bytes 256 | tf_op jit(solution)/shard_map/psum | solution.py:83
  323.2 40.4 %psum.174 = f32[32]{0:T(128)S(1)} all-reduce(f32[32]{0:T(128)S(1)} %multiply_reduce_fusion.5), channel_id=1, replica_groups=mesh['row'=8,'col'=4] {'row','col'}, use_global_device_ids=true, to_apply=%region_15.16 | all-reduce | flops 32 | bytes 256 | tf_op jit(solution)/shard_map/psum | solution.py:85
  368.1 4.8 collective-permute-start.12
  389.9 4.7 fusion.230
  394.7 41.4 %psum.175 = f32[32]{0:T(128)S(1)} all-reduce(f32[32]{0:T(128)S(1)} %get-tuple-element.275), channel_id=1, replica_groups=mesh['row'=8,'col'=4] {'row','col'}, use_global_device_ids=true, to_apply=%region_17.18 | all-reduce | flops 32 | bytes 256 | tf_op jit(solution)/shard_map/psum | solution.py:83
  439.1 40.9 %psum.176 = f32[32]{0:T(128)S(1)} all-reduce(f32[32]{0:T(128)S(1)} %multiply_reduce_fusion.4), channel_id=1, replica_groups=mesh['row'=8,'col'=4] {'row','col'}, use_global_device_ids=true, to_apply=%region_19.20 | all-reduce | flops 32 | bytes 256 | tf_op jit(solution)/shard_map/psum | solution.py:85
  490.6 39.7 %psum.178 = f32[]{:T(128)} all-reduce(f32[]{:T(128)} %get-tuple-element.172), channel_id=1, replica_groups=mesh['row'=8,'col'=4] {'row','col'}, use_global_device_ids=true, to_apply=%region_24.25 | all-reduce | flops 1 | bytes 8 | tf_op jit(solution)/shard_map/psum | solution.py:208
  534.4 4.4 fusion.205
  538.8 40.6 %all-reduce.5 = (f32[32]{0:T(128)S(1)}, f32[32]{0:T(128)S(1)}) all-reduce(f32[32]{0:T(128)S(1)} %get-tuple-element.171, f32[32]{0:T(128)S(1)} %get-tuple-element.170), channel_id=1, replica_groups=mesh['row'=8,'col'=4] {'row','col'}, use_global_device_ids=true, to_apply=%region_28.29 | all-reduce | flops 64 | bytes 512 | tf_op jit(solution)/shard_map/psum | solution.py:91
  590.9 4.8 collective-permute-start.16
  615.4 41.5 %all-reduce.4 = (f32[32]{0:T(128)S(1)}, f32[32]{0:T(128)S(1)}) all-reduce(f32[32]{0:T(128)S(1)} %get-tuple-element.169, f32[32]{0:T(128)S(1)} %get-tuple-element.168), channel_id=1, replica_groups=mesh['row'=8,'col'=4] {'row','col'}, use_global_device_ids=true, to_apply=%region_32.33 | all-reduce | flops 64 | bytes 512 | tf_op jit(solution)/shard_map/psum | solution.py:91
  660.0 40.7 %all-reduce.3 = (f32[16,32]{1,0:T(8,128)S(1)}, f32[16,32]{1,0:T(8,128)S(1)}) all-reduce(f32[16,32]{1,0:T(8,128)S(1)} %get-tuple-element.209, f32[16,32]{1,0:T(8,128)S(1)} %get-tuple-element.207), channel_id=1, replica_groups=mesh['row'=8,'col'=4] {'row','col'}, use_global_device_ids=true, to_apply=%region_35.36 | all-reduce | flops 1024 | bytes 8192 | tf_op jit(solution)/shard_map/psum | solution.py:244
  735.3 43.0 %all-reduce.2 = (f32[32]{0:T(128)S(1)}, f32[32]{0:T(128)S(1)}) all-reduce(f32[32]{0:T(128)S(1)} %get-tuple-element.167, f32[32]{0:T(128)S(1)} %get-tuple-element.166), channel_id=1, replica_groups=mesh['row'=8,'col'=4] {'row','col'}, use_global_device_ids=true, to_apply=%region_41.42 | all-reduce | flops 64 | bytes 512 | tf_op jit(solution)/shard_map/psum | solution.py:91
  808.0 41.8 %all-reduce.1 = (f32[32]{0:T(128)S(1)}, f32[32]{0:T(128)S(1)}) all-reduce(f32[32]{0:T(128)S(1)} %get-tuple-element.165, f32[32]{0:T(128)S(1)} %get-tuple-element.164), channel_id=1, replica_groups=mesh['row'=8,'col'=4] {'row','col'}, use_global_device_ids=true, to_apply=%region_45.46 | all-reduce | flops 64 | bytes 512 | tf_op jit(solution)/shard_map/psum | solution.py:91
  858.9 40.0 %all-reduce = (f32[]{:T(128)}, f32[10,2,32]{2,1,0:T(2,128)S(1)}, f32[33,3]{0,1:T(4,128)S(1)}) all-reduce(f32[]{:T(128)} %get-tuple-element.173, f32[10,2,32]{2,1,0:T(2,128)S(1)} %fusion.113, f32[33,3]{0,1:T(4,128)S(1)} %pad_maximum_fusion.37), channel_id=1, replica_groups=mesh['row'=8,'col'=4] {'row','col'}, use_global_device_ids=true, to_apply=%region_22.23 | all-reduce | flops 740 | bytes 5920 | tf_op jit(solution)/shard_map/psum | solution.py:208
  900.9 28.7 %all-reduce.8.cloned.1.call-done = f32[3,9,32,32]{3,2,1,0:T(8,128)} async-done(((f32[3,9,32,32]{3,2,1,0:T(8,128)}), f32[3,9,32,32]{3,2,1,0:T(8,128)}) %all-reduce.8.cloned.1.call-update) | async-done | bytes 110608 | tf_op jit(solution)/shard_map/psum | solution.py:284
  (466 shorter events, 207.1 us)
Async XLA Ops:
  7.2 922.4 %all-reduce.8.cloned.1.call-start = ((), (), s32[]{:S(2)}) async-start(), calls=%async_computation | async-start | bytes 884736 | tf_op jit(solution)/shard_map/psum | solution.py:284
  8.0 6.2 collective-permute-start
  12.8 5.5 collective-permute-start.1
  19.1 4.7 collective-permute-start.2
  20.4 4.9 collective-permute-start.3
  110.3 8.2 collective-permute-start.4
  114.6 6.9 collective-permute-start.5
  122.8 4.4 collective-permute-start.7
  220.4 47.9 %collective-permute-start.8 = (bf16[16,1,32,32]{3,0,2,1:T(8,128)(2,1)}, bf16[16,1,32,32]{3,0,2,1:T(8,128)(2,1)}, u32[]{:S(2)}, u32[]{:S(2)}) collective-permute-start(bf16[16,1,32,32]{3,0,2,1:T(8,128)(2,1)} %get-tuple-element.234), channel_id=1, source_target_pairs={{0,4},{4,8},{8,12},{12,16},{16,20},{20,24},{24,28},{1,5},{5,9},{9,... | collective-permute-start | bytes 98312 | tf_op jit(solution)/shard_map/ppermute | solution.py:24
  225.2 43.1 %collective-permute-start.9 = (bf16[16,1,32,32]{3,0,2,1:T(8,128)(2,1)}, bf16[16,1,32,32]{3,0,2,1:T(8,128)(2,1)}, u32[]{:S(2)}, u32[]{:S(2)}) collective-permute-start(bf16[16,1,32,32]{3,0,2,1:T(8,128)(2,1)} %get-tuple-element.235), channel_id=1, source_target_pairs={{4,0},{8,4},{12,8},{16,12},{20,16},{24,20},{28,24},{5,1},{9,5},{13... | collective-permute-start | bytes 98312 | tf_op jit(solution)/shard_map/ppermute | solution.py:27
  270.4 5.6 collective-permute-start.11
  368.1 15.1 %collective-permute-start.12 = (bf16[16,1,32,32]{3,0,2,1:T(8,128)(2,1)}, bf16[16,1,32,32]{3,0,2,1:T(8,128)(2,1)}, u32[]{:S(2)}, u32[]{:S(2)}) collective-permute-start(bf16[16,1,32,32]{3,0,2,1:T(8,128)(2,1)} %get-tuple-element.232), channel_id=1, source_target_pairs={{0,4},{4,8},{8,12},{12,16},{16,20},{20,24},{24,28},{1,5},{5,9},{9,... | collective-permute-start | bytes 98312 | tf_op jit(solution)/shard_map/ppermute | solution.py:24
  372.9 10.3 %collective-permute-start.13 = (bf16[16,1,32,32]{3,0,2,1:T(8,128)(2,1)}, bf16[16,1,32,32]{3,0,2,1:T(8,128)(2,1)}, u32[]{:S(2)}, u32[]{:S(2)}) collective-permute-start(bf16[16,1,32,32]{3,0,2,1:T(8,128)(2,1)} %get-tuple-element.233), channel_id=1, source_target_pairs={{4,0},{8,4},{12,8},{16,12},{20,16},{24,20},{28,24},{5,1},{9,5},{13... | collective-permute-start | bytes 98312 | tf_op jit(solution)/shard_map/ppermute | solution.py:27
  385.3 4.6 collective-permute-start.15
  590.9 13.8 %collective-permute-start.16 = (bf16[16,1,34,32]{3,0,2,1:T(8,128)(2,1)S(1)}, bf16[16,1,34,32]{3,0,2,1:T(8,128)(2,1)}, u32[]{:S(2)}, u32[]{:S(2)}) collective-permute-start(bf16[16,1,34,32]{3,0,2,1:T(8,128)(2,1)S(1)} %get-tuple-element.218), channel_id=1, source_target_pairs={{0,4},{4,8},{8,12},{12,16},{16,20},{20,24},{24,28},{1,5},{5,9},{9,... | collective-permute-start | bytes 104456 | tf_op jit(solution)/shard_map/ppermute | solution.py:24
  595.7 9.0 collective-permute-start.17
  608.2 4.5 collective-permute-start.19
  708.2 11.3 %collective-permute-start.20 = (bf16[16,1,34,32]{3,0,2,1:T(8,128)(2,1)S(1)}, bf16[16,1,34,32]{3,0,2,1:T(8,128)(2,1)S(1)}, u32[]{:S(2)}, u32[]{:S(2)}) collective-permute-start(bf16[16,1,34,32]{3,0,2,1:T(8,128)(2,1)S(1)} %get-tuple-element.216), channel_id=1, source_target_pairs={{0,4},{4,8},{8,12},{12,16},{16,20},{20,24},{24,28},{1,5},{5,9},{9,... | collective-permute-start | bytes 104456 | tf_op jit(solution)/shard_map/ppermute | solution.py:24
  712.4 7.0 collective-permute-start.21
  721.0 4.2 collective-permute-start.23
  785.1 7.7 collective-permute-start.24
  789.3 6.9 collective-permute-start.25
  797.8 5.5 collective-permute-start.26
  799.1 5.3 collective-permute-start.27
  (131 other events, 3334.3 us)
Sparse Core Ops, SparseCore 0:
  801.4 128.1 all-reduce.7
where the time goes:
time: 951 us; the launch traced here: 939 us
  blocking collectives  654 us (69%)
  other arithmetic  61.5 us (6%)
  matrix products  60 us (6%)
  starting transfers between devices  59.8 us (6%)
  waiting for transfers between devices  58.3 us (6%)
  local copies, waits for them, and re-layouts  28.8 us (3%)
  between operations  16.7 us (2%)
    psum x4, blocking collectives, norm_back(): lax.psum((jnp.sum(grad_norm, axis=(0, 1, 2)), jnp.sum(grad_norm * normal_...  167 us
    psum x4, blocking collectives, norm_stats(): lax.psum(jnp.sum(tensor, axis=(0, 1, 2)), ('row', 'col')) / pixel_count  166 us
    psum x4, blocking collectives, norm_stats(): lax.psum(jnp.sum(centred * centred, axis=(0, 1, 2)), ('row', 'col'))  159 us
    psum x2, blocking collectives, local(): lax.psum((jnp.sum(weights * per_pixel), jnp.sum(weights)), ('row', 'col'))  79.7 us
    psum x1, blocking collectives, local(): style = lax.psum(jnp.sum(pooled, axis=(1, 2)), ('row', 'col')) / pool_cells  41.3 us
    ppermute x14, starting transfers between devices, with_halo(): lax.ppermute(lax.slice_in_dim(block, block.shape[dim] - width, None, axis...  41.1 us
    psum x1, blocking collectives, local(): lax.psum((jnp.sum(grad_one_low.astype(jnp.float32), axis=(1, 2)), jnp.sum...  40.7 us
    dot_general x36, matrix products, tap_grads(): jnp.einsum('bhwc,bhwd->cd', padded[:, tap_row:tap_row + row_count, tap_co...  29.3 us
  transfers between devices with their start and end apart: 29, of which 12 were waited for; matrix products, arithmetic and copies ran while one was open for 5% of the time, Pallas kernels for 0%

commit v1 on v0

--- a/solution.py
+++ b/solution.py
@@ -79,18 +79,40 @@
     )
 
 
+def everywhere(*parts):
+    devices = lax.axis_size("row") * lax.axis_size("col")
+    flat = jnp.concatenate([part.reshape(-1) for part in parts])
+    lanes = -(-flat.size // 128)
+    flat = jnp.pad(flat, (0, lanes * 128 - flat.size)).reshape(1, lanes, 128)
+    spread = jnp.broadcast_to(flat, (devices, lanes, 128))
+    gathered = lax.all_to_all(spread, ("row", "col"), 0, 0).reshape(devices, lanes * 128)
+    found = []
+    start = 0
+    for part in parts:
+        found.append(gathered[:, start : start + part.size].reshape((devices,) + part.shape))
+        start += part.size
+    return found
+
+
+def total(*parts):
+    return [jnp.sum(found, axis=0) for found in everywhere(*parts)]
+
+
 def norm_stats(tensor, pixel_count):
-    average = lax.psum(jnp.sum(tensor, axis=(0, 1, 2)), ("row", "col")) / pixel_count
-    centred = tensor - average
-    spread = lax.psum(jnp.sum(centred * centred, axis=(0, 1, 2)), ("row", "col")) / pixel_count
+    local_count = float(tensor.size // tensor.shape[-1])
+    local_mean = jnp.sum(tensor, axis=(0, 1, 2)) / local_count
+    centred = tensor - local_mean
+    means, squares = everywhere(local_mean, jnp.sum(centred * centred, axis=(0, 1, 2)))
+    average = jnp.sum(means, axis=0) * (local_count / pixel_count)
+    between = jnp.sum(jnp.square(means - average), axis=0) * local_count
+    spread = (jnp.sum(squares, axis=0) + between) / pixel_count
     inverse = lax.rsqrt(spread + norm_eps)
     return ((tensor - average) * inverse, inverse)
 
 
 def norm_back(grad_norm, normal_form, inverse, scaling, pixel_count):
-    shift_grad, scale_grad = lax.psum(
-        (jnp.sum(grad_norm, axis=(0, 1, 2)), jnp.sum(grad_norm * normal_form, axis=(0, 1, 2))),
-        ("row", "col"),
+    shift_grad, scale_grad = total(
+        jnp.sum(grad_norm, axis=(0, 1, 2)), jnp.sum(grad_norm * normal_form, axis=(0, 1, 2))
     )
     grad_input = (
         scaling * inverse * (grad_norm - (shift_grad + normal_form * scale_grad) / pixel_count)
@@ -180,7 +202,7 @@
     second_normalized = second_preactivation * scale_factors[1] + shift_values[1]
     encoded = jax.nn.silu(second_normalized)
     pooled, shares = smooth_pool(encoded)
-    style = lax.psum(jnp.sum(pooled, axis=(1, 2)), ("row", "col")) / pool_cells
+    style = total(jnp.sum(pooled, axis=(1, 2)))[0] / pool_cells
     merged = (expand(pooled) + encoded).astype(jnp.bfloat16)
     padded_merged = widen(merged)
     style_one = jnp.dot(style, w_style[0], precision=highest)[:, None, None, :]
@@ -205,9 +227,7 @@
     per_pixel = (
         jnp.sum(jnp.square(flows - targets), axis=-1) + jax.nn.softplus(logits) - labels * logits
     )
-    loss_total, valid_count = lax.psum(
-        (jnp.sum(weights * per_pixel), jnp.sum(weights)), ("row", "col")
-    )
+    loss_total, valid_count = total(jnp.sum(weights * per_pixel), jnp.sum(weights))
     flow_grad = 2.0 * weights[..., None] * (flows - targets) / valid_count
     logit_grad = weights * (jax.nn.sigmoid(logits) - labels) / valid_count
     grad_out = jnp.concatenate([flow_grad, logit_grad[..., None]], axis=-1).astype(jnp.bfloat16)
@@ -241,12 +261,9 @@
     grad_one_low = grad_one_full.astype(jnp.bfloat16)
     conv_two = tap_grads(padded_merged, grad_one_low)
     grad_merged = grad_resid + conv_input_grad(grad_one_low, convs_low[1])
-    style_one_sum, style_two_sum = lax.psum(
-        (
-            jnp.sum(grad_one_low.astype(jnp.float32), axis=(1, 2)),
-            jnp.sum(grad_two_low.astype(jnp.float32), axis=(1, 2)),
-        ),
-        ("row", "col"),
+    style_one_sum, style_two_sum = total(
+        jnp.sum(grad_one_low.astype(jnp.float32), axis=(1, 2)),
+        jnp.sum(grad_two_low.astype(jnp.float32), axis=(1, 2)),
     )
     style_grad = jnp.stack(
         [

time: 951 us -> 530 us (0.56)
  blocking collectives: 654 us -> 66.6 us
  waiting for transfers between devices: 58.3 us -> 183 us
  starting transfers between devices: 59.8 us -> 97.8 us
    psum x16 -> x1, blocking collectives: 654 us -> 41.4 us  [local(): lax.psum((first_grad, jnp.stack([conv_one, conv_two, conv_three]), head_g...]
    psum x1, waiting for transfers between devices: 28.7 us -> 115 us  [local(): lax.psum((first_grad, jnp.stack([conv_one, conv_two, conv_three]), head_g...]
    all_to_all x0 -> x9, starting transfers between devices: none -> 47.6 us  [everywhere(): lax.all_to_all(spread, ('row', 'col'), 0, 0).reshape(devices, lanes * 128)]
    all_to_all x0 -> x9, waiting for transfers between devices: none -> 31.2 us  [everywhere(): lax.all_to_all(spread, ('row', 'col'), 0, 0).reshape(devices, lanes * 128)]
    all_to_all x0 -> x2, blocking collectives: none -> 25.2 us  [everywhere(): lax.all_to_all(spread, ('row', 'col'), 0, 0).reshape(devices, lanes * 128)]
    ppermute x14, starting transfers between devices: 41.1 us -> 31.2 us  [with_halo(): lax.ppermute(lax.slice_in_dim(block, block.shape[dim] - width, None, axis...]
  transfers between devices with their start and end apart: 29 -> 38, of which waited for: 12 -> 23; matrix products, arithmetic and copies ran while one was open for 5% -> 10% of each run, Pallas kernels for 0% -> 0%
where the time goes in v1:
time: 530 us; the launch traced here: 520 us
  waiting for transfers between devices  183 us (35%)
  starting transfers between devices  97.8 us (18%)
  blocking collectives  66.6 us (13%)
  other arithmetic  66.3 us (13%)
  matrix products  54.8 us (10%)
  local copies, waits for them, and re-layouts  34.1 us (6%)
  between operations  17.2 us (3%)
    psum x1, waiting for transfers between devices, local(): lax.psum((first_grad, jnp.stack([conv_one, conv_two, conv_three]), head_g...  115 us
    all_to_all x9, starting transfers between devices, everywhere(): lax.all_to_all(spread, ('row', 'col'), 0, 0).reshape(devices, lanes * 128)  47.6 us
    psum x1, blocking collectives, local(): lax.psum((first_grad, jnp.stack([conv_one, conv_two, conv_three]), head_g...  41.4 us
    ppermute x14, waiting for transfers between devices, with_halo(): lax.ppermute(lax.slice_in_dim(block, 0, width, axis=dim), axis, backward)  34.6 us
    ppermute x14, starting transfers between devices, with_halo(): lax.ppermute(lax.slice_in_dim(block, block.shape[dim] - width, None, axis...  31.2 us
    all_to_all x9, waiting for transfers between devices, everywhere(): lax.all_to_all(spread, ('row', 'col'), 0, 0).reshape(devices, lanes * 128)  31.2 us
    dot_general x36, matrix products, tap_grads(): jnp.einsum('bhwc,bhwd->cd', padded[:, tap_row:tap_row + row_count, tap_co...  26.5 us
    all_to_all x2, blocking collectives, everywhere(): lax.all_to_all(spread, ('row', 'col'), 0, 0).reshape(devices, lanes * 128)  25.2 us
  transfers between devices with their start and end apart: 38, of which 23 were waited for; matrix products, arithmetic and copies ran while one was open for 10% of the time, Pallas kernels for 0%

profile of v1, /device:TPU:0, one launch (start us, length us, event | category | flops | bytes accessed | tf_op | source)
XLA Modules:
  0.0 520.4 jit_solution(14572781272360090403)
XLA Ops:
  7.9 4.9 collective-permute-start
  28.3 7.5 %all-to-all-start = ((f32[32,1,128]{2,1,0:T(1,128)}), f32[32,1,128]{2,1,0:T(1,128)S(1)}, u32[]{:S(2)}, u32[]{:S(2)}) async-start(f32[32,1,128]{2,1,0:T(1,128)} %broadcast_in_dim.39), calls=%async_computation | async-start | bytes 32768 | tf_op jit(solution)/shard_map/all_to_all | solution.py:88
  36.5 6.4 %all-to-all-done = f32[32,1,128]{2,1,0:T(1,128)S(1)} async-done(((f32[32,1,128]{2,1,0:T(1,128)}), f32[32,1,128]{2,1,0:T(1,128)S(1)}, u32[]{:S(2)}, u32[]{:S(2)}) %all-to-all-start) | async-done | bytes 16416 | tf_op jit(solution)/shard_map/all_to_all | solution.py:88
  50.2 4.1 collective-permute-done.5
  59.7 3.3 fusion.218
  63.7 12.0 %all_to_all.55 = f32[32,1,128]{2,1,0:T(1,128)S(1)} all-to-all(f32[32,1,128]{2,1,0:T(1,128)S(1)} %broadcast_in_dim.40), channel_id=1, replica_groups=mesh['row'=8,'col'=4] {'row','col'}, dimensions={0} | all-to-all | bytes 32768 | tf_op jit(solution)/shard_map/all_to_all | solution.py:88
  89.9 3.5 all-to-all-start.2
  105.7 13.3 %all_to_all.56 = f32[32,1,128]{2,1,0:T(1,128)S(1)} all-to-all(f32[32,1,128]{2,1,0:T(1,128)S(1)} %broadcast_in_dim.45), channel_id=1, replica_groups=mesh['row'=8,'col'=4] {'row','col'}, dimensions={0} | all-to-all | bytes 32768 | tf_op jit(solution)/shard_map/all_to_all | solution.py:88
  126.4 4.1 collective-permute-done.13
  141.5 5.0 all-to-all-start.4
  147.3 6.4 %all-to-all-done.4 = f32[32,1,128]{2,1,0:T(1,128)S(1)} async-done(((f32[32,1,128]{2,1,0:T(1,128)}), f32[32,1,128]{2,1,0:T(1,128)S(1)}, u32[]{:S(2)}, u32[]{:S(2)}) %all-to-all-start.4) | async-done | bytes 16416 | tf_op jit(solution)/shard_map/all_to_all | solution.py:88
  189.8 4.5 fusion.194
  195.1 5.9 %all-to-all-start.6 = ((f32[32,1,128]{2,1,0:T(1,128)}), f32[32,1,128]{2,1,0:T(1,128)S(1)}, u32[]{:S(2)}, u32[]{:S(2)}) async-start(f32[32,1,128]{2,1,0:T(1,128)} %broadcast_in_dim.49), calls=%async_computation.6 | async-start | bytes 32768 | tf_op jit(solution)/shard_map/all_to_all | solution.py:88
  201.7 6.5 %all-to-all-done.6 = f32[32,1,128]{2,1,0:T(1,128)S(1)} async-done(((f32[32,1,128]{2,1,0:T(1,128)}), f32[32,1,128]{2,1,0:T(1,128)S(1)}, u32[]{:S(2)}, u32[]{:S(2)}) %all-to-all-start.6) | async-done | bytes 16416 | tf_op jit(solution)/shard_map/all_to_all | solution.py:88
  221.2 4.1 collective-permute-done.17
  234.2 5.1 all-to-all-start.7
  241.2 5.3 %all-to-all-done.7 = f32[32,1,128]{2,1,0:T(1,128)S(1)} async-done(((f32[32,1,128]{2,1,0:T(1,128)}), f32[32,1,128]{2,1,0:T(1,128)S(1)}, u32[]{:S(2)}, u32[]{:S(2)}) %all-to-all-start.7) | async-done | bytes 16416 | tf_op jit(solution)/shard_map/all_to_all | solution.py:88
  260.9 3.7 collective-permute-start.20
  292.6 8.6 %all-to-all-start.9 = ((f32[32,1,128]{2,1,0:T(1,128)}), f32[32,1,128]{2,1,0:T(1,128)S(1)}, u32[]{:S(2)}, u32[]{:S(2)}) async-start(f32[32,1,128]{2,1,0:T(1,128)} %broadcast_in_dim.54), calls=%async_computation.9 | async-start | bytes 32768 | tf_op jit(solution)/shard_map/all_to_all | solution.py:88
  302.2 6.1 %all-to-all-done.9 = f32[32,1,128]{2,1,0:T(1,128)S(1)} async-done(((f32[32,1,128]{2,1,0:T(1,128)}), f32[32,1,128]{2,1,0:T(1,128)S(1)}, u32[]{:S(2)}, u32[]{:S(2)}) %all-to-all-start.9) | async-done | bytes 16416 | tf_op jit(solution)/shard_map/all_to_all | solution.py:88
  321.4 3.7 collective-permute-done.25
  336.5 6.0 %all-to-all-start.10 = ((f32[32,1,128]{2,1,0:T(1,128)}), f32[32,1,128]{2,1,0:T(1,128)S(1)}, u32[]{:S(2)}, u32[]{:S(2)}) async-start(f32[32,1,128]{2,1,0:T(1,128)} %broadcast_in_dim.55), calls=%async_computation.10 | async-start | bytes 32768 | tf_op jit(solution)/shard_map/all_to_all | solution.py:88
  342.5 114.9 %all-reduce.12.cloned.1.call-done = f32[3,9,32,32]{3,2,1,0:T(8,128)} async-done(((f32[3,9,32,32]{3,2,1,0:T(8,128)}), f32[3,9,32,32]{3,2,1,0:T(8,128)}) %all-reduce.12.cloned.1.call-update) | async-done | bytes 110608 | tf_op jit(solution)/shard_map/psum | solution.py:301
  469.6 41.4 %all-reduce.9 = (f32[10,2,32]{2,1,0:T(2,128)S(1)}, f32[33,3]{0,1:T(4,128)S(1)}) all-reduce(f32[10,2,32]{2,1,0:T(2,128)S(1)} %fusion.113, f32[33,3]{0,1:T(4,128)S(1)} %copy-done.76), channel_id=1, replica_groups=mesh['row'=8,'col'=4] {'row','col'}, use_global_device_ids=true, to_apply=%region_50.51 | all-reduce | flops 739 | bytes 5912 | tf_op jit(solution)/shard_map/psum | solution.py:301
  (547 shorter events, 216.8 us)
Async XLA Ops:
  7.9 6.2 %collective-permute-start = (bf16[16,1,32,2]{2,3,1,0:T(2,128)(2,1)S(1)}, bf16[16,1,32,2]{2,3,1,0:T(2,128)(2,1)S(1)}, u32[]{:S(2)}, u32[]{:S(2)}) collective-permute-start(bf16[16,1,32,2]{2,3,1,0:T(2,128)(2,1)S(1)} %get-tuple-element.272), channel_id=1, source_target_pairs={{0,4},{4,8},{8,12},{12,16},{16,20},{20,24},{24,28},{1,5},{5,9},{9,... | collective-permute-start | bytes 6152 | tf_op jit(solution)/shard_map/ppermute | solution.py:24
  12.8 5.5 %collective-permute-start.1 = (bf16[16,1,32,2]{2,3,1,0:T(2,128)(2,1)S(1)}, bf16[16,1,32,2]{2,3,1,0:T(2,128)(2,1)S(1)}, u32[]{:S(2)}, u32[]{:S(2)}) collective-permute-start(bf16[16,1,32,2]{2,3,1,0:T(2,128)(2,1)S(1)} %get-tuple-element.271), channel_id=1, source_target_pairs={{4,0},{8,4},{12,8},{16,12},{20,16},{24,20},{28,24},{5,1},{9,5},{13... | collective-permute-start | bytes 6152 | tf_op jit(solution)/shard_map/ppermute | solution.py:27
  28.3 14.6 %all-to-all-start = ((f32[32,1,128]{2,1,0:T(1,128)}), f32[32,1,128]{2,1,0:T(1,128)S(1)}, u32[]{:S(2)}, u32[]{:S(2)}) async-start(f32[32,1,128]{2,1,0:T(1,128)} %broadcast_in_dim.39), calls=%async_computation | async-start | bytes 32768 | tf_op jit(solution)/shard_map/all_to_all | solution.py:88
  47.5 6.9 %collective-permute-start.5 = (bf16[16,1,32,32]{3,0,2,1:T(8,128)(2,1)S(1)}, bf16[16,1,32,32]{3,0,2,1:T(8,128)(2,1)S(1)}, u32[]{:S(2)}, u32[]{:S(2)}) collective-permute-start(bf16[16,1,32,32]{3,0,2,1:T(8,128)(2,1)S(1)} %get-tuple-element.254), channel_id=1, source_target_pairs={{4,0},{8,4},{12,8},{16,12},{20,16},{24,20},{28,24},{5,1},{9,5},{13... | collective-permute-start | bytes 98312 | tf_op jit(solution)/shard_map/ppermute | solution.py:27
  84.8 8.6 %collective-permute-start.8 = (bf16[16,1,32,32]{3,0,2,1:T(8,128)(2,1)}, bf16[16,1,32,32]{3,0,2,1:T(8,128)(2,1)}, u32[]{:S(2)}, u32[]{:S(2)}) collective-permute-start(bf16[16,1,32,32]{3,0,2,1:T(8,128)(2,1)} %get-tuple-element.251), channel_id=1, source_target_pairs={{0,4},{4,8},{8,12},{12,16},{16,20},{20,24},{24,28},{1,5},{5,9},{9,... | collective-permute-start | bytes 98312 | tf_op jit(solution)/shard_map/ppermute | solution.py:24
  87.9 7.2 %collective-permute-start.9 = (bf16[16,1,32,32]{3,0,2,1:T(8,128)(2,1)}, bf16[16,1,32,32]{3,0,2,1:T(8,128)(2,1)}, u32[]{:S(2)}, u32[]{:S(2)}) collective-permute-start(bf16[16,1,32,32]{3,0,2,1:T(8,128)(2,1)} %get-tuple-element.252), channel_id=1, source_target_pairs={{4,0},{8,4},{12,8},{16,12},{20,16},{24,20},{28,24},{5,1},{9,5},{13... | collective-permute-start | bytes 98312 | tf_op jit(solution)/shard_map/ppermute | solution.py:27
  89.9 10.8 %all-to-all-start.2 = ((f32[32,4,128]{2,1,0:T(4,128)}), f32[32,4,128]{2,1,0:T(4,128)}, u32[]{:S(2)}, u32[]{:S(2)}) async-start(f32[32,4,128]{2,1,0:T(4,128)} %broadcast_in_dim.44), calls=%async_computation.2 | async-start | bytes 131072 | tf_op jit(solution)/shard_map/all_to_all | solution.py:88
  96.4 5.4 %collective-permute-start.10 = (bf16[16,10,1,32]{3,0,2,1:T(8,128)(2,1)}, bf16[16,10,1,32]{3,0,2,1:T(8,128)(2,1)}, u32[]{:S(2)}, u32[]{:S(2)}) collective-permute-start(bf16[16,10,1,32]{3,0,2,1:T(8,128)(2,1)} %get-tuple-element.239), channel_id=1, source_target_pairs={{0,1},{1,2},{2,3},{4,5},{5,6},{6,7},{8,9},{9,10},{10,11},{12,13},{... | collective-permute-start | bytes 30728 | tf_op jit(solution)/shard_map/ppermute | solution.py:24
  123.6 6.9 %collective-permute-start.13 = (bf16[16,1,32,32]{3,0,2,1:T(8,128)(2,1)S(1)}, bf16[16,1,32,32]{3,0,2,1:T(8,128)(2,1)S(1)}, u32[]{:S(2)}, u32[]{:S(2)}) collective-permute-start(bf16[16,1,32,32]{3,0,2,1:T(8,128)(2,1)S(1)} %get-tuple-element.250), channel_id=1, source_target_pairs={{4,0},{8,4},{12,8},{16,12},{20,16},{24,20},{28,24},{5,1},{9,5},{13... | collective-permute-start | bytes 98312 | tf_op jit(solution)/shard_map/ppermute | solution.py:27
  141.5 12.1 %all-to-all-start.4 = ((f32[32,1,128]{2,1,0:T(1,128)}), f32[32,1,128]{2,1,0:T(1,128)S(1)}, u32[]{:S(2)}, u32[]{:S(2)}) async-start(f32[32,1,128]{2,1,0:T(1,128)} %broadcast_in_dim.46), calls=%async_computation.4 | async-start | bytes 32768 | tf_op jit(solution)/shard_map/all_to_all | solution.py:88
  168.0 14.8 %all-to-all-start.5 = ((f32[32,1,128]{2,1,0:T(1,128)}), f32[32,1,128]{2,1,0:T(1,128)}, u32[]{:S(2)}, u32[]{:S(2)}) async-start(f32[32,1,128]{2,1,0:T(1,128)} %broadcast_in_dim.47), calls=%async_computation.5 | async-start | bytes 32768 | tf_op jit(solution)/shard_map/all_to_all | solution.py:88
  195.1 13.1 %all-to-all-start.6 = ((f32[32,1,128]{2,1,0:T(1,128)}), f32[32,1,128]{2,1,0:T(1,128)S(1)}, u32[]{:S(2)}, u32[]{:S(2)}) async-start(f32[32,1,128]{2,1,0:T(1,128)} %broadcast_in_dim.49), calls=%async_computation.6 | async-start | bytes 32768 | tf_op jit(solution)/shard_map/all_to_all | solution.py:88
  215.8 5.4 %collective-permute-start.16 = (bf16[16,1,34,32]{3,0,2,1:T(8,128)(2,1)S(1)}, bf16[16,1,34,32]{3,0,2,1:T(8,128)(2,1)S(1)}, u32[]{:S(2)}, u32[]{:S(2)}) collective-permute-start(bf16[16,1,34,32]{3,0,2,1:T(8,128)(2,1)S(1)} %get-tuple-element.235), channel_id=1, source_target_pairs={{0,4},{4,8},{8,12},{12,16},{16,20},{20,24},{24,28},{1,5},{5,9},{9,... | collective-permute-start | bytes 104456 | tf_op jit(solution)/shard_map/ppermute | solution.py:24
  218.3 7.0 %collective-permute-start.17 = (bf16[16,1,34,32]{3,0,2,1:T(8,128)(2,1)S(1)}, bf16[16,1,34,32]{3,0,2,1:T(8,128)(2,1)S(1)}, u32[]{:S(2)}, u32[]{:S(2)}) collective-permute-start(bf16[16,1,34,32]{3,0,2,1:T(8,128)(2,1)S(1)} %get-tuple-element.236), channel_id=1, source_target_pairs={{4,0},{8,4},{12,8},{16,12},{20,16},{24,20},{28,24},{5,1},{9,5},{13... | collective-permute-start | bytes 104456 | tf_op jit(solution)/shard_map/ppermute | solution.py:27
  234.2 12.2 %all-to-all-start.7 = ((f32[32,1,128]{2,1,0:T(1,128)}), f32[32,1,128]{2,1,0:T(1,128)S(1)}, u32[]{:S(2)}, u32[]{:S(2)}) async-start(f32[32,1,128]{2,1,0:T(1,128)} %broadcast_in_dim.50), calls=%async_computation.7 | async-start | bytes 32768 | tf_op jit(solution)/shard_map/all_to_all | solution.py:88
  250.4 32.8 %all-to-all-start.8 = ((f32[32,8,128]{2,1,0:T(8,128)}), f32[32,8,128]{2,1,0:T(8,128)S(1)}, u32[]{:S(2)}, u32[]{:S(2)}) async-start(f32[32,8,128]{2,1,0:T(8,128)} %broadcast_in_dim.51), calls=%async_computation.8 | async-start | bytes 262144 | tf_op jit(solution)/shard_map/all_to_all | solution.py:88
  260.9 9.1 %collective-permute-start.20 = (bf16[16,1,34,32]{3,0,2,1:T(8,128)(2,1)S(1)}, bf16[16,1,34,32]{3,0,2,1:T(8,128)(2,1)S(1)}, u32[]{:S(2)}, u32[]{:S(2)}) collective-permute-start(bf16[16,1,34,32]{3,0,2,1:T(8,128)(2,1)S(1)} %get-tuple-element.233), channel_id=1, source_target_pairs={{0,4},{4,8},{8,12},{12,16},{16,20},{20,24},{24,28},{1,5},{5,9},{9,... | collective-permute-start | bytes 104456 | tf_op jit(solution)/shard_map/ppermute | solution.py:24
  264.6 7.3 %collective-permute-start.21 = (bf16[16,1,34,32]{3,0,2,1:T(8,128)(2,1)S(1)}, bf16[16,1,34,32]{3,0,2,1:T(8,128)(2,1)S(1)}, u32[]{:S(2)}, u32[]{:S(2)}) collective-permute-start(bf16[16,1,34,32]{3,0,2,1:T(8,128)(2,1)S(1)} %get-tuple-element.234), channel_id=1, source_target_pairs={{4,0},{8,4},{12,8},{16,12},{20,16},{24,20},{28,24},{5,1},{9,5},{13... | collective-permute-start | bytes 104456 | tf_op jit(solution)/shard_map/ppermute | solution.py:27
  292.6 15.7 %all-to-all-start.9 = ((f32[32,1,128]{2,1,0:T(1,128)}), f32[32,1,128]{2,1,0:T(1,128)S(1)}, u32[]{:S(2)}, u32[]{:S(2)}) async-start(f32[32,1,128]{2,1,0:T(1,128)} %broadcast_in_dim.54), calls=%async_computation.9 | async-start | bytes 32768 | tf_op jit(solution)/shard_map/all_to_all | solution.py:88
  301.2 156.2 %all-reduce.12.cloned.1.call-start = ((), (), s32[]{:S(2)}) async-start(), calls=%async_computation.11 | async-start | bytes 884736 | tf_op jit(solution)/shard_map/psum | solution.py:301
  315.7 5.7 %collective-permute-start.24 = (bf16[16,1,34,32]{3,0,2,1:T(8,128)(2,1)S(1)}, bf16[16,1,34,32]{3,0,2,1:T(8,128)(2,1)S(1)}, u32[]{:S(2)}, u32[]{:S(2)}) collective-permute-start(bf16[16,1,34,32]{3,0,2,1:T(8,128)(2,1)S(1)} %get-tuple-element.231), channel_id=1, source_target_pairs={{0,4},{4,8},{8,12},{12,16},{16,20},{20,24},{24,28},{1,5},{5,9},{9,... | collective-permute-start | bytes 104456 | tf_op jit(solution)/shard_map/ppermute | solution.py:24
  318.1 7.0 %collective-permute-start.25 = (bf16[16,1,34,32]{3,0,2,1:T(8,128)(2,1)S(1)}, bf16[16,1,34,32]{3,0,2,1:T(8,128)(2,1)S(1)}, u32[]{:S(2)}, u32[]{:S(2)}) collective-permute-start(bf16[16,1,34,32]{3,0,2,1:T(8,128)(2,1)S(1)} %get-tuple-element.232), channel_id=1, source_target_pairs={{4,0},{8,4},{12,8},{16,12},{20,16},{24,20},{28,24},{5,1},{9,5},{13... | collective-permute-start | bytes 104456 | tf_op jit(solution)/shard_map/ppermute | solution.py:27
  326.8 5.5 %collective-permute-start.26 = (bf16[16,8,1,32]{3,0,2,1:T(8,128)(2,1)S(1)}, bf16[16,8,1,32]{3,0,2,1:T(8,128)(2,1)S(1)}, u32[]{:S(2)}, u32[]{:S(2)}) collective-permute-start(bf16[16,8,1,32]{3,0,2,1:T(8,128)(2,1)S(1)} %get-tuple-element.243), channel_id=1, source_target_pairs={{0,1},{1,2},{2,3},{4,5},{5,6},{6,7},{8,9},{9,10},{10,11},{12,13},{... | collective-permute-start | bytes 24584 | tf_op jit(solution)/shard_map/ppermute | solution.py:24
  336.5 123.8 %all-to-all-start.10 = ((f32[32,1,128]{2,1,0:T(1,128)}), f32[32,1,128]{2,1,0:T(1,128)S(1)}, u32[]{:S(2)}, u32[]{:S(2)}) async-start(f32[32,1,128]{2,1,0:T(1,128)} %broadcast_in_dim.55), calls=%async_computation.10 | async-start | bytes 32768 | tf_op jit(solution)/shard_map/all_to_all | solution.py:88
  (154 other events, 2072.7 us)
Sparse Core Ops, SparseCore 0:
  330.3 127.0 all-reduce.11

commit v2 on v0

v2 whole, which is shorter than its diff:
```python
import functools

import jax
import jax.numpy as jnp
from jax import lax
from jax.experimental import pallas as pl
from jax.experimental.pallas import tpu as pltpu
from jax.sharding import PartitionSpec as P

STEP = 5

highest = lax.Precision.HIGHEST
norm_eps = 1e-05
flow_scale = 32.0
adam_eps = 1e-08
weight_decay = 0.01
beta_one = 0.5
beta_two = 0.5
rate_table = (0.2, 0.05, 0.15, 0.15, 0.2)

CH = 32
GRP = 4
LANES = 128
RIM = 8
PITCH = 64
F32 = jnp.float32
BF16 = jnp.bfloat16
VMEM_LIMIT = 40 * 1024 * 1024


def lane_of(shape):
    return lax.broadcasted_iota(jnp.int32, shape, len(shape) - 1)


def row_of(shape):
    return lax.broadcasted_iota(jnp.int32, shape, 0)


def group_of(shape):
    return lane_of(shape) >> 5


def fold(v):
    v = v + pltpu.roll(v, 64, axis=1)
    return v + pltpu.roll(v, 32, axis=1)


def spread(v, k):
    return fold(jnp.where(group_of(v.shape) == k, v, 0.0))


def partner(v):
    odd = (group_of(v.shape) & 1) == 1
    return jnp.where(odd, pltpu.roll(v, 32, axis=1), pltpu.roll(v, 96, axis=1))


def tile4(v):
    return jnp.concatenate([v, v, v, v], axis=1)


def col_sum(v):
    return jnp.sum(v, axis=0, keepdims=True)


def pack_images(v):
    group = group_of((4, LANES))
    out = jnp.zeros((4, LANES), F32)
    for b in range(4):
        out = jnp.where(group == b, v[4 * b : 4 * b + 4], out)
    return out


def unpack_images(u):
    return jnp.concatenate([spread(u, b) for b in range(4)], axis=0)


def low(v):
    return v.astype(BF16).astype(F32)


def sig_of(v):
    return 1.0 / (1.0 + jnp.exp(-v))


def slope(n, sig):
    return sig * (1.0 + n * (1.0 - sig))


def flat(v):
    return v.reshape(-1, LANES)


def conv(src, taps, row, rows, col, blocks, back=False):
    pieces = []
    for r in range(3):
        for c in range(3):
            dr, dc = (2 - r, 2 - c) if back else (r, c)
            pieces.append(flat(src[pl.ds(row + dr, rows), col + dc : col + dc + blocks]))
    wide = jnp.concatenate(pieces, axis=1)
    y = jnp.dot(wide, taps[...], preferred_element_type=F32)
    return y.reshape(rows, blocks, -1, LANES)


def loop(count, body):
    def step(i, carry):
        body(i)
        return carry

    lax.fori_loop(0, count, step, 0)


def blank_outside(ref, flags, rows, cols):
    height, width = ref.shape[0], ref.shape[1]

    @pl.when(flags[0] == 1)
    def _():
        ref[0:rows] = jnp.zeros((rows,) + ref.shape[1:], ref.dtype)

    @pl.when(flags[1] == 1)
    def _():
        ref[height - rows : height] = jnp.zeros((rows,) + ref.shape[1:], ref.dtype)

    @pl.when(flags[2] == 1)
    def _():
        ref[:, 0:cols] = jnp.zeros((height, cols) + ref.shape[2:], ref.dtype)

    @pl.when(flags[3] == 1)
    def _():
        ref[:, width - cols : width] = jnp.zeros((height, cols) + ref.shape[2:], ref.dtype)


def blank_ends(ref):
    height, width = ref.shape[0], ref.shape[1]
    ref[:, 0:1] = jnp.zeros((height, 1) + ref.shape[2:], ref.dtype)
    ref[:, width - 1 : width] = jnp.zeros((height, 1) + ref.shape[2:], ref.dtype)


def local_stats(v, count):
    mean = fold(col_sum(v)) / count
    centred = v - mean
    return mean, fold(col_sum(centred * centred))


def merge_stats(pay, local_count, pixel_count):
    devices = pay.shape[0]
    whole = col_sum(pay)
    mean = spread(whole, 0) / devices
    away = pay - mean
    between = spread(col_sum(away * away), 0)
    spread_sum = spread(whole, 1) + local_count * between
    return mean, lax.rsqrt(spread_sum / pixel_count + norm_eps)


def three(first, second, third):
    group = group_of(first.shape)
    return jnp.where(group == 0, first, jnp.where(group == 1, second, third))


def prepare(w_first, w_convs, w_style, w_head, table, banded, skip, taps, back, head_mat, head_bias, style_mat, tab):
    blocks = banded.shape[2] // LANES
    col = row_of((PITCH, LANES))
    out_col = group_of((PITCH, LANES))
    first = [[tile4(low(w_first[t][c : c + 1])) for c in range(2)] for t in range(10)]

    def one(j):
        at = pl.ds(pl.multiple_of(j * LANES, LANES), LANES)
        here = col - GRP * j - out_col
        for c in range(2):
            part = pl.ds(c * PITCH, PITCH)
            for r in range(3):
                val = jnp.zeros((PITCH, LANES), F32)
                for s in range(3):
                    val = jnp.where(here == s - 1, first[3 * r + s][c], val)
                banded[r, part, at] = val.astype(BF16)
            skip[part, at] = jnp.where(here == 0, first[9][c], 0.0).astype(BF16)

    loop(blocks, one)

    group = group_of((CH, LANES))

    def layer(i):
        for r in range(3):
            ks = [w_convs[i, 3 * r + s] for s in range(3)]
            wide = [tile4(k) for k in ks]
            tall = [jnp.concatenate([k, k, k, k], axis=0).T for k in ks]
            for d in range(3):
                for a in range(GRP):
                    at = (3 * r + d) * LANES + CH * a
                    val = jnp.zeros((CH, LANES), F32)
                    inv = jnp.zeros((CH, LANES), F32)
                    for s in range(3):
                        val = jnp.where(group == GRP * (d - 1) + a + 1 - s, wide[s], val)
                        inv = jnp.where(group == s - 1 + a - GRP * (d - 1), tall[s], inv)
                    taps[i, at : at + CH, :] = val.astype(BF16)
                    back[i, at : at + CH, :] = inv.astype(BF16)

    loop(3, layer)

    lane = lane_of((CH, 2 * LANES))
    head = jnp.zeros((CH, 2 * LANES), F32)
    bias = jnp.zeros((1, 2 * LANES), F32)
    for k in range(3):
        head = jnp.where((lane >> 6) == k, low(w_head[0:CH, k : k + 1]), head)
        bias = jnp.where((lane[0:1] >> 6) == k, low(w_head[CH : CH + 1, k : k + 1]), bias)
    head_bias[...] = bias
    for j in range(head_mat.shape[0] // LANES):
        for b in range(GRP):
            at = j * LANES + CH * b
            hit = (lane & 63) == GRP * (j + 1) + b
            head_mat[at : at + CH, :] = jnp.where(hit, head, 0.0).astype(BF16)
    for i in range(2):
        wide = tile4(w_style[i])
        for b in range(GRP):
            style_mat[i, CH * b : CH * b + CH, :] = jnp.where(group == b, wide, 0.0)
    for i in range(2):
        tab[4 * i : 4 * i + 4, :] = tile4(table[i])


def start_kernel(up, own, down, banded, valid, image, pay, *, local_count):
    rim, height, images = up.shape[0], own.shape[0], own.shape[1]
    image[0:rim] = up[:, :, 0:LANES]
    image[rim : rim + height] = own[:, :, 0:LANES]
    image[rim + height : rim + height + rim] = down[:, :, 0:LANES]
    blocks = banded.shape[2] // LANES - 4
    lo = 2 * LANES
    y = jnp.zeros((height * images, blocks * LANES), F32)
    for r in range(3):
        x = image[rim - 1 + r : rim - 1 + r + height].reshape(height * images, LANES)
        y = y + jnp.dot(x, banded[r, :, lo : lo + blocks * LANES], preferred_element_type=F32)
    total = jnp.zeros((1, LANES), F32)
    for j in range(blocks):
        total = total + col_sum(y[:, j * LANES : (j + 1) * LANES])
    mean = fold(total) / local_count
    square = jnp.zeros((1, LANES), F32)
    for j in range(blocks):
        centred = y[:, j * LANES : (j + 1) * LANES] - mean
        square = square + col_sum(centred * centred)
    count = jnp.sum(valid[...].astype(F32))
    row = three(mean, fold(square), jnp.full((1, LANES), count, F32))
    pay[...] = jnp.broadcast_to(row.reshape(1, 1, LANES), pay.shape)


def first_kernel(flags, got, image, banded, skip, taps, tab, hidden, xhat, summed, pay, vec, *, local_count, pixel_count):
    mean, inverse = merge_stats(got[:, 0, :], local_count, pixel_count)
    vec[...] = jnp.broadcast_to(inverse, vec.shape)
    gain, bias = tab[0:1], tab[4:5]
    rows, images = hidden.shape[0], hidden.shape[2]
    blocks = hidden.shape[1] - 2
    height = xhat.shape[0]
    rim = (rows - height) // 2

    def pair(jp):
        at = pl.ds(pl.multiple_of(jp * 2 * LANES, 2 * LANES), 2 * LANES)
        y = jnp.zeros((rows * images, 2 * LANES), F32)
        for r in range(3):
            x = image[r : r + rows].reshape(rows * images, LANES)
            y = y + jnp.dot(x, banded[r, :, at], preferred_element_type=F32)
        for half in range(2):
            norm = (y[:, half * LANES : (half + 1) * LANES] - mean) * inverse
            n = norm * gain + bias
            h = (n * sig_of(n)).astype(BF16)
            hidden[:, pl.ds(2 * jp + half + 1, 1)] = h.reshape(rows, 1, images, LANES)
            xhat[:, pl.ds(2 * jp + half, 1)] = norm[rim * images : (rim + height) * images].reshape(
                height, 1, images, LANES
            )

    loop(blocks // 2, pair)
    blank_ends(hidden)
    blank_outside(hidden, flags, rim, 3)
    out_rows = summed.shape[0]
    step = 4

    def chunk(i):
        row = i * step
        y = conv(hidden, taps, row, step, 0, blocks)
        x = image[pl.ds(row + 2, step)].reshape(step * images, LANES)
        side = jnp.dot(x, skip[...], preferred_element_type=F32).reshape(step, images, blocks * LANES)
        for j in range(blocks):
            summed[pl.ds(row, step), j] = y[:, j] + side[:, :, j * LANES : (j + 1) * LANES]

    loop(out_rows // step, chunk)
    low_row = (out_rows - height) // 2
    own = flat(summed[low_row : low_row + height, 2 : blocks - 2])
    m, s = local_stats(own, local_count)
    row = three(m, s, jnp.zeros((1, LANES), F32))
    pay[...] = jnp.broadcast_to(row.reshape(1, 1, LANES), pay.shape)


def pool_kernel(
    flags, got, summed, taps, tab, merged, xhat, slopes, shared, raw, pay, vec, *, local_count, pixel_count
):
    mean, inverse = merge_stats(got[:, 0, :], local_count, pixel_count)
    vec[...] = jnp.broadcast_to(inverse, vec.shape)
    gain, bias = tab[1:2], tab[5:6]
    rows, blocks, images = summed.shape[0], summed.shape[1], summed.shape[2]
    kept = xhat.shape[0]
    height = kept - 4
    skip_rows = (rows - kept) // 2

    def work(p, keep, own):
        xs, es, ns, ss = [], [], [], []
        for half in range(2):
            x = (flat(summed[2 * p + half]) - mean) * inverse
            n = x * gain + bias
            s = sig_of(n)
            xs.append(x)
            ns.append(n)
            ss.append(s)
            es.append(n * s)
        top = jnp.maximum(es[0], es[1])
        top = jnp.maximum(top, partner(top))
        exps = [jnp.exp(e - top) for e in es]
        whole = exps[0] + exps[1]
        whole = whole + partner(whole)
        pooled = top + jnp.log(whole)
        for half in range(2):
            m = (es[half] + pooled).astype(BF16)
            merged[pl.ds(2 * p + half, 1), 1 : blocks + 1] = m.reshape(1, blocks, images, LANES)
        if not keep:
            return None
        over = 1.0 / whole
        sums = []
        for half in range(2):
            ds = slope(ns[half], ss[half])
            sh = exps[half] * over * ds
            at = pl.ds(2 * p + half - skip_rows, 1)
            cut = lambda v: v.reshape(1, blocks, images, LANES)[:, 1 : blocks - 1]
            xhat[at] = cut(xs[half])
            slopes[at] = cut(ds)
            shared[at] = cut(sh)
            if own:
                sums.append((sh, sh * xs[half]))
        if not own:
            return None
        inner = lambda v: jnp.sum(v.reshape(blocks, images, LANES)[2 : blocks - 2], axis=0)
        return inner(pooled), inner(sums[0][0] + sums[1][0]), inner(sums[0][1] + sums[1][1])

    edge = skip_rows // 2
    own_lo = edge + 1
    own_pairs = height // 2

    def outer(i):
        work(i, False, False)
        work(rows // 2 - 1 - i, False, False)

    loop(edge, outer)
    work(edge, True, False)
    work(own_lo + own_pairs, True, False)

    def inner_step(i, carry):
        found = work(own_lo + i, True, True)
        return tuple(a + b for a, b in zip(carry, found))

    zero = jnp.zeros((images, LANES), F32)
    pool_sum, share_sum, share_x = lax.fori_loop(0, own_pairs, inner_step, (zero, zero, zero))
    blank_ends(merged)
    blank_outside(merged, flags, (rows - height) // 2, 3)
    out_rows = raw.shape[0]
    step = 3

    def chunk(i):
        raw[pl.ds(i * step, step)] = conv(merged, taps, i * step, step, 0, blocks)

    loop(out_rows // step, chunk)
    low_row = (out_rows - height) // 2
    own = raw[low_row : low_row + height, 2 : blocks - 2].reshape(-1, images, LANES)
    per_image = float(own.shape[0] * GRP)
    centre = fold(jnp.sum(own, axis=0)) / per_image
    away = own - centre[None]
    square = fold(col_sum(jnp.sum(away * away, axis=0)))
    devices = pay.shape[0]
    pay[:, 0] = jnp.broadcast_to(pack_images(centre)[None], (devices, 4, LANES))
    pay[:, 1] = jnp.broadcast_to(pack_images(0.5 * fold(pool_sum))[None], (devices, 4, LANES))
    pay[:, 2] = jnp.broadcast_to(square[None], (devices, 4, LANES))
    slots = jnp.concatenate([fold(share_sum), fold(share_x)], axis=0)
    pay[0 : 2 * images, 2, 1, :] = slots


def style_kernel(
    flags, got, raw, merged, taps, tab, style_mat, hidden, xhat, resid, pay, vec, style_out, *, local_count, pixel_count, pool_cells
):
    devices = got.shape[0]
    rows, blocks, images = raw.shape[0], raw.shape[1], raw.shape[2]
    centres = got[:, 0]
    packed = jnp.sum(centres, axis=0) / devices
    away = centres - packed[None]
    within = fold(col_sum(jnp.sum(away * away, axis=0)))
    style = unpack_images(jnp.sum(got[:, 1], axis=0)) / pool_cells
    style_out[...] = style
    one = jnp.dot(style, style_mat[0], precision=highest, preferred_element_type=F32)
    two = jnp.dot(style, style_mat[1], precision=highest, preferred_element_type=F32)
    centre = unpack_images(packed) + one
    mean = col_sum(centre) / images
    off = centre - mean
    between = col_sum(off * off)
    tail = jnp.sum(got[:, 2], axis=0)
    spread_sum = tail[0:1] + (local_count / images) * within + (pixel_count / images) * between
    inverse = lax.rsqrt(spread_sum / pixel_count + norm_eps)
    vec[...] = jnp.broadcast_to(inverse, vec.shape)
    gain, bias = tab[2:3], tab[6:7]
    shift = one - mean
    kept = xhat.shape[0]
    drop = (rows - kept) // 2

    def norm_row(i, keep):
        x = (raw[i] + shift[None]) * inverse[None]
        n = x * gain[None] + bias[None]
        h = (n * sig_of(n)).astype(BF16)
        hidden[i, 1 : blocks + 1] = h
        if keep:
            xhat[i - drop] = x[1 : blocks - 1]

    for i in range(drop):
        norm_row(i, False)
        norm_row(rows - 1 - i, False)
    loop(kept, lambda i: norm_row(i + drop, True))
    blank_ends(hidden)
    height = kept - 6
    blank_outside(hidden, flags, (rows - height) // 2, 3)
    out_rows = resid.shape[0]
    step = 4

    def chunk(i):
        row = i * step
        y = conv(hidden, taps, row, step, 1, blocks - 2)
        m = merged[pl.ds(row + 2, step), 2 : blocks].astype(F32)
        resid[pl.ds(row, step)] = y + two[None, None] + m

    loop(out_rows // step, chunk)
    low_row = (out_rows - height) // 2
    own = flat(resid[low_row : low_row + height, 1 : blocks - 3])
    m, s = local_stats(own, local_count)
    row = three(m, s, tail[1:2])
    pay[...] = jnp.broadcast_to(row.reshape(1, 1, LANES), pay.shape)


def head_kernel(
    got, got_count, resid, up, own, down, head_mat, head_bias, tab, grad, xhat, pay, vec, decoded, slopes, *, local_count, pixel_count
):
    mean, inverse = merge_stats(got[:, 0, :], local_count, pixel_count)
    vec[...] = jnp.broadcast_to(inverse, vec.shape)
    gain, bias = tab[3:4], tab[7:8]
    rows, blocks, images = resid.shape[0], resid.shape[1], resid.shape[2]
    height = own.shape[0]
    rim = (rows - height) // 2
    step = 2

    def norm_rows(i):
        at = pl.ds(i * step, step)
        x = (resid[at] - mean) * inverse
        n = x * gain + bias
        s = sig_of(n)
        xhat[at] = x
        slopes[at] = slope(n, s)
        decoded[at] = (n * s).astype(BF16)

    loop(rows // step, norm_rows)
    wide = jnp.concatenate([decoded[:, j].reshape(rows * images, LANES) for j in range(blocks)], axis=1)
    out = jnp.dot(wide, head_mat[...], preferred_element_type=F32) + head_bias[...]
    sides = jnp.concatenate([up[rim:], own[...], down[:rim]], axis=0)
    sides = sides.reshape(rows * images, 3 * LANES).astype(F32)
    target = sides[:, LANES : 2 * LANES] / flow_scale
    tail = sides[:, 2 * LANES :]
    swapped = pltpu.roll(tail, 64, axis=1)
    lane = lane_of(tail.shape)
    first_half = lane < 64
    mask = jnp.where(first_half, swapped, tail)
    column = lane & 63
    count = jnp.sum(got_count[:, 0, 64:65])
    diff = out[:, 0:LANES] - target
    logit = out[:, LANES:]
    label = tail
    hinge = jnp.maximum(logit, 0.0) + jnp.log1p(jnp.exp(-jnp.abs(logit)))
    loss = mask * diff * diff + jnp.where(first_half, mask * (hinge - label * logit), 0.0)
    grad_flow = (2.0 * mask * diff / count).astype(BF16)
    grad_logit = jnp.where(first_half, mask * (sig_of(logit) - label) / count, 0.0).astype(BF16)
    grad_out = jnp.concatenate([grad_flow, grad_logit], axis=1)
    mine = slice(rim * images, (rim + height) * images)
    inside = (column >= 8) & (column < 8 + GRP * (blocks - 2))
    loss_sum = jnp.sum(jnp.where(inside, loss, 0.0)[mine])
    mine_out = grad_out[mine]
    acc = jnp.zeros((2 * LANES, LANES), F32)
    at_col = (row_of((2 * LANES, LANES)) & 63) - group_of((2 * LANES, LANES))
    for j in range(1, blocks - 1):
        d = decoded[rim : rim + height, j].reshape(height * images, LANES)
        part = lax.dot_general(mine_out, d, (((0,), (0,)), ((), ())), preferred_element_type=F32)
        acc = jnp.where(at_col == GRP * (j + 1), part, acc)
    whole = [fold(col_sum(acc[PITCH * k : PITCH * k + PITCH])) for k in range(3)]
    outs = jnp.where(
        (lane_of((1, 2 * LANES)) & 63 >= 8) & (lane_of((1, 2 * LANES)) & 63 < 8 + GRP * (blocks - 2)),
        col_sum(mine_out.astype(F32)),
        0.0,
    )
    lane_one = lane_of((1, LANES))
    group = lane_one >> 5
    head_row = jnp.where(group == 0, whole[0], jnp.where(group == 1, whole[1], whole[2]))
    biases = [
        jnp.sum(jnp.where(lane_one < 64, outs[:, 0:LANES], 0.0)),
        jnp.sum(jnp.where(lane_one >= 64, outs[:, 0:LANES], 0.0)),
        jnp.sum(outs[:, LANES:]),
    ]
    for k in range(3):
        head_row = jnp.where(lane_one == 3 * CH + k, biases[k], head_row)
    shift_sum = jnp.zeros((1, LANES), F32)
    scale_sum = jnp.zeros((1, LANES), F32)
    for j in range(blocks):
        g = lax.dot_general(
            grad_out, head_mat[j * LANES : (j + 1) * LANES, :], (((1,), (1,)), ((), ())), preferred_element_type=F32
        )
        g = g * slopes[:, j].reshape(rows * images, LANES)
        grad[:, j] = g.reshape(rows, images, LANES)
        if 0 < j < blocks - 1:
            x = xhat[rim : rim + height, j].reshape(height * images, LANES)
            shift_sum = shift_sum + col_sum(g[mine])
            scale_sum = scale_sum + col_sum(g[mine] * x)
    row = three(fold(shift_sum), fold(scale_sum), jnp.full((1, LANES), loss_sum, F32))
    devices = pay.shape[0]
    pay[:, 0, :] = jnp.broadcast_to(row, (devices, LANES))
    pay[:, 1, :] = jnp.broadcast_to(head_row, (devices, LANES))


def back_sums(got):
    whole = col_sum(got)
    return spread(whole, 0), spread(whole, 1)


def residual_back_kernel(
    flags, got, grad, xhat, vec, xhat_below, back, tab, grad_low, below, kept_grad, pay, *, pixel_count
):
    shift, scale = back_sums(got[:, 0, :])
    rows, blocks, images = grad.shape[0], grad.shape[1], grad.shape[2]
    out_rows = below.shape[0]
    height = rows - 8
    factor = tab[3:4] * vec[0:1]
    shift, scale = shift / pixel_count, scale / pixel_count
    kept = kept_grad.shape[0]
    drop = (rows - kept) // 2

    def row_step(i, keep):
        g = factor[None] * (grad[i] - (shift[None] + xhat[i] * scale[None]))
        grad_low[i, 1 : blocks + 1] = g.astype(BF16)
        if keep:
            kept_grad[i - drop] = g

    for i in range(drop):
        row_step(i, False)
        row_step(rows - 1 - i, False)
    loop(kept, lambda i: row_step(i + drop, True))
    blank_ends(grad_low)
    blank_outside(grad_low, flags, (rows - height) // 2, 2)
    gain, bias = tab[2:3], tab[6:7]
    step = 2

    def chunk(i):
        row = i * step
        y = conv(grad_low, back, row, step, 0, blocks, True)
        n = xhat_below[pl.ds(row, step)] * gain + bias
        below[pl.ds(row, step)] = y * slope(n, sig_of(n))

    loop(out_rows // step, chunk)
    low_row = (out_rows - height) // 2
    g = flat(below[low_row : low_row + height, 1 : blocks - 1])
    x = flat(xhat_below[low_row : low_row + height, 1 : blocks - 1])
    mine = grad_low[(rows - height) // 2 : (rows + height) // 2, 2:blocks].astype(F32)
    image_sum = fold(jnp.sum(mine.reshape(-1, images, LANES), axis=0))
    row = three(fold(col_sum(g)), fold(col_sum(g * x)), jnp.zeros((1, LANES), F32))
    pay[...] = jnp.broadcast_to(row.reshape(1, 1, LANES), pay.shape)
    pay[0:images, 0, :] = jnp.where(group_of((images, LANES)) == 2, image_sum, row)


def merged_back_kernel(
    flags, got, grad, xhat, vec, kept_grad, slopes, shared, xhat_below, back, tab, scatter, grad_low, below, pay, *, pixel_count
):
    devices = got.shape[0]
    shift, scale = back_sums(got[:, 0, :])
    slot = spread(col_sum(got[:, 0, :]), 2)
    rows, blocks, images = grad.shape[0], grad.shape[1], grad.shape[2]
    out_rows = below.shape[0]
    height = rows - 6
    factor = tab[2:3] * vec[0:1]
    shift, scale = shift / pixel_count, scale / pixel_count

    def row_step(i):
        g = factor[None] * (grad[i] - (shift[None] + xhat[i] * scale[None]))
        grad_low[i, 1 : blocks + 1] = g.astype(BF16)

    loop(rows, row_step)
    blank_ends(grad_low)
    blank_outside(grad_low, flags, (rows - height) // 2, 2)

    def chunk(i):
        row = i * 2
        at = pl.ds(row, 2)
        g = conv(grad_low, back, row, 2, 0, blocks, True) + kept_grad[at]
        both = flat(g[0] + g[1])
        both = (both + partner(both)).reshape(1, blocks, images, LANES)
        below[at] = g * slopes[at] + both * shared[at]

    loop(out_rows // 2, chunk)
    low_row = (out_rows - height) // 2
    g = flat(below[low_row : low_row + height, 1 : blocks - 1])
    x = flat(xhat_below[low_row : low_row + height, 1 : blocks - 1])
    mine = grad_low[(rows - height) // 2 : (rows + height) // 2, 2:blocks].astype(F32)
    image_sum = fold(jnp.sum(mine.reshape(-1, images, LANES), axis=0))
    row = three(fold(col_sum(g)), fold(col_sum(g * x)), slot)
    pay[:, 0] = jnp.broadcast_to(row[None], (devices, 4, LANES))
    pay[:, 1] = jnp.broadcast_to(pack_images(image_sum)[None], (devices, 4, LANES))
    pay[0:CH, 0, 1:4, :] = scatter[:, 0:3, :]


def tap_sums(field, grad, out):
    rows, blocks = grad.shape[0], grad.shape[1]
    g = flat(grad)
    pieces = [flat(field[r : r + rows, c : c + blocks]) for r in range(3) for c in range(3)]
    found = lax.dot_general(g, jnp.concatenate(pieces, axis=1), (((0,), (0,)), ((), ())), preferred_element_type=F32)
    group = group_of((CH, LANES))
    taps = []
    for r in range(3):
        for s in range(3):
            val = jnp.zeros((CH, LANES), F32)
            for b in range(GRP):
                d, a = divmod(b + s - 1 + GRP, GRP)
                at = (3 * r + d) * LANES
                val = jnp.where(group == a, found[CH * b : CH * b + CH, at : at + LANES], val)
            taps.append(fold(val))
    for q in range(3):
        val = taps[4 * q]
        for b in range(1, min(4, 9 - 4 * q)):
            val = jnp.where(group == b, taps[4 * q + b], val)
        out[:, q, :] = val


def taps_kernel(field, grad, out, *, rows, cols, grad_rows, grad_cols):
    height, width = grad_rows[1] - grad_rows[0], grad_cols[1] - grad_cols[0]
    tap_sums(
        field[rows : rows + height + 2, cols : cols + width + 2],
        grad[grad_rows[0] : grad_rows[1], grad_cols[0] : grad_cols[1]],
        out,
    )


def summed_back_kernel(
    flags, got, got_slots, grad, shared, xhat, vec, style_mat, back, tab, xhat_below, field, scatter, grad_low, below, pay, sums, image_sums, *, pixel_count, pool_cells
):
    devices = got.shape[0]
    rows, blocks, images = grad.shape[0], grad.shape[1], grad.shape[2]
    height = xhat_below.shape[0]
    one = unpack_images(jnp.sum(got[:, 1], axis=0))
    two = spread(got[0:images, 0, 0, :], 2)
    image_sums[0] = one
    image_sums[1] = two
    dims = (((1,), (1,)), ((), ()))
    grad_style = lax.dot_general(one, style_mat[0], dims, precision=highest, preferred_element_type=F32)
    grad_style = grad_style + lax.dot_general(two, style_mat[1], dims, precision=highest, preferred_element_type=F32)
    grad_style = grad_style / pool_cells
    first = jnp.sum(got[:, 0], axis=0)[0:1]
    shift = spread(first, 0) + col_sum(grad_style * spread(got_slots[0:images, 0, :], 2))
    scale = spread(first, 1) + col_sum(grad_style * spread(got_slots[images : 2 * images, 0, :], 2))
    sums[...] = jnp.where(row_of((8, LANES)) == 0, scale, shift)
    factor = tab[1:2] * vec[0:1]
    shift, scale = shift / pixel_count, scale / pixel_count
    out_rows = grad_low.shape[0]

    def row_step(i):
        g = grad[i + 1] + shared[i + 1] * grad_style[None]
        g = factor[None] * (g - (shift[None] + xhat[i + 1] * scale[None]))
        grad_low[i, 1 : blocks + 1] = g.astype(BF16)

    loop(out_rows, row_step)
    blank_ends(grad_low)
    blank_outside(grad_low, flags, 1, 2)
    gain, bias = tab[0:1], tab[4:5]
    step = 4

    def chunk(i):
        row = i * step
        y = conv(grad_low, back, row, step, 1, blocks - 2, True)
        n = xhat_below[pl.ds(row, step), 2:blocks] * gain + bias
        below[pl.ds(row, step)] = y * slope(n, sig_of(n))

    loop(height // step, chunk)
    g = flat(below[...])
    x = flat(xhat_below[:, 2:blocks])
    row = fold(col_sum(g))
    row = three(row, fold(col_sum(g * x)), jnp.zeros((1, LANES), F32))
    gathered = jnp.sum(got[:, 0], axis=0)
    pay[:, 0] = jnp.broadcast_to(jnp.where(row_of((4, LANES)) == 0, row, gathered)[None], (devices, 4, LANES))
    pay[0:CH, 1] = scatter[...]
    if devices > CH:
        pay[CH:, 1] = jnp.zeros((devices - CH, 4, LANES), F32)
        pay[CH:, 2] = jnp.zeros((devices - CH, 4, LANES), F32)
    tap_sums(field[6 : 8 + height, 2 : blocks + 2], grad_low[1 : 1 + height, 2:blocks], pay.at[0:CH, 2])
    pay[0:CH, 2, 3, :] = jnp.zeros((CH, LANES), F32)


def pixel_taps(image, grad, row, shift):
    height, blocks, images = grad.shape[0], grad.shape[1], grad.shape[2]
    x = image[row : row + height].reshape(height * images, LANES)
    found = [jnp.zeros((LANES, LANES), F32) for _ in shift]
    here = (row_of((LANES, LANES)) & 63) - group_of((LANES, LANES))
    for j in range(blocks):
        g = grad[:, j].reshape(height * images, LANES)
        part = lax.dot_general(x, g, (((0,), (0,)), ((), ())), preferred_element_type=F32)
        for k, s in enumerate(shift):
            found[k] = jnp.where(here == GRP * (j + 2) + s, part, found[k])
    return [[fold(col_sum(f[PITCH * c : PITCH * c + PITCH])) for c in range(2)] for f in found]


def first_back_kernel(got, grad, xhat, vec, tab, image, summed_low, pay, *, pixel_count):
    devices = got.shape[0]
    height, blocks = grad.shape[0], grad.shape[1]
    whole = jnp.sum(got[:, 0], axis=0)[0:1]
    shift, scale = spread(whole, 0), spread(whole, 1)
    factor = tab[0:1] * vec[0:1]
    x = xhat[:, 2 : blocks + 2]
    low_grad = (factor * (grad[...] - (shift + x * scale) / pixel_count)).astype(BF16)
    entries = []
    for r in range(3):
        for tap in pixel_taps(image, low_grad, RIM - 1 + r, (-1, 0, 1)):
            entries.extend(tap)
    entries.extend(pixel_taps(image, summed_low[1 : 1 + height, 2 : blocks + 2], RIM, (0,))[0])
    group = group_of((1, LANES))
    rows = []
    for q in range(5):
        val = entries[4 * q]
        for b in range(1, 4):
            val = jnp.where(group == b, entries[4 * q + b], val)
        rows.append(val)
    conv_one = jnp.sum(got[:, 1], axis=0)
    conv_zero = jnp.sum(got[:, 2], axis=0)
    chunk = [
        jnp.concatenate(rows[0:4], axis=0),
        jnp.concatenate([rows[4], conv_one[0:3]], axis=0),
        conv_zero,
    ]
    for k in range(3):
        pay[:, k] = jnp.broadcast_to(chunk[k][None], (devices, 4, LANES))


def adamw(master, moment, square, grad, rate):
    new_moment = beta_one * moment + (1.0 - beta_one) * grad
    new_square = beta_two * square + (1.0 - beta_two) * grad * grad
    moment_hat = new_moment / (1.0 - beta_one**STEP)
    square_hat = new_square / (1.0 - beta_two**STEP)
    new_master = master - rate * (moment_hat / (jnp.sqrt(square_hat) + adam_eps) + weight_decay * master)
    return new_master, new_moment, new_square


def update_kernel(
    got, got_first, got_head, got_two, got_count, sums, style, image_sums,
    w_first, w_convs, w_style, w_head, table,
    m_first, m_convs, m_style, m_head, m_norms,
    s_first, s_convs, s_style, s_head, s_norms,
    loss_out, count_out,
    first_master, first_moment, first_square, first_copy,
    convs_master, convs_moment, convs_square, convs_copy,
    style_master, style_moment, style_square,
    head_master, head_moment, head_square, head_copy,
    norms_master, norms_moment, norms_square,
):
    count_out[0, 0] = jnp.sum(got_count[:, 0, 64:65])
    loss_out[0, 0] = jnp.sum(got_head[:, 0, 64:65])

    def put(at, master, moment, square, grad, rate, outs, copy):
        found = adamw(master[at], moment[at], square[at], grad, rate)
        for out, value in zip(outs, found):
            out[at] = value
        if copy is not None:
            copy[at] = found[0].astype(BF16)

    sources = [got[0:CH, 2, 0:3, :], got[0:CH, 1, 1:4, :], got_first[0:CH, 0, 1:4, :]]
    refs = (w_convs, m_convs, s_convs)
    outs = (convs_master, convs_moment, convs_square)
    for i in range(3):
        for q in range(3):
            taps = min(4, 9 - 4 * q)
            grad = sources[i][:, q, :].T
            for b in range(taps):
                put((i, 4 * q + b), *refs, grad[CH * b : CH * b + CH], rate_table[1], outs, convs_copy)

    first = jnp.concatenate([jnp.sum(got[:, 0], axis=0), jnp.sum(got[:, 1], axis=0)[0:1]], axis=0)
    for t in range(10):
        pair = [spread(first[e // 4 : e // 4 + 1], e % 4)[:, 0:CH] for e in (2 * t, 2 * t + 1)]
        grad = jnp.concatenate(pair, axis=0)
        put((t,), w_first, m_first, s_first, grad, rate_table[0], (first_master, first_moment, first_square), first_copy)

    dims = (((0,), (0,)), ((), ()))
    for i in range(2):
        grad = lax.dot_general(style[...], image_sums[i], dims, precision=highest, preferred_element_type=F32)
        put((i,), w_style, m_style, s_style, grad[0:CH, 0:CH], rate_table[2], (style_master, style_moment, style_square), None)

    head = col_sum(got_head[:, 1, :])
    shape = (40, LANES)
    entry = row_of(shape)
    lane = lane_of(shape)
    grad = jnp.zeros(shape, F32)
    for k in range(3):
        hit = lane == jnp.where(entry < CH, CH * k + entry, 3 * CH + k)
        value = jnp.sum(jnp.where(hit, head, 0.0), axis=1, keepdims=True)
        grad = jnp.where(lane == k, value, grad)
    put((slice(None),), w_head, m_head, s_head, grad[0 : CH + 1, 0:3], rate_table[3], (head_master, head_moment, head_square), head_copy)

    three_sums = col_sum(got_head[:, 0, :])
    two_sums = col_sum(got_two[:, 0, :])
    zero_sums = jnp.sum(got_first[:, 0], axis=0)[0:1]
    scales = [spread(zero_sums, 1), sums[0:1], spread(two_sums, 1), spread(three_sums, 1)]
    shifts = [spread(zero_sums, 0), sums[1:2], spread(two_sums, 0), spread(three_sums, 0)]
    for i, rows in enumerate((scales, shifts)):
        grad = jnp.concatenate(rows, axis=0)[:, 0:CH]
        put((i,), table, m_norms, s_norms, grad, rate_table[4], (norms_master, norms_moment, norms_square), None)


def call(kernel, outs, *operands, scalars=0, scratch=(), scalar_outs=(), name):
    smem = pl.BlockSpec(memory_space=pltpu.SMEM)
    vmem = pl.BlockSpec(memory_space=pltpu.VMEM)
    return pl.pallas_call(
        kernel,
        out_shape=[jax.ShapeDtypeStruct(shape, dtype) for shape, dtype in outs],
        in_specs=[smem] * scalars + [vmem] * (len(operands) - scalars),
        out_specs=[smem if i in scalar_outs else vmem for i in range(len(outs))],
        scratch_shapes=[pltpu.VMEM(shape, dtype) for shape, dtype in scratch],
        compiler_params=pltpu.CompilerParams(vmem_limit_bytes=VMEM_LIMIT),
        name=name,
    )(*operands)


def exchange(pay):
    return lax.all_to_all(pay, ("row", "col"), 0, 0)


def shifted(block, axis):
    count = lax.axis_size(axis)
    forward = [(i, i + 1) for i in range(count - 1)]
    backward = [(target, source) for source, target in forward]
    return forward, backward


def local(
    image_batch, valid_mask, flow_target, cell_labels,
    w_first, w_convs, w_style, w_head, batch_norm_table,
    mom_first, mom_convs, mom_style, mom_head, mom_norms,
    sqr_first, sqr_convs, sqr_style, sqr_head, sqr_norms,
):
    images, height, width, _ = image_batch.shape
    devices = lax.axis_size("row") * lax.axis_size("col")
    local_count = float(images * height * width)
    pixel_count = local_count * devices
    pool_cells = float(height * width * devices // 4)
    blocks = width // GRP
    wide = blocks + 4
    part = functools.partial
    counts = dict(local_count=local_count, pixel_count=pixel_count)

    row, col = lax.axis_index("row"), lax.axis_index("col")
    flags = jnp.stack(
        [row == 0, row == lax.axis_size("row") - 1, col == 0, col == lax.axis_size("col") - 1]
    ).astype(jnp.int32)

    sides = jnp.concatenate(
        [
            jnp.transpose(image_batch, (1, 0, 3, 2)),
            jnp.transpose(flow_target.astype(BF16), (1, 0, 3, 2)),
            jnp.transpose(cell_labels.astype(BF16), (1, 0, 2))[:, :, None],
            jnp.transpose(valid_mask.astype(BF16), (1, 0, 2))[:, :, None],
        ],
        axis=2,
    )
    forward, backward = shifted(sides, "col")
    left = lax.ppermute(sides[..., width - RIM :], "col", forward)
    right = lax.ppermute(sides[..., :RIM], "col", backward)
    gap = jnp.zeros(sides.shape[:3] + (PITCH - width - 2 * RIM,), BF16)
    own = jnp.concatenate([left, sides, right, gap], axis=3).reshape(height, images, 6 * PITCH)
    forward, backward = shifted(own, "row")
    up = lax.ppermute(own[height - RIM :], "row", forward)
    down = lax.ppermute(own[:RIM], "row", backward)

    banded, skip, taps, back, head_mat, head_bias, style_mat, tab = call(
        prepare,
        [
            ((3, LANES, wide * LANES), BF16),
            ((LANES, wide * LANES), BF16),
            ((3, 9 * LANES, LANES), BF16),
            ((3, 9 * LANES, LANES), BF16),
            (((blocks + 2) * LANES, 2 * LANES), BF16),
            ((1, 2 * LANES), F32),
            ((2, LANES, LANES), F32),
            ((8, LANES), F32),
        ],
        w_first, w_convs, w_style, w_head, batch_norm_table,
        name="prepare",
    )

    tail = (images, LANES)
    vec = ((8, LANES), F32)
    one_row = ((devices, 1, LANES), F32)
    image, pay = call(
        part(start_kernel, local_count=local_count),
        [((height + 2 * RIM, images, LANES), BF16), one_row],
        up, own, down, banded, valid_mask,
        name="image_stats",
    )
    got_zero = exchange(pay)

    hidden_one, xhat_zero, summed, pay, inv_zero = call(
        part(first_kernel, **counts),
        [
            ((height + 14, wide + 2) + tail, BF16),
            ((height, wide) + tail, F32),
            ((height + 12, wide) + tail, F32),
            one_row,
            vec,
        ],
        flags, got_zero, image, banded, skip, taps[0], tab,
        scalars=1, name="first_block",
    )
    got_one = exchange(pay)

    near = ((height + 4, blocks + 2) + tail, F32)
    merged, xhat_one, slope_one, shared, raw, pay, inv_one = call(
        part(pool_kernel, **counts),
        [
            ((height + 12, wide + 2) + tail, BF16),
            near,
            near,
            near,
            ((height + 10, wide) + tail, F32),
            ((devices, 3, 4, LANES), F32),
            vec,
        ],
        flags, got_one, summed, taps[1], tab,
        scalars=1, name="pool_and_merge",
    )
    got_style = exchange(pay)

    hidden_three, xhat_two, resid, pay, inv_two, style = call(
        part(style_kernel, pool_cells=pool_cells, **counts),
        [
            ((height + 10, wide + 2) + tail, BF16),
            ((height + 6, blocks + 2) + tail, F32),
            ((height + 8, blocks + 2) + tail, F32),
            one_row,
            vec,
            (tail, F32),
        ],
        flags, got_style, raw, merged, taps[2], tab, style_mat,
        scalars=1, name="decoder",
    )
    got_three = exchange(pay)

    at_head = ((height + 8, blocks + 2) + tail, F32)
    grad_three, xhat_three, pay, inv_three = call(
        part(head_kernel, **counts),
        [at_head, at_head, ((devices, 2, LANES), F32), vec],
        got_three, got_zero, resid, up, own, down, head_mat, head_bias, tab,
        scratch=[((height + 8, blocks + 2) + tail, BF16), at_head],
        name="head",
    )
    got_head = exchange(pay)

    low_two, grad_two, grad_resid, pay = call(
        part(residual_back_kernel, pixel_count=pixel_count),
        [
            ((height + 8, wide) + tail, BF16),
            ((height + 6, blocks + 2) + tail, F32),
            near,
            one_row,
        ],
        flags, got_head, grad_three, xhat_three, inv_three, xhat_two, back[2], tab,
        scalars=1, name="residual_back",
    )
    got_two = exchange(pay)
    (taps_two,) = call(
        part(taps_kernel, rows=4, cols=2, grad_rows=(4, 4 + height), grad_cols=(2, 2 + blocks)),
        [((CH, 4, LANES), F32)],
        hidden_three, low_two,
        name="taps_two",
    )

    low_one, grad_one, pay = call(
        part(merged_back_kernel, pixel_count=pixel_count),
        [((height + 6, wide) + tail, BF16), near, ((devices, 2, 4, LANES), F32)],
        flags, got_two, grad_two, xhat_two, inv_two, grad_resid, slope_one, shared, xhat_one, back[1], tab, taps_two,
        scalars=1, name="merged_back",
    )
    got_one_back = exchange(pay)
    (taps_one,) = call(
        part(taps_kernel, rows=5, cols=2, grad_rows=(3, 3 + height), grad_cols=(2, 2 + blocks)),
        [((CH, 4, LANES), F32)],
        merged, low_one,
        name="taps_one",
    )

    low_zero, grad_zero, pay, sums_one, image_sums = call(
        part(summed_back_kernel, pixel_count=pixel_count, pool_cells=pool_cells),
        [
            ((height + 2, wide) + tail, BF16),
            ((height, blocks) + tail, F32),
            ((devices, 3, 4, LANES), F32),
            vec,
            ((2,) + tail, F32),
        ],
        flags, got_one_back, got_three, grad_one, shared, xhat_one, inv_one, style_mat, back[0], tab, xhat_zero,
        hidden_one, taps_one,
        scalars=1, name="summed_back",
    )
    got_first = exchange(pay)

    (pay,) = call(
        part(first_back_kernel, pixel_count=pixel_count),
        [((devices, 3, 4, LANES), F32)],
        got_first, grad_zero, xhat_zero, inv_zero, tab, image, low_zero,
        name="first_back",
    )
    got_last = exchange(pay)

    params = (w_first, w_convs, w_style, w_head, batch_norm_table)
    moments = (mom_first, mom_convs, mom_style, mom_head, mom_norms)
    squares = (sqr_first, sqr_convs, sqr_style, sqr_head, sqr_norms)
    outs = [((1, 1), F32), ((1, 1), F32)]
    for index, param in enumerate(params):
        outs += [(param.shape, F32)] * 3
        if index in (0, 1, 3):
            outs.append((param.shape, BF16))
    found = call(
        update_kernel,
        outs,
        got_last, got_first, got_head, got_two, got_zero, sums_one, style, image_sums,
        *params, *moments, *squares,
        scalar_outs=(0, 1), name="update",
    )
    return (found[0].reshape(()), found[1].reshape(())) + tuple(found[2:])


def solution(mesh):
    field = P(None, "row", "col", None)
    plane = P(None, "row", "col")
    return jax.shard_map(
        local,
        mesh=mesh,
        in_specs=(field, plane, field, plane) + (P(),) * 15,
        out_specs=(P(),) * 20,
        check_vma=False,
    )
```

time: 951 us -> 198 us (0.21); the launches traced: 939 us -> 197 us
  blocking collectives: 654 us -> 39.5 us
  matrix products: 60 us -> 0 us
  other arithmetic: 61.5 us -> 5.95 us
  Pallas kernels: 0 us -> 40.7 us
  starting transfers between devices: 59.8 us -> 28.2 us
  waiting for transfers between devices: 58.3 us -> 35.1 us
  local copies, waits for them, and re-layouts: 28.8 us -> 45.6 us
  between operations: 16.7 us -> 1.51 us
    psum x16 -> x0, blocking collectives: 654 us -> none  [the longest x4 167 us: norm_back(): lax.psum((jnp.sum(grad_norm, axis=(0, 1, 2)), jnp.sum(grad_norm * normal_...]
    ppermute x28 -> x4, starting transfers between devices: 59.8 us -> 9.17 us  [the longest x1 4.23 us: local(): up = lax.ppermute(own[height - RIM:], 'row', forward)]
    pallas_call x0 -> x13, Pallas kernels: none -> 40.7 us  [call(): pl.pallas_call(kernel, out_shape=[jax.ShapeDtypeStruct(shape, dtype) for...]
    dot_general x47 -> x0, matrix products: 39.7 us -> none  [the longest x36 29.3 us: tap_grads(): jnp.einsum('bhwc,bhwd->cd', padded[:, tap_row:tap_row + row_count, tap_co...]
    all_to_all x0 -> x4, blocking collectives: none -> 39.5 us  [exchange(): return lax.all_to_all(pay, ('row', 'col'), 0, 0)]
    all_to_all x0 -> x5, waiting for transfers between devices: none -> 30.7 us  [exchange(): return lax.all_to_all(pay, ('row', 'col'), 0, 0)]
    psum x1 -> x0, waiting for transfers between devices: 28.7 us -> none  [local(): lax.psum((first_grad, jnp.stack([conv_one, conv_two, conv_three]), head_g...]
    reduce_sum x15 -> x0, other arithmetic: 26.7 us -> none  [the longest x3 8.46 us: norm_back(): jnp.sum(grad_norm, axis=(0, 1, 2))]
  transfers between devices with their start and end apart: 29 -> 9, of which waited for: 12 -> 7; matrix products, arithmetic and copies ran while one was open for 5% -> 2% of each run, Pallas kernels for 0% -> 2%
where the time goes in v2:
time: 198 us; the launch traced here: 197 us
  local copies, waits for them, and re-layouts  45.6 us (23%)
  Pallas kernels  40.7 us (21%)
  blocking collectives  39.5 us (20%)
  waiting for transfers between devices  35.1 us (18%)
  starting transfers between devices  28.2 us (14%)
  other arithmetic  5.95 us (3%)
    unnamed x203, local copies, waits for them, and re-layouts  41.5 us
    pallas_call x13, Pallas kernels, call(): pl.pallas_call(kernel, out_shape=[jax.ShapeDtypeStruct(shape, dtype) for...  40.7 us
    all_to_all x4, blocking collectives, exchange(): return lax.all_to_all(pay, ('row', 'col'), 0, 0)  39.5 us
    all_to_all x5, waiting for transfers between devices, exchange(): return lax.all_to_all(pay, ('row', 'col'), 0, 0)  30.7 us
    all_to_all x5, starting transfers between devices, exchange(): return lax.all_to_all(pay, ('row', 'col'), 0, 0)  19 us
    ppermute x1, waiting for transfers between devices, local(): down = lax.ppermute(own[:RIM], 'row', backward)  4.32 us
    ppermute x1, starting transfers between devices, local(): up = lax.ppermute(own[height - RIM:], 'row', forward)  4.23 us
  transfers between devices with their start and end apart: 9, of which 7 were waited for; matrix products, arithmetic and copies ran while one was open for 2% of the time, Pallas kernels for 2%

profile of v2, /device:TPU:0, one launch (start us, length us, event | category | flops | bytes accessed | tf_op | source)
XLA Modules:
  0.0 196.7 jit_solution(9968043391784355174)
XLA Ops:
  5.7 2.4 %collective-permute-start = (bf16[8,16,6,8]{3,2,0,1:T(8,128)(2,1)}, bf16[8,16,6,8]{3,2,0,1:T(8,128)(2,1)S(1)}, u32[]{:S(2)}, u32[]{:S(2)}) collective-permute-start(bf16[8,16,6,8]{3,2,0,1:T(8,128)(2,1)} %get-tuple-element.194), channel_id=1, source_target_pairs={{0,1},{1,2},{2,3},{4,5},{5,6},{6,7},{8,9},{9,10},{10,11},{12,13},{... | collective-permute-start | bytes 36872 | tf_op jit(solution)/shard_map/ppermute | solution.py:869
  16.1 4.2 %collective-permute-start.2 = (bf16[8,16,384]{2,1,0:T(8,128)(2,1)S(1)}, bf16[8,16,384]{2,1,0:T(8,128)(2,1)S(1)}, u32[]{:S(2)}, u32[]{:S(2)}) collective-permute-start(bf16[8,16,384]{2,1,0:T(8,128)(2,1)S(1)} %copy.61.own), channel_id=1, source_target_pairs={{0,4},{4,8},{8,12},{12,16},{16,20},{20,24},{24,28},{1,5},{5,9},{9,... | collective-permute-start | bytes 294920 | tf_op jit(solution)/shard_map/ppermute | solution.py:874
  22.6 4.3 %collective-permute-done.3.down = bf16[8,16,384]{2,1,0:T(8,128)(2,1)S(1)} collective-permute-done((bf16[8,16,384]{2,1,0:T(8,128)(2,1)S(1)}, bf16[8,16,384]{2,1,0:T(8,128)(2,1)S(1)}, u32[]{:S(2)}, u32[]{:S(2)}) %collective-permute-start.3) | collective-permute-done | bytes 98336 | tf_op jit(solution)/shard_map/ppermute | solution.py:875
  28.3 8.2 %all-to-all-start = ((f32[32,1,128]{2,1,0:T(1,128)}), f32[32,1,128]{2,1,0:T(1,128)S(1)}, u32[]{:S(2)}, u32[]{:S(2)}) async-start(f32[32,1,128]{2,1,0:T(1,128)} %get-tuple-element.85), calls=%async_computation | async-start | bytes 32768 | tf_op jit(solution)/shard_map/all_to_all | solution.py:828
  36.6 7.0 %all-to-all-done.got.got_count = f32[32,1,128]{2,1,0:T(1,128)S(1)} async-done(((f32[32,1,128]{2,1,0:T(1,128)}), f32[32,1,128]{2,1,0:T(1,128)S(1)}, u32[]{:S(2)}, u32[]{:S(2)}) %all-to-all-start) | async-done | bytes 16416 | tf_op jit(solution)/shard_map/all_to_all | solution.py:828
  43.6 7.1 %first_block.1 = (bf16[22,14,16,128]{3,2,1,0:T(8,128)(2,1)S(1)}, f32[8,12,16,128]{3,2,1,0:T(8,128)S(1)}, f32[20,12,16,128]{3,2,1,0:T(8,128)S(1)}, f32[32,1,128]{2,1,0:T(1,128)S(1)}, f32[8,128]{1,0:T(8,128)S(1)}) custom-call(s32[4]{0:T(128)S(1)} %add_convert_fusion.flags, f32[32,1,128]{2,1,0:T(1,128)S(1)} %all-to-all-done.got.got_count, ...), custom_call_target="tpu_custom_call" | custom-call | tf_op jit(solution)/shard_map/first_block/pallas_call | solution.py:816
  51.8 8.8 %all_to_all.45.got = f32[32,1,128]{2,1,0:T(1,128)S(1)} all-to-all(f32[32,1,128]{2,1,0:T(1,128)S(1)} %get-tuple-element.90), channel_id=1, replica_groups=mesh['row'=8,'col'=4] {'row','col'}, dimensions={0} | all-to-all | bytes 32768 | tf_op jit(solution)/shard_map/all_to_all | solution.py:828
  60.6 7.0 %pool_and_merge.1 = (bf16[20,14,16,128]{3,2,1,0:T(8,128)(2,1)S(1)}, f32[12,10,16,128]{3,2,1,0:T(8,128)S(1)}, f32[12,10,16,128]{3,2,1,0:T(8,128)S(1)}, f32[12,10,...) custom-call(s32[4]{0:T(128)S(1)} %add_convert_fusion.flags, ...), custom_call_target="tpu_custom_call" | custom-call | tf_op jit(solution)/shard_map/pool_and_merge/pallas_call | solution.py:816
  69.6 10.6 %all_to_all.46.got = f32[32,3,4,128]{3,2,1,0:T(4,128)S(1)} all-to-all(f32[32,3,4,128]{3,2,1,0:T(4,128)S(1)} %get-tuple-element.92), channel_id=1, replica_groups=mesh['row'=8,'col'=4] {'row','col'}, dimensions={0} | all-to-all | bytes 393216 | tf_op jit(solution)/shard_map/all_to_all | solution.py:828
  80.3 4.7 %decoder.1 = (bf16[18,14,16,128]{3,2,1,0:T(8,128)(2,1)S(1)}, f32[14,10,16,128]{3,2,1,0:T(8,128)S(1)}, f32[16,10,16,128]{3,2,1,0:T(8,128)S(1)}, f32[32,1,128]{2,1...) custom-call(s32[4]{0:T(128)S(1)} %add_convert_fusion.flags, f32[32,3,4,128]{3,2,1,0:T(4,128)S(1)} %all_to_all.46.got, ...), custom_call_target="tpu_custom_call" | custom-call | tf_op jit(solution)/shard_map/decoder/pallas_call | solution.py:816
  87.2 9.5 %all_to_all.47.got.got_slots = f32[32,1,128]{2,1,0:T(1,128)S(1)} all-to-all(f32[32,1,128]{2,1,0:T(1,128)S(1)} %get-tuple-element.96), channel_id=1, replica_groups=mesh['row'=8,'col'=4] {'row','col'}, dimensions={0} | all-to-all | bytes 32768 | tf_op jit(solution)/shard_map/all_to_all | solution.py:828
  96.7 2.4 %head.1 = (f32[16,10,16,128]{3,2,1,0:T(8,128)S(1)}, f32[16,10,16,128]{3,2,1,0:T(8,128)S(1)}, f32[32,2,128]{2,1,0:T(2,128)S(1)}, f32[8,128]{1,0:T(8,128)S(1)}) custom-call(f32[32,1,128]{2,1,0:T(1,128)S(1)} %all_to_all.47.got.got_slots, f32[32,1,128]{2,1,0:T(1,128)S(1)} %all-to-all-done.got.got_count, f32[16,10,16,128]{3,2,1,0:T(8,128)S(1)} %get-tuple-element.97.resid, ...), custom_call_target="tpu_custom_call" | custom-call | tf_op jit(solution)/shard_map/head/pallas_call | solution.py:816
  102.5 2.7 %all-to-all-start.4 = ((f32[32,2,128]{2,1,0:T(2,128)}), f32[32,2,128]{2,1,0:T(2,128)S(1)}, u32[]{:S(2)}, u32[]{:S(2)}) async-start(f32[32,2,128]{2,1,0:T(2,128)} %copy-done.66), calls=%async_computation.4 | async-start | bytes 65536 | tf_op jit(solution)/shard_map/all_to_all | solution.py:828
  107.3 5.2 %all-to-all-done.4.got.got_head = f32[32,2,128]{2,1,0:T(2,128)S(1)} async-done(((f32[32,2,128]{2,1,0:T(2,128)}), f32[32,2,128]{2,1,0:T(2,128)S(1)}, u32[]{:S(2)}, u32[]{:S(2)}) %all-to-all-start.4) | async-done | bytes 32800 | tf_op jit(solution)/shard_map/all_to_all | solution.py:828
  116.1 4.5 %residual_back.1 = (bf16[16,12,16,128]{3,2,1,0:T(8,128)(2,1)S(1)}, f32[14,10,16,128]{3,2,1,0:T(8,128)S(1)}, f32[12,10,16,128]{3,2,1,0:T(8,128)S(1)}, f32[32,1,128]{2,1,0:T(1,128)}) custom-call(s32[4]{0:T(128)S(1)} %copy-done.68, f32[32,2,128]{2,1,0:T(2,128)S(1)} %all-to-all-done.4.got.got_head, f32[16,10,16,128]{3,2,1,0:T(8,128)S(1)} %copy-done.9, ...), custom_call_target="tpu_custom_call" | custom-call | tf_op jit(solution)/shard_map/residual_back/pallas_call | solution.py:816
  123.5 2.7 %all-to-all-start.5 = ((f32[32,1,128]{2,1,0:T(1,128)}), f32[32,1,128]{2,1,0:T(1,128)S(1)}, u32[]{:S(2)}, u32[]{:S(2)}) async-start(f32[32,1,128]{2,1,0:T(1,128)} %get-tuple-element.106), calls=%async_computation.5 | async-start | bytes 32768 | tf_op jit(solution)/shard_map/all_to_all | solution.py:828
  129.3 4.0 %all-to-all-done.5.got.got_two = f32[32,1,128]{2,1,0:T(1,128)S(1)} async-done(((f32[32,1,128]{2,1,0:T(1,128)}), f32[32,1,128]{2,1,0:T(1,128)S(1)}, u32[]{:S(2)}, u32[]{:S(2)}) %all-to-all-start.5) | async-done | bytes 16416 | tf_op jit(solution)/shard_map/all_to_all | solution.py:828
  139.1 4.3 %merged_back.1 = (bf16[14,12,16,128]{3,2,1,0:T(8,128)(2,1)S(1)}, f32[12,10,16,128]{3,2,1,0:T(8,128)S(1)}, f32[32,2,4,128]{3,2,1,0:T(4,128)S(1)}) custom-call(s32[4]{0:T(128)S(1)} %copy-done.68, f32[32,1,128]{2,1,0:T(1,128)S(1)} %all-to-all-done.5.got.got_two, f32[14,10,16,128]{3,2,1,0:T(8,128)S(1)} %copy-done.19, ...), custom_call_target="tpu_custom_call" | custom-call | tf_op jit(solution)/shard_map/merged_back/pallas_call | solution.py:816
  146.0 2.7 %all-to-all-start.6 = ((f32[32,2,4,128]{3,2,1,0:T(4,128)}), f32[32,2,4,128]{3,2,1,0:T(4,128)S(1)}, u32[]{:S(2)}, u32[]{:S(2)}) async-start(f32[32,2,4,128]{3,2,1,0:T(4,128)} %copy-done.61), calls=%async_computation.6 | async-start | bytes 262144 | tf_op jit(solution)/shard_map/all_to_all | solution.py:828
  151.1 5.8 %all-to-all-done.6.got = f32[32,2,4,128]{3,2,1,0:T(4,128)S(1)} async-done(((f32[32,2,4,128]{3,2,1,0:T(4,128)}), f32[32,2,4,128]{3,2,1,0:T(4,128)S(1)}, u32[]{:S(2)}, u32[]{:S(2)}) %all-to-all-start.6) | async-done | bytes 131104 | tf_op jit(solution)/shard_map/all_to_all | solution.py:828
  165.1 2.9 %summed_back.1 = (bf16[10,12,16,128]{3,2,1,0:T(8,128)(2,1)S(1)}, f32[8,8,16,128]{3,2,1,0:T(8,128)S(1)}, f32[32,3,4,128]{3,2,1,0:T(4,128)S(1)}, f32[8,128]{1,0:T(8,128)S(1)}, f32[2,16,128]{2,1,0:T(8,128)S(1)}) custom-call(s32[4]{0:T(128)S(1)} %copy-done.69, f32[32,2,4,128]{3,2,1,0:T(4,128)S(1)} %all-to-all-done.6.got, f32[32,1,128]{2,1,0:T(1,128)S(1)} %copy-done.58, ...), custom_call_target="tpu_custom_call" | custom-call | tf_op jit(solution)/shard_map/summed_back/pallas_call | solution.py:816
  168.1 10.6 %all_to_all.48.got.got_first = f32[32,3,4,128]{3,2,1,0:T(4,128)S(1)} all-to-all(f32[32,3,4,128]{3,2,1,0:T(4,128)S(1)} %get-tuple-element.121), channel_id=1, replica_groups=mesh['row'=8,'col'=4] {'row','col'}, dimensions={0} | all-to-all | bytes 393216 | tf_op jit(solution)/shard_map/all_to_all | solution.py:828
  180.5 2.7 %all-to-all-start.8 = ((f32[32,3,4,128]{3,2,1,0:T(4,128)}), f32[32,3,4,128]{3,2,1,0:T(4,128)S(1)}, u32[]{:S(2)}, u32[]{:S(2)}) async-start(f32[32,3,4,128]{3,2,1,0:T(4,128)} %first_back.1), calls=%async_computation.8 | async-start | bytes 393216 | tf_op jit(solution)/shard_map/all_to_all | solution.py:828
  183.4 8.7 %all-to-all-done.8.got = f32[32,3,4,128]{3,2,1,0:T(4,128)S(1)} async-done(((f32[32,3,4,128]{3,2,1,0:T(4,128)}), f32[32,3,4,128]{3,2,1,0:T(4,128)S(1)}, u32[]{:S(2)}, u32[]{:S(2)}) %all-to-all-start.8) | async-done | bytes 196640 | tf_op jit(solution)/shard_map/all_to_all | solution.py:828
  (229 shorter events, 62.1 us)
Async XLA Ops:
  5.7 7.4 %collective-permute-start = (bf16[8,16,6,8]{3,2,0,1:T(8,128)(2,1)}, bf16[8,16,6,8]{3,2,0,1:T(8,128)(2,1)S(1)}, u32[]{:S(2)}, u32[]{:S(2)}) collective-permute-start(bf16[8,16,6,8]{3,2,0,1:T(8,128)(2,1)} %get-tuple-element.194), channel_id=1, source_target_pairs={{0,1},{1,2},{2,3},{4,5},{5,6},{6,7},{8,9},{9,10},{10,11},{12,13},{... | collective-permute-start | bytes 36872 | tf_op jit(solution)/shard_map/ppermute | solution.py:869
  8.1 5.9 %collective-permute-start.1 = (bf16[8,16,6,8]{3,2,0,1:T(8,128)(2,1)}, bf16[8,16,6,8]{3,2,0,1:T(8,128)(2,1)}, u32[]{:S(2)}, u32[]{:S(2)}) collective-permute-start(bf16[8,16,6,8]{3,2,0,1:T(8,128)(2,1)} %get-tuple-element.195), channel_id=1, source_target_pairs={{1,0},{2,1},{3,2},{5,4},{6,5},{7,6},{9,8},{10,9},{11,10},{13,12},{... | collective-permute-start | bytes 36872 | tf_op jit(solution)/shard_map/ppermute | solution.py:870
  13.2 83.5 %copy-start.50 = (f32[8,128]{1,0:T(8,128)}, f32[8,128]{1,0:T(8,128)S(1)}, u32[]{:S(2)}) copy-start(f32[8,128]{1,0:T(8,128)S(1)} %get-tuple-element.89.tab) | copy-start | bytes 12292
  16.1 6.4 %collective-permute-start.2 = (bf16[8,16,384]{2,1,0:T(8,128)(2,1)S(1)}, bf16[8,16,384]{2,1,0:T(8,128)(2,1)S(1)}, u32[]{:S(2)}, u32[]{:S(2)}) collective-permute-start(bf16[8,16,384]{2,1,0:T(8,128)(2,1)S(1)} %copy.61.own), channel_id=1, source_target_pairs={{0,4},{4,8},{8,12},{12,16},{16,20},{20,24},{24,28},{1,5},{5,9},{9,... | collective-permute-start | bytes 294920 | tf_op jit(solution)/shard_map/ppermute | solution.py:874
  20.4 6.5 %collective-permute-start.3 = (bf16[8,16,384]{2,1,0:T(8,128)(2,1)S(1)}, bf16[8,16,384]{2,1,0:T(8,128)(2,1)S(1)}, u32[]{:S(2)}, u32[]{:S(2)}) collective-permute-start(bf16[8,16,384]{2,1,0:T(8,128)(2,1)S(1)} %copy.61.own), channel_id=1, source_target_pairs={{4,0},{8,4},{12,8},{16,12},{20,16},{24,20},{28,24},{5,1},{9,5},{13... | collective-permute-start | bytes 294920 | tf_op jit(solution)/shard_map/ppermute | solution.py:875
  22.4 21.1 %copy-start.46 = (bf16[128,1536]{1,0:T(8,128)(2,1)S(1)}, bf16[128,1536]{1,0:T(8,128)(2,1)}, u32[]{:S(2)}) copy-start(bf16[128,1536]{1,0:T(8,128)(2,1)} %copy-done.45) | copy-start | bytes 1179652
  22.6 21.0 %copy-start.41 = (bf16[8,16,384]{2,1,0:T(8,128)(2,1)}, bf16[8,16,384]{2,1,0:T(8,128)(2,1)S(1)}, u32[]{:S(2)}) copy-start(bf16[8,16,384]{2,1,0:T(8,128)(2,1)S(1)} %collective-permute-done.2.up) | copy-start | bytes 294916
  26.9 16.7 %copy-start.43 = (bf16[8,16,384]{2,1,0:T(8,128)(2,1)}, bf16[8,16,384]{2,1,0:T(8,128)(2,1)S(1)}, u32[]{:S(2)}) copy-start(bf16[8,16,384]{2,1,0:T(8,128)(2,1)S(1)} %collective-permute-done.3.down) | copy-start | bytes 294916
  28.3 32.3 %copy-start.39 = (bf16[24,16,128]{2,1,0:T(8,128)(2,1)}, bf16[24,16,128]{2,1,0:T(8,128)(2,1)S(1)}, u32[]{:S(2)}) copy-start(bf16[24,16,128]{2,1,0:T(8,128)(2,1)S(1)} %get-tuple-element.86.image) | copy-start | bytes 294916
  28.3 15.3 %all-to-all-start = ((f32[32,1,128]{2,1,0:T(1,128)}), f32[32,1,128]{2,1,0:T(1,128)S(1)}, u32[]{:S(2)}, u32[]{:S(2)}) async-start(f32[32,1,128]{2,1,0:T(1,128)} %get-tuple-element.85), calls=%async_computation | async-start | bytes 32768 | tf_op jit(solution)/shard_map/all_to_all | solution.py:828
  36.6 43.6 %copy-start.67 = (s32[4]{0:T(128)}, s32[4]{0:T(128)S(1)}, u32[]{:S(2)}) copy-start(s32[4]{0:T(128)S(1)} %add_convert_fusion.flags) | copy-start | bytes 52
  51.8 28.4 %copy-start.3 = (f32[8,12,16,128]{3,2,1,0:T(8,128)}, f32[8,12,16,128]{3,2,1,0:T(8,128)S(1)}, u32[]{:S(2)}) copy-start(f32[8,12,16,128]{3,2,1,0:T(8,128)S(1)} %get-tuple-element.118.xhat_below.xhat) | copy-start | bytes 2359300
  51.8 28.4 %copy-start.80 = (f32[8,128]{1,0:T(8,128)}, f32[8,128]{1,0:T(8,128)S(1)}, u32[]{:S(2)}) copy-start(f32[8,128]{1,0:T(8,128)S(1)} %get-tuple-element.123.vec) | copy-start | bytes 12292
  60.6 19.6 %copy-start.14 = (bf16[1152,128]{1,0:T(8,128)(2,1)S(1)}, bf16[1152,128]{1,0:T(8,128)(2,1)}, u32[]{:S(2)}) copy-start(bf16[1152,128]{1,0:T(8,128)(2,1)} %get-tuple-element.191.taps) | copy-start | bytes 884740
  60.6 19.6 %copy-start.36 = (f32[2,128,128]{2,1,0:T(8,128)S(1)}, f32[2,128,128]{2,1,0:T(8,128)}, u32[]{:S(2)}) copy-start(f32[2,128,128]{2,1,0:T(8,128)} %copy-done.35) | copy-start | bytes 393220
  69.6 15.3 %copy-start.84 = (f32[8,128]{1,0:T(8,128)}, f32[8,128]{1,0:T(8,128)S(1)}, u32[]{:S(2)}) copy-start(f32[8,128]{1,0:T(8,128)S(1)} %get-tuple-element.117.vec) | copy-start | bytes 12292
  80.2 16.5 %copy-start.34 = (bf16[1280,256]{1,0:T(8,128)(2,1)S(1)}, bf16[1280,256]{1,0:T(8,128)(2,1)}, u32[]{:S(2)}) copy-start(bf16[1280,256]{1,0:T(8,128)(2,1)} %copy-done.33) | copy-start | bytes 1966084
  80.2 16.5 %copy-start.42 = (bf16[8,16,384]{2,1,0:T(8,128)(2,1)S(1)}, bf16[8,16,384]{2,1,0:T(8,128)(2,1)}, u32[]{:S(2)}) copy-start(bf16[8,16,384]{2,1,0:T(8,128)(2,1)} %copy-done.41) | copy-start | bytes 294916
  80.2 16.5 %copy-start.44 = (bf16[8,16,384]{2,1,0:T(8,128)(2,1)S(1)}, bf16[8,16,384]{2,1,0:T(8,128)(2,1)}, u32[]{:S(2)}) copy-start(bf16[8,16,384]{2,1,0:T(8,128)(2,1)} %copy-done.43) | copy-start | bytes 294916
  80.3 16.5 %copy-start.91 = (f32[1,256]{1,0:T(1,128)S(1)}, f32[1,256]{1,0:T(1,128)}, u32[]{:S(2)}) copy-start(f32[1,256]{1,0:T(1,128)} %copy-done.90) | copy-start | bytes 3076
  102.5 10.0 %all-to-all-start.4 = ((f32[32,2,128]{2,1,0:T(2,128)}), f32[32,2,128]{2,1,0:T(2,128)S(1)}, u32[]{:S(2)}, u32[]{:S(2)}) async-start(f32[32,2,128]{2,1,0:T(2,128)} %copy-done.66), calls=%async_computation.4 | async-start | bytes 65536 | tf_op jit(solution)/shard_map/all_to_all | solution.py:828
  123.5 9.8 %all-to-all-start.5 = ((f32[32,1,128]{2,1,0:T(1,128)}), f32[32,1,128]{2,1,0:T(1,128)S(1)}, u32[]{:S(2)}, u32[]{:S(2)}) async-start(f32[32,1,128]{2,1,0:T(1,128)} %get-tuple-element.106), calls=%async_computation.5 | async-start | bytes 32768 | tf_op jit(solution)/shard_map/all_to_all | solution.py:828
  146.0 10.9 %all-to-all-start.6 = ((f32[32,2,4,128]{3,2,1,0:T(4,128)}), f32[32,2,4,128]{3,2,1,0:T(4,128)S(1)}, u32[]{:S(2)}, u32[]{:S(2)}) async-start(f32[32,2,4,128]{3,2,1,0:T(4,128)} %copy-done.61), calls=%async_computation.6 | async-start | bytes 262144 | tf_op jit(solution)/shard_map/all_to_all | solution.py:828
  180.5 11.6 %all-to-all-start.8 = ((f32[32,3,4,128]{3,2,1,0:T(4,128)}), f32[32,3,4,128]{3,2,1,0:T(4,128)S(1)}, u32[]{:S(2)}, u32[]{:S(2)}) async-start(f32[32,3,4,128]{3,2,1,0:T(4,128)} %first_back.1), calls=%async_computation.8 | async-start | bytes 393216 | tf_op jit(solution)/shard_map/all_to_all | solution.py:828
  (83 other events, 494.3 us)

commit v3 on v0

v3 whole, which is shorter than its diff:
```python
import functools

import jax
import jax.numpy as jnp
from jax import lax
from jax.experimental import pallas as pl
from jax.experimental.pallas import tpu as pltpu
from jax.sharding import PartitionSpec as P

STEP = 5

highest = lax.Precision.HIGHEST
norm_eps = 1e-05
flow_scale = 32.0
adam_eps = 1e-08
weight_decay = 0.01
beta_one = 0.5
beta_two = 0.5
rate_table = (0.2, 0.05, 0.15, 0.15, 0.2)

CH = 32
GRP = 4
SEG = 8
LANES = 128
RIM = 8
FLOW, LABEL, MASK = 16, 32, 40
LEFT, RIGHT = 64, 96
F32 = jnp.float32
BF16 = jnp.bfloat16
VMEM_LIMIT = 36 * 1024 * 1024
STORE_BYTES = 32 * 1024 * 1024
FORWARD = 10 * LANES
BACK = 9 * LANES
HEAD_AT = 3 * FORWARD + 3 * BACK


def lane_of(shape):
    return lax.broadcasted_iota(jnp.int32, shape, len(shape) - 1)


def row_of(shape):
    return lax.broadcasted_iota(jnp.int32, shape, 0)


def group_of(shape):
    return lane_of(shape) >> 5


def fold(v):
    v = v + pltpu.roll(v, 64, axis=1)
    return v + pltpu.roll(v, 32, axis=1)


def spread(v, k):
    return fold(jnp.where(group_of(v.shape) == k, v, 0.0))


def partner(v):
    odd = (group_of(v.shape) & 1) == 1
    return jnp.where(odd, pltpu.roll(v, 32, axis=1), pltpu.roll(v, 96, axis=1))


def tile4(v):
    return jnp.concatenate([v, v, v, v], axis=1)


def col_sum(v):
    return jnp.sum(v, axis=0, keepdims=True)


def zero_row():
    return jnp.zeros((1, LANES), F32)


def groups(*values):
    group = group_of(values[0].shape)
    out = values[-1]
    for k in range(len(values) - 2, -1, -1):
        out = jnp.where(group == k, values[k], out)
    return out


def low(v):
    return v.astype(BF16).astype(F32)


def sig_of(v):
    return 0.5 + 0.5 * jnp.tanh(0.5 * v)


def slope(n, sig):
    return sig * (1.0 + n * (1.0 - sig))


def slope_at(x, gain, bias):
    n = x * gain + bias
    return slope(n, sig_of(n))


def flat(v):
    return v.reshape(-1, LANES)


def loop(count, body):
    def step(i, carry):
        body(i)
        return carry

    lax.fori_loop(0, count, step, 0)


def copies(sems, *pairs):
    found = []
    for i, (source, target) in enumerate(pairs):
        found.append(pltpu.make_async_copy(source, target, sems.at[i]))
        found[-1].start()
    return found


def wait(started):
    for copy in started:
        copy.wait()


def shift_segments(v, way):
    half = v.shape[1]
    at = lax.broadcasted_iota(jnp.int32, v.shape, 1)
    if way == 1:
        return jnp.where(at == 0, 0.0, pltpu.roll(v, 1, axis=1))
    return jnp.where(at == half - 1, 0.0, pltpu.roll(v, half - 1, axis=1))


def beside(first, second):
    half = first.shape[1] // 2
    left = jnp.concatenate([shift_segments(second[:, half:], 1), second[:, :half]], axis=1)
    right = jnp.concatenate([first[:, half:], shift_segments(first[:, :half], -1)], axis=1)
    return left, right


def put_low(ref, row, first, second):
    left, right = beside(first, second)
    edge = jnp.where(lane_of(left.shape) < 64, right, left)
    at = pl.ds(row + 1, first.shape[0])
    for k, v in enumerate((first, second, edge)):
        ref[at, k] = v.astype(BF16)


def blank(ref):
    zero = jnp.zeros((1,) + ref.shape[1:], ref.dtype)
    ref[0:1] = zero
    ref[ref.shape[0] - 1 : ref.shape[0]] = zero


def views(src, row, rows):
    return [flat(src[pl.ds(row + r, rows), k]) for r in range(3) for k in (2, 0, 1)]


def conv(src, mat, row, rows, *more):
    wide = jnp.concatenate(views(src, row, rows) + list(more), axis=1)
    return jnp.dot(wide, mat[...], preferred_element_type=F32)


def blocks_of(y, rows):
    return [y[:, k * LANES : (k + 1) * LANES].reshape(rows, -1, LANES) for k in range(2)]


def local_stats(v, first, rows, count):
    def add(i, total):
        return total + v[first + i, 0] + v[first + i, 1]

    zero = jnp.zeros(v.shape[2:], F32)
    mean = fold(col_sum(lax.fori_loop(0, rows, add, zero, unroll=8))) / count

    def add_square(i, total):
        a, b = v[first + i, 0] - mean, v[first + i, 1] - mean
        return total + a * a + b * b

    return mean, fold(col_sum(lax.fori_loop(0, rows, add_square, zero, unroll=8)))


def merge_stats(pay, local_count, pixel_count):
    devices = pay.shape[0]
    whole = col_sum(pay)
    mean = spread(whole, 0) / devices
    away = pay - mean
    between = spread(col_sum(away * away), 0)
    spread_sum = spread(whole, 1) + local_count * between
    return mean, lax.rsqrt(spread_sum / pixel_count + norm_eps)


def send(pay, row):
    pay[...] = jnp.broadcast_to(row.reshape(1, 1, LANES), pay.shape)


def notes(ref, *rows):
    for i, row in enumerate(rows):
        ref[i : i + 1, :] = row


def taps_at(store, i):
    return store.at[FORWARD * i : FORWARD * i + (BACK if i else FORWARD)]


def back_at(store, i):
    return store.at[3 * FORWARD + BACK * i : 3 * FORWARD + BACK * (i + 1)]


def pack_kernel(image, flow, labels, valid, out):
    images, height, _, width = image.shape
    parts = out.shape[0] // images
    fields = [image[:, :, c, :].astype(F32) for c in range(2)]
    fields += [flow[:, :, c, :].astype(F32) for c in range(2)]
    fields += [labels[...].astype(F32), valid[...].astype(F32)]
    halves = width // 16
    shape = (width, halves * LANES)
    lane = lane_of(shape)
    column = (lane >> 7) * 16 + ((lane >> 6) & 1) * 8 + (lane & 7)
    hit = row_of(shape) == column
    which = (lane >> 3) & 7
    total = jnp.zeros((images * height, halves * LANES), F32)
    for k, v in enumerate(fields):
        x = v.reshape(images * height, width).astype(BF16)
        mat = jnp.where(hit & (which == k), 1.0, 0.0).astype(BF16)
        total = total + jnp.dot(x, mat, preferred_element_type=F32)
    for b in range(images):
        rows = total[b * height : (b + 1) * height]
        slot = jnp.concatenate([rows[:, h * LANES : (h + 1) * LANES] for h in range(halves)], axis=0).astype(BF16)
        for p in range(parts):
            out[b * parts + p] = slot


def prepare(w_first, w_convs, w_style, w_head, table, store, first_mat, head_bias, style_mat, tab, mats, sems):
    lane = lane_of((LANES, 2 * LANES))
    at = row_of((LANES, 2 * LANES))
    column = lane >> 5
    kind = at >> 5
    here = (at & 7) + jnp.where(kind == LEFT // 32, -SEG, jnp.where(kind == RIGHT // 32, SEG, 0))
    image_lane = (kind != 1) & ((at & 31) < 16)
    channel = (at >> 3) & 1
    rows = [[None] * 2 for _ in range(10)]
    for t in range(10):
        for c in range(2):
            v = tile4(low(w_first[t][c : c + 1]))
            rows[t][c] = jnp.concatenate([v, v], axis=1)
    for r in range(3):
        val = jnp.zeros((LANES, 2 * LANES), F32)
        for s in range(3):
            for c in range(2):
                hit = image_lane & (channel == c) & (here == column + s - 1)
                val = jnp.where(hit, rows[3 * r + s][c], val)
        first_mat[r] = val.astype(BF16)
    val = jnp.zeros((LANES, 2 * LANES), F32)
    for c in range(2):
        val = jnp.where((at < 16) & (channel == c) & (here == column), rows[9][c], val)
    mats[BACK:FORWARD, :] = val.astype(BF16)

    out_at = group_of((CH, 2 * LANES))
    columns = ((8, None, None, -1), (0, 1, 2, 3), (4, 5, 6, 7))

    def layer(i):
        for r in range(3):
            wide, tall = [], []
            for s in range(3):
                k = tile4(w_convs[i, 3 * r + s])
                wide.append(jnp.concatenate([k, k], axis=1))
                k = w_convs[i, 3 * (2 - r) + s]
                k = jnp.concatenate([k, k, k, k], axis=0).T
                tall.append(jnp.concatenate([k, k], axis=1))
            for d in range(3):
                for a in range(GRP):
                    spot = (3 * r + d) * LANES + CH * a
                    val = jnp.zeros((CH, 2 * LANES), F32)
                    inv = jnp.zeros((CH, 2 * LANES), F32)
                    at_column = columns[d][a]
                    if at_column is not None:
                        for s in range(3):
                            val = jnp.where(out_at == at_column + 1 - s, wide[s], val)
                            inv = jnp.where(out_at == at_column + s - 1, tall[s], inv)
                    mats[pl.ds(i * FORWARD + spot, CH), :] = val.astype(BF16)
                    mats[pl.ds(3 * FORWARD + i * BACK + spot, CH), :] = inv.astype(BF16)

    loop(3, layer)

    lane = lane_of((CH, LANES))
    head = jnp.zeros((CH, LANES), F32)
    bias = zero_row()
    diagonal = row_of((CH, CH)) == lane_of((CH, CH))
    for k in range(3):
        column = jnp.sum(jnp.where(diagonal, low(w_head[k : k + 1, 0:CH]), 0.0), axis=1, keepdims=True)
        mine = (lane >> 3) == FLOW // 8 + k
        head = jnp.where(mine, column, head)
        bias = jnp.where(mine[0:1], low(w_head[k : k + 1, CH : CH + 1]), bias)
    head_bias[...] = bias
    empty = jnp.zeros((CH, LANES), F32)
    for y in range(SEG):
        val = jnp.where((lane & 7) == y, head, 0.0)
        mats[HEAD_AT + CH * y : HEAD_AT + CH * (y + 1), :] = jnp.concatenate([val, empty], axis=1).astype(BF16)
    group = group_of((CH, LANES))
    for i in range(2):
        wide = tile4(w_style[i])
        for b in range(GRP):
            style_mat[i, CH * b : CH * b + CH, :] = jnp.where(group == b, wide, 0.0)
    for i in range(2):
        tab[4 * i : 4 * i + 4, :] = tile4(table[i])
    wait(copies(sems, (mats, store.at[0 : mats.shape[0]])))


def start_kernel(place, got, first_mat, sides, raw, pay, *, local_count, height, sources):
    rows, segments = raw.shape[0], raw.shape[2]
    off, block = place[0], place[1]
    blank(sides)

    def eight(t):
        v = got[pl.ds((block + t) * sources, sources)].astype(F32)
        v = jnp.swapaxes(v.reshape(segments // 2, 8, LANES), 0, 1)
        near = lane_of(v.shape) < 64
        v = jnp.concatenate([jnp.where(near, v, 0.0), jnp.where(near, pltpu.roll(v, 64, axis=2), 0.0)], axis=1)
        pixels = jnp.where(lane_of(v.shape) < 16, v, 0.0)
        left, right = beside(pixels, pixels)
        v = v + pltpu.roll(left, LEFT, axis=2) + pltpu.roll(right, RIGHT, axis=2)
        sides[pl.ds(8 * t + 1, 8)] = v.astype(BF16)

    loop(rows // 8, eight)
    y = None
    for r in range(3):
        part = jnp.dot(flat(sides[r : r + rows]), first_mat[r], preferred_element_type=F32)
        y = part if y is None else y + part
    raw[:, 0], raw[:, 1] = blocks_of(y, rows)
    mean, square = local_stats(raw, off, height, local_count)
    mask = jnp.zeros(sides.shape[1:], F32)
    for i in range(height):
        mask = mask + sides[off + 1 + i].astype(F32)
    lane = lane_of(mask.shape)
    count = jnp.sum(jnp.where((lane >= MASK) & (lane < MASK + 8), mask, 0.0))
    send(pay, groups(mean, square, jnp.full((1, LANES), count, F32)))


def first_kernel(place, got, raw, sides, tab, weights, summed, pay, vec, fields, lows, hidden, xhat, taps, sems, *, spots, local_count, pixel_count, height):
    fetched = copies(sems, (taps_at(weights, 0), taps))
    mean, inverse = merge_stats(got[:, 0, :], local_count, pixel_count)
    notes(vec, inverse)
    gain, bias = tab[0:1], tab[4:5]
    rows = raw.shape[0]

    def norm_rows(i):
        at = pl.ds(4 * i, 4)
        out = []
        for k in range(2):
            x = (raw[at, k] - mean) * inverse
            xhat[at, k] = x
            n = x * gain + bias
            out.append(n * sig_of(n))
        put_low(hidden, 4 * i, *out)

    blank(hidden)
    loop(rows // 4, norm_rows)
    stored = copies(sems.at[1:], (xhat, spots(fields, "xhat_zero")), (hidden, spots(lows, "hidden_one")))
    wait(fetched)
    y = conv(hidden, taps, 0, rows, flat(sides[1 : rows + 1]))
    summed[:, 0], summed[:, 1] = blocks_of(y, rows)
    send(pay, groups(*local_stats(summed, place[0], height, local_count), zero_row()))
    wait(stored)


def pool_kernel(place, got, summed, tab, weights, fields_in, lows_in, raw, pay, vec, fields, lows, merged, xhat, shared, taps, sems, *, spots, local_count, pixel_count, height):
    fetched = copies(sems, (taps_at(weights, 1), taps))
    mean, inverse = merge_stats(got[:, 0, :], local_count, pixel_count)
    gain, bias = tab[1:2], tab[5:6]
    rows, segments = summed.shape[0], summed.shape[2]
    own = place[0] // 2

    def pair(p, carry):
        out = [[None, None], [None, None]]
        sums = [jnp.zeros((segments, LANES), F32) for _ in range(3)]
        for k in range(2):
            xs, es, ns, ss = [], [], [], []
            for h in range(2):
                x = (summed[2 * p + h, k] - mean) * inverse
                n = x * gain + bias
                s = sig_of(n)
                xs.append(x)
                ns.append(n)
                ss.append(s)
                es.append(n * s)
            top = jnp.maximum(es[0], es[1])
            top = jnp.maximum(top, partner(top))
            exps = [jnp.exp(e - top) for e in es]
            whole = exps[0] + exps[1]
            whole = whole + partner(whole)
            pooled = top + jnp.log(whole)
            over = 1.0 / whole
            sums[0] = sums[0] + pooled
            for h in range(2):
                share = exps[h] * over * slope(ns[h], ss[h])
                xhat[2 * p + h, k] = xs[h]
                shared[2 * p + h, k] = share
                sums[1] = sums[1] + share
                sums[2] = sums[2] + share * xs[h]
                out[h][k] = (es[h] + pooled)[None]
        for h in range(2):
            put_low(merged, 2 * p + h, *out[h])
        mine = (p >= own) & (p < own + height // 2)
        keep = jnp.where(mine, 1.0, 0.0)
        return tuple(a + keep * b for a, b in zip(carry, sums))

    blank(merged)
    zero = jnp.zeros((segments, LANES), F32)
    sums = lax.fori_loop(0, rows // 2, pair, (zero, zero, zero))
    pool_sum, share_sum, share_x = [fold(col_sum(v)) for v in sums]
    stored = copies(
        sems.at[1:],
        (xhat, spots(fields, "xhat_one")),
        (shared, spots(fields, "shared")),
        (merged, spots(lows, "merged")),
    )
    wait(fetched)
    raw[:, 0], raw[:, 1] = blocks_of(conv(merged, taps, 0, rows), rows)
    mean, square = local_stats(raw, place[0], height, local_count)
    send(pay, groups(mean, square, 0.5 * pool_sum, share_sum))
    notes(vec, inverse, share_x)
    wait(stored)


def by_image(v, parts):
    devices = v.shape[0]
    shape = (devices, devices)
    same = row_of(shape) // parts == lane_of(shape) // parts
    return jnp.dot(jnp.where(same, 1.0, 0.0), v, precision=highest, preferred_element_type=F32)


def mine_of(v, me):
    return col_sum(jnp.where(row_of(v.shape) == me, v, 0.0))


def style_kernel(place, got, raw, vec_one, tab, style_mat, weights, fields_in, lows_in, resid, pay, vec, style_out, fields, lows, hidden, xhat, merged, taps, sems, *, spots, local_count, pixel_count, pool_cells, height, parts):
    fetched = copies(sems, (taps_at(weights, 2), taps), (spots(lows_in, "merged"), merged))
    got = got[:, 0, :]
    devices = got.shape[0]
    style = by_image(spread(got, 2), parts) / pool_cells
    style_out[...] = style
    one = jnp.dot(style, style_mat[0], precision=highest, preferred_element_type=F32)
    two = jnp.dot(style, style_mat[1], precision=highest, preferred_element_type=F32)
    centre = spread(got, 0) + one
    mean = col_sum(centre) / devices
    off = centre - mean
    spread_sum = spread(col_sum(got), 1) + local_count * col_sum(off * off)
    inverse = lax.rsqrt(spread_sum / pixel_count + norm_eps)
    notes(vec, inverse)
    gain, bias = tab[2:3], tab[6:7]
    rows = raw.shape[0]
    me = place[2]
    shift = mine_of(one, me) - mean
    two = mine_of(two, me)

    def norm_rows(i):
        at = pl.ds(4 * i, 4)
        out = []
        for k in range(2):
            x = (raw[at, k] + shift) * inverse
            xhat[at, k] = x
            n = x * gain + bias
            out.append(n * sig_of(n))
        put_low(hidden, 4 * i, *out)

    blank(hidden)
    loop(rows // 4, norm_rows)
    stored = copies(sems.at[2:], (xhat, spots(fields, "xhat_two")), (hidden, spots(lows, "hidden_three")))
    wait(fetched)
    for k, y in enumerate(blocks_of(conv(hidden, taps, 0, rows), rows)):
        resid[:, k] = y + two + merged[1 : rows + 1, k].astype(F32)
    send(pay, groups(*local_stats(resid, place[0], height, local_count), vec_one[1:2]))
    wait(stored)


def head_kernel(place, got, got_count, resid, sides, head_bias, tab, weights, grad, xhat, pay, vec, decoded, slopes, mat, sems, *, local_count, pixel_count, height):
    fetched = copies(sems, (weights.at[HEAD_AT : HEAD_AT + 2 * LANES], mat))
    mean, inverse = merge_stats(got[:, 0, :], local_count, pixel_count)
    notes(vec, inverse)
    gain, bias = tab[3:4], tab[7:8]
    rows, segments = resid.shape[0], resid.shape[2]
    off = place[0]

    def norm_rows(i):
        at = pl.ds(4 * i, 4)
        for k in range(2):
            x = (resid[at, k] - mean) * inverse
            n = x * gain + bias
            s = sig_of(n)
            xhat[at, k] = x
            slopes[at, k] = slope(n, s)
            decoded[at, k] = (n * s).astype(BF16)

    loop(rows // 4, norm_rows)
    wait(fetched)
    head = mat[:, 0:LANES]
    wide = jnp.concatenate([flat(decoded[:, 0]), flat(decoded[:, 1])], axis=1)
    out = jnp.dot(wide, head, preferred_element_type=F32) + head_bias[...]
    given = flat(sides[1 : rows + 1]).astype(F32)
    lane = lane_of(given.shape)
    is_flow = lane < LABEL
    near = [pltpu.roll(given, LANES - MASK + first, axis=1) for first in (FLOW, FLOW + 8, LABEL)]
    mask = jnp.where(lane < FLOW + 8, near[0], jnp.where(is_flow, near[1], near[2]))
    mask = jnp.where((lane >= FLOW) & (lane < LABEL + 8), mask, 0.0)
    count = jnp.sum(got_count[:, 0, 64:65])
    diff = out - given / flow_scale
    hinge = jnp.maximum(out, 0.0) + jnp.log1p(jnp.exp(-jnp.abs(out)))
    loss = mask * jnp.where(is_flow, diff * diff, hinge - given * out)
    grad_out = (mask * jnp.where(is_flow, 2.0 * diff, sig_of(out) - given) / count).astype(BF16)
    at_row = lax.broadcasted_iota(jnp.int32, loss.shape, 0)
    inside = (at_row >= off * segments) & (at_row < (off + height) * segments)
    loss_sum = jnp.sum(jnp.where(inside, loss, 0.0))
    mine_out = jnp.where(inside, grad_out.astype(F32), 0.0).astype(BF16)
    outs = col_sum(mine_out.astype(F32))
    found = lax.dot_general(mine_out, wide, (((0,), (0,)), ((), ())), preferred_element_type=F32)
    shape = found.shape
    found = jnp.where((row_of(shape) & 7) == group_of(shape), found, 0.0)
    whole = [col_sum(found[FLOW + 8 * k : FLOW + 8 * k + 8]) for k in range(3)]
    whole = [fold(v[:, 0:LANES] + v[:, LANES:]) for v in whole]
    row = groups(*whole, zero_row())
    lane = lane_of((1, LANES))
    for k in range(3):
        row = jnp.where(lane == 3 * CH + k, jnp.sum(jnp.where((lane >> 3) == FLOW // 8 + k, outs, 0.0)), row)
    row = jnp.where(lane == 3 * CH + 3, loss_sum, row)
    y = lax.dot_general(grad_out, head, (((1,), (1,)), ((), ())), preferred_element_type=F32)
    for k, g in enumerate(blocks_of(y, rows)):
        grad[:, k] = g * slopes[:, k]
    shift_sum, scale_sum = own_sums(grad, xhat, off, height)
    devices = pay.shape[0]
    pay[:, 0, :] = jnp.broadcast_to(groups(shift_sum, scale_sum, zero_row()), (devices, LANES))
    pay[:, 1, :] = jnp.broadcast_to(row, (devices, LANES))


def own_sums(grad, xhat, first, rows):
    def add(i, carry):
        shift, scale = carry
        for k in range(2):
            g = grad[first + i, k]
            shift = shift + g
            scale = scale + g * xhat[first + i, k]
        return shift, scale

    zero = jnp.zeros(grad.shape[2:], F32)
    shift, scale = lax.fori_loop(0, rows, add, (zero, zero), unroll=8)
    return fold(col_sum(shift)), fold(col_sum(scale))


def back_sums(got, pixel_count):
    whole = col_sum(got)
    return spread(whole, 0) / pixel_count, spread(whole, 1) / pixel_count


def low_sum(grad_low, first, rows):
    def add(i, total):
        return total + grad_low[first + 1 + i, 0].astype(F32) + grad_low[first + 1 + i, 1].astype(F32)

    return fold(col_sum(lax.fori_loop(0, rows, add, jnp.zeros(grad_low.shape[2:], F32), unroll=8)))


def norm_back(grad, xhat, factor, shift, scale):
    return factor * (grad - (shift + xhat * scale))


def back_rows(grad_low, rows, value):
    def some(i):
        put_low(grad_low, 4 * i, *[value(pl.ds(4 * i, 4), k) for k in range(2)])

    blank(grad_low)
    loop(rows // 4, some)


def tap_sums(field, grad, first, rows, out):
    at = pl.ds(first + 1, rows)
    g = jnp.concatenate([flat(grad[at, 0]), flat(grad[at, 1])], axis=1)
    wide = jnp.concatenate(views(field, first, rows), axis=1)
    found = lax.dot_general(g, wide, (((0,), (0,)), ((), ())), preferred_element_type=F32)
    group = group_of((CH, LANES))
    taps = []
    for r in range(3):
        for s in range(3):
            val = jnp.zeros((CH, LANES), F32)
            for y in range(SEG):
                x = y + s - 1
                d, a = (0, 3) if x < 0 else (0, 0) if x == SEG else (1 + x // GRP, x % GRP)
                spot = (3 * r + d) * LANES
                val = val + jnp.where(group == a, found[CH * y : CH * y + CH, spot : spot + LANES], 0.0)
            taps.append(fold(val))
    for q in range(3):
        val = taps[4 * q]
        for b in range(1, min(4, 9 - 4 * q)):
            val = jnp.where(group == b, taps[4 * q + b], val)
        out[:, q, :] = val


def residual_kernel(place, got, grad, xhat, vec, tab, weights, fields_in, lows, below, below_x, pay, fields, grad_low, kept_grad, back, field, sems, *, spots, pixel_count, height):
    fetched = copies(sems, (back_at(weights, 2), back), (spots(fields_in, "xhat_two"), below_x), (spots(lows, "hidden_three"), field))
    devices = got.shape[0]
    shift, scale = back_sums(got[:, 0, :], pixel_count)
    factor = tab[3:4] * vec[0:1]
    rows = grad.shape[0]
    off = place[0]

    def value(at, k):
        g = norm_back(grad[at, k], xhat[at, k], factor, shift, scale)
        kept_grad[at, k] = g
        return g

    back_rows(grad_low, rows, value)
    stored = copies(sems.at[3:], (kept_grad, spots(fields, "grad_resid")))
    image_sum = low_sum(grad_low, off, height)
    gain, bias = tab[2:3], tab[6:7]
    wait(fetched)
    for k, y in enumerate(blocks_of(conv(grad_low, back, 0, rows), rows)):
        below[:, k] = y * slope_at(below_x[:, k], gain, bias)
    row = groups(*own_sums(below, below_x, off, height), image_sum, zero_row())
    pay[...] = jnp.broadcast_to(row[None], pay.shape)
    tap_sums(field, grad_low, off, height, pay.at[0:CH, 1:4])
    wait(stored)


def merged_kernel(place, got, grad, xhat, vec, tab, weights, fields, lows, below, pay, kept_grad, below_x, shared, grad_low, back, field, sems, *, spots, pixel_count, height):
    fetched = copies(
        sems,
        (back_at(weights, 1), back),
        (spots(fields, "grad_resid"), kept_grad),
        (spots(fields, "xhat_one"), below_x),
        (spots(fields, "shared"), shared),
        (spots(lows, "merged"), field),
    )
    devices = got.shape[0]
    gathered = jnp.sum(got[...], axis=0)
    shift, scale = spread(gathered[0:1], 0) / pixel_count, spread(gathered[0:1], 1) / pixel_count
    factor = tab[2:3] * vec[0:1]
    rows = grad.shape[0]
    off = place[0]
    back_rows(grad_low, rows, lambda at, k: norm_back(grad[at, k], xhat[at, k], factor, shift, scale))
    image_sum = low_sum(grad_low, off, height)
    gain, bias = tab[1:2], tab[5:6]
    wait(fetched)
    for k, y in enumerate(blocks_of(conv(grad_low, back, 0, rows), rows)):
        g = (y + kept_grad[:, k]).reshape(rows // 2, 2, -1, LANES)
        both = flat(g[:, 0] + g[:, 1])
        both = (both + partner(both)).reshape(rows // 2, 1, -1, LANES)
        g = g * slope_at(below_x[:, k], gain, bias).reshape(g.shape) + both * shared[:, k].reshape(g.shape)
        below[:, k] = g.reshape(rows, -1, LANES)
    row = groups(*own_sums(below, below_x, off, height), image_sum, zero_row())
    first = jnp.where(row_of((4, LANES)) == 0, row, gathered)
    pay[:, 0] = jnp.broadcast_to(first[None], (devices, 4, LANES))
    if devices > CH:
        pay[CH:, 1] = jnp.zeros((devices - CH, 4, LANES), F32)
    tap_sums(field, grad_low, off, height, pay.at[0:CH, 1])
    pay[0:CH, 1, 3, :] = jnp.zeros((CH, LANES), F32)


def summed_kernel(place, got, got_two, got_style, got_three, grad, vec, tab, style_mat, sides, weights, fields, lows, below, below_x, pay, more, shared, xhat, back, field, grad_low, sems, *, spots, pixel_count, pool_cells, height, parts):
    fetched = copies(
        sems,
        (spots(fields, "shared"), shared),
        (spots(fields, "xhat_one"), xhat),
        (back_at(weights, 0), back),
        (spots(fields, "xhat_zero"), below_x),
        (spots(lows, "hidden_one"), field),
    )
    devices = got.shape[0]
    off = place[0]
    rows = grad.shape[0]
    dims = (((1,), (1,)), ((), ()))
    first = got[:, 0, 0, :]
    grad_style = lax.dot_general(spread(first, 2), style_mat[0], dims, precision=highest, preferred_element_type=F32)
    grad_style = grad_style + lax.dot_general(
        spread(got_two[:, 0, :], 2), style_mat[1], dims, precision=highest, preferred_element_type=F32
    )
    grad_style = by_image(grad_style, parts) / pool_cells
    total = col_sum(first)
    shift = spread(total, 0) + col_sum(grad_style * spread(got_style[:, 0, :], 3))
    scale = spread(total, 1) + col_sum(grad_style * spread(got_three[:, 0, :], 2))
    mine = mine_of(grad_style, place[2])
    factor = tab[1:2] * vec[0:1]
    shift_mean, scale_mean = shift / pixel_count, scale / pixel_count
    wait(fetched[:2])

    def value(at, k):
        return norm_back(grad[at, k] + shared[at, k] * mine, xhat[at, k], factor, shift_mean, scale_mean)

    back_rows(grad_low, rows, value)
    gain, bias = tab[0:1], tab[4:5]
    wait(fetched[2:])
    for k, y in enumerate(blocks_of(conv(grad_low, back, 0, rows), rows)):
        below[:, k] = y * slope_at(below_x[:, k], gain, bias)
    row = groups(*own_sums(below, below_x, off, height), zero_row())
    gathered = jnp.sum(got[:, 1], axis=0)
    chunk = jnp.concatenate([row, gathered[0:3]], axis=0)
    pay[:, 0] = jnp.broadcast_to(chunk[None], (devices, 4, LANES))
    if devices > CH:
        pay[CH:, 1] = jnp.zeros((devices - CH, 4, LANES), F32)
    tap_sums(field, grad_low, off, height, pay.at[0:CH, 1])
    pay[0:CH, 1, 3, :] = jnp.zeros((CH, LANES), F32)
    at = pl.ds(off + 1, height)
    low_own = jnp.concatenate([flat(grad_low[at, 0]), flat(grad_low[at, 1])], axis=1)
    side = pixel_taps(sides, off + 1, height, low_own, (0,))[0]
    notes(more, scale, shift, *side)


def pixel_taps(sides, row, rows, grad, shift):
    x = flat(sides[pl.ds(row, rows)])
    found = lax.dot_general(x, grad, (((0,), (0,)), ((), ())), preferred_element_type=F32)
    at = row_of(found.shape)
    kind = at >> 5
    here = (at & 7) + jnp.where(kind == LEFT // 32, -SEG, jnp.where(kind == RIGHT // 32, SEG, 0)) - group_of(found.shape)
    image_lane = (kind != 1) & ((at & 31) < 16)
    out = []
    for s in shift:
        both = []
        for c in range(2):
            hit = image_lane & (((at >> 3) & 1) == c) & (here == s)
            v = col_sum(jnp.where(hit, found, 0.0))
            both.append(fold(v[:, 0:LANES] + v[:, LANES:]))
        out.append(both)
    return out


def first_back_kernel(place, got, grad, xhat, vec, more, tab, sides, pay, *, pixel_count, height):
    devices = got.shape[0]
    off = place[0]
    whole = col_sum(got[:, 0, 0, :])
    shift, scale = spread(whole, 0) / pixel_count, spread(whole, 1) / pixel_count
    factor = tab[0:1] * vec[0:1]
    at = pl.ds(off, height)
    low_grad = jnp.concatenate(
        [flat(norm_back(grad[at, k], xhat[at, k], factor, shift, scale).astype(BF16)) for k in range(2)], axis=1
    )
    entries = []
    for r in range(3):
        for tap in pixel_taps(sides, off + r, height, low_grad, (-1, 0, 1)):
            entries.extend(tap)
    entries.extend([more[2:3], more[3:4]])
    rows = [groups(*entries[4 * q : 4 * q + 4]) for q in range(5)]
    conv_zero = jnp.sum(got[:, 1], axis=0)
    chunk = [jnp.concatenate(rows[0:4], axis=0), jnp.concatenate([rows[4], conv_zero[0:3]], axis=0)]
    for k in range(2):
        pay[:, k] = jnp.broadcast_to(chunk[k][None], (devices, 4, LANES))


def adamw(master, moment, square, grad, rate):
    new_moment = beta_one * moment + (1.0 - beta_one) * grad
    new_square = beta_two * square + (1.0 - beta_two) * grad * grad
    moment_hat = new_moment / (1.0 - beta_one**STEP)
    square_hat = new_square / (1.0 - beta_two**STEP)
    new_master = master - rate * (moment_hat / (jnp.sqrt(square_hat) + adam_eps) + weight_decay * master)
    return new_master, new_moment, new_square


def put(at, refs, grad, rate, outs):
    found = adamw(*[ref[at] for ref in refs], grad, rate)
    for out, value in zip(outs, found + (found[0].astype(BF16),)):
        out[at] = value


def update_early(
    got_first, got_one_back, got_two, got_head, got_count, pay, more, style,
    w_style, w_head, table, m_style, m_head, m_norms, s_style, s_head, s_norms,
    loss_out, count_out,
    style_master, style_moment, style_square,
    head_master, head_moment, head_square, head_copy,
    norms_master, norms_moment, norms_square,
):
    count_out[0, 0] = jnp.sum(got_count[:, 0, 64:65])
    loss_out[0, 0] = jnp.sum(got_head[:, 1, 99:100])
    dims = (((0,), (0,)), ((), ()))
    for i, sums in enumerate((got_one_back[:, 0, 0, :], got_two[:, 0, :])):
        grad = lax.dot_general(style[...], spread(sums, 2), dims, precision=highest, preferred_element_type=F32)
        put(i, (w_style, m_style, s_style), grad[0:CH, 0:CH], rate_table[2], (style_master, style_moment, style_square))

    head = col_sum(got_head[:, 1, :])
    lane = lane_of((1, LANES))
    rows = []
    for k in range(3):
        last = jnp.sum(jnp.where(lane == 3 * CH + k, head, 0.0), axis=1, keepdims=True)
        rows.append(jnp.where(lane < CH, spread(head, k), last))
    grad = jnp.concatenate(rows, axis=0)[:, 0 : CH + 1]
    put(slice(None), (w_head, m_head, s_head), grad, rate_table[3], (head_master, head_moment, head_square, head_copy))

    three_sums = col_sum(got_head[:, 0, :])
    two_sums = col_sum(got_two[:, 0, :])
    zero_sums = col_sum(got_first[:, 0, 0, :])
    scales = [spread(zero_sums, 1), more[0:1], spread(two_sums, 1), spread(three_sums, 1)]
    shifts = [spread(zero_sums, 0), more[1:2], spread(two_sums, 0), spread(three_sums, 0)]
    for i, rows in enumerate((scales, shifts)):
        grad = jnp.concatenate(rows, axis=0)[:, 0:CH]
        put(i, (table, m_norms, s_norms), grad, rate_table[4], (norms_master, norms_moment, norms_square))


def update_late(
    got, got_first, got_one_back, w_first, w_convs, m_first, m_convs, s_first, s_convs,
    first_master, first_moment, first_square, first_copy,
    convs_master, convs_moment, convs_square, convs_copy,
):
    sources = [got[0:CH, 1, 1:4, :], got_first[0:CH, 0, 1:4, :], got_one_back[0:CH, 0, 1:4, :]]
    refs = (w_convs, m_convs, s_convs)
    outs = (convs_master, convs_moment, convs_square, convs_copy)
    for i in range(3):
        for q in range(3):
            grad = sources[i][:, q, :].T
            for b in range(min(4, 9 - 4 * q)):
                put((i, 4 * q + b), refs, grad[CH * b : CH * b + CH], rate_table[1], outs)

    first = jnp.concatenate([jnp.sum(got[:, 0], axis=0), jnp.sum(got[:, 1], axis=0)[0:1]], axis=0)
    refs = (w_first, m_first, s_first)
    outs = (first_master, first_moment, first_square, first_copy)
    for t in range(10):
        pair = [spread(first[e // 4 : e // 4 + 1], e % 4)[:, 0:CH] for e in (2 * t, 2 * t + 1)]
        put(t, refs, jnp.concatenate(pair, axis=0), rate_table[0], outs)


def far(x):
    return ("far", x)


def call(kernel, outs, *operands, scalars=0, scratch=(), sems=0, scalar_outs=(), aliases=None, name):
    smem = pl.BlockSpec(memory_space=pltpu.SMEM)
    vmem = pl.BlockSpec(memory_space=pltpu.VMEM)
    hbm = pl.BlockSpec(memory_space=pltpu.HBM)
    is_far = lambda x: isinstance(x, tuple) and x[0] == "far"
    in_specs = [smem if i < scalars else hbm if is_far(x) else vmem for i, x in enumerate(operands)]
    out_specs = [smem if i in scalar_outs else hbm if is_far(x) else vmem for i, x in enumerate(outs)]
    plain = lambda x: x[1] if is_far(x) else x
    shapes = [pltpu.VMEM(shape, dtype) for shape, dtype in scratch]
    if sems:
        shapes.append(pltpu.SemaphoreType.DMA((sems,)))
    return pl.pallas_call(
        kernel,
        out_shape=[jax.ShapeDtypeStruct(*plain(x)) for x in outs],
        in_specs=in_specs,
        out_specs=out_specs,
        scratch_shapes=shapes,
        input_output_aliases=aliases or {},
        compiler_params=pltpu.CompilerParams(vmem_limit_bytes=VMEM_LIMIT),
        name=name,
    )(*[plain(x) for x in operands])


def exchange(pay):
    return lax.all_to_all(pay, ("row", "col"), 0, 0)


def local(
    image_batch, valid_mask, flow_target, cell_labels,
    w_first, w_convs, w_style, w_head, batch_norm_table,
    mom_first, mom_convs, mom_style, mom_head, mom_norms,
    sqr_first, sqr_convs, sqr_style, sqr_head, sqr_norms,
):
    images, block_rows, block_cols, _ = image_batch.shape
    row_count, col_count = lax.axis_size("row"), lax.axis_size("col")
    devices = row_count * col_count
    parts = devices // images
    image_rows, image_cols = row_count * block_rows, col_count * block_cols
    assert devices == parts * images and block_rows == RIM and block_cols == 2 * block_rows * 2
    assert image_rows % (parts * RIM) == 0 and devices >= CH
    height = image_rows // parts
    rows = min(image_rows, height + RIM * min(2, parts - 1))
    segments = image_cols // SEG
    local_count = float(height * image_cols)
    pixel_count = local_count * devices
    pool_cells = float(image_rows * image_cols // 4)
    part = functools.partial
    counts = dict(local_count=local_count, pixel_count=pixel_count, height=height)
    backs = dict(pixel_count=pixel_count, height=height)
    styled = dict(pool_cells=pool_cells, parts=parts)

    me = lax.axis_index("row") * col_count + lax.axis_index("col")
    first_row = (me % parts) * height
    start = jnp.clip(first_row - RIM, 0, image_rows - rows)
    place = jnp.stack([first_row - start, start // block_rows, me]).astype(jnp.int32)

    field = ((rows, 2, segments, LANES), F32)
    low_field = ((rows + 2, 3, segments, LANES), BF16)
    vec = ((8, LANES), F32)
    one_row = ((devices, 1, LANES), F32)
    two_chunks = ((devices, 2, 4, LANES), F32)
    taps_scratch = ((FORWARD, 2 * LANES), BF16)
    nine_scratch = ((BACK, 2 * LANES), BF16)

    places = {
        name: i * count
        for count, names in (
            (rows, ("xhat_zero", "xhat_one", "shared", "xhat_two", "grad_resid")),
            (rows + 2, ("hidden_one", "hidden_three", "merged")),
        )
        for i, name in enumerate(names)
    }

    def spots(store, name):
        count = rows if name[0] in "xsg" else rows + 2
        return store.at[places[name] : places[name] + count]

    def store_of(like):
        shape, dtype = like
        row_bytes = shape[1] * segments * LANES * jnp.dtype(dtype).itemsize
        return far(((-(-STORE_BYTES // row_bytes),) + shape[1:], dtype))

    (pay,) = call(
        pack_kernel,
        [((devices, 16, LANES), BF16)],
        jnp.transpose(image_batch, (0, 1, 3, 2)), jnp.transpose(flow_target, (0, 1, 3, 2)), cell_labels, valid_mask,
        name="pack",
    )
    got_inputs = exchange(pay)
    weights, first_mat, head_bias, style_mat, tab = call(
        prepare,
        [
            far(((STORE_BYTES // (4 * LANES), 2 * LANES), BF16)),
            ((3, LANES, 2 * LANES), BF16),
            ((1, LANES), F32),
            ((2, LANES, LANES), F32),
            vec,
        ],
        w_first, w_convs, w_style, w_head.T, batch_norm_table,
        scratch=[((HEAD_AT + 2 * LANES, 2 * LANES), BF16)], sems=1, name="prepare",
    )

    sides, raw, pay = call(
        part(start_kernel, local_count=local_count, height=height, sources=col_count),
        [((rows + 2, segments, LANES), BF16), field, one_row],
        place, got_inputs, first_mat,
        scalars=1, name="image_conv",
    )
    got_zero = exchange(pay)

    summed, pay, inv_zero, fields, lows = call(
        part(first_kernel, spots=spots, **counts),
        [field, one_row, vec, store_of(field), store_of(low_field)],
        place, got_zero, raw, sides, tab, far(weights),
        scalars=1, scratch=[low_field, field, taps_scratch], sems=3, name="first_block",
    )
    got_one = exchange(pay)

    raw, pay, inv_one, fields, lows = call(
        part(pool_kernel, spots=spots, **counts),
        [field, one_row, vec, store_of(field), store_of(low_field)],
        place, got_one, summed, tab, far(weights), far(fields), far(lows),
        scalars=1, scratch=[low_field, field, field, nine_scratch], sems=4,
        aliases={5: 3, 6: 4}, name="pool_and_merge",
    )
    got_style = exchange(pay)

    resid, pay, inv_two, style, fields, lows = call(
        part(style_kernel, spots=spots, **styled, **counts),
        [field, one_row, vec, ((devices, LANES), F32), store_of(field), store_of(low_field)],
        place, got_style, raw, inv_one, tab, style_mat, far(weights), far(fields), far(lows),
        scalars=1, scratch=[low_field, field, low_field, nine_scratch], sems=4,
        aliases={7: 4, 8: 5}, name="decoder",
    )
    got_three = exchange(pay)

    grad_three, xhat_three, pay, inv_three = call(
        part(head_kernel, **counts),
        [field, field, ((devices, 2, LANES), F32), vec],
        place, got_three, got_zero, resid, sides, head_bias, tab, far(weights),
        scalars=1, scratch=[((rows, 2, segments, LANES), BF16), field, ((2 * LANES, 2 * LANES), BF16)], sems=1,
        name="head",
    )
    got_head = exchange(pay)

    grad_two, xhat_two, pay, fields = call(
        part(residual_kernel, spots=spots, **backs),
        [field, field, ((devices, 4, LANES), F32), store_of(field)],
        place, got_head, grad_three, xhat_three, inv_three, tab, far(weights), far(fields), far(lows),
        scalars=1, scratch=[low_field, field, nine_scratch, low_field], sems=4,
        aliases={7: 3}, name="residual_back",
    )
    got_two = exchange(pay)

    grad_one, pay = call(
        part(merged_kernel, spots=spots, **backs),
        [field, two_chunks],
        place, got_two, grad_two, xhat_two, inv_two, tab, far(weights), far(fields), far(lows),
        scalars=1, scratch=[field, field, field, low_field, nine_scratch, low_field], sems=5, name="merged_back",
    )
    got_one_back = exchange(pay)

    grad_zero, xhat_zero, pay, more = call(
        part(summed_kernel, spots=spots, **styled, **backs),
        [field, field, two_chunks, vec],
        place, got_one_back, got_two, got_style, got_three, grad_one, inv_one, tab, style_mat, sides,
        far(weights), far(fields), far(lows),
        scalars=1, scratch=[field, field, nine_scratch, low_field, low_field], sems=5, name="summed_back",
    )
    got_first = exchange(pay)

    (pay,) = call(
        part(first_back_kernel, **backs),
        [two_chunks],
        place, got_first, grad_zero, xhat_zero, inv_zero, more, tab, sides,
        scalars=1, name="first_back",
    )
    got_last = exchange(pay)

    def results(param, copy):
        return [(param.shape, F32)] * 3 + [(param.shape, BF16)] * copy

    head_rows = w_head.T
    early = call(
        update_early,
        [((1, 1), F32), ((1, 1), F32)] + results(w_style, 0) + results(head_rows, 1) + results(batch_norm_table, 0),
        got_first, got_one_back, got_two, got_head, got_zero, far(pay), more, style,
        w_style, head_rows, batch_norm_table, mom_style, mom_head.T, mom_norms, sqr_style, sqr_head.T, sqr_norms,
        scalar_outs=(0, 1), name="update_early",
    )
    late = call(
        update_late,
        results(w_first, 1) + results(w_convs, 1),
        got_last, got_first, got_one_back, w_first, w_convs, mom_first, mom_convs, sqr_first, sqr_convs,
        name="update_late",
    )
    loss, count = early[0].reshape(()), early[1].reshape(())
    head = tuple(value.T for value in early[5:9])
    return (loss, count, *late, *early[2:5], *head, *early[9:12])


def solution(mesh):
    field = P(None, "row", "col", None)
    plane = P(None, "row", "col")
    return jax.shard_map(
        local,
        mesh=mesh,
        in_specs=(field, plane, field, plane) + (P(),) * 15,
        out_specs=(P(),) * 20,
        check_vma=False,
    )
```

time: 951 us -> 143 us (0.15); the launches traced: 939 us -> 143 us
  blocking collectives: 654 us -> 76.8 us
  other arithmetic: 61.5 us -> 0.08 us
  matrix products: 60 us -> 0 us
  waiting for transfers between devices: 58.3 us -> 7.48 us
  starting transfers between devices: 59.8 us -> 9.87 us
  Pallas kernels: 0 us -> 40 us
  local copies, waits for them, and re-layouts: 28.8 us -> 7.33 us
  between operations: 16.7 us -> 1 us
    psum x16 -> x0, blocking collectives: 654 us -> none  [the longest x4 167 us: norm_back(): lax.psum((jnp.sum(grad_norm, axis=(0, 1, 2)), jnp.sum(grad_norm * normal_...]
    all_to_all x0 -> x8, blocking collectives: none -> 76.8 us  [exchange(): return lax.all_to_all(pay, ('row', 'col'), 0, 0)]
    ppermute x28 -> x0, starting transfers between devices: 59.8 us -> none  [the longest x14 41.1 us: with_halo(): lax.ppermute(lax.slice_in_dim(block, block.shape[dim] - width, None, axis...]
    pallas_call x0 -> x13, Pallas kernels: none -> 40 us  [call(): pl.pallas_call(kernel, out_shape=[jax.ShapeDtypeStruct(*plain(x)) for x i...]
    dot_general x47 -> x0, matrix products: 39.7 us -> none  [the longest x36 29.3 us: tap_grads(): jnp.einsum('bhwc,bhwd->cd', padded[:, tap_row:tap_row + row_count, tap_co...]
    ppermute x28 -> x0, waiting for transfers between devices: 29.6 us -> none  [the longest x14 27.5 us: with_halo(): lax.ppermute(lax.slice_in_dim(block, 0, width, axis=dim), axis, backward)]
    psum x1 -> x0, waiting for transfers between devices: 28.7 us -> none  [local(): lax.psum((first_grad, jnp.stack([conv_one, conv_two, conv_three]), head_g...]
    reduce_sum x15 -> x0, other arithmetic: 26.7 us -> none  [the longest x3 8.46 us: norm_back(): jnp.sum(grad_norm, axis=(0, 1, 2))]
  transfers between devices with their start and end apart: 29 -> 2, of which waited for: 12 -> 2; matrix products, arithmetic and copies ran while one was open for 5% -> 0% of each run, Pallas kernels for 0% -> 3%
where the time goes in v3:
time: 143 us
  blocking collectives  76.8 us (54%)
  Pallas kernels  40 us (28%)
  starting transfers between devices  9.87 us (7%)
  waiting for transfers between devices  7.48 us (5%)
  local copies, waits for them, and re-layouts  7.33 us (5%)
    all_to_all x8, blocking collectives, exchange(): return lax.all_to_all(pay, ('row', 'col'), 0, 0)  76.8 us
    pallas_call x13, Pallas kernels, call(): pl.pallas_call(kernel, out_shape=[jax.ShapeDtypeStruct(*plain(x)) for x i...  40 us
    all_to_all x2, starting transfers between devices, exchange(): return lax.all_to_all(pay, ('row', 'col'), 0, 0)  9.87 us
    all_to_all x2, waiting for transfers between devices, exchange(): return lax.all_to_all(pay, ('row', 'col'), 0, 0)  7.48 us
    unnamed x48, local copies, waits for them, and re-layouts  7.33 us
  transfers between devices with their start and end apart: 2, of which 2 were waited for; matrix products, arithmetic and copies ran while one was open for 0% of the time, Pallas kernels for 3%

profile of v3, /device:TPU:0, one launch (start us, length us, event | category | flops | bytes accessed | tf_op | source)
XLA Modules:
  0.0 142.5 jit_solution(1399859503413298050)
XLA Ops:
  4.1 1.1 pack.1
  5.1 7.3 %all-to-all-start = ((bf16[32,16,128]{2,1,0:T(8,128)(2,1)}), bf16[32,16,128]{2,1,0:T(8,128)(2,1)S(1)}, u32[]{:S(2)}, u32[]{:S(2)}) async-start(bf16[32,16,128]{2,1,0:T(8,128)(2,1)} %pack.1), calls=%async_computation | async-start | bytes 262144 | tf_op jit(solution)/shard_map/all_to_all | solution.py:842
  16.3 3.8 %prepare.1 = (bf16[65536,256]{1,0:T(8,128)(2,1)}, bf16[3,128,256]{2,1,0:T(8,128)(2,1)S(1)}, f32[1,128]{1,0:T(1,128)S(1)}, f32[2,128,128]{2,1,0:T(8,128)S(1)}, f32[8,128]{1,0:T(8,128)S(1)}) custom-call(f32[10,2,32]{2,1,0:T(2,128)S(1)} %copy-done.10, f32[3,9,32,32]{3,2,1,0:T(8,128)S(1)} %copy-done, f32[2,32,32]{2,1,0:T(8,128)S(1)} %copy-done.5, ...), custom_call_target="tpu_custom_call" | custom-call | tf_op jit(solution)/shard_map/prepare/pallas_call | solution.py:829
  20.7 2.3 %image_conv.1 = (bf16[42,16,128]{2,1,0:T(8,128)(2,1)S(1)}, f32[40,2,16,128]{3,2,1,0:T(8,128)S(1)}, f32[32,1,128]{2,1,0:T(1,128)S(1)}) custom-call(s32[3]{0:T(128)S(1)} %pad_add_fusion.place, bf16[32,16,128]{2,1,0:T(8,128)(2,1)S(1)} %all-to-all-done.got, bf16[3,128,256]{2,1,0:T(8,128)(2,1)S(1)} %get-tuple-element.78.first_mat), custom_call_target="tpu_custom_call" | custom-call | tf_op jit(solution)/shard_map/image_conv/pallas_call | solution.py:829
  23.0 12.4 %all_to_all.50.got.got_count = f32[32,1,128]{2,1,0:T(1,128)S(1)} all-to-all(f32[32,1,128]{2,1,0:T(1,128)S(1)} %get-tuple-element.79), channel_id=1, replica_groups=mesh['row'=8,'col'=4] {'row','col'}, dimensions={0} | all-to-all | bytes 32768 | tf_op jit(solution)/shard_map/all_to_all | solution.py:842
  35.4 2.7 %first_block.1 = (f32[40,2,16,128]{3,2,1,0:T(8,128)S(1)}, f32[32,1,128]{2,1,0:T(1,128)S(1)}, f32[8,128]{1,0:T(8,128)S(1)}, f32[2048,2,16,128]{3,2,1,0:T(8,128)}, bf16[2731,3,16,128]{3,2,1,0:T(8,128)(2,1)}) custom-call(s32[3]{0:T(128)S(1)} %pad_add_fusion.place, f32[32,1,128]{2,1,0:T(1,128)S(1)} %all_to_all.50.got.got_count, ...), custom_call_target="tpu_custom_call" | custom-call | tf_op jit(solution)/shard_map/first_block/pallas_call | solution.py:829
  38.1 8.8 %all_to_all.51.got = f32[32,1,128]{2,1,0:T(1,128)S(1)} all-to-all(f32[32,1,128]{2,1,0:T(1,128)S(1)} %get-tuple-element.84), channel_id=1, replica_groups=mesh['row'=8,'col'=4] {'row','col'}, dimensions={0} | all-to-all | bytes 32768 | tf_op jit(solution)/shard_map/all_to_all | solution.py:842
  46.9 5.9 %pool_and_merge.1 = (f32[40,2,16,128]{3,2,1,0:T(8,128)S(1)}, f32[32,1,128]{2,1,0:T(1,128)S(1)}, f32[8,128]{1,0:T(8,128)S(1)}, f32[2048,2,16,128]{3,2,1,0:T(8,128)}, bf16[2731,3,16,128]{3,2,1,0:T(8,128)(2,1)}) custom-call(s32[3]{0:T(128)S(1)} %pad_add_fusion.place, f32[32,1,128]{2,1,0:T(1,128)S(1)} %all_to_all.51.got, ...), custom_call_target="tpu_custom_call", output_to_operand_aliasing={{3}: (5, {}), {4}: (6, {})} | custom-call | tf_op jit(solution)/shard_map/pool_and_merge/pallas_call | solution.py:829
  52.9 8.8 %all_to_all.52.got.got_style = f32[32,1,128]{2,1,0:T(1,128)S(1)} all-to-all(f32[32,1,128]{2,1,0:T(1,128)S(1)} %get-tuple-element.88), channel_id=1, replica_groups=mesh['row'=8,'col'=4] {'row','col'}, dimensions={0} | all-to-all | bytes 32768 | tf_op jit(solution)/shard_map/all_to_all | solution.py:842
  61.7 3.2 %decoder.1 = (f32[40,2,16,128]{3,2,1,0:T(8,128)S(1)}, f32[32,1,128]{2,1,0:T(1,128)S(1)}, f32[8,128]{1,0:T(8,128)S(1)}, f32[32,128]{1,0:T(8,128)S(1)}, f32[2048,2...) custom-call(s32[3]{0:T(128)S(1)} %pad_add_fusion.place, ...), custom_call_target="tpu_custom_call", output_to_operand_aliasing={{4}: (7, {}), {5}: (8, {})} | custom-call | tf_op jit(solution)/shard_map/decoder/pallas_call | solution.py:829
  64.9 8.8 %all_to_all.53.got.got_three = f32[32,1,128]{2,1,0:T(1,128)S(1)} all-to-all(f32[32,1,128]{2,1,0:T(1,128)S(1)} %get-tuple-element.94), channel_id=1, replica_groups=mesh['row'=8,'col'=4] {'row','col'}, dimensions={0} | all-to-all | bytes 32768 | tf_op jit(solution)/shard_map/all_to_all | solution.py:842
  73.7 2.7 %head.1 = (f32[40,2,16,128]{3,2,1,0:T(8,128)S(1)}, f32[40,2,16,128]{3,2,1,0:T(8,128)S(1)}, f32[32,2,128]{2,1,0:T(2,128)S(1)}, f32[8,128]{1,0:T(8,128)S(1)}) custom-call(s32[3]{0:T(128)S(1)} %pad_add_fusion.place, f32[32,1,128]{2,1,0:T(1,128)S(1)} %all_to_all.53.got.got_three, f32[32,1,128]{2,1,0:T(1,128)S(1)} %all_to_all.50.got.got_count, ...), custom_call_target="tpu_custom_call" | custom-call | tf_op jit(solution)/shard_map/head/pallas_call | solution.py:829
  76.4 8.9 %all_to_all.54.got.got_head = f32[32,2,128]{2,1,0:T(2,128)S(1)} all-to-all(f32[32,2,128]{2,1,0:T(2,128)S(1)} %get-tuple-element.97), channel_id=1, replica_groups=mesh['row'=8,'col'=4] {'row','col'}, dimensions={0} | all-to-all | bytes 65536 | tf_op jit(solution)/shard_map/all_to_all | solution.py:842
  85.3 4.2 %residual_back.1 = (f32[40,2,16,128]{3,2,1,0:T(8,128)S(1)}, f32[40,2,16,128]{3,2,1,0:T(8,128)S(1)}, f32[32,4,128]{2,1,0:T(4,128)S(1)}, f32[2048,2,16,128]{3,2,1,0:T(8,128)}) custom-call(s32[3]{0:T(128)S(1)} %pad_add_fusion.place, f32[32,2,128]{2,1,0:T(2,128)S(1)} %all_to_all.54.got.got_head, ...), custom_call_target="tpu_custom_call", output_to_operand_aliasing={{3}: (7, {})} | custom-call | tf_op jit(solution)/shard_map/residual_back/pallas_call | solution.py:829
  89.6 9.1 %all_to_all.55.got.got_two = f32[32,4,128]{2,1,0:T(4,128)S(1)} all-to-all(f32[32,4,128]{2,1,0:T(4,128)S(1)} %get-tuple-element.103), channel_id=1, replica_groups=mesh['row'=8,'col'=4] {'row','col'}, dimensions={0} | all-to-all | bytes 131072 | tf_op jit(solution)/shard_map/all_to_all | solution.py:842
  98.7 4.5 %merged_back.1 = (f32[40,2,16,128]{3,2,1,0:T(8,128)S(1)}, f32[32,2,4,128]{3,2,1,0:T(4,128)S(1)}) custom-call(s32[3]{0:T(128)S(1)} %pad_add_fusion.place, f32[32,4,128]{2,1,0:T(4,128)S(1)} %all_to_all.55.got.got_two, f32[40,2,16,128]{3,2,1,0:T(8,128)S(1)} %get-tuple-element.104.grad, f32[40,2,16,128]{3,2,1,0:T(8,128)S(1)} %get-tuple-element.105.xhat, ...), custom_call_target="tpu_custom_call" | custom-call | tf_op jit(solution)/shard_map/merged_back/pallas_call | solution.py:829
  103.2 9.9 %all_to_all.56.got.got_one_back = f32[32,2,4,128]{3,2,1,0:T(4,128)S(1)} all-to-all(f32[32,2,4,128]{3,2,1,0:T(4,128)S(1)} %get-tuple-element.108), channel_id=1, replica_groups=mesh['row'=8,'col'=4] {'row','col'}, dimensions={0} | all-to-all | bytes 262144 | tf_op jit(solution)/shard_map/all_to_all | solution.py:842
  113.3 4.9 %summed_back.1 = (f32[40,2,16,128]{3,2,1,0:T(8,128)S(1)}, f32[40,2,16,128]{3,2,1,0:T(8,128)S(1)}, f32[32,2,4,128]{3,2,1,0:T(4,128)S(1)}, f32[8,128]{1,0:T(8,128)S(1)}) custom-call(s32[3]{0:T(128)S(1)} %pad_add_fusion.place, f32[32,2,4,128]{3,2,1,0:T(4,128)S(1)} %all_to_all.56.got.got_one_back, f32[32,4,128]{2,1,0:T(4,128)S(1)} %all_to_all.55.got.got_two, ...), custom_call_target="tpu_custom_call" | custom-call | tf_op jit(solution)/shard_map/summed_back/pallas_call | solution.py:829
  118.2 9.9 %all_to_all.57.got.got_first = f32[32,2,4,128]{3,2,1,0:T(4,128)S(1)} all-to-all(f32[32,2,4,128]{3,2,1,0:T(4,128)S(1)} %get-tuple-element.110), channel_id=1, replica_groups=mesh['row'=8,'col'=4] {'row','col'}, dimensions={0} | all-to-all | bytes 262144 | tf_op jit(solution)/shard_map/all_to_all | solution.py:842
  128.1 1.9 %first_back.1.pay = f32[32,2,4,128]{3,2,1,0:T(4,128)} custom-call(s32[3]{0:T(128)S(1)} %pad_add_fusion.place, f32[32,2,4,128]{3,2,1,0:T(4,128)S(1)} %all_to_all.57.got.got_first, f32[40,2,16,128]{3,2,1,0:T(8,128)S(1)} %get-tuple-element.111.grad, f32[40,2,16,128]{3,2,1,0:T(8,128)S(1)} %get-tuple-element.112.xhat, f32[8,128]{1,0:T(8,128)S(1)} %get-tuple-element.113.vec, ...), custom_call_target="tpu_custom_call" | custom-call | tf_op jit(solution)/shard_map/first_back/pallas_call | solution.py:829
  130.0 2.6 %all-to-all-start.9 = ((f32[32,2,4,128]{3,2,1,0:T(4,128)}), f32[32,2,4,128]{3,2,1,0:T(4,128)S(1)}, u32[]{:S(2)}, u32[]{:S(2)}) async-start(f32[32,2,4,128]{3,2,1,0:T(4,128)} %first_back.1.pay), calls=%async_computation.9 | async-start | bytes 262144 | tf_op jit(solution)/shard_map/all_to_all | solution.py:842
  132.7 1.1 update_early.1
  133.8 7.1 %all-to-all-done.9.got = f32[32,2,4,128]{3,2,1,0:T(4,128)S(1)} async-done(((f32[32,2,4,128]{3,2,1,0:T(4,128)}), f32[32,2,4,128]{3,2,1,0:T(4,128)S(1)}, u32[]{:S(2)}, u32[]{:S(2)}) %all-to-all-start.9) | async-done | bytes 131104 | tf_op jit(solution)/shard_map/all_to_all | solution.py:842
  140.9 1.7 %update_late.1 = (f32[10,2,32]{2,1,0:T(2,128)}, f32[10,2,32]{2,1,0:T(2,128)}, f32[10,2,32]{2,1,0:T(2,128)}, bf16[10,2,32]{2,1,0:T(2,128)(2,1)}, f32[3,9,32,32]{3...) custom-call(f32[32,2,4,128]{3,2,1,0:T(4,128)S(1)} %all-to-all-done.9.got, ...), custom_call_target="tpu_custom_call" | custom-call | tf_op jit(solution)/shard_map/update_late/pallas_call | solution.py:829
  (50 shorter events, 7.8 us)
Async XLA Ops:
  0.7 0.9 copy-start.4
  1.6 0.8 copy-start.7
  2.4 0.8 copy-start.8
  3.2 0.8 copy-start.9
  5.1 15.5 %all-to-all-start = ((bf16[32,16,128]{2,1,0:T(8,128)(2,1)}), bf16[32,16,128]{2,1,0:T(8,128)(2,1)S(1)}, u32[]{:S(2)}, u32[]{:S(2)}) async-start(bf16[32,16,128]{2,1,0:T(8,128)(2,1)} %pack.1), calls=%async_computation | async-start | bytes 262144 | tf_op jit(solution)/shard_map/all_to_all | solution.py:842
  12.5 1.0 copy-start
  13.5 0.8 copy-start.5
  14.2 0.7 copy-start.10
  113.1 19.5 %copy-start.6 = (f32[2,32,32]{2,1,0:T(8,128)S(1)}, f32[2,32,32]{2,1,0:T(8,128)}, u32[]{:S(2)}) copy-start(f32[2,32,32]{2,1,0:T(8,128)} %w_style.3) | copy-start | bytes 24580
  113.1 19.5 %copy-start.12 = (f32[2,32,32]{2,1,0:T(8,128)S(1)}, f32[2,32,32]{2,1,0:T(8,128)}, u32[]{:S(2)}) copy-start(f32[2,32,32]{2,1,0:T(8,128)} %m_style.1) | copy-start | bytes 24580
  113.2 19.5 %copy-start.13 = (f32[2,32,32]{2,1,0:T(8,128)S(1)}, f32[2,32,32]{2,1,0:T(8,128)}, u32[]{:S(2)}) copy-start(f32[2,32,32]{2,1,0:T(8,128)} %s_style.1) | copy-start | bytes 24580
  113.2 19.5 %copy-start.15 = (f32[2,4,32]{2,1,0:T(4,128)S(1)}, f32[2,4,32]{2,1,0:T(4,128)}, u32[]{:S(2)}) copy-start(f32[2,4,32]{2,1,0:T(4,128)} %table.3) | copy-start | bytes 3076
  113.2 19.5 %copy-start.19 = (f32[33,3]{0,1:T(4,128)S(1)}, f32[33,3]{0,1:T(4,128)}, u32[]{:S(2)}) copy-start(f32[33,3]{0,1:T(4,128)} %param.26) | copy-start | bytes 1192
  113.2 19.5 %copy-start.20 = (f32[2,4,32]{2,1,0:T(4,128)S(1)}, f32[2,4,32]{2,1,0:T(4,128)}, u32[]{:S(2)}) copy-start(f32[2,4,32]{2,1,0:T(4,128)} %m_norms.1) | copy-start | bytes 3076
  113.2 19.5 %copy-start.21 = (f32[2,4,32]{2,1,0:T(4,128)S(1)}, f32[2,4,32]{2,1,0:T(4,128)}, u32[]{:S(2)}) copy-start(f32[2,4,32]{2,1,0:T(4,128)} %s_norms.1) | copy-start | bytes 3076
  113.2 19.5 %copy-start.22 = (f32[33,3]{0,1:T(4,128)S(1)}, f32[33,3]{0,1:T(4,128)}, u32[]{:S(2)}) copy-start(f32[33,3]{0,1:T(4,128)} %param.31) | copy-start | bytes 1192
  113.2 19.5 %copy-start.23 = (f32[33,3]{0,1:T(4,128)S(1)}, f32[33,3]{0,1:T(4,128)}, u32[]{:S(2)}) copy-start(f32[33,3]{0,1:T(4,128)} %param.36) | copy-start | bytes 1192
  113.2 27.6 %copy-start.1 = (f32[3,9,32,32]{3,2,1,0:T(8,128)S(1)}, f32[3,9,32,32]{3,2,1,0:T(8,128)}, u32[]{:S(2)}) copy-start(f32[3,9,32,32]{3,2,1,0:T(8,128)} %w_convs.3) | copy-start | bytes 331780
  113.2 27.6 %copy-start.2 = (f32[3,9,32,32]{3,2,1,0:T(8,128)S(1)}, f32[3,9,32,32]{3,2,1,0:T(8,128)}, u32[]{:S(2)}) copy-start(f32[3,9,32,32]{3,2,1,0:T(8,128)} %m_convs.1) | copy-start | bytes 331780
  113.2 27.6 %copy-start.3 = (f32[3,9,32,32]{3,2,1,0:T(8,128)S(1)}, f32[3,9,32,32]{3,2,1,0:T(8,128)}, u32[]{:S(2)}) copy-start(f32[3,9,32,32]{3,2,1,0:T(8,128)} %s_convs.1) | copy-start | bytes 331780
  113.3 27.6 %copy-start.11 = (f32[10,2,32]{2,1,0:T(2,128)S(1)}, f32[10,2,32]{2,1,0:T(2,128)}, u32[]{:S(2)}) copy-start(f32[10,2,32]{2,1,0:T(2,128)} %w_first.3) | copy-start | bytes 7684
  113.3 27.6 %copy-start.16 = (f32[10,2,32]{2,1,0:T(2,128)S(1)}, f32[10,2,32]{2,1,0:T(2,128)}, u32[]{:S(2)}) copy-start(f32[10,2,32]{2,1,0:T(2,128)} %m_first.1) | copy-start | bytes 7684
  113.3 27.6 %copy-start.17 = (f32[10,2,32]{2,1,0:T(2,128)S(1)}, f32[10,2,32]{2,1,0:T(2,128)}, u32[]{:S(2)}) copy-start(f32[10,2,32]{2,1,0:T(2,128)} %s_first.1) | copy-start | bytes 7684
  130.0 10.8 %all-to-all-start.9 = ((f32[32,2,4,128]{3,2,1,0:T(4,128)}), f32[32,2,4,128]{3,2,1,0:T(4,128)S(1)}, u32[]{:S(2)}, u32[]{:S(2)}) async-start(f32[32,2,4,128]{3,2,1,0:T(4,128)} %first_back.1.pay), calls=%async_computation.9 | async-start | bytes 262144 | tf_op jit(solution)/shard_map/all_to_all | solution.py:842
  (2 other events, 1.4 us)

commit v4 on v3

--- a/solution.py
+++ b/solution.py
@@ -28,10 +28,10 @@
 F32 = jnp.float32
 BF16 = jnp.bfloat16
 VMEM_LIMIT = 36 * 1024 * 1024
+WHOLE_VMEM = 56 * 1024 * 1024
 STORE_BYTES = 32 * 1024 * 1024
 FORWARD = 10 * LANES
 BACK = 9 * LANES
-HEAD_AT = 3 * FORWARD + 3 * BACK
 
 
 def lane_of(shape):
@@ -47,8 +47,7 @@
 
 
 def fold(v):
-    v = v + pltpu.roll(v, 64, axis=1)
-    return v + pltpu.roll(v, 32, axis=1)
+    return v + pltpu.roll(v, 32, axis=1) + (pltpu.roll(v, 64, axis=1) + pltpu.roll(v, 96, axis=1))
 
 
 def spread(v, k):
@@ -106,7 +105,7 @@
         body(i)
         return carry
 
-    lax.fori_loop(0, count, step, 0)
+    lax.fori_loop(0, count, step, 0, unroll=min(count, 5))
 
 
 def copies(sems, *pairs):
@@ -164,32 +163,61 @@
     return [y[:, k * LANES : (k + 1) * LANES].reshape(rows, -1, LANES) for k in range(2)]
 
 
+def narrow(v):
+    while v.shape[0] > 1:
+        half = v.shape[0] // 2
+        v = v[:half] + v[half:]
+    return v[0]
+
+
+def row_sums(first, rows, values):
+    step = 4
+
+    def add(i, carry):
+        found = [values(pl.ds(first + step * i, step), k) for k in range(2)]
+        return tuple(c + a + b for c, a, b in zip(carry, *found))
+
+    shapes = jax.eval_shape(lambda: values(pl.ds(0, step), 0))
+    zeros = tuple(jnp.zeros(v.shape, F32) for v in shapes)
+    found = lax.fori_loop(0, rows // step, add, zeros, unroll=min(rows // step, 8))
+    return [col_sum(narrow(v)) for v in found]
+
+
 def local_stats(v, first, rows, count):
-    def add(i, total):
-        return total + v[first + i, 0] + v[first + i, 1]
-
-    zero = jnp.zeros(v.shape[2:], F32)
-    mean = fold(col_sum(lax.fori_loop(0, rows, add, zero, unroll=8))) / count
-
-    def add_square(i, total):
-        a, b = v[first + i, 0] - mean, v[first + i, 1] - mean
-        return total + a * a + b * b
-
-    return mean, fold(col_sum(lax.fori_loop(0, rows, add_square, zero, unroll=8)))
-
-
-def merge_stats(pay, local_count, pixel_count):
-    devices = pay.shape[0]
-    whole = col_sum(pay)
-    mean = spread(whole, 0) / devices
-    away = pay - mean
-    between = spread(col_sum(away * away), 0)
-    spread_sum = spread(whole, 1) + local_count * between
-    return mean, lax.rsqrt(spread_sum / pixel_count + norm_eps)
-
-
-def send(pay, row):
-    pay[...] = jnp.broadcast_to(row.reshape(1, 1, LANES), pay.shape)
+    mean = row_sums(first, rows, lambda at, k: (v[at, k],))[0] * (GRP / count)
+
+    def square(at, k):
+        away = v[at, k] - mean
+        return (away * away,)
+
+    return mean, row_sums(first, rows, square)[0]
+
+
+def merge_stats(means, squares, local_count, pixel_count):
+    mean = fold(col_sum(means)) / (GRP * means.shape[0])
+    away = means - mean
+    total = fold(col_sum(squares + (local_count / GRP) * (away * away)))
+    return mean, lax.rsqrt(total / pixel_count + norm_eps)
+
+
+def send(pay, *rows):
+    value = rows[-1]
+    if len(rows) > 1:
+        at = row_of(pay.shape[1:])
+        value = jnp.broadcast_to(value, pay.shape[1:])
+        for k in range(len(rows) - 2, -1, -1):
+            value = jnp.where(at == k, rows[k], value)
+    pay[...] = jnp.broadcast_to(value[None], pay.shape)
+
+
+def affine(table, q):
+    return tile4(table[0, q : q + 1, :]), tile4(table[1, q : q + 1, :])
+
+
+def diagonal_blocks(mat):
+    wide = tile4(mat)
+    group = group_of(wide.shape)
+    return jnp.concatenate([jnp.where(group == b, wide, 0.0) for b in range(GRP)], axis=0)
 
 
 def notes(ref, *rows):
@@ -201,13 +229,11 @@
     return store.at[FORWARD * i : FORWARD * i + (BACK if i else FORWARD)]
 
 
-def back_at(store, i):
-    return store.at[3 * FORWARD + BACK * i : 3 * FORWARD + BACK * (i + 1)]
-
-
-def pack_kernel(image, flow, labels, valid, out):
+def pack_kernel(image_in, flow_in, labels_in, valid_in, out, image, flow, labels, valid, sems):
+    fetched = copies(sems, (image_in, image), (flow_in, flow), (labels_in, labels), (valid_in, valid))
     images, height, _, width = image.shape
     parts = out.shape[0] // images
+    wait(fetched)
     fields = [image[:, :, c, :].astype(F32) for c in range(2)]
     fields += [flow[:, :, c, :].astype(F32) for c in range(2)]
     fields += [labels[...].astype(F32), valid[...].astype(F32)]
@@ -229,83 +255,78 @@
             out[b * parts + p] = slot
 
 
-def prepare(w_first, w_convs, w_style, w_head, table, store, first_mat, head_bias, style_mat, tab, mats, sems):
-    lane = lane_of((LANES, 2 * LANES))
-    at = row_of((LANES, 2 * LANES))
-    column = lane >> 5
+COLUMNS = ((8, None, None, -1), (0, 1, 2, 3), (4, 5, 6, 7))
+
+
+def conv_matrix(taps, mats, base, back):
+    out_at = group_of((CH, 2 * LANES))
+    for r in range(3):
+        wide = []
+        for s in range(3):
+            if back:
+                k = taps[3 * (2 - r) + s]
+                k = jnp.concatenate([k, k, k, k], axis=0).T
+            else:
+                k = tile4(taps[3 * r + s])
+            wide.append(jnp.concatenate([k, k], axis=1))
+        for d in range(3):
+            for a in range(GRP):
+                val = jnp.zeros((CH, 2 * LANES), F32)
+                column = COLUMNS[d][a]
+                if column is not None:
+                    for s in range(3):
+                        val = jnp.where(out_at == (column + s - 1 if back else column + 1 - s), wide[s], val)
+                mats[pl.ds(base + (3 * r + d) * LANES + CH * a, CH), :] = val.astype(BF16)
+
+
+def image_lanes(shape):
+    at = row_of(shape)
     kind = at >> 5
-    here = (at & 7) + jnp.where(kind == LEFT // 32, -SEG, jnp.where(kind == RIGHT // 32, SEG, 0))
-    image_lane = (kind != 1) & ((at & 31) < 16)
-    channel = (at >> 3) & 1
-    rows = [[None] * 2 for _ in range(10)]
-    for t in range(10):
-        for c in range(2):
-            v = tile4(low(w_first[t][c : c + 1]))
-            rows[t][c] = jnp.concatenate([v, v], axis=1)
-    for r in range(3):
-        val = jnp.zeros((LANES, 2 * LANES), F32)
-        for s in range(3):
-            for c in range(2):
-                hit = image_lane & (channel == c) & (here == column + s - 1)
-                val = jnp.where(hit, rows[3 * r + s][c], val)
-        first_mat[r] = val.astype(BF16)
-    val = jnp.zeros((LANES, 2 * LANES), F32)
-    for c in range(2):
-        val = jnp.where((at < 16) & (channel == c) & (here == column), rows[9][c], val)
+    column = (at & 7) + jnp.where(kind == LEFT // 32, -SEG, jnp.where(kind == RIGHT // 32, SEG, 0))
+    return (kind != 1) & ((at & 31) < 16), (at >> 3) & 1, column
+
+
+def first_taps(w_first, t):
+    found = [tile4(low(w_first[t][c : c + 1])) for c in range(2)]
+    return [jnp.concatenate([v, v], axis=1) for v in found]
+
+
+def image_matrix(w_first, r):
+    shape = (LANES, 2 * LANES)
+    inside, channel, here = image_lanes(shape)
+    val = jnp.zeros(shape, F32)
+    for s in range(3):
+        for c, tap in enumerate(first_taps(w_first, 3 * r + s)):
+            val = jnp.where(inside & (channel == c) & (here == group_of(shape) + s - 1), tap, val)
+    return val.astype(BF16)
+
+
+def prepare(w_first_in, w_convs_in, w_head_in, store, back_zero, back_one, back_two, head_mat, w_first, w_convs, w_head, mats, sems):
+    wait(copies(sems, (w_first_in, w_first), (w_convs_in, w_convs), (w_head_in, w_head)))
+    shape = (LANES, 2 * LANES)
+    inside, channel, here = image_lanes(shape)
+    val = jnp.zeros(shape, F32)
+    for c, tap in enumerate(first_taps(w_first, 9)):
+        val = jnp.where((row_of(shape) < 16) & (channel == c) & (here == group_of(shape)), tap, val)
     mats[BACK:FORWARD, :] = val.astype(BF16)
-
-    out_at = group_of((CH, 2 * LANES))
-    columns = ((8, None, None, -1), (0, 1, 2, 3), (4, 5, 6, 7))
-
-    def layer(i):
-        for r in range(3):
-            wide, tall = [], []
-            for s in range(3):
-                k = tile4(w_convs[i, 3 * r + s])
-                wide.append(jnp.concatenate([k, k], axis=1))
-                k = w_convs[i, 3 * (2 - r) + s]
-                k = jnp.concatenate([k, k, k, k], axis=0).T
-                tall.append(jnp.concatenate([k, k], axis=1))
-            for d in range(3):
-                for a in range(GRP):
-                    spot = (3 * r + d) * LANES + CH * a
-                    val = jnp.zeros((CH, 2 * LANES), F32)
-                    inv = jnp.zeros((CH, 2 * LANES), F32)
-                    at_column = columns[d][a]
-                    if at_column is not None:
-                        for s in range(3):
-                            val = jnp.where(out_at == at_column + 1 - s, wide[s], val)
-                            inv = jnp.where(out_at == at_column + s - 1, tall[s], inv)
-                    mats[pl.ds(i * FORWARD + spot, CH), :] = val.astype(BF16)
-                    mats[pl.ds(3 * FORWARD + i * BACK + spot, CH), :] = inv.astype(BF16)
-
-    loop(3, layer)
-
+    stored = []
+    for i in range(3):
+        conv_matrix(w_convs.at[i], mats, FORWARD * i, False)
+        stored += copies(sems.at[i:], (taps_at(mats, i), taps_at(store, i)))
+    for i, back in enumerate((back_zero, back_one, back_two)):
+        conv_matrix(w_convs.at[i], back, 0, True)
     lane = lane_of((CH, LANES))
     head = jnp.zeros((CH, LANES), F32)
-    bias = zero_row()
     diagonal = row_of((CH, CH)) == lane_of((CH, CH))
     for k in range(3):
         column = jnp.sum(jnp.where(diagonal, low(w_head[k : k + 1, 0:CH]), 0.0), axis=1, keepdims=True)
-        mine = (lane >> 3) == FLOW // 8 + k
-        head = jnp.where(mine, column, head)
-        bias = jnp.where(mine[0:1], low(w_head[k : k + 1, CH : CH + 1]), bias)
-    head_bias[...] = bias
-    empty = jnp.zeros((CH, LANES), F32)
+        head = jnp.where((lane >> 3) == FLOW // 8 + k, column, head)
     for y in range(SEG):
-        val = jnp.where((lane & 7) == y, head, 0.0)
-        mats[HEAD_AT + CH * y : HEAD_AT + CH * (y + 1), :] = jnp.concatenate([val, empty], axis=1).astype(BF16)
-    group = group_of((CH, LANES))
-    for i in range(2):
-        wide = tile4(w_style[i])
-        for b in range(GRP):
-            style_mat[i, CH * b : CH * b + CH, :] = jnp.where(group == b, wide, 0.0)
-    for i in range(2):
-        tab[4 * i : 4 * i + 4, :] = tile4(table[i])
-    wait(copies(sems, (mats, store.at[0 : mats.shape[0]])))
-
-
-def start_kernel(place, got, first_mat, sides, raw, pay, *, local_count, height, sources):
+        head_mat[CH * y : CH * (y + 1), :] = jnp.where((lane & 7) == y, head, 0.0).astype(BF16)
+    wait(stored)
+
+
+def start_kernel(place, got, w_first, prepared, sides, raw, pay, vec, *, local_count, height, sources):
     rows, segments = raw.shape[0], raw.shape[2]
     off, block = place[0], place[1]
     blank(sides)
@@ -323,7 +344,7 @@
     loop(rows // 8, eight)
     y = None
     for r in range(3):
-        part = jnp.dot(flat(sides[r : r + rows]), first_mat[r], preferred_element_type=F32)
+        part = jnp.dot(flat(sides[r : r + rows]), image_matrix(w_first, r), preferred_element_type=F32)
         y = part if y is None else y + part
     raw[:, 0], raw[:, 1] = blocks_of(y, rows)
     mean, square = local_stats(raw, off, height, local_count)
@@ -332,14 +353,15 @@
         mask = mask + sides[off + 1 + i].astype(F32)
     lane = lane_of(mask.shape)
     count = jnp.sum(jnp.where((lane >= MASK) & (lane < MASK + 8), mask, 0.0))
-    send(pay, groups(mean, square, jnp.full((1, LANES), count, F32)))
-
-
-def first_kernel(place, got, raw, sides, tab, weights, summed, pay, vec, fields, lows, hidden, xhat, taps, sems, *, spots, local_count, pixel_count, height):
+    send(pay, mean, square)
+    notes(vec, jnp.full((1, LANES), count, F32))
+
+
+def first_kernel(place, got, raw, sides, table, weights, summed, pay, vec, fields, lows, hidden, xhat, taps, sems, *, spots, local_count, pixel_count, height):
     fetched = copies(sems, (taps_at(weights, 0), taps))
-    mean, inverse = merge_stats(got[:, 0, :], local_count, pixel_count)
+    mean, inverse = merge_stats(got[:, 0, :], got[:, 1, :], local_count, pixel_count)
     notes(vec, inverse)
-    gain, bias = tab[0:1], tab[4:5]
+    gain, bias = affine(table, 0)
     rows = raw.shape[0]
 
     def norm_rows(i):
@@ -358,54 +380,51 @@
     wait(fetched)
     y = conv(hidden, taps, 0, rows, flat(sides[1 : rows + 1]))
     summed[:, 0], summed[:, 1] = blocks_of(y, rows)
-    send(pay, groups(*local_stats(summed, place[0], height, local_count), zero_row()))
+    send(pay, *local_stats(summed, place[0], height, local_count))
     wait(stored)
 
 
-def pool_kernel(place, got, summed, tab, weights, fields_in, lows_in, raw, pay, vec, fields, lows, merged, xhat, shared, taps, sems, *, spots, local_count, pixel_count, height):
+def pool_kernel(place, got, summed, count_in, table, weights, fields_in, lows_in, raw, pay, vec, fields, lows, merged, xhat, shared, taps, sems, *, spots, local_count, pixel_count, height):
     fetched = copies(sems, (taps_at(weights, 1), taps))
-    mean, inverse = merge_stats(got[:, 0, :], local_count, pixel_count)
-    gain, bias = tab[1:2], tab[5:6]
+    mean, inverse = merge_stats(got[:, 0, :], got[:, 1, :], local_count, pixel_count)
+    gain, bias = affine(table, 1)
     rows, segments = summed.shape[0], summed.shape[2]
-    own = place[0] // 2
-
-    def pair(p, carry):
-        out = [[None, None], [None, None]]
-        sums = [jnp.zeros((segments, LANES), F32) for _ in range(3)]
+    off = place[0]
+
+    step = 4
+
+    def some(i, carry):
+        at = pl.ds(step * i, step)
+        pairs = (step // 2, 2, segments, LANES)
+        outs, sums = [], [jnp.zeros((step // 2 * segments, LANES), F32) for _ in range(3)]
         for k in range(2):
-            xs, es, ns, ss = [], [], [], []
-            for h in range(2):
-                x = (summed[2 * p + h, k] - mean) * inverse
-                n = x * gain + bias
-                s = sig_of(n)
-                xs.append(x)
-                ns.append(n)
-                ss.append(s)
-                es.append(n * s)
-            top = jnp.maximum(es[0], es[1])
+            x = (summed[at, k] - mean) * inverse
+            n = x * gain + bias
+            sig = sig_of(n)
+            e = (n * sig).reshape(pairs)
+            top = flat(jnp.maximum(e[:, 0], e[:, 1]))
             top = jnp.maximum(top, partner(top))
-            exps = [jnp.exp(e - top) for e in es]
-            whole = exps[0] + exps[1]
+            wide_top = top.reshape(step // 2, 1, segments, LANES)
+            exps = jnp.exp(e - wide_top)
+            whole = flat(exps[:, 0] + exps[:, 1])
             whole = whole + partner(whole)
             pooled = top + jnp.log(whole)
-            over = 1.0 / whole
+            outs.append((e + pooled.reshape(wide_top.shape)).reshape(step, segments, LANES))
+            share = exps * (1.0 / whole).reshape(wide_top.shape) * slope(n, sig).reshape(pairs)
+            share_x = share * x.reshape(pairs)
+            xhat[at, k] = x
+            shared[at, k] = share.reshape(step, segments, LANES)
             sums[0] = sums[0] + pooled
-            for h in range(2):
-                share = exps[h] * over * slope(ns[h], ss[h])
-                xhat[2 * p + h, k] = xs[h]
-                shared[2 * p + h, k] = share
-                sums[1] = sums[1] + share
-                sums[2] = sums[2] + share * xs[h]
-                out[h][k] = (es[h] + pooled)[None]
-        for h in range(2):
-            put_low(merged, 2 * p + h, *out[h])
-        mine = (p >= own) & (p < own + height // 2)
+            sums[1] = sums[1] + flat(share[:, 0] + share[:, 1])
+            sums[2] = sums[2] + flat(share_x[:, 0] + share_x[:, 1])
+        put_low(merged, step * i, *outs)
+        mine = (step * i >= off) & (step * i < off + height)
         keep = jnp.where(mine, 1.0, 0.0)
         return tuple(a + keep * b for a, b in zip(carry, sums))
 
     blank(merged)
-    zero = jnp.zeros((segments, LANES), F32)
-    sums = lax.fori_loop(0, rows // 2, pair, (zero, zero, zero))
+    zero = jnp.zeros((step // 2 * segments, LANES), F32)
+    sums = lax.fori_loop(0, rows // step, some, (zero, zero, zero), unroll=min(rows // step, 5))
     pool_sum, share_sum, share_x = [fold(col_sum(v)) for v in sums]
     stored = copies(
         sems.at[1:],
@@ -416,37 +435,35 @@
     wait(fetched)
     raw[:, 0], raw[:, 1] = blocks_of(conv(merged, taps, 0, rows), rows)
     mean, square = local_stats(raw, place[0], height, local_count)
-    send(pay, groups(mean, square, 0.5 * pool_sum, share_sum))
-    notes(vec, inverse, share_x)
+    send(pay, mean, square, groups(0.5 * pool_sum, share_sum, share_x, count_in[0:1]))
+    notes(vec, inverse)
     wait(stored)
 
 
 def by_image(v, parts):
     devices = v.shape[0]
-    shape = (devices, devices)
-    same = row_of(shape) // parts == lane_of(shape) // parts
-    return jnp.dot(jnp.where(same, 1.0, 0.0), v, precision=highest, preferred_element_type=F32)
+    step = 1
+    while step < parts:
+        upper = (row_of(v.shape) // step) % 2 == 1
+        v = v + jnp.where(upper, pltpu.roll(v, step, axis=0), pltpu.roll(v, devices - step, axis=0))
+        step *= 2
+    return v
 
 
 def mine_of(v, me):
     return col_sum(jnp.where(row_of(v.shape) == me, v, 0.0))
 
 
-def style_kernel(place, got, raw, vec_one, tab, style_mat, weights, fields_in, lows_in, resid, pay, vec, style_out, fields, lows, hidden, xhat, merged, taps, sems, *, spots, local_count, pixel_count, pool_cells, height, parts):
+def style_kernel(place, got, raw, table, w_style, weights, fields_in, lows_in, resid, pay, vec, style_out, fields, lows, hidden, xhat, merged, taps, sems, *, spots, local_count, pixel_count, pool_cells, height, parts):
     fetched = copies(sems, (taps_at(weights, 2), taps), (spots(lows_in, "merged"), merged))
-    got = got[:, 0, :]
-    devices = got.shape[0]
-    style = by_image(spread(got, 2), parts) / pool_cells
+    style = by_image(spread(got[:, 2, :], 0), parts) / pool_cells
     style_out[...] = style
-    one = jnp.dot(style, style_mat[0], precision=highest, preferred_element_type=F32)
-    two = jnp.dot(style, style_mat[1], precision=highest, preferred_element_type=F32)
-    centre = spread(got, 0) + one
-    mean = col_sum(centre) / devices
-    off = centre - mean
-    spread_sum = spread(col_sum(got), 1) + local_count * col_sum(off * off)
-    inverse = lax.rsqrt(spread_sum / pixel_count + norm_eps)
+    one, two = [
+        jnp.dot(style, diagonal_blocks(w_style[i]), precision=highest, preferred_element_type=F32) for i in range(2)
+    ]
+    mean, inverse = merge_stats(got[:, 0, :] + one, got[:, 1, :], local_count, pixel_count)
     notes(vec, inverse)
-    gain, bias = tab[2:3], tab[6:7]
+    gain, bias = affine(table, 2)
     rows = raw.shape[0]
     me = place[2]
     shift = mine_of(one, me) - mean
@@ -468,15 +485,14 @@
     wait(fetched)
     for k, y in enumerate(blocks_of(conv(hidden, taps, 0, rows), rows)):
         resid[:, k] = y + two + merged[1 : rows + 1, k].astype(F32)
-    send(pay, groups(*local_stats(resid, place[0], height, local_count), vec_one[1:2]))
+    send(pay, *local_stats(resid, place[0], height, local_count))
     wait(stored)
 
 
-def head_kernel(place, got, got_count, resid, sides, head_bias, tab, weights, grad, xhat, pay, vec, decoded, slopes, mat, sems, *, local_count, pixel_count, height):
-    fetched = copies(sems, (weights.at[HEAD_AT : HEAD_AT + 2 * LANES], mat))
-    mean, inverse = merge_stats(got[:, 0, :], local_count, pixel_count)
+def head_kernel(place, got, got_style, resid, sides, head_mat, w_head, table, grad, xhat, pay, vec, decoded, slopes, *, local_count, pixel_count, height):
+    mean, inverse = merge_stats(got[:, 0, :], got[:, 1, :], local_count, pixel_count)
     notes(vec, inverse)
-    gain, bias = tab[3:4], tab[7:8]
+    gain, bias = affine(table, 3)
     rows, segments = resid.shape[0], resid.shape[2]
     off = place[0]
 
@@ -491,17 +507,20 @@
             decoded[at, k] = (n * s).astype(BF16)
 
     loop(rows // 4, norm_rows)
-    wait(fetched)
-    head = mat[:, 0:LANES]
+    head = head_mat[...]
     wide = jnp.concatenate([flat(decoded[:, 0]), flat(decoded[:, 1])], axis=1)
-    out = jnp.dot(wide, head, preferred_element_type=F32) + head_bias[...]
+    bias_row = zero_row()
+    for k in range(3):
+        mine = (lane_of((1, LANES)) >> 3) == FLOW // 8 + k
+        bias_row = jnp.where(mine, low(w_head[k : k + 1, CH : CH + 1]), bias_row)
+    out = jnp.dot(wide, head, preferred_element_type=F32) + bias_row
     given = flat(sides[1 : rows + 1]).astype(F32)
     lane = lane_of(given.shape)
     is_flow = lane < LABEL
     near = [pltpu.roll(given, LANES - MASK + first, axis=1) for first in (FLOW, FLOW + 8, LABEL)]
     mask = jnp.where(lane < FLOW + 8, near[0], jnp.where(is_flow, near[1], near[2]))
     mask = jnp.where((lane >= FLOW) & (lane < LABEL + 8), mask, 0.0)
-    count = jnp.sum(got_count[:, 0, 64:65])
+    count = jnp.sum(got_style[:, 2, 3 * CH : 3 * CH + 1])
     diff = out - given / flow_scale
     hinge = jnp.maximum(out, 0.0) + jnp.log1p(jnp.exp(-jnp.abs(out)))
     loss = mask * jnp.where(is_flow, diff * diff, hinge - given * out)
@@ -531,17 +550,11 @@
 
 
 def own_sums(grad, xhat, first, rows):
-    def add(i, carry):
-        shift, scale = carry
-        for k in range(2):
-            g = grad[first + i, k]
-            shift = shift + g
-            scale = scale + g * xhat[first + i, k]
-        return shift, scale
-
-    zero = jnp.zeros(grad.shape[2:], F32)
-    shift, scale = lax.fori_loop(0, rows, add, (zero, zero), unroll=8)
-    return fold(col_sum(shift)), fold(col_sum(scale))
+    def both(at, k):
+        g = grad[at, k]
+        return g, g * xhat[at, k]
+
+    return [fold(v) for v in row_sums(first, rows, both)]
 
 
 def back_sums(got, pixel_count):
@@ -550,10 +563,7 @@
 
 
 def low_sum(grad_low, first, rows):
-    def add(i, total):
-        return total + grad_low[first + 1 + i, 0].astype(F32) + grad_low[first + 1 + i, 1].astype(F32)
-
-    return fold(col_sum(lax.fori_loop(0, rows, add, jnp.zeros(grad_low.shape[2:], F32), unroll=8)))
+    return fold(row_sums(first + 1, rows, lambda at, k: (grad_low[at, k].astype(F32),))[0])
 
 
 def norm_back(grad, xhat, factor, shift, scale):
@@ -591,11 +601,11 @@
         out[:, q, :] = val
 
 
-def residual_kernel(place, got, grad, xhat, vec, tab, weights, fields_in, lows, below, below_x, pay, fields, grad_low, kept_grad, back, field, sems, *, spots, pixel_count, height):
-    fetched = copies(sems, (back_at(weights, 2), back), (spots(fields_in, "xhat_two"), below_x), (spots(lows, "hidden_three"), field))
+def residual_kernel(place, got, grad, xhat, vec, table, back, fields_in, lows, below, below_x, pay, fields, grad_low, kept_grad, field, sems, *, spots, pixel_count, height):
+    fetched = copies(sems, (spots(fields_in, "xhat_two"), below_x), (spots(lows, "hidden_three"), field))
     devices = got.shape[0]
     shift, scale = back_sums(got[:, 0, :], pixel_count)
-    factor = tab[3:4] * vec[0:1]
+    factor = affine(table, 3)[0] * vec[0:1]
     rows = grad.shape[0]
     off = place[0]
 
@@ -605,22 +615,21 @@
         return g
 
     back_rows(grad_low, rows, value)
-    stored = copies(sems.at[3:], (kept_grad, spots(fields, "grad_resid")))
+    stored = copies(sems.at[2:], (kept_grad, spots(fields, "grad_resid")))
     image_sum = low_sum(grad_low, off, height)
-    gain, bias = tab[2:3], tab[6:7]
+    gain, bias = affine(table, 2)
     wait(fetched)
     for k, y in enumerate(blocks_of(conv(grad_low, back, 0, rows), rows)):
         below[:, k] = y * slope_at(below_x[:, k], gain, bias)
     row = groups(*own_sums(below, below_x, off, height), image_sum, zero_row())
-    pay[...] = jnp.broadcast_to(row[None], pay.shape)
+    send(pay, row)
     tap_sums(field, grad_low, off, height, pay.at[0:CH, 1:4])
     wait(stored)
 
 
-def merged_kernel(place, got, grad, xhat, vec, tab, weights, fields, lows, below, pay, kept_grad, below_x, shared, grad_low, back, field, sems, *, spots, pixel_count, height):
+def merged_kernel(place, got, grad, xhat, vec, table, back, fields, lows, below, below_x, shared, pay, kept_grad, grad_low, field, sems, *, spots, pixel_count, height):
     fetched = copies(
         sems,
-        (back_at(weights, 1), back),
         (spots(fields, "grad_resid"), kept_grad),
         (spots(fields, "xhat_one"), below_x),
         (spots(fields, "shared"), shared),
@@ -629,12 +638,12 @@
     devices = got.shape[0]
     gathered = jnp.sum(got[...], axis=0)
     shift, scale = spread(gathered[0:1], 0) / pixel_count, spread(gathered[0:1], 1) / pixel_count
-    factor = tab[2:3] * vec[0:1]
+    factor = affine(table, 2)[0] * vec[0:1]
     rows = grad.shape[0]
     off = place[0]
     back_rows(grad_low, rows, lambda at, k: norm_back(grad[at, k], xhat[at, k], factor, shift, scale))
     image_sum = low_sum(grad_low, off, height)
-    gain, bias = tab[1:2], tab[5:6]
+    gain, bias = affine(table, 1)
     wait(fetched)
     for k, y in enumerate(blocks_of(conv(grad_low, back, 0, rows), rows)):
         g = (y + kept_grad[:, k]).reshape(rows // 2, 2, -1, LANES)
@@ -651,12 +660,9 @@
     pay[0:CH, 1, 3, :] = jnp.zeros((CH, LANES), F32)
 
 
-def summed_kernel(place, got, got_two, got_style, got_three, grad, vec, tab, style_mat, sides, weights, fields, lows, below, below_x, pay, more, shared, xhat, back, field, grad_low, sems, *, spots, pixel_count, pool_cells, height, parts):
+def summed_kernel(place, got, got_two, got_style, grad, xhat, shared, vec, table, w_style, sides, back, fields, lows, below, below_x, pay, more, field, grad_low, sems, *, spots, pixel_count, pool_cells, height, parts):
     fetched = copies(
         sems,
-        (spots(fields, "shared"), shared),
-        (spots(fields, "xhat_one"), xhat),
-        (back_at(weights, 0), back),
         (spots(fields, "xhat_zero"), below_x),
         (spots(lows, "hidden_one"), field),
     )
@@ -665,25 +671,24 @@
     rows = grad.shape[0]
     dims = (((1,), (1,)), ((), ()))
     first = got[:, 0, 0, :]
-    grad_style = lax.dot_general(spread(first, 2), style_mat[0], dims, precision=highest, preferred_element_type=F32)
-    grad_style = grad_style + lax.dot_general(
-        spread(got_two[:, 0, :], 2), style_mat[1], dims, precision=highest, preferred_element_type=F32
-    )
-    grad_style = by_image(grad_style, parts) / pool_cells
+    each = lax.dot_general(
+        spread(first, 2), diagonal_blocks(w_style[0]), dims, precision=highest, preferred_element_type=F32
+    ) + lax.dot_general(
+        spread(got_two[:, 0, :], 2), diagonal_blocks(w_style[1]), dims, precision=highest, preferred_element_type=F32
+    )
+    each = each / pool_cells
     total = col_sum(first)
-    shift = spread(total, 0) + col_sum(grad_style * spread(got_style[:, 0, :], 3))
-    scale = spread(total, 1) + col_sum(grad_style * spread(got_three[:, 0, :], 2))
-    mine = mine_of(grad_style, place[2])
-    factor = tab[1:2] * vec[0:1]
+    shift = spread(total, 0) + col_sum(each * by_image(spread(got_style[:, 2, :], 1), parts))
+    scale = spread(total, 1) + col_sum(each * by_image(spread(got_style[:, 2, :], 2), parts))
+    mine = col_sum(jnp.where(row_of(each.shape) // parts == place[2] // parts, each, 0.0))
+    factor = affine(table, 1)[0] * vec[0:1]
     shift_mean, scale_mean = shift / pixel_count, scale / pixel_count
-    wait(fetched[:2])
-
     def value(at, k):
         return norm_back(grad[at, k] + shared[at, k] * mine, xhat[at, k], factor, shift_mean, scale_mean)
 
     back_rows(grad_low, rows, value)
-    gain, bias = tab[0:1], tab[4:5]
-    wait(fetched[2:])
+    gain, bias = affine(table, 0)
+    wait(fetched)
     for k, y in enumerate(blocks_of(conv(grad_low, back, 0, rows), rows)):
         below[:, k] = y * slope_at(below_x[:, k], gain, bias)
     row = groups(*own_sums(below, below_x, off, height), zero_row())
@@ -703,27 +708,25 @@
 def pixel_taps(sides, row, rows, grad, shift):
     x = flat(sides[pl.ds(row, rows)])
     found = lax.dot_general(x, grad, (((0,), (0,)), ((), ())), preferred_element_type=F32)
-    at = row_of(found.shape)
-    kind = at >> 5
-    here = (at & 7) + jnp.where(kind == LEFT // 32, -SEG, jnp.where(kind == RIGHT // 32, SEG, 0)) - group_of(found.shape)
-    image_lane = (kind != 1) & ((at & 31) < 16)
+    inside, channel, here = image_lanes(found.shape)
+    here = here - group_of(found.shape)
     out = []
     for s in shift:
         both = []
         for c in range(2):
-            hit = image_lane & (((at >> 3) & 1) == c) & (here == s)
+            hit = inside & (channel == c) & (here == s)
             v = col_sum(jnp.where(hit, found, 0.0))
             both.append(fold(v[:, 0:LANES] + v[:, LANES:]))
         out.append(both)
     return out
 
 
-def first_back_kernel(place, got, grad, xhat, vec, more, tab, sides, pay, *, pixel_count, height):
+def first_back_kernel(place, got, grad, xhat, vec, more, table, sides, pay, *, pixel_count, height):
     devices = got.shape[0]
     off = place[0]
     whole = col_sum(got[:, 0, 0, :])
     shift, scale = spread(whole, 0) / pixel_count, spread(whole, 1) / pixel_count
-    factor = tab[0:1] * vec[0:1]
+    factor = affine(table, 0)[0] * vec[0:1]
     at = pl.ds(off, height)
     low_grad = jnp.concatenate(
         [flat(norm_back(grad[at, k], xhat[at, k], factor, shift, scale).astype(BF16)) for k in range(2)], axis=1
@@ -756,14 +759,14 @@
 
 
 def update_early(
-    got_first, got_one_back, got_two, got_head, got_count, pay, more, style,
+    got_first, got_one_back, got_two, got_head, got_style, pay, more, style,
     w_style, w_head, table, m_style, m_head, m_norms, s_style, s_head, s_norms,
     loss_out, count_out,
     style_master, style_moment, style_square,
     head_master, head_moment, head_square, head_copy,
     norms_master, norms_moment, norms_square,
 ):
-    count_out[0, 0] = jnp.sum(got_count[:, 0, 64:65])
+    count_out[0, 0] = jnp.sum(got_style[:, 2, 3 * CH : 3 * CH + 1])
     loss_out[0, 0] = jnp.sum(got_head[:, 1, 99:100])
     dims = (((0,), (0,)), ((), ()))
     for i, sums in enumerate((got_one_back[:, 0, 0, :], got_two[:, 0, :])):
@@ -815,7 +818,7 @@
     return ("far", x)
 
 
-def call(kernel, outs, *operands, scalars=0, scratch=(), sems=0, scalar_outs=(), aliases=None, name):
+def call(kernel, outs, *operands, scalars=0, scratch=(), sems=0, scalar_outs=(), aliases=None, limit=VMEM_LIMIT, name):
     smem = pl.BlockSpec(memory_space=pltpu.SMEM)
     vmem = pl.BlockSpec(memory_space=pltpu.VMEM)
     hbm = pl.BlockSpec(memory_space=pltpu.HBM)
@@ -833,7 +836,7 @@
         out_specs=out_specs,
         scratch_shapes=shapes,
         input_output_aliases=aliases or {},
-        compiler_params=pltpu.CompilerParams(vmem_limit_bytes=VMEM_LIMIT),
+        compiler_params=pltpu.CompilerParams(vmem_limit_bytes=limit),
         name=name,
     )(*[plain(x) for x in operands])
 
@@ -874,10 +877,11 @@
     field = ((rows, 2, segments, LANES), F32)
     low_field = ((rows + 2, 3, segments, LANES), BF16)
     vec = ((8, LANES), F32)
-    one_row = ((devices, 1, LANES), F32)
+    two_rows = ((devices, 2, LANES), F32)
+    four_rows = ((devices, 4, LANES), F32)
     two_chunks = ((devices, 2, 4, LANES), F32)
+    nine = ((BACK, 2 * LANES), BF16)
     taps_scratch = ((FORWARD, 2 * LANES), BF16)
-    nine_scratch = ((BACK, 2 * LANES), BF16)
 
     places = {
         name: i * count
@@ -897,99 +901,97 @@
         row_bytes = shape[1] * segments * LANES * jnp.dtype(dtype).itemsize
         return far(((-(-STORE_BYTES // row_bytes),) + shape[1:], dtype))
 
+    inputs = (
+        jnp.transpose(image_batch, (0, 1, 3, 2)), jnp.transpose(flow_target, (0, 1, 3, 2)), cell_labels, valid_mask
+    )
     (pay,) = call(
         pack_kernel,
         [((devices, 16, LANES), BF16)],
-        jnp.transpose(image_batch, (0, 1, 3, 2)), jnp.transpose(flow_target, (0, 1, 3, 2)), cell_labels, valid_mask,
-        name="pack",
+        *[far(v) for v in inputs],
+        scratch=[(v.shape, v.dtype) for v in inputs], sems=4, limit=WHOLE_VMEM, name="pack",
     )
     got_inputs = exchange(pay)
-    weights, first_mat, head_bias, style_mat, tab = call(
+    head_rows = w_head.T
+    weights, *back, head_mat = call(
         prepare,
-        [
-            far(((STORE_BYTES // (4 * LANES), 2 * LANES), BF16)),
-            ((3, LANES, 2 * LANES), BF16),
-            ((1, LANES), F32),
-            ((2, LANES, LANES), F32),
-            vec,
-        ],
-        w_first, w_convs, w_style, w_head.T, batch_norm_table,
-        scratch=[((HEAD_AT + 2 * LANES, 2 * LANES), BF16)], sems=1, name="prepare",
-    )
-
-    sides, raw, pay = call(
+        [far(((STORE_BYTES // (4 * LANES), 2 * LANES), BF16)), nine, nine, nine, ((2 * LANES, LANES), BF16)],
+        far(w_first), far(w_convs), far(head_rows),
+        scratch=[(w_first.shape, F32), (w_convs.shape, F32), (head_rows.shape, F32), ((3 * FORWARD, 2 * LANES), BF16)],
+        sems=3, limit=WHOLE_VMEM, name="prepare",
+    )
+
+    sides, raw, pay, count = call(
         part(start_kernel, local_count=local_count, height=height, sources=col_count),
-        [((rows + 2, segments, LANES), BF16), field, one_row],
-        place, got_inputs, first_mat,
+        [((rows + 2, segments, LANES), BF16), field, two_rows, vec],
+        place, got_inputs, w_first, far(weights),
         scalars=1, name="image_conv",
     )
     got_zero = exchange(pay)
-
     summed, pay, inv_zero, fields, lows = call(
         part(first_kernel, spots=spots, **counts),
-        [field, one_row, vec, store_of(field), store_of(low_field)],
-        place, got_zero, raw, sides, tab, far(weights),
+        [field, two_rows, vec, store_of(field), store_of(low_field)],
+        place, got_zero, raw, sides, batch_norm_table, far(weights),
         scalars=1, scratch=[low_field, field, taps_scratch], sems=3, name="first_block",
     )
     got_one = exchange(pay)
 
     raw, pay, inv_one, fields, lows = call(
         part(pool_kernel, spots=spots, **counts),
-        [field, one_row, vec, store_of(field), store_of(low_field)],
-        place, got_one, summed, tab, far(weights), far(fields), far(lows),
-        scalars=1, scratch=[low_field, field, field, nine_scratch], sems=4,
-        aliases={5: 3, 6: 4}, name="pool_and_merge",
+        [field, four_rows, vec, store_of(field), store_of(low_field)],
+        place, got_one, summed, count, batch_norm_table, far(weights), far(fields), far(lows),
+        scalars=1, scratch=[low_field, field, field, nine], sems=4,
+        aliases={6: 3, 7: 4}, name="pool_and_merge",
     )
     got_style = exchange(pay)
 
     resid, pay, inv_two, style, fields, lows = call(
         part(style_kernel, spots=spots, **styled, **counts),
-        [field, one_row, vec, ((devices, LANES), F32), store_of(field), store_of(low_field)],
-        place, got_style, raw, inv_one, tab, style_mat, far(weights), far(fields), far(lows),
-        scalars=1, scratch=[low_field, field, low_field, nine_scratch], sems=4,
-        aliases={7: 4, 8: 5}, name="decoder",
+        [field, two_rows, vec, ((devices, LANES), F32), store_of(field), store_of(low_field)],
+        place, got_style, raw, batch_norm_table, w_style, far(weights), far(fields), far(lows),
+        scalars=1, scratch=[low_field, field, low_field, nine], sems=4,
+        aliases={6: 4, 7: 5}, name="decoder",
     )
     got_three = exchange(pay)
 
     grad_three, xhat_three, pay, inv_three = call(
         part(head_kernel, **counts),
-        [field, field, ((devices, 2, LANES), F32), vec],
-        place, got_three, got_zero, resid, sides, head_bias, tab, far(weights),
-        scalars=1, scratch=[((rows, 2, segments, LANES), BF16), field, ((2 * LANES, 2 * LANES), BF16)], sems=1,
+        [field, field, two_rows, vec],
+        place, got_three, got_style, resid, sides, head_mat, head_rows, batch_norm_table,
+        scalars=1, scratch=[((rows, 2, segments, LANES), BF16), field],
         name="head",
     )
     got_head = exchange(pay)
 
     grad_two, xhat_two, pay, fields = call(
         part(residual_kernel, spots=spots, **backs),
-        [field, field, ((devices, 4, LANES), F32), store_of(field)],
-        place, got_head, grad_three, xhat_three, inv_three, tab, far(weights), far(fields), far(lows),
-        scalars=1, scratch=[low_field, field, nine_scratch, low_field], sems=4,
+        [field, field, four_rows, store_of(field)],
+        place, got_head, grad_three, xhat_three, inv_three, batch_norm_table, back[2], far(fields), far(lows),
+        scalars=1, scratch=[low_field, field, low_field], sems=3,
         aliases={7: 3}, name="residual_back",
     )
     got_two = exchange(pay)
 
-    grad_one, pay = call(
+    grad_one, xhat_one, shared, pay = call(
         part(merged_kernel, spots=spots, **backs),
-        [field, two_chunks],
-        place, got_two, grad_two, xhat_two, inv_two, tab, far(weights), far(fields), far(lows),
-        scalars=1, scratch=[field, field, field, low_field, nine_scratch, low_field], sems=5, name="merged_back",
+        [field, field, field, two_chunks],
+        place, got_two, grad_two, xhat_two, inv_two, batch_norm_table, back[1], far(fields), far(lows),
+        scalars=1, scratch=[field, low_field, low_field], sems=4, name="merged_back",
     )
     got_one_back = exchange(pay)
 
     grad_zero, xhat_zero, pay, more = call(
         part(summed_kernel, spots=spots, **styled, **backs),
         [field, field, two_chunks, vec],
-        place, got_one_back, got_two, got_style, got_three, grad_one, inv_one, tab, style_mat, sides,
-        far(weights), far(fields), far(lows),
-        scalars=1, scratch=[field, field, nine_scratch, low_field, low_field], sems=5, name="summed_back",
+        place, got_one_back, got_two, got_style, grad_one, xhat_one, shared, inv_one, batch_norm_table, w_style, sides,
+        back[0], far(fields), far(lows),
+        scalars=1, scratch=[low_field, low_field], sems=2, name="summed_back",
     )
     got_first = exchange(pay)
 
     (pay,) = call(
         part(first_back_kernel, **backs),
         [two_chunks],
-        place, got_first, grad_zero, xhat_zero, inv_zero, more, tab, sides,
+        place, got_first, grad_zero, xhat_zero, inv_zero, more, batch_norm_table, sides,
         scalars=1, name="first_back",
     )
     got_last = exchange(pay)
@@ -997,11 +999,10 @@
     def results(param, copy):
         return [(param.shape, F32)] * 3 + [(param.shape, BF16)] * copy
 
-    head_rows = w_head.T
     early = call(
         update_early,
         [((1, 1), F32), ((1, 1), F32)] + results(w_style, 0) + results(head_rows, 1) + results(batch_norm_table, 0),
-        got_first, got_one_back, got_two, got_head, got_zero, far(pay), more, style,
+        got_first, got_one_back, got_two, got_head, got_style, far(pay), more, style,
         w_style, head_rows, batch_norm_table, mom_style, mom_head.T, mom_norms, sqr_style, sqr_head.T, sqr_norms,
         scalar_outs=(0, 1), name="update_early",
     )

time: 143 us -> 129 us (0.902)
  Pallas kernels: 40 us -> 32 us
  local copies, waits for them, and re-layouts: 7.33 us -> 0.8 us
  waiting for transfers between devices: 7.48 us -> 10.9 us
  blocking collectives: 76.8 us -> 74.1 us
    pallas_call x13, Pallas kernels: 40 us -> 32 us  [call(): pl.pallas_call(kernel, out_shape=[jax.ShapeDtypeStruct(*plain(x)) for x i...]
    unnamed x48 -> x40, local copies, waits for them, and re-layouts: 7.33 us -> 0.8 us
    all_to_all x2, waiting for transfers between devices: 7.48 us -> 10.9 us  [exchange(): return lax.all_to_all(pay, ('row', 'col'), 0, 0)]
    all_to_all x8, blocking collectives: 76.8 us -> 74.1 us  [exchange(): return lax.all_to_all(pay, ('row', 'col'), 0, 0)]
  transfers between devices with their start and end apart: 2 -> 2, of which waited for: 2 -> 2; matrix products, arithmetic and copies ran while one was open for 0% -> 0% of each run, Pallas kernels for 3% -> 4%
where the time goes in v4:
time: 129 us
  blocking collectives  74.1 us (57%)
  Pallas kernels  32 us (25%)
  waiting for transfers between devices  10.9 us (8%)
  starting transfers between devices  9.88 us (8%)
    all_to_all x8, blocking collectives, exchange(): return lax.all_to_all(pay, ('row', 'col'), 0, 0)  74.1 us
    pallas_call x13, Pallas kernels, call(): pl.pallas_call(kernel, out_shape=[jax.ShapeDtypeStruct(*plain(x)) for x i...  32 us
    all_to_all x2, waiting for transfers between devices, exchange(): return lax.all_to_all(pay, ('row', 'col'), 0, 0)  10.9 us
    all_to_all x2, starting transfers between devices, exchange(): return lax.all_to_all(pay, ('row', 'col'), 0, 0)  9.88 us
  transfers between devices with their start and end apart: 2, of which 2 were waited for; matrix products, arithmetic and copies ran while one was open for 0% of the time, Pallas kernels for 4%

profile of v4, /device:TPU:0, one launch (start us, length us, event | category | flops | bytes accessed | tf_op | source)
XLA Modules:
  0.0 128.7 jit_solution(3838451728552595794)
XLA Ops:
  0.7 2.0 %pack.1 = bf16[32,16,128]{2,1,0:T(8,128)(2,1)} custom-call(bf16[16,8,2,32]{3,2,1,0:T(2,128)(2,1)} %bitcast.20, s32[16,8,2,32]{3,2,1,0:T(2,128)} %bitcast.19, s32[16,8,32]{2,1,0:T(8,128)} %labels_in.1, s32[16,8,32]{2,1,0:T(8,128)} %valid_in.1), custom_call_target="tpu_custom_call" | custom-call | tf_op jit(solution)/shard_map/pack/pallas_call | solution.py:832
  2.7 7.3 %all-to-all-start = ((bf16[32,16,128]{2,1,0:T(8,128)(2,1)}), bf16[32,16,128]{2,1,0:T(8,128)(2,1)S(1)}, u32[]{:S(2)}, u32[]{:S(2)}) async-start(bf16[32,16,128]{2,1,0:T(8,128)(2,1)} %pack.1), calls=%async_computation | async-start | bytes 262144 | tf_op jit(solution)/shard_map/all_to_all | solution.py:845
  10.1 4.4 %prepare.1 = (bf16[65536,256]{1,0:T(8,128)(2,1)}, bf16[1152,256]{1,0:T(8,128)(2,1)}, bf16[1152,256]{1,0:T(8,128)(2,1)}, bf16[1152,256]{1,0:T(8,128)(2,1)}, bf16[256,128]{1,0:T(8,128)(2,1)}) custom-call(f32[10,2,32]{2,1,0:T(2,128)} %w_first.3, f32[3,9,32,32]{3,2,1,0:T(8,128)} %w_convs.1, f32[3,33]{1,0:T(4,128)} %bitcast.14), custom_call_target="tpu_custom_call" | custom-call | tf_op jit(solution)/shard_map/prepare/pallas_call | solution.py:832
  14.5 3.7 %all-to-all-done.got = bf16[32,16,128]{2,1,0:T(8,128)(2,1)S(1)} async-done(((bf16[32,16,128]{2,1,0:T(8,128)(2,1)}), bf16[32,16,128]{2,1,0:T(8,128)(2,1)S(1)}, u32[]{:S(2)}, u32[]{:S(2)}) %all-to-all-start) | async-done | bytes 131104 | tf_op jit(solution)/shard_map/all_to_all | solution.py:845
  19.0 1.4 %image_conv.1 = (bf16[42,16,128]{2,1,0:T(8,128)(2,1)S(1)}, f32[40,2,16,128]{3,2,1,0:T(8,128)S(1)}, f32[32,2,128]{2,1,0:T(2,128)S(1)}, f32[8,128]{1,0:T(8,128)S(1)}) custom-call(s32[3]{0:T(128)S(1)} %pad_add_fusion.place, bf16[32,16,128]{2,1,0:T(8,128)(2,1)S(1)} %all-to-all-done.got, f32[10,2,32]{2,1,0:T(2,128)S(1)} %copy-done.8, ...), custom_call_target="tpu_custom_call" | custom-call | tf_op jit(solution)/shard_map/image_conv/pallas_call | solution.py:832
  20.4 9.2 %all_to_all.50.got = f32[32,2,128]{2,1,0:T(2,128)S(1)} all-to-all(f32[32,2,128]{2,1,0:T(2,128)S(1)} %get-tuple-element.82), channel_id=1, replica_groups=mesh['row'=8,'col'=4] {'row','col'}, dimensions={0} | all-to-all | bytes 65536 | tf_op jit(solution)/shard_map/all_to_all | solution.py:845
  29.5 2.4 %first_block.1 = (f32[40,2,16,128]{3,2,1,0:T(8,128)S(1)}, f32[32,2,128]{2,1,0:T(2,128)S(1)}, f32[8,128]{1,0:T(8,128)S(1)}, f32[2048,2,16,128]{3,2,1,0:T(8,128)}, bf16[2731,3,16,128]{3,2,1,0:T(8,128)(2,1)}) custom-call(s32[3]{0:T(128)S(1)} %pad_add_fusion.place, f32[32,2,128]{2,1,0:T(2,128)S(1)} %all_to_all.50.got, ...), custom_call_target="tpu_custom_call" | custom-call | tf_op jit(solution)/shard_map/first_block/pallas_call | solution.py:832
  31.9 8.9 %all_to_all.51.got = f32[32,2,128]{2,1,0:T(2,128)S(1)} all-to-all(f32[32,2,128]{2,1,0:T(2,128)S(1)} %get-tuple-element.85), channel_id=1, replica_groups=mesh['row'=8,'col'=4] {'row','col'}, dimensions={0} | all-to-all | bytes 65536 | tf_op jit(solution)/shard_map/all_to_all | solution.py:845
  40.9 2.6 %pool_and_merge.1 = (f32[40,2,16,128]{3,2,1,0:T(8,128)S(1)}, f32[32,4,128]{2,1,0:T(4,128)S(1)}, f32[8,128]{1,0:T(8,128)S(1)}, f32[2048,2,16,128]{3,2,1,0:T(8,128)}, bf16[2731,3,16,128]{3,2,1,0:T(8,128)(2,1)}) custom-call(s32[3]{0:T(128)S(1)} %pad_add_fusion.place, f32[32,2,128]{2,1,0:T(2,128)S(1)} %all_to_all.51.got, ...), custom_call_target="tpu_custom_call", output_to_operand_aliasing={{3}: (6, {}), {4}: (7, {})} | custom-call | tf_op jit(solution)/shard_map/pool_and_merge/pallas_call | solution.py:832
  43.5 9.1 %all_to_all.52.got.got_style = f32[32,4,128]{2,1,0:T(4,128)S(1)} all-to-all(f32[32,4,128]{2,1,0:T(4,128)S(1)} %get-tuple-element.90), channel_id=1, replica_groups=mesh['row'=8,'col'=4] {'row','col'}, dimensions={0} | all-to-all | bytes 131072 | tf_op jit(solution)/shard_map/all_to_all | solution.py:845
  52.6 2.8 %decoder.1 = (f32[40,2,16,128]{3,2,1,0:T(8,128)S(1)}, f32[32,2,128]{2,1,0:T(2,128)S(1)}, f32[8,128]{1,0:T(8,128)S(1)}, f32[32,128]{1,0:T(8,128)S(1)}, f32[2048,2...) custom-call(s32[3]{0:T(128)S(1)} %pad_add_fusion.place, ...), custom_call_target="tpu_custom_call", output_to_operand_aliasing={{4}: (6, {}), {5}: (7, {})} | custom-call | tf_op jit(solution)/shard_map/decoder/pallas_call | solution.py:832
  55.4 8.9 %all_to_all.53.got = f32[32,2,128]{2,1,0:T(2,128)S(1)} all-to-all(f32[32,2,128]{2,1,0:T(2,128)S(1)} %get-tuple-element.94), channel_id=1, replica_groups=mesh['row'=8,'col'=4] {'row','col'}, dimensions={0} | all-to-all | bytes 65536 | tf_op jit(solution)/shard_map/all_to_all | solution.py:845
  64.3 2.2 %head.1 = (f32[40,2,16,128]{3,2,1,0:T(8,128)S(1)}, f32[40,2,16,128]{3,2,1,0:T(8,128)S(1)}, f32[32,2,128]{2,1,0:T(2,128)S(1)}, f32[8,128]{1,0:T(8,128)S(1)}) custom-call(s32[3]{0:T(128)S(1)} %pad_add_fusion.place, f32[32,2,128]{2,1,0:T(2,128)S(1)} %all_to_all.53.got, f32[32,4,128]{2,1,0:T(4,128)S(1)} %all_to_all.52.got.got_style, ...), custom_call_target="tpu_custom_call" | custom-call | tf_op jit(solution)/shard_map/head/pallas_call | solution.py:832
  66.5 8.9 %all_to_all.54.got.got_head = f32[32,2,128]{2,1,0:T(2,128)S(1)} all-to-all(f32[32,2,128]{2,1,0:T(2,128)S(1)} %get-tuple-element.97), channel_id=1, replica_groups=mesh['row'=8,'col'=4] {'row','col'}, dimensions={0} | all-to-all | bytes 65536 | tf_op jit(solution)/shard_map/all_to_all | solution.py:845
  75.4 3.2 %residual_back.1 = (f32[40,2,16,128]{3,2,1,0:T(8,128)S(1)}, f32[40,2,16,128]{3,2,1,0:T(8,128)S(1)}, f32[32,4,128]{2,1,0:T(4,128)S(1)}, f32[2048,2,16,128]{3,2,1,0:T(8,128)}) custom-call(s32[3]{0:T(128)S(1)} %pad_add_fusion.place, f32[32,2,128]{2,1,0:T(2,128)S(1)} %all_to_all.54.got.got_head, ...), custom_call_target="tpu_custom_call", output_to_operand_aliasing={{3}: (7, {})} | custom-call | tf_op jit(solution)/shard_map/residual_back/pallas_call | solution.py:832
  78.7 9.1 %all_to_all.55.got.got_two = f32[32,4,128]{2,1,0:T(4,128)S(1)} all-to-all(f32[32,4,128]{2,1,0:T(4,128)S(1)} %get-tuple-element.104), channel_id=1, replica_groups=mesh['row'=8,'col'=4] {'row','col'}, dimensions={0} | all-to-all | bytes 131072 | tf_op jit(solution)/shard_map/all_to_all | solution.py:845
  87.8 3.5 %merged_back.1 = (f32[40,2,16,128]{3,2,1,0:T(8,128)S(1)}, f32[40,2,16,128]{3,2,1,0:T(8,128)S(1)}, f32[40,2,16,128]{3,2,1,0:T(8,128)S(1)}, f32[32,2,4,128]{3,2,1,0:T(4,128)S(1)}) custom-call(s32[3]{0:T(128)S(1)} %pad_add_fusion.place, f32[32,4,128]{2,1,0:T(4,128)S(1)} %all_to_all.55.got.got_two, f32[40,2,16,128]{3,2,1,0:T(8,128)S(1)} %get-tuple-element.105.grad, ...), custom_call_target="tpu_custom_call" | custom-call | tf_op jit(solution)/shard_map/merged_back/pallas_call | solution.py:832
  91.3 9.9 %all_to_all.56.got.got_one_back = f32[32,2,4,128]{3,2,1,0:T(4,128)S(1)} all-to-all(f32[32,2,4,128]{3,2,1,0:T(4,128)S(1)} %get-tuple-element.110), channel_id=1, replica_groups=mesh['row'=8,'col'=4] {'row','col'}, dimensions={0} | all-to-all | bytes 262144 | tf_op jit(solution)/shard_map/all_to_all | solution.py:845
  101.4 3.2 %summed_back.1 = (f32[40,2,16,128]{3,2,1,0:T(8,128)S(1)}, f32[40,2,16,128]{3,2,1,0:T(8,128)S(1)}, f32[32,2,4,128]{3,2,1,0:T(4,128)S(1)}, f32[8,128]{1,0:T(8,128)S(1)}) custom-call(s32[3]{0:T(128)S(1)} %pad_add_fusion.place, f32[32,2,4,128]{3,2,1,0:T(4,128)S(1)} %all_to_all.56.got.got_one_back, f32[32,4,128]{2,1,0:T(4,128)S(1)} %all_to_all.55.got.got_two, ...), custom_call_target="tpu_custom_call" | custom-call | tf_op jit(solution)/shard_map/summed_back/pallas_call | solution.py:832
  104.5 9.9 %all_to_all.57.got.got_first = f32[32,2,4,128]{3,2,1,0:T(4,128)S(1)} all-to-all(f32[32,2,4,128]{3,2,1,0:T(4,128)S(1)} %get-tuple-element.116), channel_id=1, replica_groups=mesh['row'=8,'col'=4] {'row','col'}, dimensions={0} | all-to-all | bytes 262144 | tf_op jit(solution)/shard_map/all_to_all | solution.py:845
  114.5 1.8 %first_back.1.pay = f32[32,2,4,128]{3,2,1,0:T(4,128)} custom-call(s32[3]{0:T(128)S(1)} %pad_add_fusion.place, f32[32,2,4,128]{3,2,1,0:T(4,128)S(1)} %all_to_all.57.got.got_first, f32[40,2,16,128]{3,2,1,0:T(8,128)S(1)} %get-tuple-element.117.grad, f32[40,2,16,128]{3,2,1,0:T(8,128)S(1)} %get-tuple-element.118.xhat, f32[8,128]{1,0:T(8,128)S(1)} %get-tuple-element.119.vec, ...), custom_call_target="tpu_custom_call" | custom-call | tf_op jit(solution)/shard_map/first_back/pallas_call | solution.py:832
  116.3 2.6 %all-to-all-start.9 = ((f32[32,2,4,128]{3,2,1,0:T(4,128)}), f32[32,2,4,128]{3,2,1,0:T(4,128)S(1)}, u32[]{:S(2)}, u32[]{:S(2)}) async-start(f32[32,2,4,128]{3,2,1,0:T(4,128)} %first_back.1.pay), calls=%async_computation.9 | async-start | bytes 262144 | tf_op jit(solution)/shard_map/all_to_all | solution.py:845
  119.9 7.1 %all-to-all-done.9.got = f32[32,2,4,128]{3,2,1,0:T(4,128)S(1)} async-done(((f32[32,2,4,128]{3,2,1,0:T(4,128)}), f32[32,2,4,128]{3,2,1,0:T(4,128)S(1)}, u32[]{:S(2)}, u32[]{:S(2)}) %all-to-all-start.9) | async-done | bytes 131104 | tf_op jit(solution)/shard_map/all_to_all | solution.py:845
  127.1 1.6 %update_late.1 = (f32[10,2,32]{2,1,0:T(2,128)}, f32[10,2,32]{2,1,0:T(2,128)}, f32[10,2,32]{2,1,0:T(2,128)}, bf16[10,2,32]{2,1,0:T(2,128)(2,1)}, f32[3,9,32,32]{3...) custom-call(f32[32,2,4,128]{3,2,1,0:T(4,128)S(1)} %all-to-all-done.9.got, ...), custom_call_target="tpu_custom_call" | custom-call | tf_op jit(solution)/shard_map/update_late/pallas_call | solution.py:832
  (42 shorter events, 1.9 us)
Async XLA Ops:
  0.7 28.9 %copy-start.6 = (f32[2,4,32]{2,1,0:T(4,128)S(1)}, f32[2,4,32]{2,1,0:T(4,128)}, u32[]{:S(2)}) copy-start(f32[2,4,32]{2,1,0:T(4,128)} %table.17) | copy-start | bytes 3076
  2.7 15.5 %all-to-all-start = ((bf16[32,16,128]{2,1,0:T(8,128)(2,1)}), bf16[32,16,128]{2,1,0:T(8,128)(2,1)S(1)}, u32[]{:S(2)}, u32[]{:S(2)}) async-start(bf16[32,16,128]{2,1,0:T(8,128)(2,1)} %pack.1), calls=%async_computation | async-start | bytes 262144 | tf_op jit(solution)/shard_map/all_to_all | solution.py:845
  18.3 0.7 copy-start.8
  40.9 11.7 %copy-start.7 = (f32[2,32,32]{2,1,0:T(8,128)S(1)}, f32[2,32,32]{2,1,0:T(8,128)}, u32[]{:S(2)}) copy-start(f32[2,32,32]{2,1,0:T(8,128)} %w_style.5) | copy-start | bytes 24580
  52.6 11.7 %copy-start.10 = (bf16[256,128]{1,0:T(8,128)(2,1)S(1)}, bf16[256,128]{1,0:T(8,128)(2,1)}, u32[]{:S(2)}) copy-start(bf16[256,128]{1,0:T(8,128)(2,1)} %get-tuple-element.96.head_mat) | copy-start | bytes 196612
  52.6 11.7 %copy-start.13 = (f32[33,3]{0,1:T(4,128)S(1)}, f32[33,3]{0,1:T(4,128)}, u32[]{:S(2)}) copy-start(f32[33,3]{0,1:T(4,128)} %param.26) | copy-start | bytes 1192
  52.6 22.8 %copy-start.3 = (bf16[1152,256]{1,0:T(8,128)(2,1)S(1)}, bf16[1152,256]{1,0:T(8,128)(2,1)}, u32[]{:S(2)}) copy-start(bf16[1152,256]{1,0:T(8,128)(2,1)} %get-tuple-element.101.back) | copy-start | bytes 1769476
  75.4 12.3 %copy-start.2 = (bf16[1152,256]{1,0:T(8,128)(2,1)S(1)}, bf16[1152,256]{1,0:T(8,128)(2,1)}, u32[]{:S(2)}) copy-start(bf16[1152,256]{1,0:T(8,128)(2,1)} %get-tuple-element.108.back) | copy-start | bytes 1769476
  87.8 13.5 %copy-start.1 = (bf16[1152,256]{1,0:T(8,128)(2,1)S(1)}, bf16[1152,256]{1,0:T(8,128)(2,1)}, u32[]{:S(2)}) copy-start(bf16[1152,256]{1,0:T(8,128)(2,1)} %get-tuple-element.115.back) | copy-start | bytes 1769476
  101.3 17.6 %copy-start.11 = (f32[2,32,32]{2,1,0:T(8,128)S(1)}, f32[2,32,32]{2,1,0:T(8,128)}, u32[]{:S(2)}) copy-start(f32[2,32,32]{2,1,0:T(8,128)} %m_style.1) | copy-start | bytes 24580
  101.3 17.6 %copy-start.12 = (f32[2,32,32]{2,1,0:T(8,128)S(1)}, f32[2,32,32]{2,1,0:T(8,128)}, u32[]{:S(2)}) copy-start(f32[2,32,32]{2,1,0:T(8,128)} %s_style.1) | copy-start | bytes 24580
  101.3 17.6 %copy-start.16 = (f32[2,4,32]{2,1,0:T(4,128)S(1)}, f32[2,4,32]{2,1,0:T(4,128)}, u32[]{:S(2)}) copy-start(f32[2,4,32]{2,1,0:T(4,128)} %m_norms.1) | copy-start | bytes 3076
  101.3 17.6 %copy-start.17 = (f32[2,4,32]{2,1,0:T(4,128)S(1)}, f32[2,4,32]{2,1,0:T(4,128)}, u32[]{:S(2)}) copy-start(f32[2,4,32]{2,1,0:T(4,128)} %s_norms.1) | copy-start | bytes 3076
  101.3 17.6 %copy-start.18 = (f32[33,3]{0,1:T(4,128)S(1)}, f32[33,3]{0,1:T(4,128)}, u32[]{:S(2)}) copy-start(f32[33,3]{0,1:T(4,128)} %param.31) | copy-start | bytes 1192
  101.3 17.6 %copy-start.19 = (f32[33,3]{0,1:T(4,128)S(1)}, f32[33,3]{0,1:T(4,128)}, u32[]{:S(2)}) copy-start(f32[33,3]{0,1:T(4,128)} %param.36) | copy-start | bytes 1192
  101.3 25.8 %copy-start = (f32[3,9,32,32]{3,2,1,0:T(8,128)S(1)}, f32[3,9,32,32]{3,2,1,0:T(8,128)}, u32[]{:S(2)}) copy-start(f32[3,9,32,32]{3,2,1,0:T(8,128)} %w_convs.1) | copy-start | bytes 331780
  101.3 25.8 %copy-start.4 = (f32[3,9,32,32]{3,2,1,0:T(8,128)S(1)}, f32[3,9,32,32]{3,2,1,0:T(8,128)}, u32[]{:S(2)}) copy-start(f32[3,9,32,32]{3,2,1,0:T(8,128)} %m_convs.1) | copy-start | bytes 331780
  101.3 25.7 %copy-start.5 = (f32[3,9,32,32]{3,2,1,0:T(8,128)S(1)}, f32[3,9,32,32]{3,2,1,0:T(8,128)}, u32[]{:S(2)}) copy-start(f32[3,9,32,32]{3,2,1,0:T(8,128)} %s_convs.1) | copy-start | bytes 331780
  101.3 25.7 %copy-start.9 = (f32[10,2,32]{2,1,0:T(2,128)S(1)}, f32[10,2,32]{2,1,0:T(2,128)}, u32[]{:S(2)}) copy-start(f32[10,2,32]{2,1,0:T(2,128)} %w_first.3) | copy-start | bytes 7684
  101.4 25.7 %copy-start.14 = (f32[10,2,32]{2,1,0:T(2,128)S(1)}, f32[10,2,32]{2,1,0:T(2,128)}, u32[]{:S(2)}) copy-start(f32[10,2,32]{2,1,0:T(2,128)} %m_first.1) | copy-start | bytes 7684
  101.4 25.7 %copy-start.15 = (f32[10,2,32]{2,1,0:T(2,128)S(1)}, f32[10,2,32]{2,1,0:T(2,128)}, u32[]{:S(2)}) copy-start(f32[10,2,32]{2,1,0:T(2,128)} %s_first.1) | copy-start | bytes 7684
  116.3 10.8 %all-to-all-start.9 = ((f32[32,2,4,128]{3,2,1,0:T(4,128)}), f32[32,2,4,128]{3,2,1,0:T(4,128)S(1)}, u32[]{:S(2)}, u32[]{:S(2)}) async-start(f32[32,2,4,128]{3,2,1,0:T(4,128)} %first_back.1.pay), calls=%async_computation.9 | async-start | bytes 262144 | tf_op jit(solution)/shard_map/all_to_all | solution.py:845

commit v5 on v4

--- a/solution.py
+++ b/solution.py
@@ -25,6 +25,7 @@
 RIM = 8
 FLOW, LABEL, MASK = 16, 32, 40
 LEFT, RIGHT = 64, 96
+AFTER, ROW, BEFORE = 32, 33, 64
 F32 = jnp.float32
 BF16 = jnp.bfloat16
 VMEM_LIMIT = 36 * 1024 * 1024
@@ -136,9 +137,15 @@
     return left, right
 
 
-def put_low(ref, row, first, second):
+def put_low(ref, row, first, second, marked=False):
     left, right = beside(first, second)
-    edge = jnp.where(lane_of(left.shape) < 64, right, left)
+    lane = lane_of(left.shape)
+    edge = jnp.where(lane < 64, right, left)
+    if marked:
+        at = lax.broadcasted_iota(jnp.int32, left.shape, 1)
+        edge = jnp.where(lane == ROW, 1.0, edge)
+        edge = jnp.where(lane == AFTER, jnp.where(at == left.shape[1] - 1, 0.0, 1.0), edge)
+        edge = jnp.where(lane == BEFORE, jnp.where(at == 0, 0.0, 1.0), edge)
     at = pl.ds(row + 1, first.shape[0])
     for k, v in enumerate((first, second, edge)):
         ref[at, k] = v.astype(BF16)
@@ -454,8 +461,8 @@
     return col_sum(jnp.where(row_of(v.shape) == me, v, 0.0))
 
 
-def style_kernel(place, got, raw, table, w_style, weights, fields_in, lows_in, resid, pay, vec, style_out, fields, lows, hidden, xhat, merged, taps, sems, *, spots, local_count, pixel_count, pool_cells, height, parts):
-    fetched = copies(sems, (taps_at(weights, 2), taps), (spots(lows_in, "merged"), merged))
+def style_kernel(place, got, raw, table, w_style, w_convs_in, weights, fields_in, lows_in, resid, pay, vec, style_out, fields, lows, hidden, xhat, merged, slopes, w_conv, taps, sems, *, spots, local_count, pixel_count, pool_cells, height, parts):
+    fetched = copies(sems, (taps_at(weights, 2), taps), (spots(lows_in, "merged"), merged), (w_convs_in.at[2], w_conv))
     style = by_image(spread(got[:, 2, :], 0), parts) / pool_cells
     style_out[...] = style
     one, two = [
@@ -476,22 +483,83 @@
             x = (raw[at, k] + shift) * inverse
             xhat[at, k] = x
             n = x * gain + bias
-            out.append(n * sig_of(n))
+            sig = sig_of(n)
+            slopes[at, k] = slope(n, sig)
+            out.append(n * sig)
         put_low(hidden, 4 * i, *out)
 
     blank(hidden)
     loop(rows // 4, norm_rows)
-    stored = copies(sems.at[2:], (xhat, spots(fields, "xhat_two")), (hidden, spots(lows, "hidden_three")))
+    stored = copies(sems.at[3:], (xhat, spots(fields, "xhat_two")), (hidden, spots(lows, "hidden_three")))
     wait(fetched)
     for k, y in enumerate(blocks_of(conv(hidden, taps, 0, rows), rows)):
         resid[:, k] = y + two + merged[1 : rows + 1, k].astype(F32)
-    send(pay, *local_stats(resid, place[0], height, local_count))
     wait(stored)
-
-
-def head_kernel(place, got, got_style, resid, sides, head_mat, w_head, table, grad, xhat, pay, vec, decoded, slopes, *, local_count, pixel_count, height):
+    off = place[0]
+    means, squares = local_stats(resid, off, height, local_count)
+    centre = fold(means) / GRP
+    at = pl.ds(off, height)
+    probe = [slopes[at, k] for k in range(2)]
+    probe += [slopes[at, k] * xhat[at, k] for k in range(2)]
+    probe = jnp.concatenate([flat(v).astype(BF16) for v in probe], axis=1)
+
+    def centred(i):
+        at = pl.ds(4 * i, 4)
+        put_low(hidden, 4 * i, resid[at, 0] - centre, resid[at, 1] - centre, True)
+
+    loop(rows // 4, centred)
+    send(pay, means, squares)
+    pay[0:CH, 2, :] = norm_links(hidden, probe, off, height, w_conv, centre)
+
+
+def norm_links(field, probe, first, rows, taps, centre):
+    wide = jnp.concatenate(views(field, first, rows), axis=1)
+    found = lax.dot_general(probe, wide, (((0,), (0,)), ((), ())), preferred_element_type=F32)
+    group = group_of((CH, LANES))
+    out = []
+    for half in range(2):
+
+        def piece(y, chunk):
+            at = 2 * LANES * half + CH * y
+            return found[at : at + CH, chunk * LANES : (chunk + 1) * LANES]
+
+        plain = jnp.zeros((CH, LANES), F32)
+        moved = jnp.zeros((CH, LANES), F32)
+        for r in range(3):
+            first_edge, last_edge = piece(0, 3 * r), piece(SEG - 1, 3 * r)
+            edge = first_edge + last_edge
+            for y in range(1, SEG - 1):
+                edge = edge + piece(y, 3 * r)
+            inside = edge[:, ROW : ROW + 1]
+            counts = (
+                inside + (first_edge[:, BEFORE : BEFORE + 1] - first_edge[:, ROW : ROW + 1]),
+                inside,
+                inside + (last_edge[:, AFTER : AFTER + 1] - last_edge[:, ROW : ROW + 1]),
+            )
+            for c in range(3):
+                tap = tile4(low(taps[3 * (2 - r) + 2 - c]))
+                val = jnp.zeros((CH, LANES), F32)
+                for y in range(SEG):
+                    d, a = spot_of(y + c - 1)
+                    val = val + jnp.where(group == a, piece(y, 3 * r + d), 0.0)
+                plain = plain + tap * counts[c]
+                moved = moved + tap * val
+        out += [plain, fold(moved) + centre * plain]
+    return groups(*out)
+
+
+def spot_of(x):
+    if x < 0:
+        return 0, 3
+    if x == SEG:
+        return 0, 0
+    return 1 + x // GRP, x % GRP
+
+
+def head_kernel(place, got, got_style, resid, sides, head_mat, w_head, table, back, fields, grad, xhat, pay, vec, decoded, slopes, grad_low, below_x, sems, *, spots, local_count, pixel_count, height):
+    fetched = copies(sems, (spots(fields, "xhat_two"), below_x))
     mean, inverse = merge_stats(got[:, 0, :], got[:, 1, :], local_count, pixel_count)
-    notes(vec, inverse)
+    notes(vec, inverse, mean)
     gain, bias = affine(table, 3)
     rows, segments = resid.shape[0], resid.shape[2]
     off = place[0]
@@ -543,10 +611,21 @@
     y = lax.dot_general(grad_out, head, (((1,), (1,)), ((), ())), preferred_element_type=F32)
     for k, g in enumerate(blocks_of(y, rows)):
         grad[:, k] = g * slopes[:, k]
+    factor = gain * inverse
+    back_rows(grad_low, rows, lambda at, k: factor * grad[at, k])
     shift_sum, scale_sum = own_sums(grad, xhat, off, height)
-    devices = pay.shape[0]
-    pay[:, 0, :] = jnp.broadcast_to(groups(shift_sum, scale_sum, zero_row()), (devices, LANES))
-    pay[:, 1, :] = jnp.broadcast_to(row, (devices, LANES))
+    wait(fetched)
+    y = conv(grad_low, back, 0, rows)
+    slopes[:, 0], slopes[:, 1] = blocks_of(y, rows)
+    gain, bias = affine(table, 2)
+
+    def links(at, k):
+        x = below_x[at, k]
+        g = slopes[at, k] * slope_at(x, gain, bias)
+        return g, g * x
+
+    below = [fold(v) for v in row_sums(off, height, links)]
+    send(pay, groups(shift_sum, scale_sum, *below), row, col_sum(got[:, 2, :]))
 
 
 def own_sums(grad, xhat, first, rows):
@@ -590,7 +669,7 @@
             val = jnp.zeros((CH, LANES), F32)
             for y in range(SEG):
                 x = y + s - 1
-                d, a = (0, 3) if x < 0 else (0, 0) if x == SEG else (1 + x // GRP, x % GRP)
+                d, a = spot_of(x)
                 spot = (3 * r + d) * LANES
                 val = val + jnp.where(group == a, found[CH * y : CH * y + CH, spot : spot + LANES], 0.0)
             taps.append(fold(val))
@@ -601,66 +680,73 @@
         out[:, q, :] = val
 
 
-def residual_kernel(place, got, grad, xhat, vec, table, back, fields_in, lows, below, below_x, pay, fields, grad_low, kept_grad, field, sems, *, spots, pixel_count, height):
-    fetched = copies(sems, (spots(fields_in, "xhat_two"), below_x), (spots(lows, "hidden_three"), field))
+def decoder_back_kernel(place, got, grad, xhat, vec, vec_two, table, back_two, back_one, fields, lows, below, below_x, shared, pay, more, kept_grad, mid_x, mid, low_two, low_one, field_two, field_one, sems, *, spots, pixel_count, height):
+    fetched = copies(
+        sems,
+        (spots(fields, "xhat_two"), mid_x),
+        (spots(fields, "xhat_one"), below_x),
+        (spots(fields, "shared"), shared),
+        (spots(lows, "hidden_three"), field_two),
+        (spots(lows, "merged"), field_one),
+    )
     devices = got.shape[0]
-    shift, scale = back_sums(got[:, 0, :], pixel_count)
-    factor = affine(table, 3)[0] * vec[0:1]
     rows = grad.shape[0]
     off = place[0]
+    total = col_sum(got[:, 0, :])
+    shift, scale = spread(total, 0) / pixel_count, spread(total, 1) / pixel_count
+    inverse, mean = vec[0:1], vec[1:2]
+    factor = affine(table, 3)[0] * inverse
+    slant = scale * inverse
+    held, carried = factor * (shift - slant * mean), factor * slant
+    links = got[0:CH, 2, :] * groups(held, carried, held, carried)
+    group = group_of(links.shape)
+    mine = (lane_of(links.shape) & 31) == row_of(links.shape)
+
+    def across(pick):
+        column = jnp.sum(jnp.where(pick, links, 0.0), axis=1, keepdims=True)
+        return col_sum(jnp.where(mine, column, 0.0))
+
+    shift_two = spread(total, 2) - across(group < 2)
+    scale_two = spread(total, 3) - across(group >= 2)
+    notes(more, scale_two, shift_two)
 
     def value(at, k):
         g = norm_back(grad[at, k], xhat[at, k], factor, shift, scale)
         kept_grad[at, k] = g
         return g
 
-    back_rows(grad_low, rows, value)
-    stored = copies(sems.at[2:], (kept_grad, spots(fields, "grad_resid")))
-    image_sum = low_sum(grad_low, off, height)
+    back_rows(low_two, rows, value)
+    wait(fetched)
+    mid[:, 0], mid[:, 1] = blocks_of(conv(low_two, back_two, 0, rows), rows)
     gain, bias = affine(table, 2)
-    wait(fetched)
-    for k, y in enumerate(blocks_of(conv(grad_low, back, 0, rows), rows)):
-        below[:, k] = y * slope_at(below_x[:, k], gain, bias)
-    row = groups(*own_sums(below, below_x, off, height), image_sum, zero_row())
-    send(pay, row)
-    tap_sums(field, grad_low, off, height, pay.at[0:CH, 1:4])
-    wait(stored)
-
-
-def merged_kernel(place, got, grad, xhat, vec, table, back, fields, lows, below, below_x, shared, pay, kept_grad, grad_low, field, sems, *, spots, pixel_count, height):
-    fetched = copies(
-        sems,
-        (spots(fields, "grad_resid"), kept_grad),
-        (spots(fields, "xhat_one"), below_x),
-        (spots(fields, "shared"), shared),
-        (spots(lows, "merged"), field),
-    )
-    devices = got.shape[0]
-    gathered = jnp.sum(got[...], axis=0)
-    shift, scale = spread(gathered[0:1], 0) / pixel_count, spread(gathered[0:1], 1) / pixel_count
-    factor = affine(table, 2)[0] * vec[0:1]
-    rows = grad.shape[0]
-    off = place[0]
-    back_rows(grad_low, rows, lambda at, k: norm_back(grad[at, k], xhat[at, k], factor, shift, scale))
-    image_sum = low_sum(grad_low, off, height)
+    factor = gain * vec_two[0:1]
+    shift, scale = shift_two / pixel_count, scale_two / pixel_count
+
+    def value_two(at, k):
+        x = mid_x[at, k]
+        return norm_back(mid[at, k] * slope_at(x, gain, bias), x, factor, shift, scale)
+
+    back_rows(low_one, rows, value_two)
+    sum_two = low_sum(low_two, off, height)
+    sum_one = low_sum(low_one, off, height)
+    y = conv(low_one, back_one, 0, rows)
     gain, bias = affine(table, 1)
-    wait(fetched)
-    for k, y in enumerate(blocks_of(conv(grad_low, back, 0, rows), rows)):
+    for k, y in enumerate(blocks_of(y, rows)):
         g = (y + kept_grad[:, k]).reshape(rows // 2, 2, -1, LANES)
         both = flat(g[:, 0] + g[:, 1])
         both = (both + partner(both)).reshape(rows // 2, 1, -1, LANES)
         g = g * slope_at(below_x[:, k], gain, bias).reshape(g.shape) + both * shared[:, k].reshape(g.shape)
         below[:, k] = g.reshape(rows, -1, LANES)
-    row = groups(*own_sums(below, below_x, off, height), image_sum, zero_row())
-    first = jnp.where(row_of((4, LANES)) == 0, row, gathered)
-    pay[:, 0] = jnp.broadcast_to(first[None], (devices, 4, LANES))
+    row = groups(*own_sums(below, below_x, off, height), sum_one, sum_two)
+    pay[:, 0] = jnp.broadcast_to(row[None], (devices, 4, LANES))
     if devices > CH:
         pay[CH:, 1] = jnp.zeros((devices - CH, 4, LANES), F32)
-    tap_sums(field, grad_low, off, height, pay.at[0:CH, 1])
+    tap_sums(field_two, low_two, off, height, pay.at[0:CH, 0, 1:4])
+    tap_sums(field_one, low_one, off, height, pay.at[0:CH, 1])
     pay[0:CH, 1, 3, :] = jnp.zeros((CH, LANES), F32)
 
 
-def summed_kernel(place, got, got_two, got_style, grad, xhat, shared, vec, table, w_style, sides, back, fields, lows, below, below_x, pay, more, field, grad_low, sems, *, spots, pixel_count, pool_cells, height, parts):
+def summed_kernel(place, got, got_style, grad, xhat, shared, vec, table, w_style, sides, back, fields, lows, below, below_x, pay, more, field, grad_low, sems, *, spots, pixel_count, pool_cells, height, parts):
     fetched = copies(
         sems,
         (spots(fields, "xhat_zero"), below_x),
@@ -674,7 +760,7 @@
     each = lax.dot_general(
         spread(first, 2), diagonal_blocks(w_style[0]), dims, precision=highest, preferred_element_type=F32
     ) + lax.dot_general(
-        spread(got_two[:, 0, :], 2), diagonal_blocks(w_style[1]), dims, precision=highest, preferred_element_type=F32
+        spread(first, 3), diagonal_blocks(w_style[1]), dims, precision=highest, preferred_element_type=F32
     )
     each = each / pool_cells
     total = col_sum(first)
@@ -691,14 +777,12 @@
     wait(fetched)
     for k, y in enumerate(blocks_of(conv(grad_low, back, 0, rows), rows)):
         below[:, k] = y * slope_at(below_x[:, k], gain, bias)
-    row = groups(*own_sums(below, below_x, off, height), zero_row())
-    gathered = jnp.sum(got[:, 1], axis=0)
-    chunk = jnp.concatenate([row, gathered[0:3]], axis=0)
+    two, one = jnp.sum(got[:, 0], axis=0), jnp.sum(got[:, 1], axis=0)
+    row = groups(*own_sums(below, below_x, off, height), two[3:4], one[2:3])
+    chunk = jnp.concatenate([row, two[1:3], one[0:1]], axis=0)
     pay[:, 0] = jnp.broadcast_to(chunk[None], (devices, 4, LANES))
-    if devices > CH:
-        pay[CH:, 1] = jnp.zeros((devices - CH, 4, LANES), F32)
-    tap_sums(field, grad_low, off, height, pay.at[0:CH, 1])
-    pay[0:CH, 1, 3, :] = jnp.zeros((CH, LANES), F32)
+    pay[:, 1] = jnp.broadcast_to(one[1:2][None], (devices, 4, LANES))
+    tap_sums(field, grad_low, off, height, pay.at[0:CH, 1, 1:4])
     at = pl.ds(off + 1, height)
     low_own = jnp.concatenate([flat(grad_low[at, 0]), flat(grad_low[at, 1])], axis=1)
     side = pixel_taps(sides, off + 1, height, low_own, (0,))[0]
@@ -738,7 +822,7 @@
     entries.extend([more[2:3], more[3:4]])
     rows = [groups(*entries[4 * q : 4 * q + 4]) for q in range(5)]
     conv_zero = jnp.sum(got[:, 1], axis=0)
-    chunk = [jnp.concatenate(rows[0:4], axis=0), jnp.concatenate([rows[4], conv_zero[0:3]], axis=0)]
+    chunk = [jnp.concatenate(rows[0:4], axis=0), jnp.concatenate([rows[4], conv_zero[1:4]], axis=0)]
     for k in range(2):
         pay[:, k] = jnp.broadcast_to(chunk[k][None], (devices, 4, LANES))
 
@@ -759,7 +843,7 @@
 
 
 def update_early(
-    got_first, got_one_back, got_two, got_head, got_style, pay, more, style,
+    got_first, got_one_back, got_head, got_style, pay, more, more_two, style,
     w_style, w_head, table, m_style, m_head, m_norms, s_style, s_head, s_norms,
     loss_out, count_out,
     style_master, style_moment, style_square,
@@ -769,8 +853,9 @@
     count_out[0, 0] = jnp.sum(got_style[:, 2, 3 * CH : 3 * CH + 1])
     loss_out[0, 0] = jnp.sum(got_head[:, 1, 99:100])
     dims = (((0,), (0,)), ((), ()))
-    for i, sums in enumerate((got_one_back[:, 0, 0, :], got_two[:, 0, :])):
-        grad = lax.dot_general(style[...], spread(sums, 2), dims, precision=highest, preferred_element_type=F32)
+    for i in range(2):
+        sums = spread(got_one_back[:, 0, 0, :], 2 + i)
+        grad = lax.dot_general(style[...], sums, dims, precision=highest, preferred_element_type=F32)
         put(i, (w_style, m_style, s_style), grad[0:CH, 0:CH], rate_table[2], (style_master, style_moment, style_square))
 
     head = col_sum(got_head[:, 1, :])
@@ -783,28 +868,31 @@
     put(slice(None), (w_head, m_head, s_head), grad, rate_table[3], (head_master, head_moment, head_square, head_copy))
 
     three_sums = col_sum(got_head[:, 0, :])
-    two_sums = col_sum(got_two[:, 0, :])
     zero_sums = col_sum(got_first[:, 0, 0, :])
-    scales = [spread(zero_sums, 1), more[0:1], spread(two_sums, 1), spread(three_sums, 1)]
-    shifts = [spread(zero_sums, 0), more[1:2], spread(two_sums, 0), spread(three_sums, 0)]
+    scales = [spread(zero_sums, 1), more[0:1], more_two[0:1], spread(three_sums, 1)]
+    shifts = [spread(zero_sums, 0), more[1:2], more_two[1:2], spread(three_sums, 0)]
     for i, rows in enumerate((scales, shifts)):
         grad = jnp.concatenate(rows, axis=0)[:, 0:CH]
         put(i, (table, m_norms, s_norms), grad, rate_table[4], (norms_master, norms_moment, norms_square))
 
 
 def update_late(
-    got, got_first, got_one_back, w_first, w_convs, m_first, m_convs, s_first, s_convs,
+    got, got_first, w_first, w_convs, m_first, m_convs, s_first, s_convs,
     first_master, first_moment, first_square, first_copy,
     convs_master, convs_moment, convs_square, convs_copy,
 ):
-    sources = [got[0:CH, 1, 1:4, :], got_first[0:CH, 0, 1:4, :], got_one_back[0:CH, 0, 1:4, :]]
     refs = (w_convs, m_convs, s_convs)
     outs = (convs_master, convs_moment, convs_square, convs_copy)
-    for i in range(3):
-        for q in range(3):
-            grad = sources[i][:, q, :].T
-            for b in range(min(4, 9 - 4 * q)):
-                put((i, 4 * q + b), refs, grad[CH * b : CH * b + CH], rate_table[1], outs)
+    last = got_first[0:CH, 0, 0, :].T
+    packs = (
+        [got[0:CH, 1, q, :].T for q in (1, 2, 3)],
+        [got_first[0:CH, 0, 3, :].T, got_first[0:CH, 1, 0, :].T, last[3 * CH :]],
+        [got_first[0:CH, 0, 1, :].T, got_first[0:CH, 0, 2, :].T, last[2 * CH : 3 * CH]],
+    )
+    for i, pack in enumerate(packs):
+        for t in range(9):
+            b = t % 4
+            put((i, t), refs, pack[t // 4][CH * b : CH * b + CH], rate_table[1], outs)
 
     first = jnp.concatenate([jnp.sum(got[:, 0], axis=0), jnp.sum(got[:, 1], axis=0)[0:1]], axis=0)
     refs = (w_first, m_first, s_first)
@@ -886,14 +974,14 @@
     places = {
         name: i * count
         for count, names in (
-            (rows, ("xhat_zero", "xhat_one", "shared", "xhat_two", "grad_resid")),
+            (rows, ("xhat_zero", "xhat_one", "shared", "xhat_two")),
             (rows + 2, ("hidden_one", "hidden_three", "merged")),
         )
         for i, name in enumerate(names)
     }
 
     def spots(store, name):
-        count = rows if name[0] in "xsg" else rows + 2
+        count = rows if name[0] in "xs" else rows + 2
         return store.at[places[name] : places[name] + count]
 
     def store_of(like):
@@ -946,43 +1034,35 @@
 
     resid, pay, inv_two, style, fields, lows = call(
         part(style_kernel, spots=spots, **styled, **counts),
-        [field, two_rows, vec, ((devices, LANES), F32), store_of(field), store_of(low_field)],
-        place, got_style, raw, batch_norm_table, w_style, far(weights), far(fields), far(lows),
-        scalars=1, scratch=[low_field, field, low_field, nine], sems=4,
-        aliases={6: 4, 7: 5}, name="decoder",
+        [field, four_rows, vec, ((devices, LANES), F32), store_of(field), store_of(low_field)],
+        place, got_style, raw, batch_norm_table, w_style, far(w_convs), far(weights), far(fields), far(lows),
+        scalars=1, scratch=[low_field, field, low_field, field, (w_convs.shape[1:], F32), nine], sems=5,
+        aliases={7: 4, 8: 5}, name="decoder",
     )
     got_three = exchange(pay)
 
     grad_three, xhat_three, pay, inv_three = call(
-        part(head_kernel, **counts),
-        [field, field, two_rows, vec],
-        place, got_three, got_style, resid, sides, head_mat, head_rows, batch_norm_table,
-        scalars=1, scratch=[((rows, 2, segments, LANES), BF16), field],
-        name="head",
+        part(head_kernel, spots=spots, **counts),
+        [field, field, four_rows, vec],
+        place, got_three, got_style, resid, sides, head_mat, head_rows, batch_norm_table, back[2], far(fields),
+        scalars=1, scratch=[((rows, 2, segments, LANES), BF16), field, low_field, field], sems=1, name="head",
     )
     got_head = exchange(pay)
 
-    grad_two, xhat_two, pay, fields = call(
-        part(residual_kernel, spots=spots, **backs),
-        [field, field, four_rows, store_of(field)],
-        place, got_head, grad_three, xhat_three, inv_three, batch_norm_table, back[2], far(fields), far(lows),
-        scalars=1, scratch=[low_field, field, low_field], sems=3,
-        aliases={7: 3}, name="residual_back",
-    )
-    got_two = exchange(pay)
-
-    grad_one, xhat_one, shared, pay = call(
-        part(merged_kernel, spots=spots, **backs),
-        [field, field, field, two_chunks],
-        place, got_two, grad_two, xhat_two, inv_two, batch_norm_table, back[1], far(fields), far(lows),
-        scalars=1, scratch=[field, low_field, low_field], sems=4, name="merged_back",
+    grad_one, xhat_one, shared, pay, more_two = call(
+        part(decoder_back_kernel, spots=spots, **backs),
+        [field, field, field, two_chunks, vec],
+        place, got_head, grad_three, xhat_three, inv_three, inv_two, batch_norm_table, back[2], back[1],
+        far(fields), far(lows),
+        scalars=1, scratch=[field, field, field, low_field, low_field, low_field, low_field], sems=5,
+        name="decoder_back",
     )
     got_one_back = exchange(pay)
 
     grad_zero, xhat_zero, pay, more = call(
         part(summed_kernel, spots=spots, **styled, **backs),
         [field, field, two_chunks, vec],
-        place, got_one_back, got_two, got_style, grad_one, xhat_one, shared, inv_one, batch_norm_table, w_style, sides,
+        place, got_one_back, got_style, grad_one, xhat_one, shared, inv_one, batch_norm_table, w_style, sides,
         back[0], far(fields), far(lows),
         scalars=1, scratch=[low_field, low_field], sems=2, name="summed_back",
     )
@@ -1002,14 +1082,14 @@
     early = call(
         update_early,
         [((1, 1), F32), ((1, 1), F32)] + results(w_style, 0) + results(head_rows, 1) + results(batch_norm_table, 0),
-        got_first, got_one_back, got_two, got_head, got_style, far(pay), more, style,
+        got_first, got_one_back, got_head, got_style, far(pay), more, more_two, style,
         w_style, head_rows, batch_norm_table, mom_style, mom_head.T, mom_norms, sqr_style, sqr_head.T, sqr_norms,
         scalar_outs=(0, 1), name="update_early",
     )
     late = call(
         update_late,
         results(w_first, 1) + results(w_convs, 1),
-        got_last, got_first, got_one_back, w_first, w_convs, mom_first, mom_convs, sqr_first, sqr_convs,
+        got_last, got_first, w_first, w_convs, mom_first, mom_convs, sqr_first, sqr_convs,
         name="update_late",
     )
     loss, count = early[0].reshape(()), early[1].reshape(())

time: 129 us -> 123 us (0.953)
  blocking collectives: 74.1 us -> 65.4 us
  Pallas kernels: 32 us -> 34.2 us
    all_to_all x8 -> x7, blocking collectives: 74.1 us -> 65.4 us  [exchange(): return lax.all_to_all(pay, ('row', 'col'), 0, 0)]
    pallas_call x13 -> x12, Pallas kernels: 32 us -> 34.2 us  [call(): pl.pallas_call(kernel, out_shape=[jax.ShapeDtypeStruct(*plain(x)) for x i...]
where the time goes in v5:
time: 123 us; the launch traced here: 122 us
  blocking collectives  65.4 us (53%)
  Pallas kernels  34.2 us (28%)
  waiting for transfers between devices  10.9 us (9%)
  starting transfers between devices  9.88 us (8%)
    all_to_all x7, blocking collectives, exchange(): return lax.all_to_all(pay, ('row', 'col'), 0, 0)  65.4 us
    pallas_call x12, Pallas kernels, call(): pl.pallas_call(kernel, out_shape=[jax.ShapeDtypeStruct(*plain(x)) for x i...  34.2 us
    all_to_all x2, waiting for transfers between devices, exchange(): return lax.all_to_all(pay, ('row', 'col'), 0, 0)  10.9 us
    all_to_all x2, starting transfers between devices, exchange(): return lax.all_to_all(pay, ('row', 'col'), 0, 0)  9.88 us
  transfers between devices with their start and end apart: 2, of which 2 were waited for; matrix products, arithmetic and copies ran while one was open for 0% of the time, Pallas kernels for 4%

profile of v5, /device:TPU:0, one launch (start us, length us, event | category | flops | bytes accessed | tf_op | source)
XLA Modules:
  0.0 122.2 jit_solution(8534732315048805453)
XLA Ops:
  0.7 2.0 %pack.1 = bf16[32,16,128]{2,1,0:T(8,128)(2,1)} custom-call(bf16[16,8,2,32]{3,2,1,0:T(2,128)(2,1)} %bitcast.20, s32[16,8,2,32]{3,2,1,0:T(2,128)} %bitcast.19, s32[16,8,32]{2,1,0:T(8,128)} %labels_in.1, s32[16,8,32]{2,1,0:T(8,128)} %valid_in.1), custom_call_target="tpu_custom_call" | custom-call | tf_op jit(solution)/shard_map/pack/pallas_call | solution.py:920
  2.7 7.3 %all-to-all-start = ((bf16[32,16,128]{2,1,0:T(8,128)(2,1)}), bf16[32,16,128]{2,1,0:T(8,128)(2,1)S(1)}, u32[]{:S(2)}, u32[]{:S(2)}) async-start(bf16[32,16,128]{2,1,0:T(8,128)(2,1)} %pack.1), calls=%async_computation | async-start | bytes 262144 | tf_op jit(solution)/shard_map/all_to_all | solution.py:933
  10.1 4.4 %prepare.1 = (bf16[65536,256]{1,0:T(8,128)(2,1)}, bf16[1152,256]{1,0:T(8,128)(2,1)}, bf16[1152,256]{1,0:T(8,128)(2,1)}, bf16[1152,256]{1,0:T(8,128)(2,1)}, bf16[256,128]{1,0:T(8,128)(2,1)}) custom-call(f32[10,2,32]{2,1,0:T(2,128)} %w_first.3, f32[3,9,32,32]{3,2,1,0:T(8,128)} %w_convs.1, f32[3,33]{1,0:T(4,128)} %bitcast.14), custom_call_target="tpu_custom_call" | custom-call | tf_op jit(solution)/shard_map/prepare/pallas_call | solution.py:920
  14.5 3.7 %all-to-all-done.got = bf16[32,16,128]{2,1,0:T(8,128)(2,1)S(1)} async-done(((bf16[32,16,128]{2,1,0:T(8,128)(2,1)}), bf16[32,16,128]{2,1,0:T(8,128)(2,1)S(1)}, u32[]{:S(2)}, u32[]{:S(2)}) %all-to-all-start) | async-done | bytes 131104 | tf_op jit(solution)/shard_map/all_to_all | solution.py:933
  18.3 0.7 copy-done.8
  19.0 1.4 %image_conv.1 = (bf16[42,16,128]{2,1,0:T(8,128)(2,1)S(1)}, f32[40,2,16,128]{3,2,1,0:T(8,128)S(1)}, f32[32,2,128]{2,1,0:T(2,128)S(1)}, f32[8,128]{1,0:T(8,128)S(1)}) custom-call(s32[3]{0:T(128)S(1)} %pad_add_fusion.place, bf16[32,16,128]{2,1,0:T(8,128)(2,1)S(1)} %all-to-all-done.got, f32[10,2,32]{2,1,0:T(2,128)S(1)} %copy-done.8, ...), custom_call_target="tpu_custom_call" | custom-call | tf_op jit(solution)/shard_map/image_conv/pallas_call | solution.py:920
  20.4 9.2 %all_to_all.45.got = f32[32,2,128]{2,1,0:T(2,128)S(1)} all-to-all(f32[32,2,128]{2,1,0:T(2,128)S(1)} %get-tuple-element.79), channel_id=1, replica_groups=mesh['row'=8,'col'=4] {'row','col'}, dimensions={0} | all-to-all | bytes 65536 | tf_op jit(solution)/shard_map/all_to_all | solution.py:933
  29.5 2.4 %first_block.1 = (f32[40,2,16,128]{3,2,1,0:T(8,128)S(1)}, f32[32,2,128]{2,1,0:T(2,128)S(1)}, f32[8,128]{1,0:T(8,128)S(1)}, f32[2048,2,16,128]{3,2,1,0:T(8,128)}, bf16[2731,3,16,128]{3,2,1,0:T(8,128)(2,1)}) custom-call(s32[3]{0:T(128)S(1)} %pad_add_fusion.place, f32[32,2,128]{2,1,0:T(2,128)S(1)} %all_to_all.45.got, ...), custom_call_target="tpu_custom_call" | custom-call | tf_op jit(solution)/shard_map/first_block/pallas_call | solution.py:920
  31.9 8.9 %all_to_all.46.got = f32[32,2,128]{2,1,0:T(2,128)S(1)} all-to-all(f32[32,2,128]{2,1,0:T(2,128)S(1)} %get-tuple-element.82), channel_id=1, replica_groups=mesh['row'=8,'col'=4] {'row','col'}, dimensions={0} | all-to-all | bytes 65536 | tf_op jit(solution)/shard_map/all_to_all | solution.py:933
  40.9 2.6 %pool_and_merge.1 = (f32[40,2,16,128]{3,2,1,0:T(8,128)S(1)}, f32[32,4,128]{2,1,0:T(4,128)S(1)}, f32[8,128]{1,0:T(8,128)S(1)}, f32[2048,2,16,128]{3,2,1,0:T(8,128)}, bf16[2731,3,16,128]{3,2,1,0:T(8,128)(2,1)}) custom-call(s32[3]{0:T(128)S(1)} %pad_add_fusion.place, f32[32,2,128]{2,1,0:T(2,128)S(1)} %all_to_all.46.got, ...), custom_call_target="tpu_custom_call", output_to_operand_aliasing={{3}: (6, {}), {4}: (7, {})} | custom-call | tf_op jit(solution)/shard_map/pool_and_merge/pallas_call | solution.py:920
  43.5 9.1 %all_to_all.47.got.got_style = f32[32,4,128]{2,1,0:T(4,128)S(1)} all-to-all(f32[32,4,128]{2,1,0:T(4,128)S(1)} %get-tuple-element.87), channel_id=1, replica_groups=mesh['row'=8,'col'=4] {'row','col'}, dimensions={0} | all-to-all | bytes 131072 | tf_op jit(solution)/shard_map/all_to_all | solution.py:933
  52.6 4.7 %decoder.1 = (f32[40,2,16,128]{3,2,1,0:T(8,128)S(1)}, f32[32,4,128]{2,1,0:T(4,128)S(1)}, f32[8,128]{1,0:T(8,128)S(1)}, f32[32,128]{1,0:T(8,128)S(1)}, f32[2048,2...) custom-call(s32[3]{0:T(128)S(1)} %pad_add_fusion.place, ...), custom_call_target="tpu_custom_call", output_to_operand_aliasing={{4}: (7, {}), {5}: (8, {})} | custom-call | tf_op jit(solution)/shard_map/decoder/pallas_call | solution.py:920
  57.3 9.2 %all_to_all.48.got = f32[32,4,128]{2,1,0:T(4,128)S(1)} all-to-all(f32[32,4,128]{2,1,0:T(4,128)S(1)} %get-tuple-element.91), channel_id=1, replica_groups=mesh['row'=8,'col'=4] {'row','col'}, dimensions={0} | all-to-all | bytes 131072 | tf_op jit(solution)/shard_map/all_to_all | solution.py:933
  66.6 3.4 %head.1 = (f32[40,2,16,128]{3,2,1,0:T(8,128)S(1)}, f32[40,2,16,128]{3,2,1,0:T(8,128)S(1)}, f32[32,4,128]{2,1,0:T(4,128)S(1)}, f32[8,128]{1,0:T(8,128)S(1)}) custom-call(s32[3]{0:T(128)S(1)} %pad_add_fusion.place, f32[32,4,128]{2,1,0:T(4,128)S(1)} %all_to_all.48.got, f32[32,4,128]{2,1,0:T(4,128)S(1)} %all_to_all.47.got.got_style, ...), custom_call_target="tpu_custom_call" | custom-call | tf_op jit(solution)/shard_map/head/pallas_call | solution.py:920
  69.9 9.1 %all_to_all.49.got.got_head = f32[32,4,128]{2,1,0:T(4,128)S(1)} all-to-all(f32[32,4,128]{2,1,0:T(4,128)S(1)} %get-tuple-element.96), channel_id=1, replica_groups=mesh['row'=8,'col'=4] {'row','col'}, dimensions={0} | all-to-all | bytes 131072 | tf_op jit(solution)/shard_map/all_to_all | solution.py:933
  79.0 5.8 %decoder_back.1 = (f32[40,2,16,128]{3,2,1,0:T(8,128)S(1)}, f32[40,2,16,128]{3,2,1,0:T(8,128)S(1)}, f32[40,2,16,128]{3,2,1,0:T(8,128)S(1)}, f32[32,2,4,128]{3,2,1,0:T(4,128)S(1)}, f32[8,128]{1,0:T(8,128)S(1)}) custom-call(s32[3]{0:T(128)S(1)} %pad_add_fusion.place, f32[32,4,128]{2,1,0:T(4,128)S(1)} %all_to_all.49.got.got_head, ...), custom_call_target="tpu_custom_call" | custom-call | tf_op jit(solution)/shard_map/decoder_back/pallas_call | solution.py:920
  84.9 9.9 %all_to_all.50.got.got_one_back = f32[32,2,4,128]{3,2,1,0:T(4,128)S(1)} all-to-all(f32[32,2,4,128]{3,2,1,0:T(4,128)S(1)} %get-tuple-element.103), channel_id=1, replica_groups=mesh['row'=8,'col'=4] {'row','col'}, dimensions={0} | all-to-all | bytes 262144 | tf_op jit(solution)/shard_map/all_to_all | solution.py:933
  94.9 3.1 %summed_back.1 = (f32[40,2,16,128]{3,2,1,0:T(8,128)S(1)}, f32[40,2,16,128]{3,2,1,0:T(8,128)S(1)}, f32[32,2,4,128]{3,2,1,0:T(4,128)S(1)}, f32[8,128]{1,0:T(8,128)S(1)}) custom-call(s32[3]{0:T(128)S(1)} %pad_add_fusion.place, f32[32,2,4,128]{3,2,1,0:T(4,128)S(1)} %all_to_all.50.got.got_one_back, f32[32,4,128]{2,1,0:T(4,128)S(1)} %all_to_all.47.got.got_style, ...), custom_call_target="tpu_custom_call" | custom-call | tf_op jit(solution)/shard_map/summed_back/pallas_call | solution.py:920
  98.1 9.9 %all_to_all.51.got.got_first = f32[32,2,4,128]{3,2,1,0:T(4,128)S(1)} all-to-all(f32[32,2,4,128]{3,2,1,0:T(4,128)S(1)} %get-tuple-element.109), channel_id=1, replica_groups=mesh['row'=8,'col'=4] {'row','col'}, dimensions={0} | all-to-all | bytes 262144 | tf_op jit(solution)/shard_map/all_to_all | solution.py:933
  108.0 1.8 %first_back.1.pay = f32[32,2,4,128]{3,2,1,0:T(4,128)} custom-call(s32[3]{0:T(128)S(1)} %pad_add_fusion.place, f32[32,2,4,128]{3,2,1,0:T(4,128)S(1)} %all_to_all.51.got.got_first, f32[40,2,16,128]{3,2,1,0:T(8,128)S(1)} %get-tuple-element.110.grad, f32[40,2,16,128]{3,2,1,0:T(8,128)S(1)} %get-tuple-element.111.xhat, f32[8,128]{1,0:T(8,128)S(1)} %get-tuple-element.112.vec, ...), custom_call_target="tpu_custom_call" | custom-call | tf_op jit(solution)/shard_map/first_back/pallas_call | solution.py:920
  109.8 2.6 %all-to-all-start.8 = ((f32[32,2,4,128]{3,2,1,0:T(4,128)}), f32[32,2,4,128]{3,2,1,0:T(4,128)S(1)}, u32[]{:S(2)}, u32[]{:S(2)}) async-start(f32[32,2,4,128]{3,2,1,0:T(4,128)} %first_back.1.pay), calls=%async_computation.8 | async-start | bytes 262144 | tf_op jit(solution)/shard_map/all_to_all | solution.py:933
  112.4 1.0 update_early.1
  113.5 7.1 %all-to-all-done.8.got = f32[32,2,4,128]{3,2,1,0:T(4,128)S(1)} async-done(((f32[32,2,4,128]{3,2,1,0:T(4,128)}), f32[32,2,4,128]{3,2,1,0:T(4,128)S(1)}, u32[]{:S(2)}, u32[]{:S(2)}) %all-to-all-start.8) | async-done | bytes 131104 | tf_op jit(solution)/shard_map/all_to_all | solution.py:933
  120.6 1.6 %update_late.1 = (f32[10,2,32]{2,1,0:T(2,128)}, f32[10,2,32]{2,1,0:T(2,128)}, f32[10,2,32]{2,1,0:T(2,128)}, bf16[10,2,32]{2,1,0:T(2,128)(2,1)}, f32[3,9,32,32]{3...) custom-call(f32[32,2,4,128]{3,2,1,0:T(4,128)S(1)} %all-to-all-done.8.got, ...), custom_call_target="tpu_custom_call" | custom-call | tf_op jit(solution)/shard_map/update_late/pallas_call | solution.py:920
  (40 shorter events, 0.2 us)
Async XLA Ops:
  0.7 28.9 %copy-start.7 = (f32[2,4,32]{2,1,0:T(4,128)S(1)}, f32[2,4,32]{2,1,0:T(4,128)}, u32[]{:S(2)}) copy-start(f32[2,4,32]{2,1,0:T(4,128)} %table.15) | copy-start | bytes 3076
  2.7 15.5 %all-to-all-start = ((bf16[32,16,128]{2,1,0:T(8,128)(2,1)}), bf16[32,16,128]{2,1,0:T(8,128)(2,1)S(1)}, u32[]{:S(2)}, u32[]{:S(2)}) async-start(bf16[32,16,128]{2,1,0:T(8,128)(2,1)} %pack.1), calls=%async_computation | async-start | bytes 262144 | tf_op jit(solution)/shard_map/all_to_all | solution.py:933
  18.3 0.7 copy-start.8
  40.9 11.7 %copy-start = (f32[3,9,32,32]{3,2,1,0:T(8,128)S(1)}, f32[3,9,32,32]{3,2,1,0:T(8,128)}, u32[]{:S(2)}) copy-start(f32[3,9,32,32]{3,2,1,0:T(8,128)} %w_convs.1) | copy-start | bytes 331780
  40.9 11.7 %copy-start.6 = (f32[2,32,32]{2,1,0:T(8,128)S(1)}, f32[2,32,32]{2,1,0:T(8,128)}, u32[]{:S(2)}) copy-start(f32[2,32,32]{2,1,0:T(8,128)} %w_style.5) | copy-start | bytes 24580
  52.6 13.9 %copy-start.1 = (bf16[1152,256]{1,0:T(8,128)(2,1)S(1)}, bf16[1152,256]{1,0:T(8,128)(2,1)}, u32[]{:S(2)}) copy-start(bf16[1152,256]{1,0:T(8,128)(2,1)} %get-tuple-element.94.back.back_two) | copy-start | bytes 1769476
  52.6 13.9 %copy-start.10 = (bf16[256,128]{1,0:T(8,128)(2,1)S(1)}, bf16[256,128]{1,0:T(8,128)(2,1)}, u32[]{:S(2)}) copy-start(bf16[256,128]{1,0:T(8,128)(2,1)} %get-tuple-element.93.head_mat) | copy-start | bytes 196612
  52.6 13.9 %copy-start.13 = (f32[33,3]{0,1:T(4,128)S(1)}, f32[33,3]{0,1:T(4,128)}, u32[]{:S(2)}) copy-start(f32[33,3]{0,1:T(4,128)} %param.26) | copy-start | bytes 1192
  57.3 21.7 %copy-start.2 = (bf16[1152,256]{1,0:T(8,128)(2,1)S(1)}, bf16[1152,256]{1,0:T(8,128)(2,1)}, u32[]{:S(2)}) copy-start(bf16[1152,256]{1,0:T(8,128)(2,1)} %get-tuple-element.101.back_one) | copy-start | bytes 1769476
  79.0 15.8 %copy-start.3 = (bf16[1152,256]{1,0:T(8,128)(2,1)S(1)}, bf16[1152,256]{1,0:T(8,128)(2,1)}, u32[]{:S(2)}) copy-start(bf16[1152,256]{1,0:T(8,128)(2,1)} %get-tuple-element.108.back) | copy-start | bytes 1769476
  94.8 17.6 %copy-start.11 = (f32[2,32,32]{2,1,0:T(8,128)S(1)}, f32[2,32,32]{2,1,0:T(8,128)}, u32[]{:S(2)}) copy-start(f32[2,32,32]{2,1,0:T(8,128)} %m_style.1) | copy-start | bytes 24580
  94.8 17.6 %copy-start.12 = (f32[2,32,32]{2,1,0:T(8,128)S(1)}, f32[2,32,32]{2,1,0:T(8,128)}, u32[]{:S(2)}) copy-start(f32[2,32,32]{2,1,0:T(8,128)} %s_style.1) | copy-start | bytes 24580
  94.8 17.6 %copy-start.16 = (f32[2,4,32]{2,1,0:T(4,128)S(1)}, f32[2,4,32]{2,1,0:T(4,128)}, u32[]{:S(2)}) copy-start(f32[2,4,32]{2,1,0:T(4,128)} %m_norms.1) | copy-start | bytes 3076
  94.8 17.6 %copy-start.17 = (f32[2,4,32]{2,1,0:T(4,128)S(1)}, f32[2,4,32]{2,1,0:T(4,128)}, u32[]{:S(2)}) copy-start(f32[2,4,32]{2,1,0:T(4,128)} %s_norms.1) | copy-start | bytes 3076
  94.8 17.6 %copy-start.18 = (f32[33,3]{0,1:T(4,128)S(1)}, f32[33,3]{0,1:T(4,128)}, u32[]{:S(2)}) copy-start(f32[33,3]{0,1:T(4,128)} %param.31) | copy-start | bytes 1192
  94.8 17.6 %copy-start.19 = (f32[33,3]{0,1:T(4,128)S(1)}, f32[33,3]{0,1:T(4,128)}, u32[]{:S(2)}) copy-start(f32[33,3]{0,1:T(4,128)} %param.36) | copy-start | bytes 1192
  94.9 25.7 %copy-start.4 = (f32[3,9,32,32]{3,2,1,0:T(8,128)S(1)}, f32[3,9,32,32]{3,2,1,0:T(8,128)}, u32[]{:S(2)}) copy-start(f32[3,9,32,32]{3,2,1,0:T(8,128)} %m_convs.1) | copy-start | bytes 331780
  94.9 25.7 %copy-start.5 = (f32[3,9,32,32]{3,2,1,0:T(8,128)S(1)}, f32[3,9,32,32]{3,2,1,0:T(8,128)}, u32[]{:S(2)}) copy-start(f32[3,9,32,32]{3,2,1,0:T(8,128)} %s_convs.1) | copy-start | bytes 331780
  94.9 25.7 %copy-start.9 = (f32[10,2,32]{2,1,0:T(2,128)S(1)}, f32[10,2,32]{2,1,0:T(2,128)}, u32[]{:S(2)}) copy-start(f32[10,2,32]{2,1,0:T(2,128)} %w_first.3) | copy-start | bytes 7684
  94.9 25.7 %copy-start.14 = (f32[10,2,32]{2,1,0:T(2,128)S(1)}, f32[10,2,32]{2,1,0:T(2,128)}, u32[]{:S(2)}) copy-start(f32[10,2,32]{2,1,0:T(2,128)} %m_first.1) | copy-start | bytes 7684
  94.9 25.7 %copy-start.15 = (f32[10,2,32]{2,1,0:T(2,128)S(1)}, f32[10,2,32]{2,1,0:T(2,128)}, u32[]{:S(2)}) copy-start(f32[10,2,32]{2,1,0:T(2,128)} %s_first.1) | copy-start | bytes 7684
  109.8 10.8 %all-to-all-start.8 = ((f32[32,2,4,128]{3,2,1,0:T(4,128)}), f32[32,2,4,128]{3,2,1,0:T(4,128)S(1)}, u32[]{:S(2)}, u32[]{:S(2)}) async-start(f32[32,2,4,128]{3,2,1,0:T(4,128)} %first_back.1.pay), calls=%async_computation.8 | async-start | bytes 262144 | tf_op jit(solution)/shard_map/all_to_all | solution.py:933

commit v6 on v5

--- a/solution.py
+++ b/solution.py
@@ -33,6 +33,7 @@
 STORE_BYTES = 32 * 1024 * 1024
 FORWARD = 10 * LANES
 BACK = 9 * LANES
+IMAGE_AT = 3 * FORWARD
 
 
 def lane_of(shape):
@@ -234,6 +235,10 @@
 
 def taps_at(store, i):
     return store.at[FORWARD * i : FORWARD * i + (BACK if i else FORWARD)]
+
+
+def image_at(store):
+    return store.at[IMAGE_AT : IMAGE_AT + 3 * LANES]
 
 
 def pack_kernel(image_in, flow_in, labels_in, valid_in, out, image, flow, labels, valid, sems):
@@ -316,10 +321,12 @@
     for c, tap in enumerate(first_taps(w_first, 9)):
         val = jnp.where((row_of(shape) < 16) & (channel == c) & (here == group_of(shape)), tap, val)
     mats[BACK:FORWARD, :] = val.astype(BF16)
-    stored = []
+    for r in range(3):
+        mats[IMAGE_AT + LANES * r : IMAGE_AT + LANES * (r + 1), :] = image_matrix(w_first, r)
+    stored = copies(sems, (image_at(mats), image_at(store)))
     for i in range(3):
         conv_matrix(w_convs.at[i], mats, FORWARD * i, False)
-        stored += copies(sems.at[i:], (taps_at(mats, i), taps_at(store, i)))
+        stored += copies(sems.at[1 + i :], (taps_at(mats, i), taps_at(store, i)))
     for i, back in enumerate((back_zero, back_one, back_two)):
         conv_matrix(w_convs.at[i], back, 0, True)
     lane = lane_of((CH, LANES))
@@ -333,7 +340,8 @@
     wait(stored)
 
 
-def start_kernel(place, got, w_first, prepared, sides, raw, pay, vec, *, local_count, height, sources):
+def start_kernel(place, got, weights, sides, raw, pay, vec, taps, first_mat, sems, *, local_count, height, sources):
+    fetched = copies(sems, (image_at(weights), first_mat), (taps_at(weights, 0), taps))
     rows, segments = raw.shape[0], raw.shape[2]
     off, block = place[0], place[1]
     blank(sides)
@@ -349,9 +357,10 @@
         sides[pl.ds(8 * t + 1, 8)] = v.astype(BF16)
 
     loop(rows // 8, eight)
+    wait(fetched[:1])
     y = None
     for r in range(3):
-        part = jnp.dot(flat(sides[r : r + rows]), image_matrix(w_first, r), preferred_element_type=F32)
+        part = jnp.dot(flat(sides[r : r + rows]), first_mat[LANES * r : LANES * (r + 1)], preferred_element_type=F32)
         y = part if y is None else y + part
     raw[:, 0], raw[:, 1] = blocks_of(y, rows)
     mean, square = local_stats(raw, off, height, local_count)
@@ -362,10 +371,10 @@
     count = jnp.sum(jnp.where((lane >= MASK) & (lane < MASK + 8), mask, 0.0))
     send(pay, mean, square)
     notes(vec, jnp.full((1, LANES), count, F32))
-
-
-def first_kernel(place, got, raw, sides, table, weights, summed, pay, vec, fields, lows, hidden, xhat, taps, sems, *, spots, local_count, pixel_count, height):
-    fetched = copies(sems, (taps_at(weights, 0), taps))
+    wait(fetched[1:])
+
+
+def first_kernel(place, got, raw, sides, table, taps, summed, pay, vec, fields, lows, hidden, xhat, sems, *, spots, local_count, pixel_count, height):
     mean, inverse = merge_stats(got[:, 0, :], got[:, 1, :], local_count, pixel_count)
     notes(vec, inverse)
     gain, bias = affine(table, 0)
@@ -383,16 +392,19 @@
 
     blank(hidden)
     loop(rows // 4, norm_rows)
-    stored = copies(sems.at[1:], (xhat, spots(fields, "xhat_zero")), (hidden, spots(lows, "hidden_one")))
-    wait(fetched)
-    y = conv(hidden, taps, 0, rows, flat(sides[1 : rows + 1]))
-    summed[:, 0], summed[:, 1] = blocks_of(y, rows)
+    stored = copies(sems, (xhat, spots(fields, "xhat_zero")), (hidden, spots(lows, "hidden_one")))
+
+    @pl.when(place[0] >= 0)
+    def _():
+        y = conv(hidden, taps, 0, rows, flat(sides[1 : rows + 1]))
+        summed[:, 0], summed[:, 1] = blocks_of(y, rows)
+
     send(pay, *local_stats(summed, place[0], height, local_count))
     wait(stored)
 
 
-def pool_kernel(place, got, summed, count_in, table, weights, fields_in, lows_in, raw, pay, vec, fields, lows, merged, xhat, shared, taps, sems, *, spots, local_count, pixel_count, height):
-    fetched = copies(sems, (taps_at(weights, 1), taps))
+def pool_kernel(place, got, summed, count_in, table, weights, fields_in, lows_in, raw, pay, vec, merged, taps_next, fields, lows, xhat, shared, taps, sems, *, spots, local_count, pixel_count, height):
+    fetched = copies(sems, (taps_at(weights, 1), taps), (taps_at(weights, 2), taps_next))
     mean, inverse = merge_stats(got[:, 0, :], got[:, 1, :], local_count, pixel_count)
     gain, bias = affine(table, 1)
     rows, segments = summed.shape[0], summed.shape[2]
@@ -434,7 +446,7 @@
     sums = lax.fori_loop(0, rows // step, some, (zero, zero, zero), unroll=min(rows // step, 5))
     pool_sum, share_sum, share_x = [fold(col_sum(v)) for v in sums]
     stored = copies(
-        sems.at[1:],
+        sems.at[2:],
         (xhat, spots(fields, "xhat_one")),
         (shared, spots(fields, "shared")),
         (merged, spots(lows, "merged")),
@@ -461,8 +473,8 @@
     return col_sum(jnp.where(row_of(v.shape) == me, v, 0.0))
 
 
-def style_kernel(place, got, raw, table, w_style, w_convs_in, weights, fields_in, lows_in, resid, pay, vec, style_out, fields, lows, hidden, xhat, merged, slopes, w_conv, taps, sems, *, spots, local_count, pixel_count, pool_cells, height, parts):
-    fetched = copies(sems, (taps_at(weights, 2), taps), (spots(lows_in, "merged"), merged), (w_convs_in.at[2], w_conv))
+def style_kernel(place, got, raw, merged, table, w_style, w_convs_in, taps, lows_in, resid, pay, vec, style_out, xhat, lows, hidden, slopes, w_conv, sems, *, spots, local_count, pixel_count, pool_cells, height, parts):
+    fetched = copies(sems, (w_convs_in.at[2], w_conv))
     style = by_image(spread(got[:, 2, :], 0), parts) / pool_cells
     style_out[...] = style
     one, two = [
@@ -490,11 +502,14 @@
 
     blank(hidden)
     loop(rows // 4, norm_rows)
-    stored = copies(sems.at[3:], (xhat, spots(fields, "xhat_two")), (hidden, spots(lows, "hidden_three")))
-    wait(fetched)
-    for k, y in enumerate(blocks_of(conv(hidden, taps, 0, rows), rows)):
-        resid[:, k] = y + two + merged[1 : rows + 1, k].astype(F32)
-    wait(stored)
+    stored = copies(sems.at[1:], (hidden, spots(lows, "hidden_three")))
+
+    @pl.when(place[0] >= 0)
+    def _():
+        for k, y in enumerate(blocks_of(conv(hidden, taps, 0, rows), rows)):
+            resid[:, k] = y + two + merged[1 : rows + 1, k].astype(F32)
+
+    wait(fetched + stored)
     off = place[0]
     means, squares = local_stats(resid, off, height, local_count)
     centre = fold(means) / GRP
@@ -556,8 +571,7 @@
     return 1 + x // GRP, x % GRP
 
 
-def head_kernel(place, got, got_style, resid, sides, head_mat, w_head, table, back, fields, grad, xhat, pay, vec, decoded, slopes, grad_low, below_x, sems, *, spots, local_count, pixel_count, height):
-    fetched = copies(sems, (spots(fields, "xhat_two"), below_x))
+def head_kernel(place, got, got_style, resid, sides, head_mat, w_head, below_x, table, back, grad, xhat, pay, vec, decoded, slopes, grad_low, *, local_count, pixel_count, height):
     mean, inverse = merge_stats(got[:, 0, :], got[:, 1, :], local_count, pixel_count)
     notes(vec, inverse, mean)
     gain, bias = affine(table, 3)
@@ -614,17 +628,20 @@
     factor = gain * inverse
     back_rows(grad_low, rows, lambda at, k: factor * grad[at, k])
     shift_sum, scale_sum = own_sums(grad, xhat, off, height)
-    wait(fetched)
-    y = conv(grad_low, back, 0, rows)
-    slopes[:, 0], slopes[:, 1] = blocks_of(y, rows)
+
+    @pl.when(place[0] >= 0)
+    def _():
+        y = conv(grad_low, back, off, height)
+        slopes[0:height, 0], slopes[0:height, 1] = blocks_of(y, height)
+
     gain, bias = affine(table, 2)
 
     def links(at, k):
-        x = below_x[at, k]
+        x = below_x[pl.ds(off + at.start, at.size), k]
         g = slopes[at, k] * slope_at(x, gain, bias)
         return g, g * x
 
-    below = [fold(v) for v in row_sums(off, height, links)]
+    below = [fold(v) for v in row_sums(0, height, links)]
     send(pay, groups(shift_sum, scale_sum, *below), row, col_sum(got[:, 2, :]))
 
 
@@ -680,10 +697,9 @@
         out[:, q, :] = val
 
 
-def decoder_back_kernel(place, got, grad, xhat, vec, vec_two, table, back_two, back_one, fields, lows, below, below_x, shared, pay, more, kept_grad, mid_x, mid, low_two, low_one, field_two, field_one, sems, *, spots, pixel_count, height):
+def decoder_back_kernel(place, got, grad, xhat, mid_x, vec, vec_two, table, back_two, back_one, fields, lows, below, below_x, shared, pay, more, kept_grad, mid, low_two, low_one, field_two, field_one, sems, *, spots, pixel_count, height):
     fetched = copies(
         sems,
-        (spots(fields, "xhat_two"), mid_x),
         (spots(fields, "xhat_one"), below_x),
         (spots(fields, "shared"), shared),
         (spots(lows, "hidden_three"), field_two),
@@ -716,8 +732,11 @@
         return g
 
     back_rows(low_two, rows, value)
-    wait(fetched)
-    mid[:, 0], mid[:, 1] = blocks_of(conv(low_two, back_two, 0, rows), rows)
+
+    @pl.when(place[0] >= 0)
+    def _():
+        mid[:, 0], mid[:, 1] = blocks_of(conv(low_two, back_two, 0, rows), rows)
+
     gain, bias = affine(table, 2)
     factor = gain * vec_two[0:1]
     shift, scale = shift_two / pixel_count, scale_two / pixel_count
@@ -727,6 +746,7 @@
         return norm_back(mid[at, k] * slope_at(x, gain, bias), x, factor, shift, scale)
 
     back_rows(low_one, rows, value_two)
+    wait(fetched)
     sum_two = low_sum(low_two, off, height)
     sum_one = low_sum(low_one, off, height)
     y = conv(low_one, back_one, 0, rows)
@@ -746,14 +766,15 @@
     pay[0:CH, 1, 3, :] = jnp.zeros((CH, LANES), F32)
 
 
-def summed_kernel(place, got, got_style, grad, xhat, shared, vec, table, w_style, sides, back, fields, lows, below, below_x, pay, more, field, grad_low, sems, *, spots, pixel_count, pool_cells, height, parts):
+def summed_kernel(place, got, got_style, grad, xhat, shared, vec, table, w_style, sides, back, fields, lows, below, below_x, pay, more, field, grad_low, sems, *, spots, pixel_count, pool_cells, parts):
+    off = place[0]
+    height = below.shape[0]
     fetched = copies(
         sems,
-        (spots(fields, "xhat_zero"), below_x),
+        (spots(fields, "xhat_zero").at[pl.ds(off, height)], below_x),
         (spots(lows, "hidden_one"), field),
     )
     devices = got.shape[0]
-    off = place[0]
     rows = grad.shape[0]
     dims = (((1,), (1,)), ((), ()))
     first = got[:, 0, 0, :]
@@ -775,10 +796,10 @@
     back_rows(grad_low, rows, value)
     gain, bias = affine(table, 0)
     wait(fetched)
-    for k, y in enumerate(blocks_of(conv(grad_low, back, 0, rows), rows)):
+    for k, y in enumerate(blocks_of(conv(grad_low, back, off, height), height)):
         below[:, k] = y * slope_at(below_x[:, k], gain, bias)
     two, one = jnp.sum(got[:, 0], axis=0), jnp.sum(got[:, 1], axis=0)
-    row = groups(*own_sums(below, below_x, off, height), two[3:4], one[2:3])
+    row = groups(*own_sums(below, below_x, 0, height), two[3:4], one[2:3])
     chunk = jnp.concatenate([row, two[1:3], one[0:1]], axis=0)
     pay[:, 0] = jnp.broadcast_to(chunk[None], (devices, 4, LANES))
     pay[:, 1] = jnp.broadcast_to(one[1:2][None], (devices, 4, LANES))
@@ -811,9 +832,8 @@
     whole = col_sum(got[:, 0, 0, :])
     shift, scale = spread(whole, 0) / pixel_count, spread(whole, 1) / pixel_count
     factor = affine(table, 0)[0] * vec[0:1]
-    at = pl.ds(off, height)
     low_grad = jnp.concatenate(
-        [flat(norm_back(grad[at, k], xhat[at, k], factor, shift, scale).astype(BF16)) for k in range(2)], axis=1
+        [flat(norm_back(grad[:, k], xhat[:, k], factor, shift, scale).astype(BF16)) for k in range(2)], axis=1
     )
     entries = []
     for r in range(3):
@@ -963,18 +983,19 @@
     place = jnp.stack([first_row - start, start // block_rows, me]).astype(jnp.int32)
 
     field = ((rows, 2, segments, LANES), F32)
+    own_field = ((height,) + field[0][1:], F32)
     low_field = ((rows + 2, 3, segments, LANES), BF16)
     vec = ((8, LANES), F32)
     two_rows = ((devices, 2, LANES), F32)
     four_rows = ((devices, 4, LANES), F32)
     two_chunks = ((devices, 2, 4, LANES), F32)
     nine = ((BACK, 2 * LANES), BF16)
-    taps_scratch = ((FORWARD, 2 * LANES), BF16)
+    ten = ((FORWARD, 2 * LANES), BF16)
 
     places = {
         name: i * count
         for count, names in (
-            (rows, ("xhat_zero", "xhat_one", "shared", "xhat_two")),
+            (rows, ("xhat_zero", "xhat_one", "shared")),
             (rows + 2, ("hidden_one", "hidden_three", "merged")),
         )
         for i, name in enumerate(names)
@@ -1004,64 +1025,63 @@
         prepare,
         [far(((STORE_BYTES // (4 * LANES), 2 * LANES), BF16)), nine, nine, nine, ((2 * LANES, LANES), BF16)],
         far(w_first), far(w_convs), far(head_rows),
-        scratch=[(w_first.shape, F32), (w_convs.shape, F32), (head_rows.shape, F32), ((3 * FORWARD, 2 * LANES), BF16)],
-        sems=3, limit=WHOLE_VMEM, name="prepare",
-    )
-
-    sides, raw, pay, count = call(
+        scratch=[(w_first.shape, F32), (w_convs.shape, F32), (head_rows.shape, F32), ((IMAGE_AT + 3 * LANES, 2 * LANES), BF16)],
+        sems=4, limit=WHOLE_VMEM, name="prepare",
+    )
+
+    sides, raw, pay, count, taps = call(
         part(start_kernel, local_count=local_count, height=height, sources=col_count),
-        [((rows + 2, segments, LANES), BF16), field, two_rows, vec],
-        place, got_inputs, w_first, far(weights),
-        scalars=1, name="image_conv",
+        [((rows + 2, segments, LANES), BF16), field, two_rows, vec, ten],
+        place, got_inputs, far(weights),
+        scalars=1, scratch=[((3 * LANES, 2 * LANES), BF16)], sems=2, name="image_conv",
     )
     got_zero = exchange(pay)
     summed, pay, inv_zero, fields, lows = call(
         part(first_kernel, spots=spots, **counts),
         [field, two_rows, vec, store_of(field), store_of(low_field)],
-        place, got_zero, raw, sides, batch_norm_table, far(weights),
-        scalars=1, scratch=[low_field, field, taps_scratch], sems=3, name="first_block",
+        place, got_zero, raw, sides, batch_norm_table, taps,
+        scalars=1, scratch=[low_field, field], sems=2, name="first_block",
     )
     got_one = exchange(pay)
 
-    raw, pay, inv_one, fields, lows = call(
+    raw, pay, inv_one, merged, taps, fields, lows = call(
         part(pool_kernel, spots=spots, **counts),
-        [field, four_rows, vec, store_of(field), store_of(low_field)],
+        [field, four_rows, vec, low_field, nine, store_of(field), store_of(low_field)],
         place, got_one, summed, count, batch_norm_table, far(weights), far(fields), far(lows),
-        scalars=1, scratch=[low_field, field, field, nine], sems=4,
-        aliases={6: 3, 7: 4}, name="pool_and_merge",
+        scalars=1, scratch=[field, field, nine], sems=5,
+        aliases={6: 5, 7: 6}, name="pool_and_merge",
     )
     got_style = exchange(pay)
 
-    resid, pay, inv_two, style, fields, lows = call(
+    resid, pay, inv_two, style, xhat_two, lows = call(
         part(style_kernel, spots=spots, **styled, **counts),
-        [field, four_rows, vec, ((devices, LANES), F32), store_of(field), store_of(low_field)],
-        place, got_style, raw, batch_norm_table, w_style, far(w_convs), far(weights), far(fields), far(lows),
-        scalars=1, scratch=[low_field, field, low_field, field, (w_convs.shape[1:], F32), nine], sems=5,
-        aliases={7: 4, 8: 5}, name="decoder",
+        [field, four_rows, vec, ((devices, LANES), F32), field, store_of(low_field)],
+        place, got_style, raw, merged, batch_norm_table, w_style, far(w_convs), taps, far(lows),
+        scalars=1, scratch=[low_field, field, (w_convs.shape[1:], F32)], sems=2,
+        aliases={8: 5}, name="decoder",
     )
     got_three = exchange(pay)
 
     grad_three, xhat_three, pay, inv_three = call(
-        part(head_kernel, spots=spots, **counts),
+        part(head_kernel, **counts),
         [field, field, four_rows, vec],
-        place, got_three, got_style, resid, sides, head_mat, head_rows, batch_norm_table, back[2], far(fields),
-        scalars=1, scratch=[((rows, 2, segments, LANES), BF16), field, low_field, field], sems=1, name="head",
+        place, got_three, got_style, resid, sides, head_mat, head_rows, xhat_two, batch_norm_table, back[2],
+        scalars=1, scratch=[((rows, 2, segments, LANES), BF16), field, low_field], name="head",
     )
     got_head = exchange(pay)
 
     grad_one, xhat_one, shared, pay, more_two = call(
         part(decoder_back_kernel, spots=spots, **backs),
         [field, field, field, two_chunks, vec],
-        place, got_head, grad_three, xhat_three, inv_three, inv_two, batch_norm_table, back[2], back[1],
+        place, got_head, grad_three, xhat_three, xhat_two, inv_three, inv_two, batch_norm_table, back[2], back[1],
         far(fields), far(lows),
-        scalars=1, scratch=[field, field, field, low_field, low_field, low_field, low_field], sems=5,
-        name="decoder_back",
+        scalars=1, scratch=[field, field, low_field, low_field, low_field, low_field], sems=4, name="decoder_back",
     )
     got_one_back = exchange(pay)
 
     grad_zero, xhat_zero, pay, more = call(
-        part(summed_kernel, spots=spots, **styled, **backs),
-        [field, field, two_chunks, vec],
+        part(summed_kernel, spots=spots, pixel_count=pixel_count, **styled),
+        [own_field, own_field, two_chunks, vec],
         place, got_one_back, got_style, grad_one, xhat_one, shared, inv_one, batch_norm_table, w_style, sides,
         back[0], far(fields), far(lows),
         scalars=1, scratch=[low_field, low_field], sems=2, name="summed_back",

time: 123 us -> 120 us (0.976)
  Pallas kernels: 34.2 us -> 31.7 us
    pallas_call x12, Pallas kernels: 34.2 us -> 31.7 us  [call(): pl.pallas_call(kernel, out_shape=[jax.ShapeDtypeStruct(*plain(x)) for x i...]
  transfers between devices with their start and end apart: 2 -> 2, of which waited for: 2 -> 2; matrix products, arithmetic and copies ran while one was open for 0% -> 0% of each run, Pallas kernels for 4% -> 5%
where the time goes in v6:
time: 120 us; the launch traced here: 119 us
  blocking collectives  65.7 us (55%)
  Pallas kernels  31.7 us (26%)
  waiting for transfers between devices  10.6 us (9%)
  starting transfers between devices  9.88 us (8%)
    all_to_all x7, blocking collectives, exchange(): return lax.all_to_all(pay, ('row', 'col'), 0, 0)  65.7 us
    pallas_call x12, Pallas kernels, call(): pl.pallas_call(kernel, out_shape=[jax.ShapeDtypeStruct(*plain(x)) for x i...  31.7 us
    all_to_all x2, waiting for transfers between devices, exchange(): return lax.all_to_all(pay, ('row', 'col'), 0, 0)  10.6 us
    all_to_all x2, starting transfers between devices, exchange(): return lax.all_to_all(pay, ('row', 'col'), 0, 0)  9.88 us
  transfers between devices with their start and end apart: 2, of which 2 were waited for; matrix products, arithmetic and copies ran while one was open for 0% of the time, Pallas kernels for 5%

profile of v6, /device:TPU:0, one launch (start us, length us, event | category | flops | bytes accessed | tf_op | source)
XLA Modules:
  0.0 119.0 jit_solution(14056965589984874891)
XLA Ops:
  0.7 2.0 %pack.1 = bf16[32,16,128]{2,1,0:T(8,128)(2,1)} custom-call(bf16[16,8,2,32]{3,2,1,0:T(2,128)(2,1)} %bitcast.20, s32[16,8,2,32]{3,2,1,0:T(2,128)} %bitcast.19, s32[16,8,32]{2,1,0:T(8,128)} %labels_in.1, s32[16,8,32]{2,1,0:T(8,128)} %valid_in.1), custom_call_target="tpu_custom_call" | custom-call | tf_op jit(solution)/shard_map/pack/pallas_call | solution.py:940
  2.7 7.3 %all-to-all-start = ((bf16[32,16,128]{2,1,0:T(8,128)(2,1)}), bf16[32,16,128]{2,1,0:T(8,128)(2,1)S(1)}, u32[]{:S(2)}, u32[]{:S(2)}) async-start(bf16[32,16,128]{2,1,0:T(8,128)(2,1)} %pack.1), calls=%async_computation | async-start | bytes 262144 | tf_op jit(solution)/shard_map/all_to_all | solution.py:953
  10.1 4.6 %prepare.1 = (bf16[65536,256]{1,0:T(8,128)(2,1)}, bf16[1152,256]{1,0:T(8,128)(2,1)}, bf16[1152,256]{1,0:T(8,128)(2,1)}, bf16[1152,256]{1,0:T(8,128)(2,1)}, bf16[256,128]{1,0:T(8,128)(2,1)}) custom-call(f32[10,2,32]{2,1,0:T(2,128)} %w_first.1, f32[3,9,32,32]{3,2,1,0:T(8,128)} %w_convs.1, f32[3,33]{1,0:T(4,128)} %bitcast.14), custom_call_target="tpu_custom_call" | custom-call | tf_op jit(solution)/shard_map/prepare/pallas_call | solution.py:940
  14.7 0.1 pad_add_fusion.place
  14.8 3.5 %all-to-all-done.got = bf16[32,16,128]{2,1,0:T(8,128)(2,1)S(1)} async-done(((bf16[32,16,128]{2,1,0:T(8,128)(2,1)}), bf16[32,16,128]{2,1,0:T(8,128)(2,1)S(1)}, u32[]{:S(2)}, u32[]{:S(2)}) %all-to-all-start) | async-done | bytes 131104 | tf_op jit(solution)/shard_map/all_to_all | solution.py:953
  18.3 2.0 %image_conv.1 = (bf16[42,16,128]{2,1,0:T(8,128)(2,1)S(1)}, f32[40,2,16,128]{3,2,1,0:T(8,128)S(1)}, f32[32,2,128]{2,1,0:T(2,128)S(1)}, f32[8,128]{1,0:T(8,128)S(1)}, bf16[1280,256]{1,0:T(8,128)(2,1)S(1)}) custom-call(s32[3]{0:T(128)S(1)} %pad_add_fusion.place, bf16[32,16,128]{2,1,0:T(8,128)(2,1)S(1)} %all-to-all-done.got, ...), custom_call_target="tpu_custom_call" | custom-call | tf_op jit(solution)/shard_map/image_conv/pallas_call | solution.py:940
  20.3 9.4 %all_to_all.45.got = f32[32,2,128]{2,1,0:T(2,128)S(1)} all-to-all(f32[32,2,128]{2,1,0:T(2,128)S(1)} %get-tuple-element.82), channel_id=1, replica_groups=mesh['row'=8,'col'=4] {'row','col'}, dimensions={0} | all-to-all | bytes 65536 | tf_op jit(solution)/shard_map/all_to_all | solution.py:953
  29.7 2.0 %first_block.1 = (f32[40,2,16,128]{3,2,1,0:T(8,128)S(1)}, f32[32,2,128]{2,1,0:T(2,128)S(1)}, f32[8,128]{1,0:T(8,128)S(1)}, f32[2048,2,16,128]{3,2,1,0:T(8,128)}, bf16[2731,3,16,128]{3,2,1,0:T(8,128)(2,1)}) custom-call(s32[3]{0:T(128)S(1)} %pad_add_fusion.place, f32[32,2,128]{2,1,0:T(2,128)S(1)} %all_to_all.45.got, ...), custom_call_target="tpu_custom_call" | custom-call | tf_op jit(solution)/shard_map/first_block/pallas_call | solution.py:940
  31.7 8.9 %all_to_all.46.got = f32[32,2,128]{2,1,0:T(2,128)S(1)} all-to-all(f32[32,2,128]{2,1,0:T(2,128)S(1)} %get-tuple-element.86), channel_id=1, replica_groups=mesh['row'=8,'col'=4] {'row','col'}, dimensions={0} | all-to-all | bytes 65536 | tf_op jit(solution)/shard_map/all_to_all | solution.py:953
  40.7 2.7 %pool_and_merge.1 = (f32[40,2,16,128]{3,2,1,0:T(8,128)S(1)}, f32[32,4,128]{2,1,0:T(4,128)S(1)}, f32[8,128]{1,0:T(8,128)S(1)}, bf16[42,3,16,128]{3,2,1,0:T(8,128)...) custom-call(s32[3]{0:T(128)S(1)} %pad_add_fusion.place, ...), custom_call_target="tpu_custom_call", output_to_operand_aliasing={{5}: (6, {}), {6}: (7, {})} | custom-call | tf_op jit(solution)/shard_map/pool_and_merge/pallas_call | solution.py:940
  43.4 9.2 %all_to_all.47.got.got_style = f32[32,4,128]{2,1,0:T(4,128)S(1)} all-to-all(f32[32,4,128]{2,1,0:T(4,128)S(1)} %get-tuple-element.91), channel_id=1, replica_groups=mesh['row'=8,'col'=4] {'row','col'}, dimensions={0} | all-to-all | bytes 131072 | tf_op jit(solution)/shard_map/all_to_all | solution.py:953
  52.7 3.8 %decoder.1 = (f32[40,2,16,128]{3,2,1,0:T(8,128)S(1)}, f32[32,4,128]{2,1,0:T(4,128)S(1)}, f32[8,128]{1,0:T(8,128)S(1)}, f32[32,128]{1,0:T(8,128)S(1)}, f32[40,2,1...) custom-call(s32[3]{0:T(128)S(1)} %pad_add_fusion.place, ...), custom_call_target="tpu_custom_call", output_to_operand_aliasing={{5}: (8, {})} | custom-call | tf_op jit(solution)/shard_map/decoder/pallas_call | solution.py:940
  56.5 9.1 %all_to_all.48.got = f32[32,4,128]{2,1,0:T(4,128)S(1)} all-to-all(f32[32,4,128]{2,1,0:T(4,128)S(1)} %get-tuple-element.96), channel_id=1, replica_groups=mesh['row'=8,'col'=4] {'row','col'}, dimensions={0} | all-to-all | bytes 131072 | tf_op jit(solution)/shard_map/all_to_all | solution.py:953
  65.6 3.2 %head.1 = (f32[40,2,16,128]{3,2,1,0:T(8,128)S(1)}, f32[40,2,16,128]{3,2,1,0:T(8,128)S(1)}, f32[32,4,128]{2,1,0:T(4,128)S(1)}, f32[8,128]{1,0:T(8,128)S(1)}) custom-call(s32[3]{0:T(128)S(1)} %pad_add_fusion.place, f32[32,4,128]{2,1,0:T(4,128)S(1)} %all_to_all.48.got, f32[32,4,128]{2,1,0:T(4,128)S(1)} %all_to_all.47.got.got_style, ...), custom_call_target="tpu_custom_call" | custom-call | tf_op jit(solution)/shard_map/head/pallas_call | solution.py:940
  68.8 9.1 %all_to_all.49.got.got_head = f32[32,4,128]{2,1,0:T(4,128)S(1)} all-to-all(f32[32,4,128]{2,1,0:T(4,128)S(1)} %get-tuple-element.101), channel_id=1, replica_groups=mesh['row'=8,'col'=4] {'row','col'}, dimensions={0} | all-to-all | bytes 131072 | tf_op jit(solution)/shard_map/all_to_all | solution.py:953
  77.9 3.9 %decoder_back.1 = (f32[40,2,16,128]{3,2,1,0:T(8,128)S(1)}, f32[40,2,16,128]{3,2,1,0:T(8,128)S(1)}, f32[40,2,16,128]{3,2,1,0:T(8,128)S(1)}, f32[32,2,4,128]{3,2,1,0:T(4,128)S(1)}, f32[8,128]{1,0:T(8,128)S(1)}) custom-call(s32[3]{0:T(128)S(1)} %pad_add_fusion.place, f32[32,4,128]{2,1,0:T(4,128)S(1)} %all_to_all.49.got.got_head, ...), custom_call_target="tpu_custom_call" | custom-call | tf_op jit(solution)/shard_map/decoder_back/pallas_call | solution.py:940
  81.7 9.9 %all_to_all.50.got.got_one_back = f32[32,2,4,128]{3,2,1,0:T(4,128)S(1)} all-to-all(f32[32,2,4,128]{3,2,1,0:T(4,128)S(1)} %get-tuple-element.109), channel_id=1, replica_groups=mesh['row'=8,'col'=4] {'row','col'}, dimensions={0} | all-to-all | bytes 262144 | tf_op jit(solution)/shard_map/all_to_all | solution.py:953
  91.8 3.1 %summed_back.1 = (f32[32,2,16,128]{3,2,1,0:T(8,128)S(1)}, f32[32,2,16,128]{3,2,1,0:T(8,128)S(1)}, f32[32,2,4,128]{3,2,1,0:T(4,128)S(1)}, f32[8,128]{1,0:T(8,128)S(1)}) custom-call(s32[3]{0:T(128)S(1)} %pad_add_fusion.place, f32[32,2,4,128]{3,2,1,0:T(4,128)S(1)} %all_to_all.50.got.got_one_back, f32[32,4,128]{2,1,0:T(4,128)S(1)} %all_to_all.47.got.got_style, ...), custom_call_target="tpu_custom_call" | custom-call | tf_op jit(solution)/shard_map/summed_back/pallas_call | solution.py:940
  94.9 9.9 %all_to_all.51.got.got_first = f32[32,2,4,128]{3,2,1,0:T(4,128)S(1)} all-to-all(f32[32,2,4,128]{3,2,1,0:T(4,128)S(1)} %get-tuple-element.115), channel_id=1, replica_groups=mesh['row'=8,'col'=4] {'row','col'}, dimensions={0} | all-to-all | bytes 262144 | tf_op jit(solution)/shard_map/all_to_all | solution.py:953
  104.8 1.8 %first_back.1.pay = f32[32,2,4,128]{3,2,1,0:T(4,128)} custom-call(s32[3]{0:T(128)S(1)} %pad_add_fusion.place, f32[32,2,4,128]{3,2,1,0:T(4,128)S(1)} %all_to_all.51.got.got_first, f32[32,2,16,128]{3,2,1,0:T(8,128)S(1)} %get-tuple-element.116.grad, f32[32,2,16,128]{3,2,1,0:T(8,128)S(1)} %get-tuple-element.117.xhat, f32[8,128]{1,0:T(8,128)S(1)} %get-tuple-element.118.vec, ...), custom_call_target="tpu_custom_call" | custom-call | tf_op jit(solution)/shard_map/first_back/pallas_call | solution.py:940
  106.6 2.6 %all-to-all-start.8 = ((f32[32,2,4,128]{3,2,1,0:T(4,128)}), f32[32,2,4,128]{3,2,1,0:T(4,128)S(1)}, u32[]{:S(2)}, u32[]{:S(2)}) async-start(f32[32,2,4,128]{3,2,1,0:T(4,128)} %first_back.1.pay), calls=%async_computation.8 | async-start | bytes 262144 | tf_op jit(solution)/shard_map/all_to_all | solution.py:953
  109.2 1.0 update_early.1
  110.3 7.1 %all-to-all-done.8.got = f32[32,2,4,128]{3,2,1,0:T(4,128)S(1)} async-done(((f32[32,2,4,128]{3,2,1,0:T(4,128)}), f32[32,2,4,128]{3,2,1,0:T(4,128)S(1)}, u32[]{:S(2)}, u32[]{:S(2)}) %all-to-all-start.8) | async-done | bytes 131104 | tf_op jit(solution)/shard_map/all_to_all | solution.py:953
  117.4 1.6 %update_late.1 = (f32[10,2,32]{2,1,0:T(2,128)}, f32[10,2,32]{2,1,0:T(2,128)}, f32[10,2,32]{2,1,0:T(2,128)}, bf16[10,2,32]{2,1,0:T(2,128)(2,1)}, f32[3,9,32,32]{3...) custom-call(f32[32,2,4,128]{3,2,1,0:T(4,128)S(1)} %all-to-all-done.8.got, ...), custom_call_target="tpu_custom_call" | custom-call | tf_op jit(solution)/shard_map/update_late/pallas_call | solution.py:940
  (38 shorter events, 0.1 us)
Async XLA Ops:
  0.7 29.0 %copy-start.7 = (f32[2,4,32]{2,1,0:T(4,128)S(1)}, f32[2,4,32]{2,1,0:T(4,128)}, u32[]{:S(2)}) copy-start(f32[2,4,32]{2,1,0:T(4,128)} %table.15) | copy-start | bytes 3076
  2.7 15.5 %all-to-all-start = ((bf16[32,16,128]{2,1,0:T(8,128)(2,1)}), bf16[32,16,128]{2,1,0:T(8,128)(2,1)S(1)}, u32[]{:S(2)}, u32[]{:S(2)}) async-start(bf16[32,16,128]{2,1,0:T(8,128)(2,1)} %pack.1), calls=%async_computation | async-start | bytes 262144 | tf_op jit(solution)/shard_map/all_to_all | solution.py:953
  40.7 12.0 %copy-start = (f32[3,9,32,32]{3,2,1,0:T(8,128)S(1)}, f32[3,9,32,32]{3,2,1,0:T(8,128)}, u32[]{:S(2)}) copy-start(f32[3,9,32,32]{3,2,1,0:T(8,128)} %w_convs.1) | copy-start | bytes 331780
  40.7 12.0 %copy-start.6 = (f32[2,32,32]{2,1,0:T(8,128)S(1)}, f32[2,32,32]{2,1,0:T(8,128)}, u32[]{:S(2)}) copy-start(f32[2,32,32]{2,1,0:T(8,128)} %w_style.5) | copy-start | bytes 24580
  43.4 22.2 %copy-start.1 = (bf16[1152,256]{1,0:T(8,128)(2,1)S(1)}, bf16[1152,256]{1,0:T(8,128)(2,1)}, u32[]{:S(2)}) copy-start(bf16[1152,256]{1,0:T(8,128)(2,1)} %get-tuple-element.100.back.back_two) | copy-start | bytes 1769476
  43.4 22.2 %copy-start.8 = (bf16[256,128]{1,0:T(8,128)(2,1)S(1)}, bf16[256,128]{1,0:T(8,128)(2,1)}, u32[]{:S(2)}) copy-start(bf16[256,128]{1,0:T(8,128)(2,1)} %get-tuple-element.98.head_mat) | copy-start | bytes 196612
  43.4 22.2 %copy-start.12 = (f32[33,3]{0,1:T(4,128)S(1)}, f32[33,3]{0,1:T(4,128)}, u32[]{:S(2)}) copy-start(f32[33,3]{0,1:T(4,128)} %param.26) | copy-start | bytes 1192
  43.4 34.5 %copy-start.2 = (bf16[1152,256]{1,0:T(8,128)(2,1)S(1)}, bf16[1152,256]{1,0:T(8,128)(2,1)}, u32[]{:S(2)}) copy-start(bf16[1152,256]{1,0:T(8,128)(2,1)} %get-tuple-element.106.back_one) | copy-start | bytes 1769476
  77.9 13.8 %copy-start.3 = (bf16[1152,256]{1,0:T(8,128)(2,1)S(1)}, bf16[1152,256]{1,0:T(8,128)(2,1)}, u32[]{:S(2)}) copy-start(bf16[1152,256]{1,0:T(8,128)(2,1)} %get-tuple-element.114.back) | copy-start | bytes 1769476
  91.7 17.5 %copy-start.10 = (f32[2,32,32]{2,1,0:T(8,128)S(1)}, f32[2,32,32]{2,1,0:T(8,128)}, u32[]{:S(2)}) copy-start(f32[2,32,32]{2,1,0:T(8,128)} %m_style.1) | copy-start | bytes 24580
  91.7 17.5 %copy-start.11 = (f32[2,32,32]{2,1,0:T(8,128)S(1)}, f32[2,32,32]{2,1,0:T(8,128)}, u32[]{:S(2)}) copy-start(f32[2,32,32]{2,1,0:T(8,128)} %s_style.1) | copy-start | bytes 24580
  91.7 17.5 %copy-start.15 = (f32[2,4,32]{2,1,0:T(4,128)S(1)}, f32[2,4,32]{2,1,0:T(4,128)}, u32[]{:S(2)}) copy-start(f32[2,4,32]{2,1,0:T(4,128)} %m_norms.1) | copy-start | bytes 3076
  91.7 17.5 %copy-start.16 = (f32[2,4,32]{2,1,0:T(4,128)S(1)}, f32[2,4,32]{2,1,0:T(4,128)}, u32[]{:S(2)}) copy-start(f32[2,4,32]{2,1,0:T(4,128)} %s_norms.1) | copy-start | bytes 3076
  91.7 17.5 %copy-start.17 = (f32[33,3]{0,1:T(4,128)S(1)}, f32[33,3]{0,1:T(4,128)}, u32[]{:S(2)}) copy-start(f32[33,3]{0,1:T(4,128)} %param.31) | copy-start | bytes 1192
  91.7 17.5 %copy-start.18 = (f32[33,3]{0,1:T(4,128)S(1)}, f32[33,3]{0,1:T(4,128)}, u32[]{:S(2)}) copy-start(f32[33,3]{0,1:T(4,128)} %param.36) | copy-start | bytes 1192
  91.7 25.7 %copy-start.4 = (f32[3,9,32,32]{3,2,1,0:T(8,128)S(1)}, f32[3,9,32,32]{3,2,1,0:T(8,128)}, u32[]{:S(2)}) copy-start(f32[3,9,32,32]{3,2,1,0:T(8,128)} %m_convs.1) | copy-start | bytes 331780
  91.7 25.7 %copy-start.5 = (f32[3,9,32,32]{3,2,1,0:T(8,128)S(1)}, f32[3,9,32,32]{3,2,1,0:T(8,128)}, u32[]{:S(2)}) copy-start(f32[3,9,32,32]{3,2,1,0:T(8,128)} %s_convs.1) | copy-start | bytes 331780
  91.8 25.7 %copy-start.9 = (f32[10,2,32]{2,1,0:T(2,128)S(1)}, f32[10,2,32]{2,1,0:T(2,128)}, u32[]{:S(2)}) copy-start(f32[10,2,32]{2,1,0:T(2,128)} %w_first.1) | copy-start | bytes 7684
  91.8 25.7 %copy-start.13 = (f32[10,2,32]{2,1,0:T(2,128)S(1)}, f32[10,2,32]{2,1,0:T(2,128)}, u32[]{:S(2)}) copy-start(f32[10,2,32]{2,1,0:T(2,128)} %m_first.1) | copy-start | bytes 7684
  91.8 25.6 %copy-start.14 = (f32[10,2,32]{2,1,0:T(2,128)S(1)}, f32[10,2,32]{2,1,0:T(2,128)}, u32[]{:S(2)}) copy-start(f32[10,2,32]{2,1,0:T(2,128)} %s_first.1) | copy-start | bytes 7684
  106.6 10.8 %all-to-all-start.8 = ((f32[32,2,4,128]{3,2,1,0:T(4,128)}), f32[32,2,4,128]{3,2,1,0:T(4,128)S(1)}, u32[]{:S(2)}, u32[]{:S(2)}) async-start(f32[32,2,4,128]{3,2,1,0:T(4,128)} %first_back.1.pay), calls=%async_computation.8 | async-start | bytes 262144 | tf_op jit(solution)/shard_map/all_to_all | solution.py:953

commit v7 on v6

--- a/solution.py
+++ b/solution.py
@@ -34,6 +34,7 @@
 FORWARD = 10 * LANES
 BACK = 9 * LANES
 IMAGE_AT = 3 * FORWARD
+BACK_AT = IMAGE_AT + 3 * LANES
 
 
 def lane_of(shape):
@@ -208,14 +209,25 @@
     return mean, lax.rsqrt(total / pixel_count + norm_eps)
 
 
+def row_of_each(got, r):
+    return got[:, r, 0, :]
+
+
+def total_of(got, r):
+    return col_sum(row_of_each(got, r))
+
+
 def send(pay, *rows):
-    value = rows[-1]
-    if len(rows) > 1:
-        at = row_of(pay.shape[1:])
-        value = jnp.broadcast_to(value, pay.shape[1:])
-        for k in range(len(rows) - 2, -1, -1):
-            value = jnp.where(at == k, rows[k], value)
-    pay[...] = jnp.broadcast_to(value[None], pay.shape)
+    for r, row in enumerate(rows):
+        pay[:, r, 0, :] = jnp.broadcast_to(row, (pay.shape[0], LANES))
+
+
+def send_parts(pay, first, count):
+    devices = pay.shape[0]
+    if devices > CH:
+        for r in range(first, first + count):
+            pay[CH:, r, 0, :] = jnp.zeros((devices - CH, LANES), F32)
+    return pay.at[0:CH, first : first + count, 0]
 
 
 def affine(table, q):
@@ -239,6 +251,10 @@
 
 def image_at(store):
     return store.at[IMAGE_AT : IMAGE_AT + 3 * LANES]
+
+
+def back_at(store):
+    return store.at[BACK_AT : BACK_AT + BACK]
 
 
 def pack_kernel(image_in, flow_in, labels_in, valid_in, out, image, flow, labels, valid, sems):
@@ -313,7 +329,7 @@
     return val.astype(BF16)
 
 
-def prepare(w_first_in, w_convs_in, w_head_in, store, back_zero, back_one, back_two, head_mat, w_first, w_convs, w_head, mats, sems):
+def prepare(w_first_in, w_convs_in, w_head_in, store, back_zero, back_two, head_mat, w_first, w_convs, w_head, mats, sems):
     wait(copies(sems, (w_first_in, w_first), (w_convs_in, w_convs), (w_head_in, w_head)))
     shape = (LANES, 2 * LANES)
     inside, channel, here = image_lanes(shape)
@@ -327,8 +343,10 @@
     for i in range(3):
         conv_matrix(w_convs.at[i], mats, FORWARD * i, False)
         stored += copies(sems.at[1 + i :], (taps_at(mats, i), taps_at(store, i)))
-    for i, back in enumerate((back_zero, back_one, back_two)):
-        conv_matrix(w_convs.at[i], back, 0, True)
+    conv_matrix(w_convs.at[1], mats, BACK_AT, True)
+    stored += copies(sems.at[4:], (back_at(mats), back_at(store)))
+    conv_matrix(w_convs.at[2], back_two, 0, True)
+    conv_matrix(w_convs.at[0], back_zero, 0, True)
     lane = lane_of((CH, LANES))
     head = jnp.zeros((CH, LANES), F32)
     diagonal = row_of((CH, CH)) == lane_of((CH, CH))
@@ -375,7 +393,7 @@
 
 
 def first_kernel(place, got, raw, sides, table, taps, summed, pay, vec, fields, lows, hidden, xhat, sems, *, spots, local_count, pixel_count, height):
-    mean, inverse = merge_stats(got[:, 0, :], got[:, 1, :], local_count, pixel_count)
+    mean, inverse = merge_stats(row_of_each(got, 0), row_of_each(got, 1), local_count, pixel_count)
     notes(vec, inverse)
     gain, bias = affine(table, 0)
     rows = raw.shape[0]
@@ -405,7 +423,7 @@
 
 def pool_kernel(place, got, summed, count_in, table, weights, fields_in, lows_in, raw, pay, vec, merged, taps_next, fields, lows, xhat, shared, taps, sems, *, spots, local_count, pixel_count, height):
     fetched = copies(sems, (taps_at(weights, 1), taps), (taps_at(weights, 2), taps_next))
-    mean, inverse = merge_stats(got[:, 0, :], got[:, 1, :], local_count, pixel_count)
+    mean, inverse = merge_stats(row_of_each(got, 0), row_of_each(got, 1), local_count, pixel_count)
     gain, bias = affine(table, 1)
     rows, segments = summed.shape[0], summed.shape[2]
     off = place[0]
@@ -475,12 +493,12 @@
 
 def style_kernel(place, got, raw, merged, table, w_style, w_convs_in, taps, lows_in, resid, pay, vec, style_out, xhat, lows, hidden, slopes, w_conv, sems, *, spots, local_count, pixel_count, pool_cells, height, parts):
     fetched = copies(sems, (w_convs_in.at[2], w_conv))
-    style = by_image(spread(got[:, 2, :], 0), parts) / pool_cells
+    style = by_image(spread(row_of_each(got, 2), 0), parts) / pool_cells
     style_out[...] = style
     one, two = [
         jnp.dot(style, diagonal_blocks(w_style[i]), precision=highest, preferred_element_type=F32) for i in range(2)
     ]
-    mean, inverse = merge_stats(got[:, 0, :] + one, got[:, 1, :], local_count, pixel_count)
+    mean, inverse = merge_stats(row_of_each(got, 0) + one, row_of_each(got, 1), local_count, pixel_count)
     notes(vec, inverse)
     gain, bias = affine(table, 2)
     rows = raw.shape[0]
@@ -524,7 +542,8 @@
 
     loop(rows // 4, centred)
     send(pay, means, squares)
-    pay[0:CH, 2, :] = norm_links(hidden, probe, off, height, w_conv, centre)
+    links = norm_links(hidden, probe, off, height, w_conv, centre)
+    send_parts(pay, 2, 1)[:, 0, :] = links
 
 
 def norm_links(field, probe, first, rows, taps, centre):
@@ -571,8 +590,53 @@
     return 1 + x // GRP, x % GRP
 
 
-def head_kernel(place, got, got_style, resid, sides, head_mat, w_head, below_x, table, back, grad, xhat, pay, vec, decoded, slopes, grad_low, *, local_count, pixel_count, height):
-    mean, inverse = merge_stats(got[:, 0, :], got[:, 1, :], local_count, pixel_count)
+def ahead_kernel(place, pay, sides, fields, lows, out, sums, below_x, xhat, shared, field, sems, *, spots, local_count):
+    off = place[0]
+    height = xhat.shape[0]
+    own = pl.ds(off, height)
+    fetched = copies(
+        sems,
+        (spots(fields, "xhat_one").at[own], xhat),
+        (spots(fields, "shared").at[own], shared),
+        (spots(fields, "xhat_zero").at[own], below_x),
+        (spots(lows, "hidden_one"), field),
+    )
+    wait(fetched)
+    at = pl.ds(0, height)
+    centres = [fold(v) / local_count for v in row_sums(0, height, lambda at, k: (xhat[at, k], shared[at, k]))]
+    probe = [flat(v[at, k] - c).astype(BF16) for v, c in zip((xhat, shared), centres) for k in range(2)]
+    wide = jnp.concatenate(views(field, off, height), axis=1)
+    found = lax.dot_general(
+        jnp.concatenate(probe, axis=1), wide, (((0,), (0,)), ((), ())), preferred_element_type=F32
+    )
+    ones = jnp.ones((8, wide.shape[0]), BF16)
+    plain = jnp.dot(ones, wide, preferred_element_type=F32)[0:1]
+    group = group_of((1, LANES))
+    hidden = []
+    for r in range(3):
+        for s in range(3):
+            val = zero_row()
+            for y in range(SEG):
+                d, a = spot_of(y + s - 1)
+                spot = (3 * r + d) * LANES
+                val = val + jnp.where(group == a, plain[:, spot : spot + LANES], 0.0)
+            hidden.append(fold(val))
+    packed = [groups(*hidden[0:4]), groups(*hidden[4:8]), hidden[8]]
+    notes(sums, *packed)
+    packed = jnp.concatenate(packed, axis=0)
+    for k in range(2):
+        put_taps(found[2 * LANES * k : 2 * LANES * (k + 1)], out.at[:, 3 * k + 1 : 3 * k + 4, 0], (centres[k], packed))
+    low_x = jnp.concatenate([own_lanes(below_x, at), jnp.ones((wide.shape[0], LANES), BF16)], axis=1)
+    entries = []
+    for r in range(3):
+        for tap, alone in pixel_taps(sides, off + r, height, low_x, (-1, 0, 1), True):
+            entries.extend(zip(tap, alone))
+    rows = [groups(*entry, hidden[e] if e < 9 else zero_row(), zero_row()) for e, entry in enumerate(entries)]
+    out[:, 0, 0, :] = jnp.concatenate(rows + [jnp.zeros((CH - len(rows), LANES), F32)], axis=0)
+
+
+def head_kernel(place, got, got_style, resid, sides, head_mat, w_head, below_x, ahead, table, back, grad, xhat, pay, vec, decoded, slopes, grad_low, *, local_count, pixel_count, height):
+    mean, inverse = merge_stats(row_of_each(got, 0), row_of_each(got, 1), local_count, pixel_count)
     notes(vec, inverse, mean)
     gain, bias = affine(table, 3)
     rows, segments = resid.shape[0], resid.shape[2]
@@ -602,7 +666,7 @@
     near = [pltpu.roll(given, LANES - MASK + first, axis=1) for first in (FLOW, FLOW + 8, LABEL)]
     mask = jnp.where(lane < FLOW + 8, near[0], jnp.where(is_flow, near[1], near[2]))
     mask = jnp.where((lane >= FLOW) & (lane < LABEL + 8), mask, 0.0)
-    count = jnp.sum(got_style[:, 2, 3 * CH : 3 * CH + 1])
+    count = jnp.sum(got_style[:, 2, 0, 3 * CH : 3 * CH + 1])
     diff = out - given / flow_scale
     hinge = jnp.maximum(out, 0.0) + jnp.log1p(jnp.exp(-jnp.abs(out)))
     loss = mask * jnp.where(is_flow, diff * diff, hinge - given * out)
@@ -642,7 +706,9 @@
         return g, g * x
 
     below = [fold(v) for v in row_sums(0, height, links)]
-    send(pay, groups(shift_sum, scale_sum, *below), row, col_sum(got[:, 2, :]))
+    send(pay, groups(shift_sum, scale_sum, *below), row, total_of(got, 2))
+    send_parts(pay, 3, 7)
+    pay[0:CH, 3:10] = ahead[...]
 
 
 def own_sums(grad, xhat, first, rows):
@@ -674,19 +740,24 @@
     loop(rows // 4, some)
 
 
-def tap_sums(field, grad, first, rows, out):
-    at = pl.ds(first + 1, rows)
-    g = jnp.concatenate([flat(grad[at, 0]), flat(grad[at, 1])], axis=1)
+def own_lanes(grad, at):
+    return jnp.concatenate([flat(grad[at, k]).astype(BF16) for k in range(2)], axis=1)
+
+
+def tap_sums(field, grad, first, rows, out, more=None):
     wide = jnp.concatenate(views(field, first, rows), axis=1)
-    found = lax.dot_general(g, wide, (((0,), (0,)), ((), ())), preferred_element_type=F32)
+    found = lax.dot_general(grad, wide, (((0,), (0,)), ((), ())), preferred_element_type=F32)
+    put_taps(found, out, more)
+
+
+def put_taps(found, out, more=None):
     group = group_of((CH, LANES))
     taps = []
     for r in range(3):
         for s in range(3):
             val = jnp.zeros((CH, LANES), F32)
             for y in range(SEG):
-                x = y + s - 1
-                d, a = spot_of(x)
+                d, a = spot_of(y + s - 1)
                 spot = (3 * r + d) * LANES
                 val = val + jnp.where(group == a, found[CH * y : CH * y + CH, spot : spot + LANES], 0.0)
             taps.append(fold(val))
@@ -694,27 +765,41 @@
         val = taps[4 * q]
         for b in range(1, min(4, 9 - 4 * q)):
             val = jnp.where(group == b, taps[4 * q + b], val)
+        if more is not None:
+            centre, sums = more
+            val = val + column_of(centre) * sums[q : q + 1]
         out[:, q, :] = val
 
 
-def decoder_back_kernel(place, got, grad, xhat, mid_x, vec, vec_two, table, back_two, back_one, fields, lows, below, below_x, shared, pay, more, kept_grad, mid, low_two, low_one, field_two, field_one, sems, *, spots, pixel_count, height):
+def column_of(v):
+    shape = (CH, LANES)
+    return jnp.sum(jnp.where(row_of(shape) == lane_of(shape), v, 0.0), axis=1, keepdims=True)
+
+
+def at_lane(v, k):
+    return jnp.sum(jnp.where(lane_of(v.shape) == k, v, 0.0), axis=1, keepdims=True)
+
+
+def decoder_back_kernel(place, got, grad, xhat, mid_x, vec, vec_two, sums, table, back_two, weights, fields, lows, below, below_x, shared, pay, more, kept_grad, mid, low_two, low_one, field_two, field_one, field_zero, back_one, sems, *, spots, local_count, pixel_count, height):
     fetched = copies(
         sems,
+        (back_at(weights), back_one),
         (spots(fields, "xhat_one"), below_x),
         (spots(fields, "shared"), shared),
         (spots(lows, "hidden_three"), field_two),
         (spots(lows, "merged"), field_one),
+        (spots(lows, "hidden_one"), field_zero),
     )
     devices = got.shape[0]
     rows = grad.shape[0]
     off = place[0]
-    total = col_sum(got[:, 0, :])
+    total = total_of(got, 0)
     shift, scale = spread(total, 0) / pixel_count, spread(total, 1) / pixel_count
     inverse, mean = vec[0:1], vec[1:2]
     factor = affine(table, 3)[0] * inverse
     slant = scale * inverse
     held, carried = factor * (shift - slant * mean), factor * slant
-    links = got[0:CH, 2, :] * groups(held, carried, held, carried)
+    links = got[0:CH, 2, 0, :] * groups(held, carried, held, carried)
     group = group_of(links.shape)
     mine = (lane_of(links.shape) & 31) == row_of(links.shape)
 
@@ -724,7 +809,7 @@
 
     shift_two = spread(total, 2) - across(group < 2)
     scale_two = spread(total, 3) - across(group >= 2)
-    notes(more, scale_two, shift_two)
+    notes(more, scale_two, shift_two, *[total_of(got, r) for r in (4, 5, 6)])
 
     def value(at, k):
         g = norm_back(grad[at, k], xhat[at, k], factor, shift, scale)
@@ -757,27 +842,26 @@
         both = (both + partner(both)).reshape(rows // 2, 1, -1, LANES)
         g = g * slope_at(below_x[:, k], gain, bias).reshape(g.shape) + both * shared[:, k].reshape(g.shape)
         below[:, k] = g.reshape(rows, -1, LANES)
-    row = groups(*own_sums(below, below_x, off, height), sum_one, sum_two)
-    pay[:, 0] = jnp.broadcast_to(row[None], (devices, 4, LANES))
-    if devices > CH:
-        pay[CH:, 1] = jnp.zeros((devices - CH, 4, LANES), F32)
-    tap_sums(field_two, low_two, off, height, pay.at[0:CH, 0, 1:4])
-    tap_sums(field_one, low_one, off, height, pay.at[0:CH, 1])
-    pay[0:CH, 1, 3, :] = jnp.zeros((CH, LANES), F32)
-
-
-def summed_kernel(place, got, got_style, grad, xhat, shared, vec, table, w_style, sides, back, fields, lows, below, below_x, pay, more, field, grad_low, sems, *, spots, pixel_count, pool_cells, parts):
+    shift_sum, scale_sum = own_sums(below, below_x, off, height)
+    send(pay, groups(shift_sum, scale_sum, sum_one, sum_two))
+    pay[:, 7, 0, :] = jnp.broadcast_to(total_of(got, 3), (devices, LANES))
+    at = pl.ds(off + 1, height)
+    tap_sums(field_two, own_lanes(low_two, at), off, height, send_parts(pay, 1, 3))
+    tap_sums(field_one, own_lanes(low_one, at), off, height, send_parts(pay, 4, 3))
+    centre = shift_sum / local_count
+    at = pl.ds(off, height)
+    grad = jnp.concatenate([flat(below[at, k] - centre).astype(BF16) for k in range(2)], axis=1)
+    tap_sums(field_zero, grad, off, height, send_parts(pay, 8, 3), (centre, sums))
+
+
+def summed_kernel(place, got, got_style, got_head, grad, xhat, shared, vec, more_two, table, w_style, sides, back, fields, pay, more, below, below_x, grad_low, sems, *, spots, pixel_count, pool_cells, parts):
     off = place[0]
     height = below.shape[0]
-    fetched = copies(
-        sems,
-        (spots(fields, "xhat_zero").at[pl.ds(off, height)], below_x),
-        (spots(lows, "hidden_one"), field),
-    )
+    fetched = copies(sems, (spots(fields, "xhat_zero").at[pl.ds(off, height)], below_x))
     devices = got.shape[0]
     rows = grad.shape[0]
     dims = (((1,), (1,)), ((), ()))
-    first = got[:, 0, 0, :]
+    first = row_of_each(got, 0)
     each = lax.dot_general(
         spread(first, 2), diagonal_blocks(w_style[0]), dims, precision=highest, preferred_element_type=F32
     ) + lax.dot_general(
@@ -785,8 +869,8 @@
     )
     each = each / pool_cells
     total = col_sum(first)
-    shift = spread(total, 0) + col_sum(each * by_image(spread(got_style[:, 2, :], 1), parts))
-    scale = spread(total, 1) + col_sum(each * by_image(spread(got_style[:, 2, :], 2), parts))
+    shift = spread(total, 0) + col_sum(each * by_image(spread(row_of_each(got_style, 2), 1), parts))
+    scale = spread(total, 1) + col_sum(each * by_image(spread(row_of_each(got_style, 2), 2), parts))
     mine = col_sum(jnp.where(row_of(each.shape) // parts == place[2] // parts, each, 0.0))
     factor = affine(table, 1)[0] * vec[0:1]
     shift_mean, scale_mean = shift / pixel_count, scale / pixel_count
@@ -798,53 +882,53 @@
     wait(fetched)
     for k, y in enumerate(blocks_of(conv(grad_low, back, off, height), height)):
         below[:, k] = y * slope_at(below_x[:, k], gain, bias)
-    two, one = jnp.sum(got[:, 0], axis=0), jnp.sum(got[:, 1], axis=0)
-    row = groups(*own_sums(below, below_x, 0, height), two[3:4], one[2:3])
-    chunk = jnp.concatenate([row, two[1:3], one[0:1]], axis=0)
-    pay[:, 0] = jnp.broadcast_to(chunk[None], (devices, 4, LANES))
-    pay[:, 1] = jnp.broadcast_to(one[1:2][None], (devices, 4, LANES))
-    tap_sums(field, grad_low, off, height, pay.at[0:CH, 1, 1:4])
+    me = place[2]
+    weights = at_lane(by_image(each, parts), me)
+    entries = got[0:CH, 7, 0, :]
+    hidden = spread(entries, 2)
+    hidden = [groups(*[hidden[t : t + 1] for t in range(4 * q, min(4 * q + 4, 9))]) for q in range(3)]
+    shard = []
+    for q in range(3):
+        val = total_of(got, 8 + q) + col_sum(weights * row_of_each(got_head, 7 + q))
+        val = val - at_lane(shift_mean, me) * hidden[q] - at_lane(scale_mean, me) * more_two[2 + q : 3 + q]
+        shard.append(at_lane(factor, me) * val)
     at = pl.ds(off + 1, height)
-    low_own = jnp.concatenate([flat(grad_low[at, 0]), flat(grad_low[at, 1])], axis=1)
-    side = pixel_taps(sides, off + 1, height, low_own, (0,))[0]
-    notes(more, scale, shift, *side)
-
-
-def pixel_taps(sides, row, rows, grad, shift):
+    side = pixel_taps(sides, off + 1, height, own_lanes(grad_low, at), (0,))[0]
+    low_below = own_lanes(below, pl.ds(0, height))
+    taps = []
+    for r in range(3):
+        for tap in pixel_taps(sides, off + r, height, low_below, (-1, 0, 1)):
+            taps.extend(tap)
+    two, one = [total_of(got, r) for r in (1, 2, 3)], [total_of(got, r) for r in (4, 5, 6)]
+    taps = [shard[2]] + taps + side
+    send(
+        pay,
+        groups(*own_sums(below, below_x, 0, height), two[2], one[2]),
+        *two[0:2],
+        *one[0:2],
+        *shard[0:2],
+        *[groups(*(taps[4 * q : 4 * q + 4] + [zero_row()])[0:4]) for q in range(6)],
+    )
+    notes(more, scale, shift)
+
+
+def pixel_taps(sides, row, rows, grad, shift, alone=False):
     x = flat(sides[pl.ds(row, rows)])
     found = lax.dot_general(x, grad, (((0,), (0,)), ((), ())), preferred_element_type=F32)
-    inside, channel, here = image_lanes(found.shape)
-    here = here - group_of(found.shape)
+    inside, channel, column = image_lanes((LANES, 2 * LANES))
+    here = column - group_of((LANES, 2 * LANES))
     out = []
     for s in shift:
-        both = []
+        both, bare = [], []
         for c in range(2):
-            hit = inside & (channel == c) & (here == s)
-            v = col_sum(jnp.where(hit, found, 0.0))
+            v = col_sum(jnp.where(inside & (channel == c) & (here == s), found[:, 0 : 2 * LANES], 0.0))
             both.append(fold(v[:, 0:LANES] + v[:, LANES:]))
-        out.append(both)
+            if alone:
+                cut = slice(0, LANES)
+                hit = (inside & (channel == c) & (column >= s) & (column < s + SEG))[:, cut]
+                bare.append(col_sum(jnp.where(hit, found[:, 2 * LANES :], 0.0)))
+        out.append((both, bare) if alone else both)
     return out
-
-
-def first_back_kernel(place, got, grad, xhat, vec, more, table, sides, pay, *, pixel_count, height):
-    devices = got.shape[0]
-    off = place[0]
-    whole = col_sum(got[:, 0, 0, :])
-    shift, scale = spread(whole, 0) / pixel_count, spread(whole, 1) / pixel_count
-    factor = affine(table, 0)[0] * vec[0:1]
-    low_grad = jnp.concatenate(
-        [flat(norm_back(grad[:, k], xhat[:, k], factor, shift, scale).astype(BF16)) for k in range(2)], axis=1
-    )
-    entries = []
-    for r in range(3):
-        for tap in pixel_taps(sides, off + r, height, low_grad, (-1, 0, 1)):
-            entries.extend(tap)
-    entries.extend([more[2:3], more[3:4]])
-    rows = [groups(*entries[4 * q : 4 * q + 4]) for q in range(5)]
-    conv_zero = jnp.sum(got[:, 1], axis=0)
-    chunk = [jnp.concatenate(rows[0:4], axis=0), jnp.concatenate([rows[4], conv_zero[1:4]], axis=0)]
-    for k in range(2):
-        pay[:, k] = jnp.broadcast_to(chunk[k][None], (devices, 4, LANES))
 
 
 def adamw(master, moment, square, grad, rate):
@@ -863,22 +947,18 @@
 
 
 def update_early(
-    got_first, got_one_back, got_head, got_style, pay, more, more_two, style,
-    w_style, w_head, table, m_style, m_head, m_norms, s_style, s_head, s_norms,
-    loss_out, count_out,
-    style_master, style_moment, style_square,
-    head_master, head_moment, head_square, head_copy,
-    norms_master, norms_moment, norms_square,
+    got_one_back, got_head, got_style, pay, style, w_style, w_head, m_style, m_head, s_style, s_head,
+    loss_out, count_out, style_master, style_moment, style_square, head_master, head_moment, head_square, head_copy,
 ):
-    count_out[0, 0] = jnp.sum(got_style[:, 2, 3 * CH : 3 * CH + 1])
-    loss_out[0, 0] = jnp.sum(got_head[:, 1, 99:100])
+    count_out[0, 0] = jnp.sum(got_style[:, 2, 0, 3 * CH : 3 * CH + 1])
+    loss_out[0, 0] = jnp.sum(got_head[:, 1, 0, 99:100])
     dims = (((0,), (0,)), ((), ()))
     for i in range(2):
-        sums = spread(got_one_back[:, 0, 0, :], 2 + i)
+        sums = spread(row_of_each(got_one_back, 0), 2 + i)
         grad = lax.dot_general(style[...], sums, dims, precision=highest, preferred_element_type=F32)
         put(i, (w_style, m_style, s_style), grad[0:CH, 0:CH], rate_table[2], (style_master, style_moment, style_square))
 
-    head = col_sum(got_head[:, 1, :])
+    head = total_of(got_head, 1)
     lane = lane_of((1, LANES))
     rows = []
     for k in range(3):
@@ -887,39 +967,45 @@
     grad = jnp.concatenate(rows, axis=0)[:, 0 : CH + 1]
     put(slice(None), (w_head, m_head, s_head), grad, rate_table[3], (head_master, head_moment, head_square, head_copy))
 
-    three_sums = col_sum(got_head[:, 0, :])
-    zero_sums = col_sum(got_first[:, 0, 0, :])
-    scales = [spread(zero_sums, 1), more[0:1], more_two[0:1], spread(three_sums, 1)]
-    shifts = [spread(zero_sums, 0), more[1:2], more_two[1:2], spread(three_sums, 0)]
+
+def update_late(
+    got, got_one_back, got_head, more, more_two, vec, w_first, w_convs, table, m_first, m_convs, m_norms, s_first, s_convs, s_norms,
+    first_master, first_moment, first_square, first_copy,
+    convs_master, convs_moment, convs_square, convs_copy,
+    norms_master, norms_moment, norms_square, *, pixel_count
+):
+    refs = (w_convs, m_convs, s_convs)
+    outs = (convs_master, convs_moment, convs_square, convs_copy)
+    packs = [[got[0:CH, k, 0, :].T for k in ks] for ks in ((5, 6, 7), (3, 4, 0), (1, 2, 0))]
+    for i, pack in enumerate(packs):
+        for t in range(9):
+            b = t % 4 if t < 8 else (0, 3, 2)[i]
+            put((i, t), refs, pack[t // 4][CH * b : CH * b + CH], rate_table[1], outs)
+
+    zero_sums = total_of(got, 0)
+    totals = [total_of(got, r) for r in range(7, 13)]
+    shift, scale = spread(zero_sums, 0), spread(zero_sums, 1)
+    factor = affine(table, 0)[0] * vec[0:1]
+    entries = got_one_back[0:CH, 7, 0, :]
+    by_x, alone = spread(entries, 0), spread(entries, 1)
+    refs = (w_first, m_first, s_first)
+    outs = (first_master, first_moment, first_square, first_copy)
+    for t in range(10):
+        pair = []
+        for e in (2 * t, 2 * t + 1):
+            k, b = divmod(1 + e, 4)
+            v = spread(totals[k], b)
+            if t < 9:
+                v = factor * (v - (alone[e : e + 1] * shift + by_x[e : e + 1] * scale) / pixel_count)
+            pair.append(v[:, 0:CH])
+        put(t, refs, jnp.concatenate(pair, axis=0), rate_table[0], outs)
+
+    three_sums = total_of(got_head, 0)
+    scales = [scale, more[0:1], more_two[0:1], spread(three_sums, 1)]
+    shifts = [shift, more[1:2], more_two[1:2], spread(three_sums, 0)]
     for i, rows in enumerate((scales, shifts)):
         grad = jnp.concatenate(rows, axis=0)[:, 0:CH]
         put(i, (table, m_norms, s_norms), grad, rate_table[4], (norms_master, norms_moment, norms_square))
-
-
-def update_late(
-    got, got_first, w_first, w_convs, m_first, m_convs, s_first, s_convs,
-    first_master, first_moment, first_square, first_copy,
-    convs_master, convs_moment, convs_square, convs_copy,
-):
-    refs = (w_convs, m_convs, s_convs)
-    outs = (convs_master, convs_moment, convs_square, convs_copy)
-    last = got_first[0:CH, 0, 0, :].T
-    packs = (
-        [got[0:CH, 1, q, :].T for q in (1, 2, 3)],
-        [got_first[0:CH, 0, 3, :].T, got_first[0:CH, 1, 0, :].T, last[3 * CH :]],
-        [got_first[0:CH, 0, 1, :].T, got_first[0:CH, 0, 2, :].T, last[2 * CH : 3 * CH]],
-    )
-    for i, pack in enumerate(packs):
-        for t in range(9):
-            b = t % 4
-            put((i, t), refs, pack[t // 4][CH * b : CH * b + CH], rate_table[1], outs)
-
-    first = jnp.concatenate([jnp.sum(got[:, 0], axis=0), jnp.sum(got[:, 1], axis=0)[0:1]], axis=0)
-    refs = (w_first, m_first, s_first)
-    outs = (first_master, first_moment, first_square, first_copy)
-    for t in range(10):
-        pair = [spread(first[e // 4 : e // 4 + 1], e % 4)[:, 0:CH] for e in (2 * t, 2 * t + 1)]
-        put(t, refs, jnp.concatenate(pair, axis=0), rate_table[0], outs)
 
 
 def far(x):
@@ -974,7 +1060,6 @@
     pool_cells = float(image_rows * image_cols // 4)
     part = functools.partial
     counts = dict(local_count=local_count, pixel_count=pixel_count, height=height)
-    backs = dict(pixel_count=pixel_count, height=height)
     styled = dict(pool_cells=pool_cells, parts=parts)
 
     me = lax.axis_index("row") * col_count + lax.axis_index("col")
@@ -986,9 +1071,10 @@
     own_field = ((height,) + field[0][1:], F32)
     low_field = ((rows + 2, 3, segments, LANES), BF16)
     vec = ((8, LANES), F32)
-    two_rows = ((devices, 2, LANES), F32)
-    four_rows = ((devices, 4, LANES), F32)
-    two_chunks = ((devices, 2, 4, LANES), F32)
+
+    def payload(count):
+        return ((devices, count, 1, LANES), F32)
+
     nine = ((BACK, 2 * LANES), BF16)
     ten = ((FORWARD, 2 * LANES), BF16)
 
@@ -1021,24 +1107,26 @@
     )
     got_inputs = exchange(pay)
     head_rows = w_head.T
-    weights, *back, head_mat = call(
+    weights, back_zero, back_two, head_mat = call(
         prepare,
-        [far(((STORE_BYTES // (4 * LANES), 2 * LANES), BF16)), nine, nine, nine, ((2 * LANES, LANES), BF16)],
+        [far(((STORE_BYTES // (4 * LANES), 2 * LANES), BF16)), nine, nine, ((2 * LANES, LANES), BF16)],
         far(w_first), far(w_convs), far(head_rows),
-        scratch=[(w_first.shape, F32), (w_convs.shape, F32), (head_rows.shape, F32), ((IMAGE_AT + 3 * LANES, 2 * LANES), BF16)],
-        sems=4, limit=WHOLE_VMEM, name="prepare",
+        scratch=[
+            (w_first.shape, F32), (w_convs.shape, F32), (head_rows.shape, F32), ((BACK_AT + BACK, 2 * LANES), BF16)
+        ],
+        sems=5, limit=WHOLE_VMEM, name="prepare",
     )
 
     sides, raw, pay, count, taps = call(
         part(start_kernel, local_count=local_count, height=height, sources=col_count),
-        [((rows + 2, segments, LANES), BF16), field, two_rows, vec, ten],
+        [((rows + 2, segments, LANES), BF16), field, payload(2), vec, ten],
         place, got_inputs, far(weights),
         scalars=1, scratch=[((3 * LANES, 2 * LANES), BF16)], sems=2, name="image_conv",
     )
     got_zero = exchange(pay)
     summed, pay, inv_zero, fields, lows = call(
         part(first_kernel, spots=spots, **counts),
-        [field, two_rows, vec, store_of(field), store_of(low_field)],
+        [field, payload(2), vec, store_of(field), store_of(low_field)],
         place, got_zero, raw, sides, batch_norm_table, taps,
         scalars=1, scratch=[low_field, field], sems=2, name="first_block",
     )
@@ -1046,7 +1134,7 @@
 
     raw, pay, inv_one, merged, taps, fields, lows = call(
         part(pool_kernel, spots=spots, **counts),
-        [field, four_rows, vec, low_field, nine, store_of(field), store_of(low_field)],
+        [field, payload(3), vec, low_field, nine, store_of(field), store_of(low_field)],
         place, got_one, summed, count, batch_norm_table, far(weights), far(fields), far(lows),
         scalars=1, scratch=[field, field, nine], sems=5,
         aliases={6: 5, 7: 6}, name="pool_and_merge",
@@ -1055,44 +1143,43 @@
 
     resid, pay, inv_two, style, xhat_two, lows = call(
         part(style_kernel, spots=spots, **styled, **counts),
-        [field, four_rows, vec, ((devices, LANES), F32), field, store_of(low_field)],
+        [field, payload(3), vec, ((devices, LANES), F32), field, store_of(low_field)],
         place, got_style, raw, merged, batch_norm_table, w_style, far(w_convs), taps, far(lows),
         scalars=1, scratch=[low_field, field, (w_convs.shape[1:], F32)], sems=2,
         aliases={8: 5}, name="decoder",
     )
     got_three = exchange(pay)
+    ahead, hidden_sums = call(
+        part(ahead_kernel, spots=spots, local_count=local_count),
+        [((CH, 7, 1, LANES), F32), vec],
+        place, far(pay), sides, far(fields), far(lows),
+        scalars=1, scratch=[own_field, own_field, own_field, low_field], sems=4, name="ahead",
+    )
 
     grad_three, xhat_three, pay, inv_three = call(
         part(head_kernel, **counts),
-        [field, field, four_rows, vec],
-        place, got_three, got_style, resid, sides, head_mat, head_rows, xhat_two, batch_norm_table, back[2],
+        [field, field, payload(10), vec],
+        place, got_three, got_style, resid, sides, head_mat, head_rows, xhat_two, ahead, batch_norm_table, back_two,
         scalars=1, scratch=[((rows, 2, segments, LANES), BF16), field, low_field], name="head",
     )
     got_head = exchange(pay)
 
     grad_one, xhat_one, shared, pay, more_two = call(
-        part(decoder_back_kernel, spots=spots, **backs),
-        [field, field, field, two_chunks, vec],
-        place, got_head, grad_three, xhat_three, xhat_two, inv_three, inv_two, batch_norm_table, back[2], back[1],
+        part(decoder_back_kernel, spots=spots, **counts),
+        [field, field, field, payload(11), vec],
+        place, got_head, grad_three, xhat_three, xhat_two, inv_three, inv_two, hidden_sums, batch_norm_table, back_two, far(weights),
         far(fields), far(lows),
-        scalars=1, scratch=[field, field, low_field, low_field, low_field, low_field], sems=4, name="decoder_back",
+        scalars=1, scratch=[field, field, low_field, low_field, low_field, low_field, low_field, nine], sems=6,
+        name="decoder_back",
     )
     got_one_back = exchange(pay)
 
-    grad_zero, xhat_zero, pay, more = call(
+    pay, more = call(
         part(summed_kernel, spots=spots, pixel_count=pixel_count, **styled),
-        [own_field, own_field, two_chunks, vec],
-        place, got_one_back, got_style, grad_one, xhat_one, shared, inv_one, batch_norm_table, w_style, sides,
-        back[0], far(fields), far(lows),
-        scalars=1, scratch=[low_field, low_field], sems=2, name="summed_back",
-    )
-    got_first = exchange(pay)
-
-    (pay,) = call(
-        part(first_back_kernel, **backs),
-        [two_chunks],
-        place, got_first, grad_zero, xhat_zero, inv_zero, more, batch_norm_table, sides,
-        scalars=1, name="first_back",
+        [payload(13), vec],
+        place, got_one_back, got_style, got_head, grad_one, xhat_one, shared, inv_one, more_two, batch_norm_table, w_style,
+        sides, back_zero, far(fields),
+        scalars=1, scratch=[own_field, own_field, low_field], sems=1, name="summed_back",
     )
     got_last = exchange(pay)
 
@@ -1101,20 +1188,21 @@
 
     early = call(
         update_early,
-        [((1, 1), F32), ((1, 1), F32)] + results(w_style, 0) + results(head_rows, 1) + results(batch_norm_table, 0),
-        got_first, got_one_back, got_head, got_style, far(pay), more, more_two, style,
-        w_style, head_rows, batch_norm_table, mom_style, mom_head.T, mom_norms, sqr_style, sqr_head.T, sqr_norms,
+        [((1, 1), F32), ((1, 1), F32)] + results(w_style, 0) + results(head_rows, 1),
+        got_one_back, got_head, got_style, far(pay), style,
+        w_style, head_rows, mom_style, mom_head.T, sqr_style, sqr_head.T,
         scalar_outs=(0, 1), name="update_early",
     )
     late = call(
-        update_late,
-        results(w_first, 1) + results(w_convs, 1),
-        got_last, got_first, w_first, w_convs, mom_first, mom_convs, sqr_first, sqr_convs,
+        part(update_late, pixel_count=pixel_count),
+        results(w_first, 1) + results(w_convs, 1) + results(batch_norm_table, 0),
+        got_last, got_one_back, got_head, more, more_two, inv_zero,
+        w_first, w_convs, batch_norm_table, mom_first, mom_convs, mom_norms, sqr_first, sqr_convs, sqr_norms,
         name="update_late",
     )
     loss, count = early[0].reshape(()), early[1].reshape(())
     head = tuple(value.T for value in early[5:9])
-    return (loss, count, *late, *early[2:5], *head, *early[9:12])
+    return (loss, count, *late[0:8], *early[2:5], *head, *late[8:11])
 
 
 def solution(mesh):

time: 120 us -> 114 us (0.950)
  blocking collectives: 65.7 us -> 49.1 us
  waiting for transfers between devices: 10.6 us -> 15.2 us
  Pallas kernels: 31.7 us -> 35.9 us
  starting transfers between devices: 9.88 us -> 12.5 us
    all_to_all x7 -> x5, blocking collectives: 65.7 us -> 49.1 us  [exchange(): return lax.all_to_all(pay, ('row', 'col'), 0, 0)]
    all_to_all x2 -> x3, waiting for transfers between devices: 10.6 us -> 15.2 us  [exchange(): return lax.all_to_all(pay, ('row', 'col'), 0, 0)]
    pallas_call x12, Pallas kernels: 31.7 us -> 35.9 us  [call(): pl.pallas_call(kernel, out_shape=[jax.ShapeDtypeStruct(*plain(x)) for x i...]
    all_to_all x2 -> x3, starting transfers between devices: 9.88 us -> 12.5 us  [exchange(): return lax.all_to_all(pay, ('row', 'col'), 0, 0)]
  transfers between devices with their start and end apart: 2 -> 3, of which waited for: 2 -> 3; matrix products, arithmetic and copies ran while one was open for 0% -> 0% of each run, Pallas kernels for 5% -> 8%
where the time goes in v7:
time: 114 us
  blocking collectives  49.1 us (43%)
  Pallas kernels  35.9 us (31%)
  waiting for transfers between devices  15.2 us (13%)
  starting transfers between devices  12.5 us (11%)
    all_to_all x5, blocking collectives, exchange(): return lax.all_to_all(pay, ('row', 'col'), 0, 0)  49.1 us
    pallas_call x12, Pallas kernels, call(): pl.pallas_call(kernel, out_shape=[jax.ShapeDtypeStruct(*plain(x)) for x i...  35.9 us
    all_to_all x3, waiting for transfers between devices, exchange(): return lax.all_to_all(pay, ('row', 'col'), 0, 0)  15.2 us
    all_to_all x3, starting transfers between devices, exchange(): return lax.all_to_all(pay, ('row', 'col'), 0, 0)  12.5 us
  transfers between devices with their start and end apart: 3, of which 3 were waited for; matrix products, arithmetic and copies ran while one was open for 0% of the time, Pallas kernels for 8%

profile of v7, /device:TPU:0, one launch (start us, length us, event | category | flops | bytes accessed | tf_op | source)
XLA Modules:
  0.0 113.9 jit_solution(10836967067040484410)
XLA Ops:
  0.7 2.0 %pack.1 = bf16[32,16,128]{2,1,0:T(8,128)(2,1)} custom-call(bf16[16,8,2,32]{3,2,1,0:T(2,128)(2,1)} %bitcast.20, s32[16,8,2,32]{3,2,1,0:T(2,128)} %bitcast.19, s32[16,8,32]{2,1,0:T(8,128)} %labels_in.1, s32[16,8,32]{2,1,0:T(8,128)} %valid_in.1), custom_call_target="tpu_custom_call" | custom-call | tf_op jit(solution)/shard_map/pack/pallas_call | solution.py:1026
  2.7 7.3 %all-to-all-start = ((bf16[32,16,128]{2,1,0:T(8,128)(2,1)}), bf16[32,16,128]{2,1,0:T(8,128)(2,1)S(1)}, u32[]{:S(2)}, u32[]{:S(2)}) async-start(bf16[32,16,128]{2,1,0:T(8,128)(2,1)} %pack.1), calls=%async_computation | async-start | bytes 262144 | tf_op jit(solution)/shard_map/all_to_all | solution.py:1039
  10.1 4.7 %prepare.1 = (bf16[65536,256]{1,0:T(8,128)(2,1)}, bf16[1152,256]{1,0:T(8,128)(2,1)}, bf16[1152,256]{1,0:T(8,128)(2,1)}, bf16[256,128]{1,0:T(8,128)(2,1)}) custom-call(f32[10,2,32]{2,1,0:T(2,128)} %w_first.1, f32[3,9,32,32]{3,2,1,0:T(8,128)} %w_convs.1, f32[3,33]{1,0:T(4,128)} %bitcast.14), custom_call_target="tpu_custom_call" | custom-call | tf_op jit(solution)/shard_map/prepare/pallas_call | solution.py:1026
  14.8 0.1 pad_add_fusion.place
  14.9 3.4 %all-to-all-done.got = bf16[32,16,128]{2,1,0:T(8,128)(2,1)S(1)} async-done(((bf16[32,16,128]{2,1,0:T(8,128)(2,1)}), bf16[32,16,128]{2,1,0:T(8,128)(2,1)S(1)}, u32[]{:S(2)}, u32[]{:S(2)}) %all-to-all-start) | async-done | bytes 131104 | tf_op jit(solution)/shard_map/all_to_all | solution.py:1039
  18.3 2.0 %image_conv.1 = (bf16[42,16,128]{2,1,0:T(8,128)(2,1)S(1)}, f32[40,2,16,128]{3,2,1,0:T(8,128)S(1)}, f32[32,2,1,128]{3,2,1,0:T(1,128)S(1)}, f32[8,128]{1,0:T(8,128)S(1)}, bf16[1280,256]{1,0:T(8,128)(2,1)S(1)}) custom-call(s32[3]{0:T(128)S(1)} %pad_add_fusion.place, bf16[32,16,128]{2,1,0:T(8,128)(2,1)S(1)} %all-to-all-done.got, ...), custom_call_target="tpu_custom_call" | custom-call | tf_op jit(solution)/shard_map/image_conv/pallas_call | solution.py:1026
  20.3 9.5 %all_to_all.40.got = f32[32,2,1,128]{3,2,1,0:T(1,128)S(1)} all-to-all(f32[32,2,1,128]{3,2,1,0:T(1,128)S(1)} %get-tuple-element.81), channel_id=1, replica_groups=mesh['row'=8,'col'=4] {'row','col'}, dimensions={0} | all-to-all | bytes 65536 | tf_op jit(solution)/shard_map/all_to_all | solution.py:1039
  29.8 2.0 %first_block.1 = (f32[40,2,16,128]{3,2,1,0:T(8,128)S(1)}, f32[32,2,1,128]{3,2,1,0:T(1,128)S(1)}, f32[8,128]{1,0:T(8,128)S(1)}, f32[2048,2,16,128]{3,2,1,0:T(8,128)}, bf16[2731,3,16,128]{3,2,1,0:T(8,128)(2,1)}) custom-call(s32[3]{0:T(128)S(1)} %pad_add_fusion.place, f32[32,2,1,128]{3,2,1,0:T(1,128)S(1)} %all_to_all.40.got, ...), custom_call_target="tpu_custom_call" | custom-call | tf_op jit(solution)/shard_map/first_block/pallas_call | solution.py:1026
  31.8 8.9 %all_to_all.41.got = f32[32,2,1,128]{3,2,1,0:T(1,128)S(1)} all-to-all(f32[32,2,1,128]{3,2,1,0:T(1,128)S(1)} %get-tuple-element.85), channel_id=1, replica_groups=mesh['row'=8,'col'=4] {'row','col'}, dimensions={0} | all-to-all | bytes 65536 | tf_op jit(solution)/shard_map/all_to_all | solution.py:1039
  40.8 2.8 %pool_and_merge.1 = (f32[40,2,16,128]{3,2,1,0:T(8,128)S(1)}, f32[32,3,1,128]{3,2,1,0:T(1,128)S(1)}, f32[8,128]{1,0:T(8,128)S(1)}, bf16[42,3,16,128]{3,2,1,0:T(8,...) custom-call(s32[3]{0:T(128)S(1)} %pad_add_fusion.place, ...), custom_call_target="tpu_custom_call", output_to_operand_aliasing={{5}: (6, {}), {6}: (7, {})} | custom-call | tf_op jit(solution)/shard_map/pool_and_merge/pallas_call | solution.py:1026
  43.5 9.0 %all_to_all.42.got.got_style = f32[32,3,1,128]{3,2,1,0:T(1,128)S(1)} all-to-all(f32[32,3,1,128]{3,2,1,0:T(1,128)S(1)} %get-tuple-element.90), channel_id=1, replica_groups=mesh['row'=8,'col'=4] {'row','col'}, dimensions={0} | all-to-all | bytes 98304 | tf_op jit(solution)/shard_map/all_to_all | solution.py:1039
  52.6 4.4 %decoder.1 = (f32[40,2,16,128]{3,2,1,0:T(8,128)S(1)}, f32[32,3,1,128]{3,2,1,0:T(1,128)}, f32[8,128]{1,0:T(8,128)S(1)}, f32[32,128]{1,0:T(8,128)S(1)}, f32[40,2,1...) custom-call(s32[3]{0:T(128)S(1)} %pad_add_fusion.place, ...), custom_call_target="tpu_custom_call", output_to_operand_aliasing={{5}: (8, {})} | custom-call | tf_op jit(solution)/shard_map/decoder/pallas_call | solution.py:1026
  57.0 2.6 %all-to-all-start.4 = ((f32[32,3,1,128]{3,2,1,0:T(1,128)}), f32[32,3,1,128]{3,2,1,0:T(1,128)S(1)}, u32[]{:S(2)}, u32[]{:S(2)}) async-start(f32[32,3,1,128]{3,2,1,0:T(1,128)} %get-tuple-element.95.pay), calls=%async_computation.4 | async-start | bytes 98304 | tf_op jit(solution)/shard_map/all_to_all | solution.py:1039
  59.6 3.8 %ahead.1 = (f32[32,7,1,128]{3,2,1,0:T(1,128)S(1)}, f32[8,128]{1,0:T(8,128)S(1)}) custom-call(s32[3]{0:T(128)S(1)} %pad_add_fusion.place, f32[32,3,1,128]{3,2,1,0:T(1,128)} %get-tuple-element.95.pay, bf16[42,16,128]{2,1,0:T(8,128)(2,1)S(1)} %get-tuple-element.83.sides, f32[2048,2,16,128]{3,2,1,0:T(8,128)} %get-tuple-element.99.fields, ...), custom_call_target="tpu_custom_call" | custom-call | tf_op jit(solution)/shard_map/ahead/pallas_call | solution.py:1026
  63.4 3.5 %all-to-all-done.4.got = f32[32,3,1,128]{3,2,1,0:T(1,128)S(1)} async-done(((f32[32,3,1,128]{3,2,1,0:T(1,128)}), f32[32,3,1,128]{3,2,1,0:T(1,128)S(1)}, u32[]{:S(2)}, u32[]{:S(2)}) %all-to-all-start.4) | async-done | bytes 49184 | tf_op jit(solution)/shard_map/all_to_all | solution.py:1039
  66.9 3.2 %head.1 = (f32[40,2,16,128]{3,2,1,0:T(8,128)S(1)}, f32[40,2,16,128]{3,2,1,0:T(8,128)S(1)}, f32[32,10,1,128]{3,2,1,0:T(1,128)S(1)}, f32[8,128]{1,0:T(8,128)S(1)}) custom-call(s32[3]{0:T(128)S(1)} %pad_add_fusion.place, f32[32,3,1,128]{3,2,1,0:T(1,128)S(1)} %all-to-all-done.4.got, f32[32,3,1,128]{3,2,1,0:T(1,128)S(1)} %all_to_all.42.got.got_style, ...), custom_call_target="tpu_custom_call" | custom-call | tf_op jit(solution)/shard_map/head/pallas_call | solution.py:1026
  70.1 10.8 %all_to_all.43.got.got_head = f32[32,10,1,128]{3,2,1,0:T(1,128)S(1)} all-to-all(f32[32,10,1,128]{3,2,1,0:T(1,128)S(1)} %get-tuple-element.103), channel_id=1, replica_groups=mesh['row'=8,'col'=4] {'row','col'}, dimensions={0} | all-to-all | bytes 327680 | tf_op jit(solution)/shard_map/all_to_all | solution.py:1039
  80.9 4.6 %decoder_back.1 = (f32[40,2,16,128]{3,2,1,0:T(8,128)S(1)}, f32[40,2,16,128]{3,2,1,0:T(8,128)S(1)}, f32[40,2,16,128]{3,2,1,0:T(8,128)S(1)}, f32[32,11,1,128]{3,2,1,0:T(1,128)S(1)}, f32[8,128]{1,0:T(8,128)S(1)}) custom-call(s32[3]{0:T(128)S(1)} %pad_add_fusion.place, f32[32,10,1,128]{3,2,1,0:T(1,128)S(1)} %all_to_all.43.got.got_head, ...), custom_call_target="tpu_custom_call" | custom-call | tf_op jit(solution)/shard_map/decoder_back/pallas_call | solution.py:1026
  85.7 10.9 %all_to_all.44.got.got_one_back = f32[32,11,1,128]{3,2,1,0:T(1,128)S(1)} all-to-all(f32[32,11,1,128]{3,2,1,0:T(1,128)S(1)} %get-tuple-element.109), channel_id=1, replica_groups=mesh['row'=8,'col'=4] {'row','col'}, dimensions={0} | all-to-all | bytes 360448 | tf_op jit(solution)/shard_map/all_to_all | solution.py:1039
  96.5 3.6 %summed_back.1 = (f32[32,13,1,128]{3,2,1,0:T(1,128)}, f32[8,128]{1,0:T(8,128)S(1)}) custom-call(s32[3]{0:T(128)S(1)} %pad_add_fusion.place, f32[32,11,1,128]{3,2,1,0:T(1,128)S(1)} %all_to_all.44.got.got_one_back, f32[32,3,1,128]{3,2,1,0:T(1,128)S(1)} %all_to_all.42.got.got_style, f32[32,10,1,128]{3,2,1,0:T(1,128)S(1)} %all_to_all.43.got.got_head, ...), custom_call_target="tpu_custom_call" | custom-call | tf_op jit(solution)/shard_map/summed_back/pallas_call | solution.py:1026
  100.2 2.6 %all-to-all-start.7 = ((f32[32,13,1,128]{3,2,1,0:T(1,128)}), f32[32,13,1,128]{3,2,1,0:T(1,128)S(1)}, u32[]{:S(2)}, u32[]{:S(2)}) async-start(f32[32,13,1,128]{3,2,1,0:T(1,128)} %get-tuple-element.116.pay), calls=%async_computation.7 | async-start | bytes 425984 | tf_op jit(solution)/shard_map/all_to_all | solution.py:1039
  102.8 1.0 update_early.1
  103.8 8.3 %all-to-all-done.7.got = f32[32,13,1,128]{3,2,1,0:T(1,128)S(1)} async-done(((f32[32,13,1,128]{3,2,1,0:T(1,128)}), f32[32,13,1,128]{3,2,1,0:T(1,128)S(1)}, u32[]{:S(2)}, u32[]{:S(2)}) %all-to-all-start.7) | async-done | bytes 213024 | tf_op jit(solution)/shard_map/all_to_all | solution.py:1039
  112.2 1.7 %update_late.1 = (f32[10,2,32]{2,1,0:T(2,128)}, f32[10,2,32]{2,1,0:T(2,128)}, f32[10,2,32]{2,1,0:T(2,128)}, bf16[10,2,32]{2,1,0:T(2,128)(2,1)}, f32[3,9,32,32]{3...) custom-call(f32[32,13,1,128]{3,2,1,0:T(1,128)S(1)} %all-to-all-done., ...), custom_call_target="tpu_custom_call" | custom-call | tf_op jit(solution)/shard_map/update_late/pallas_call | solution.py:1026
  (36 shorter events, 0.1 us)
Async XLA Ops:
  0.7 29.1 %copy-start.6 = (f32[2,4,32]{2,1,0:T(4,128)S(1)}, f32[2,4,32]{2,1,0:T(4,128)}, u32[]{:S(2)}) copy-start(f32[2,4,32]{2,1,0:T(4,128)} %table.13) | copy-start | bytes 3076
  2.7 15.5 %all-to-all-start = ((bf16[32,16,128]{2,1,0:T(8,128)(2,1)}), bf16[32,16,128]{2,1,0:T(8,128)(2,1)S(1)}, u32[]{:S(2)}, u32[]{:S(2)}) async-start(bf16[32,16,128]{2,1,0:T(8,128)(2,1)} %pack.1), calls=%async_computation | async-start | bytes 262144 | tf_op jit(solution)/shard_map/all_to_all | solution.py:1039
  40.8 11.8 %copy-start = (f32[3,9,32,32]{3,2,1,0:T(8,128)S(1)}, f32[3,9,32,32]{3,2,1,0:T(8,128)}, u32[]{:S(2)}) copy-start(f32[3,9,32,32]{3,2,1,0:T(8,128)} %w_convs.1) | copy-start | bytes 331780
  40.8 11.8 %copy-start.5 = (f32[2,32,32]{2,1,0:T(8,128)S(1)}, f32[2,32,32]{2,1,0:T(8,128)}, u32[]{:S(2)}) copy-start(f32[2,32,32]{2,1,0:T(8,128)} %w_style.5) | copy-start | bytes 24580
  57.0 9.9 %all-to-all-start.4 = ((f32[32,3,1,128]{3,2,1,0:T(1,128)}), f32[32,3,1,128]{3,2,1,0:T(1,128)S(1)}, u32[]{:S(2)}, u32[]{:S(2)}) async-start(f32[32,3,1,128]{3,2,1,0:T(1,128)} %get-tuple-element.95.pay), calls=%async_computation.4 | async-start | bytes 98304 | tf_op jit(solution)/shard_map/all_to_all | solution.py:1039
  59.6 7.3 %copy-start.1 = (bf16[1152,256]{1,0:T(8,128)(2,1)S(1)}, bf16[1152,256]{1,0:T(8,128)(2,1)}, u32[]{:S(2)}) copy-start(bf16[1152,256]{1,0:T(8,128)(2,1)} %get-tuple-element.102.back.back_two) | copy-start | bytes 1769476
  59.6 7.3 %copy-start.7 = (bf16[256,128]{1,0:T(8,128)(2,1)S(1)}, bf16[256,128]{1,0:T(8,128)(2,1)}, u32[]{:S(2)}) copy-start(bf16[256,128]{1,0:T(8,128)(2,1)} %get-tuple-element.97.head_mat) | copy-start | bytes 196612
  59.6 7.3 %copy-start.11 = (f32[33,3]{0,1:T(4,128)S(1)}, f32[33,3]{0,1:T(4,128)}, u32[]{:S(2)}) copy-start(f32[33,3]{0,1:T(4,128)} %param.26) | copy-start | bytes 1192
  80.9 15.6 %copy-start.2 = (bf16[1152,256]{1,0:T(8,128)(2,1)S(1)}, bf16[1152,256]{1,0:T(8,128)(2,1)}, u32[]{:S(2)}) copy-start(bf16[1152,256]{1,0:T(8,128)(2,1)} %get-tuple-element.115.back) | copy-start | bytes 1769476
  85.5 17.3 %copy-start.9 = (f32[2,32,32]{2,1,0:T(8,128)S(1)}, f32[2,32,32]{2,1,0:T(8,128)}, u32[]{:S(2)}) copy-start(f32[2,32,32]{2,1,0:T(8,128)} %m_style.1) | copy-start | bytes 24580
  85.5 17.3 %copy-start.10 = (f32[2,32,32]{2,1,0:T(8,128)S(1)}, f32[2,32,32]{2,1,0:T(8,128)}, u32[]{:S(2)}) copy-start(f32[2,32,32]{2,1,0:T(8,128)} %s_style.1) | copy-start | bytes 24580
  85.5 17.3 %copy-start.16 = (f32[33,3]{0,1:T(4,128)S(1)}, f32[33,3]{0,1:T(4,128)}, u32[]{:S(2)}) copy-start(f32[33,3]{0,1:T(4,128)} %param.31) | copy-start | bytes 1192
  85.6 17.3 %copy-start.17 = (f32[33,3]{0,1:T(4,128)S(1)}, f32[33,3]{0,1:T(4,128)}, u32[]{:S(2)}) copy-start(f32[33,3]{0,1:T(4,128)} %param.36) | copy-start | bytes 1192
  85.6 26.6 %copy-start.3 = (f32[3,9,32,32]{3,2,1,0:T(8,128)S(1)}, f32[3,9,32,32]{3,2,1,0:T(8,128)}, u32[]{:S(2)}) copy-start(f32[3,9,32,32]{3,2,1,0:T(8,128)} %m_convs.1) | copy-start | bytes 331780
  85.6 26.6 %copy-start.4 = (f32[3,9,32,32]{3,2,1,0:T(8,128)S(1)}, f32[3,9,32,32]{3,2,1,0:T(8,128)}, u32[]{:S(2)}) copy-start(f32[3,9,32,32]{3,2,1,0:T(8,128)} %s_convs.1) | copy-start | bytes 331780
  85.6 26.6 %copy-start.8 = (f32[10,2,32]{2,1,0:T(2,128)S(1)}, f32[10,2,32]{2,1,0:T(2,128)}, u32[]{:S(2)}) copy-start(f32[10,2,32]{2,1,0:T(2,128)} %w_first.1) | copy-start | bytes 7684
  85.6 26.6 %copy-start.12 = (f32[10,2,32]{2,1,0:T(2,128)S(1)}, f32[10,2,32]{2,1,0:T(2,128)}, u32[]{:S(2)}) copy-start(f32[10,2,32]{2,1,0:T(2,128)} %m_first.1) | copy-start | bytes 7684
  85.6 26.6 %copy-start.13 = (f32[10,2,32]{2,1,0:T(2,128)S(1)}, f32[10,2,32]{2,1,0:T(2,128)}, u32[]{:S(2)}) copy-start(f32[10,2,32]{2,1,0:T(2,128)} %s_first.1) | copy-start | bytes 7684
  85.6 26.6 %copy-start.14 = (f32[2,4,32]{2,1,0:T(4,128)S(1)}, f32[2,4,32]{2,1,0:T(4,128)}, u32[]{:S(2)}) copy-start(f32[2,4,32]{2,1,0:T(4,128)} %m_norms.1) | copy-start | bytes 3076
  85.6 26.6 %copy-start.15 = (f32[2,4,32]{2,1,0:T(4,128)S(1)}, f32[2,4,32]{2,1,0:T(4,128)}, u32[]{:S(2)}) copy-start(f32[2,4,32]{2,1,0:T(4,128)} %s_norms.1) | copy-start | bytes 3076
  100.2 12.0 %all-to-all-start.7 = ((f32[32,13,1,128]{3,2,1,0:T(1,128)}), f32[32,13,1,128]{3,2,1,0:T(1,128)S(1)}, u32[]{:S(2)}, u32[]{:S(2)}) async-start(f32[32,13,1,128]{3,2,1,0:T(1,128)} %get-tuple-element.116.pay), calls=%async_computation.7 | async-start | bytes 425984 | tf_op jit(solution)/shard_map/all_to_all | solution.py:1039

commit v8 on v7

--- a/solution.py
+++ b/solution.py
@@ -25,6 +25,7 @@
 RIM = 8
 FLOW, LABEL, MASK = 16, 32, 40
 LEFT, RIGHT = 64, 96
+ALONE = 100
 AFTER, ROW, BEFORE = 32, 33, 64
 F32 = jnp.float32
 BF16 = jnp.bfloat16
@@ -103,12 +104,12 @@
     return v.reshape(-1, LANES)
 
 
-def loop(count, body):
+def loop(count, body, unroll=5):
     def step(i, carry):
         body(i)
         return carry
 
-    lax.fori_loop(0, count, step, 0, unroll=min(count, 5))
+    lax.fori_loop(0, count, step, 0, unroll=min(count, unroll))
 
 
 def copies(sems, *pairs):
@@ -193,13 +194,15 @@
 
 
 def local_stats(v, first, rows, count):
-    mean = row_sums(first, rows, lambda at, k: (v[at, k],))[0] * (GRP / count)
-
-    def square(at, k):
-        away = v[at, k] - mean
-        return (away * away,)
-
-    return mean, row_sums(first, rows, square)[0]
+    count = count / GRP
+    pivot = col_sum(v[first, 0] + v[first, 1]) / (2 * v.shape[2])
+
+    def moments(at, k):
+        away = v[at, k] - pivot
+        return away, away * away
+
+    total, square = row_sums(first, rows, moments)
+    return pivot + total / count, square - total * (total / count)
 
 
 def merge_stats(means, squares, local_count, pixel_count):
@@ -487,6 +490,22 @@
     return v
 
 
+def wide_dot(a, b, dims=(((1,), (0,)), ((), ()))):
+    (a_high, a_low), (b_high, b_low) = [[v.astype(BF16) for v in in_parts(x, 2)] for x in (a, b)]
+    axis_a, axis_b = dims[0][0][0], dims[0][1][0]
+    left = jnp.concatenate([a_high, a_high, a_low], axis=axis_a)
+    right = jnp.concatenate([b_high, b_low, b_high], axis=axis_b)
+    return lax.dot_general(left, right, dims, preferred_element_type=F32)
+
+
+def in_parts(v, count):
+    out = []
+    for _ in range(count):
+        out.append(low(v))
+        v = v - out[-1]
+    return out
+
+
 def mine_of(v, me):
     return col_sum(jnp.where(row_of(v.shape) == me, v, 0.0))
 
@@ -496,7 +515,7 @@
     style = by_image(spread(row_of_each(got, 2), 0), parts) / pool_cells
     style_out[...] = style
     one, two = [
-        jnp.dot(style, diagonal_blocks(w_style[i]), precision=highest, preferred_element_type=F32) for i in range(2)
+        wide_dot(style, diagonal_blocks(w_style[i])) for i in range(2)
     ]
     mean, inverse = merge_stats(row_of_each(got, 0) + one, row_of_each(got, 1), local_count, pixel_count)
     notes(vec, inverse)
@@ -596,13 +615,22 @@
     own = pl.ds(off, height)
     fetched = copies(
         sems,
+        (spots(fields, "xhat_zero").at[own], below_x),
         (spots(fields, "xhat_one").at[own], xhat),
         (spots(fields, "shared").at[own], shared),
-        (spots(fields, "xhat_zero").at[own], below_x),
         (spots(lows, "hidden_one"), field),
     )
-    wait(fetched)
+    wait(fetched[:1])
     at = pl.ds(0, height)
+    low_x = jnp.concatenate([own_lanes(below_x, at), jnp.ones((height * field.shape[2], LANES), BF16)], axis=1)
+    entries, alone = [], zero_row()
+    lane = lane_of((1, LANES))
+    for r in range(3):
+        for tap, bare in pixel_taps(sides, off + r, height, low_x, (-1, 0, 1), True):
+            for v, b in zip(tap, bare):
+                alone = jnp.where(lane == ALONE + len(entries), b, alone)
+                entries.append(v)
+    wait(fetched[1:])
     centres = [fold(v) / local_count for v in row_sums(0, height, lambda at, k: (xhat[at, k], shared[at, k]))]
     probe = [flat(v[at, k] - c).astype(BF16) for v, c in zip((xhat, shared), centres) for k in range(2)]
     wide = jnp.concatenate(views(field, off, height), axis=1)
@@ -622,20 +650,20 @@
                 val = val + jnp.where(group == a, plain[:, spot : spot + LANES], 0.0)
             hidden.append(fold(val))
     packed = [groups(*hidden[0:4]), groups(*hidden[4:8]), hidden[8]]
-    notes(sums, *packed)
-    packed = jnp.concatenate(packed, axis=0)
-    for k in range(2):
-        put_taps(found[2 * LANES * k : 2 * LANES * (k + 1)], out.at[:, 3 * k + 1 : 3 * k + 4, 0], (centres[k], packed))
-    low_x = jnp.concatenate([own_lanes(below_x, at), jnp.ones((wide.shape[0], LANES), BF16)], axis=1)
-    entries = []
-    for r in range(3):
-        for tap, alone in pixel_taps(sides, off + r, height, low_x, (-1, 0, 1), True):
-            entries.extend(zip(tap, alone))
-    rows = [groups(*entry, hidden[e] if e < 9 else zero_row(), zero_row()) for e, entry in enumerate(entries)]
-    out[:, 0, 0, :] = jnp.concatenate(rows + [jnp.zeros((CH - len(rows), LANES), F32)], axis=0)
-
-
-def head_kernel(place, got, got_style, resid, sides, head_mat, w_head, below_x, ahead, table, back, grad, xhat, pay, vec, decoded, slopes, grad_low, *, local_count, pixel_count, height):
+    all_hidden = jnp.concatenate(packed, axis=0)
+    last = [
+        put_taps(
+            found[2 * LANES * k : 2 * LANES * (k + 1)], out.at[:, 2 * k + 1 : 2 * k + 3, 0], (centres[k], all_hidden)
+        )
+        for k in range(2)
+    ]
+    entries += hidden
+    entries.append(jnp.zeros((CH - len(entries), LANES), F32))
+    out[:, 0, 0, :] = groups(jnp.concatenate(entries, axis=0), *last, jnp.zeros((CH, LANES), F32))
+    notes(sums, *packed, alone)
+
+
+def head_kernel(place, got, got_style, resid, sides, head_mat, w_head, below_x, ahead, image_sums, table, back, grad, xhat, pay, vec, decoded, slopes, grad_low, *, local_count, pixel_count, height):
     mean, inverse = merge_stats(row_of_each(got, 0), row_of_each(got, 1), local_count, pixel_count)
     notes(vec, inverse, mean)
     gain, bias = affine(table, 3)
@@ -652,7 +680,7 @@
             slopes[at, k] = slope(n, s)
             decoded[at, k] = (n * s).astype(BF16)
 
-    loop(rows // 4, norm_rows)
+    loop(rows // 4, norm_rows, 10)
     head = head_mat[...]
     wide = jnp.concatenate([flat(decoded[:, 0]), flat(decoded[:, 1])], axis=1)
     bias_row = zero_row()
@@ -690,14 +718,10 @@
     for k, g in enumerate(blocks_of(y, rows)):
         grad[:, k] = g * slopes[:, k]
     factor = gain * inverse
-    back_rows(grad_low, rows, lambda at, k: factor * grad[at, k])
+    back_rows(grad_low, rows, lambda at, k: factor * grad[at, k], 10)
     shift_sum, scale_sum = own_sums(grad, xhat, off, height)
-
-    @pl.when(place[0] >= 0)
-    def _():
-        y = conv(grad_low, back, off, height)
-        slopes[0:height, 0], slopes[0:height, 1] = blocks_of(y, height)
-
+    y = conv(grad_low, back, off, height)
+    slopes[0:height, 0], slopes[0:height, 1] = blocks_of(y, height)
     gain, bias = affine(table, 2)
 
     def links(at, k):
@@ -706,9 +730,9 @@
         return g, g * x
 
     below = [fold(v) for v in row_sums(0, height, links)]
-    send(pay, groups(shift_sum, scale_sum, *below), row, total_of(got, 2))
-    send_parts(pay, 3, 7)
-    pay[0:CH, 3:10] = ahead[...]
+    send(pay, groups(shift_sum, scale_sum, *below), row + image_sums[3:4], total_of(got, 2))
+    send_parts(pay, 3, 5)
+    pay[0:CH, 3:8] = ahead[...]
 
 
 def own_sums(grad, xhat, first, rows):
@@ -732,12 +756,12 @@
     return factor * (grad - (shift + xhat * scale))
 
 
-def back_rows(grad_low, rows, value):
+def back_rows(grad_low, rows, value, unroll=5):
     def some(i):
         put_low(grad_low, 4 * i, *[value(pl.ds(4 * i, 4), k) for k in range(2)])
 
     blank(grad_low)
-    loop(rows // 4, some)
+    loop(rows // 4, some, unroll)
 
 
 def own_lanes(grad, at):
@@ -747,7 +771,7 @@
 def tap_sums(field, grad, first, rows, out, more=None):
     wide = jnp.concatenate(views(field, first, rows), axis=1)
     found = lax.dot_general(grad, wide, (((0,), (0,)), ((), ())), preferred_element_type=F32)
-    put_taps(found, out, more)
+    return put_taps(found, out, more)
 
 
 def put_taps(found, out, more=None):
@@ -768,6 +792,8 @@
         if more is not None:
             centre, sums = more
             val = val + column_of(centre) * sums[q : q + 1]
+        if q == 2:
+            return val
         out[:, q, :] = val
 
 
@@ -809,7 +835,8 @@
 
     shift_two = spread(total, 2) - across(group < 2)
     scale_two = spread(total, 3) - across(group >= 2)
-    notes(more, scale_two, shift_two, *[total_of(got, r) for r in (4, 5, 6)])
+    entry = total_of(got, 3)
+    notes(more, scale_two, shift_two, total_of(got, 4), total_of(got, 5), spread(entry, 1))
 
     def value(at, k):
         g = norm_back(grad[at, k], xhat[at, k], factor, shift, scale)
@@ -844,14 +871,16 @@
         below[:, k] = g.reshape(rows, -1, LANES)
     shift_sum, scale_sum = own_sums(below, below_x, off, height)
     send(pay, groups(shift_sum, scale_sum, sum_one, sum_two))
-    pay[:, 7, 0, :] = jnp.broadcast_to(total_of(got, 3), (devices, LANES))
+    entry = spread(entry, 0)
+    pay[:, 1, 0, :] = jnp.broadcast_to(entry, (devices, LANES))
     at = pl.ds(off + 1, height)
-    tap_sums(field_two, own_lanes(low_two, at), off, height, send_parts(pay, 1, 3))
-    tap_sums(field_one, own_lanes(low_one, at), off, height, send_parts(pay, 4, 3))
+    last_two = tap_sums(field_two, own_lanes(low_two, at), off, height, send_parts(pay, 2, 2))
+    last_one = tap_sums(field_one, own_lanes(low_one, at), off, height, send_parts(pay, 4, 2))
     centre = shift_sum / local_count
     at = pl.ds(off, height)
     grad = jnp.concatenate([flat(below[at, k] - centre).astype(BF16) for k in range(2)], axis=1)
-    tap_sums(field_zero, grad, off, height, send_parts(pay, 8, 3), (centre, sums))
+    last_zero = tap_sums(field_zero, grad, off, height, send_parts(pay, 6, 2), (centre, sums))
+    pay[0:CH, 1, 0, :] = groups(last_two, last_one, last_zero, jnp.broadcast_to(entry, (CH, LANES)))
 
 
 def summed_kernel(place, got, got_style, got_head, grad, xhat, shared, vec, more_two, table, w_style, sides, back, fields, pay, more, below, below_x, grad_low, sems, *, spots, pixel_count, pool_cells, parts):
@@ -862,10 +891,8 @@
     rows = grad.shape[0]
     dims = (((1,), (1,)), ((), ()))
     first = row_of_each(got, 0)
-    each = lax.dot_general(
-        spread(first, 2), diagonal_blocks(w_style[0]), dims, precision=highest, preferred_element_type=F32
-    ) + lax.dot_general(
-        spread(first, 3), diagonal_blocks(w_style[1]), dims, precision=highest, preferred_element_type=F32
+    each = wide_dot(spread(first, 2), diagonal_blocks(w_style[0]), dims) + wide_dot(
+        spread(first, 3), diagonal_blocks(w_style[1]), dims
     )
     each = each / pool_cells
     total = col_sum(first)
@@ -884,12 +911,14 @@
         below[:, k] = y * slope_at(below_x[:, k], gain, bias)
     me = place[2]
     weights = at_lane(by_image(each, parts), me)
-    entries = got[0:CH, 7, 0, :]
-    hidden = spread(entries, 2)
-    hidden = [groups(*[hidden[t : t + 1] for t in range(4 * q, min(4 * q + 4, 9))]) for q in range(3)]
+    hidden = spread(got[0:CH, 1, 0, :], 3)
+    hidden = [groups(*[hidden[18 + t : 19 + t] for t in range(4 * q, min(4 * q + 4, 9))]) for q in range(3)]
+    last = total_of(got, 1)
+    direct = [total_of(got, 6), total_of(got, 7), spread(last, 2)]
+    shares = [row_of_each(got_head, 6), row_of_each(got_head, 7), spread(row_of_each(got_head, 3), 2)]
     shard = []
     for q in range(3):
-        val = total_of(got, 8 + q) + col_sum(weights * row_of_each(got_head, 7 + q))
+        val = direct[q] + col_sum(weights * shares[q])
         val = val - at_lane(shift_mean, me) * hidden[q] - at_lane(scale_mean, me) * more_two[2 + q : 3 + q]
         shard.append(at_lane(factor, me) * val)
     at = pl.ds(off + 1, height)
@@ -899,13 +928,11 @@
     for r in range(3):
         for tap in pixel_taps(sides, off + r, height, low_below, (-1, 0, 1)):
             taps.extend(tap)
-    two, one = [total_of(got, r) for r in (1, 2, 3)], [total_of(got, r) for r in (4, 5, 6)]
     taps = [shard[2]] + taps + side
     send(
         pay,
-        groups(*own_sums(below, below_x, 0, height), two[2], one[2]),
-        *two[0:2],
-        *one[0:2],
+        groups(*own_sums(below, below_x, 0, height), spread(last, 0), spread(last, 1)),
+        *[total_of(got, r) for r in range(2, 6)],
         *shard[0:2],
         *[groups(*(taps[4 * q : 4 * q + 4] + [zero_row()])[0:4]) for q in range(6)],
     )
@@ -986,8 +1013,8 @@
     totals = [total_of(got, r) for r in range(7, 13)]
     shift, scale = spread(zero_sums, 0), spread(zero_sums, 1)
     factor = affine(table, 0)[0] * vec[0:1]
-    entries = got_one_back[0:CH, 7, 0, :]
-    by_x, alone = spread(entries, 0), spread(entries, 1)
+    by_x = spread(got_one_back[0:CH, 1, 0, :], 3)
+    alone = total_of(got_head, 1)
     refs = (w_first, m_first, s_first)
     outs = (first_master, first_moment, first_square, first_copy)
     for t in range(10):
@@ -996,7 +1023,7 @@
             k, b = divmod(1 + e, 4)
             v = spread(totals[k], b)
             if t < 9:
-                v = factor * (v - (alone[e : e + 1] * shift + by_x[e : e + 1] * scale) / pixel_count)
+                v = factor * (v - (at_lane(alone, ALONE + e) * shift + by_x[e : e + 1] * scale) / pixel_count)
             pair.append(v[:, 0:CH])
         put(t, refs, jnp.concatenate(pair, axis=0), rate_table[0], outs)
 
@@ -1151,22 +1178,22 @@
     got_three = exchange(pay)
     ahead, hidden_sums = call(
         part(ahead_kernel, spots=spots, local_count=local_count),
-        [((CH, 7, 1, LANES), F32), vec],
+        [((CH, 5, 1, LANES), F32), vec],
         place, far(pay), sides, far(fields), far(lows),
         scalars=1, scratch=[own_field, own_field, own_field, low_field], sems=4, name="ahead",
     )
 
     grad_three, xhat_three, pay, inv_three = call(
         part(head_kernel, **counts),
-        [field, field, payload(10), vec],
-        place, got_three, got_style, resid, sides, head_mat, head_rows, xhat_two, ahead, batch_norm_table, back_two,
+        [field, field, payload(8), vec],
+        place, got_three, got_style, resid, sides, head_mat, head_rows, xhat_two, ahead, hidden_sums, batch_norm_table, back_two,
         scalars=1, scratch=[((rows, 2, segments, LANES), BF16), field, low_field], name="head",
     )
     got_head = exchange(pay)
 
     grad_one, xhat_one, shared, pay, more_two = call(
         part(decoder_back_kernel, spots=spots, **counts),
-        [field, field, field, payload(11), vec],
+        [field, field, field, payload(8), vec],
         place, got_head, grad_three, xhat_three, xhat_two, inv_three, inv_two, hidden_sums, batch_norm_table, back_two, far(weights),
         far(fields), far(lows),
         scalars=1, scratch=[field, field, low_field, low_field, low_field, low_field, low_field, nine], sems=6,

time: 114 us -> 113 us (level)
  blocking collectives: 49.1 us -> 47.8 us
    all_to_all x5, blocking collectives: 49.1 us -> 47.8 us  [exchange(): return lax.all_to_all(pay, ('row', 'col'), 0, 0)]
where the time goes in v8:
time: 113 us; the launch traced here: 112 us
  blocking collectives  47.8 us (42%)
  Pallas kernels  35.2 us (31%)
  waiting for transfers between devices  15.4 us (14%)
  starting transfers between devices  12.5 us (11%)
    all_to_all x5, blocking collectives, exchange(): return lax.all_to_all(pay, ('row', 'col'), 0, 0)  47.8 us
    pallas_call x12, Pallas kernels, call(): pl.pallas_call(kernel, out_shape=[jax.ShapeDtypeStruct(*plain(x)) for x i...  35.2 us
    all_to_all x3, waiting for transfers between devices, exchange(): return lax.all_to_all(pay, ('row', 'col'), 0, 0)  15.4 us
    all_to_all x3, starting transfers between devices, exchange(): return lax.all_to_all(pay, ('row', 'col'), 0, 0)  12.5 us
  transfers between devices with their start and end apart: 3, of which 3 were waited for; matrix products, arithmetic and copies ran while one was open for 0% of the time, Pallas kernels for 8%

profile of v8, /device:TPU:0, one launch (start us, length us, event | category | flops | bytes accessed | tf_op | source)
XLA Modules:
  0.0 112.0 jit_solution(16373100619252882240)
XLA Ops:
  0.7 2.0 %pack.1 = bf16[32,16,128]{2,1,0:T(8,128)(2,1)} custom-call(bf16[16,8,2,32]{3,2,1,0:T(2,128)(2,1)} %bitcast.20, s32[16,8,2,32]{3,2,1,0:T(2,128)} %bitcast.19, s32[16,8,32]{2,1,0:T(8,128)} %labels_in.1, s32[16,8,32]{2,1,0:T(8,128)} %valid_in.1), custom_call_target="tpu_custom_call" | custom-call | tf_op jit(solution)/shard_map/pack/pallas_call | solution.py:1053
  2.7 7.3 %all-to-all-start = ((bf16[32,16,128]{2,1,0:T(8,128)(2,1)}), bf16[32,16,128]{2,1,0:T(8,128)(2,1)S(1)}, u32[]{:S(2)}, u32[]{:S(2)}) async-start(bf16[32,16,128]{2,1,0:T(8,128)(2,1)} %pack.1), calls=%async_computation | async-start | bytes 262144 | tf_op jit(solution)/shard_map/all_to_all | solution.py:1066
  10.1 4.7 %prepare.1 = (bf16[65536,256]{1,0:T(8,128)(2,1)}, bf16[1152,256]{1,0:T(8,128)(2,1)}, bf16[1152,256]{1,0:T(8,128)(2,1)}, bf16[256,128]{1,0:T(8,128)(2,1)}) custom-call(f32[10,2,32]{2,1,0:T(2,128)} %w_first.1, f32[3,9,32,32]{3,2,1,0:T(8,128)} %w_convs.1, f32[3,33]{1,0:T(4,128)} %bitcast.14), custom_call_target="tpu_custom_call" | custom-call | tf_op jit(solution)/shard_map/prepare/pallas_call | solution.py:1053
  14.8 0.1 pad_add_fusion.place
  14.9 3.4 %all-to-all-done.got = bf16[32,16,128]{2,1,0:T(8,128)(2,1)S(1)} async-done(((bf16[32,16,128]{2,1,0:T(8,128)(2,1)}), bf16[32,16,128]{2,1,0:T(8,128)(2,1)S(1)}, u32[]{:S(2)}, u32[]{:S(2)}) %all-to-all-start) | async-done | bytes 131104 | tf_op jit(solution)/shard_map/all_to_all | solution.py:1066
  18.3 2.0 %image_conv.1 = (bf16[42,16,128]{2,1,0:T(8,128)(2,1)S(1)}, f32[40,2,16,128]{3,2,1,0:T(8,128)S(1)}, f32[32,2,1,128]{3,2,1,0:T(1,128)S(1)}, f32[8,128]{1,0:T(8,128)S(1)}, bf16[1280,256]{1,0:T(8,128)(2,1)S(1)}) custom-call(s32[3]{0:T(128)S(1)} %pad_add_fusion.place, bf16[32,16,128]{2,1,0:T(8,128)(2,1)S(1)} %all-to-all-done.got, ...), custom_call_target="tpu_custom_call" | custom-call | tf_op jit(solution)/shard_map/image_conv/pallas_call | solution.py:1053
  20.3 9.5 %all_to_all.40.got = f32[32,2,1,128]{3,2,1,0:T(1,128)S(1)} all-to-all(f32[32,2,1,128]{3,2,1,0:T(1,128)S(1)} %get-tuple-element.81), channel_id=1, replica_groups=mesh['row'=8,'col'=4] {'row','col'}, dimensions={0} | all-to-all | bytes 65536 | tf_op jit(solution)/shard_map/all_to_all | solution.py:1066
  29.8 2.0 %first_block.1 = (f32[40,2,16,128]{3,2,1,0:T(8,128)S(1)}, f32[32,2,1,128]{3,2,1,0:T(1,128)S(1)}, f32[8,128]{1,0:T(8,128)S(1)}, f32[2048,2,16,128]{3,2,1,0:T(8,128)}, bf16[2731,3,16,128]{3,2,1,0:T(8,128)(2,1)}) custom-call(s32[3]{0:T(128)S(1)} %pad_add_fusion.place, f32[32,2,1,128]{3,2,1,0:T(1,128)S(1)} %all_to_all.40.got, ...), custom_call_target="tpu_custom_call" | custom-call | tf_op jit(solution)/shard_map/first_block/pallas_call | solution.py:1053
  31.8 8.9 %all_to_all.41.got = f32[32,2,1,128]{3,2,1,0:T(1,128)S(1)} all-to-all(f32[32,2,1,128]{3,2,1,0:T(1,128)S(1)} %get-tuple-element.85), channel_id=1, replica_groups=mesh['row'=8,'col'=4] {'row','col'}, dimensions={0} | all-to-all | bytes 65536 | tf_op jit(solution)/shard_map/all_to_all | solution.py:1066
  40.8 2.8 %pool_and_merge.1 = (f32[40,2,16,128]{3,2,1,0:T(8,128)S(1)}, f32[32,3,1,128]{3,2,1,0:T(1,128)S(1)}, f32[8,128]{1,0:T(8,128)S(1)}, bf16[42,3,16,128]{3,2,1,0:T(8,...) custom-call(s32[3]{0:T(128)S(1)} %pad_add_fusion.place, ...), custom_call_target="tpu_custom_call", output_to_operand_aliasing={{5}: (6, {}), {6}: (7, {})} | custom-call | tf_op jit(solution)/shard_map/pool_and_merge/pallas_call | solution.py:1053
  43.5 9.0 %all_to_all.42.got.got_style = f32[32,3,1,128]{3,2,1,0:T(1,128)S(1)} all-to-all(f32[32,3,1,128]{3,2,1,0:T(1,128)S(1)} %get-tuple-element.90), channel_id=1, replica_groups=mesh['row'=8,'col'=4] {'row','col'}, dimensions={0} | all-to-all | bytes 98304 | tf_op jit(solution)/shard_map/all_to_all | solution.py:1066
  52.6 4.3 %decoder.1 = (f32[40,2,16,128]{3,2,1,0:T(8,128)S(1)}, f32[32,3,1,128]{3,2,1,0:T(1,128)}, f32[8,128]{1,0:T(8,128)S(1)}, f32[32,128]{1,0:T(8,128)S(1)}, f32[40,2,1...) custom-call(s32[3]{0:T(128)S(1)} %pad_add_fusion.place, ...), custom_call_target="tpu_custom_call", output_to_operand_aliasing={{5}: (8, {})} | custom-call | tf_op jit(solution)/shard_map/decoder/pallas_call | solution.py:1053
  56.9 2.6 %all-to-all-start.4 = ((f32[32,3,1,128]{3,2,1,0:T(1,128)}), f32[32,3,1,128]{3,2,1,0:T(1,128)S(1)}, u32[]{:S(2)}, u32[]{:S(2)}) async-start(f32[32,3,1,128]{3,2,1,0:T(1,128)} %get-tuple-element.95.pay), calls=%async_computation.4 | async-start | bytes 98304 | tf_op jit(solution)/shard_map/all_to_all | solution.py:1066
  59.5 3.6 %ahead.1 = (f32[32,5,1,128]{3,2,1,0:T(1,128)S(1)}, f32[8,128]{1,0:T(8,128)S(1)}) custom-call(s32[3]{0:T(128)S(1)} %pad_add_fusion.place, f32[32,3,1,128]{3,2,1,0:T(1,128)} %get-tuple-element.95.pay, bf16[42,16,128]{2,1,0:T(8,128)(2,1)S(1)} %get-tuple-element.83.sides, f32[2048,2,16,128]{3,2,1,0:T(8,128)} %get-tuple-element.99.fields, ...), custom_call_target="tpu_custom_call" | custom-call | tf_op jit(solution)/shard_map/ahead/pallas_call | solution.py:1053
  63.1 3.7 %all-to-all-done.4.got = f32[32,3,1,128]{3,2,1,0:T(1,128)S(1)} async-done(((f32[32,3,1,128]{3,2,1,0:T(1,128)}), f32[32,3,1,128]{3,2,1,0:T(1,128)S(1)}, u32[]{:S(2)}, u32[]{:S(2)}) %all-to-all-start.4) | async-done | bytes 49184 | tf_op jit(solution)/shard_map/all_to_all | solution.py:1066
  66.8 2.8 %head.1 = (f32[40,2,16,128]{3,2,1,0:T(8,128)S(1)}, f32[40,2,16,128]{3,2,1,0:T(8,128)S(1)}, f32[32,8,1,128]{3,2,1,0:T(1,128)S(1)}, f32[8,128]{1,0:T(8,128)S(1)}) custom-call(s32[3]{0:T(128)S(1)} %pad_add_fusion.place, f32[32,3,1,128]{3,2,1,0:T(1,128)S(1)} %all-to-all-done.4.got, f32[32,3,1,128]{3,2,1,0:T(1,128)S(1)} %all_to_all.42.got.got_style, ...), custom_call_target="tpu_custom_call" | custom-call | tf_op jit(solution)/shard_map/head/pallas_call | solution.py:1053
  69.7 10.2 %all_to_all.43.got.got_head = f32[32,8,1,128]{3,2,1,0:T(1,128)S(1)} all-to-all(f32[32,8,1,128]{3,2,1,0:T(1,128)S(1)} %get-tuple-element.104), channel_id=1, replica_groups=mesh['row'=8,'col'=4] {'row','col'}, dimensions={0} | all-to-all | bytes 262144 | tf_op jit(solution)/shard_map/all_to_all | solution.py:1066
  79.9 4.7 %decoder_back.1 = (f32[40,2,16,128]{3,2,1,0:T(8,128)S(1)}, f32[40,2,16,128]{3,2,1,0:T(8,128)S(1)}, f32[40,2,16,128]{3,2,1,0:T(8,128)S(1)}, f32[32,8,1,128]{3,2,1,0:T(1,128)S(1)}, f32[8,128]{1,0:T(8,128)S(1)}) custom-call(s32[3]{0:T(128)S(1)} %pad_add_fusion.place, f32[32,8,1,128]{3,2,1,0:T(1,128)S(1)} %all_to_all.43.got.got_head, ...), custom_call_target="tpu_custom_call" | custom-call | tf_op jit(solution)/shard_map/decoder_back/pallas_call | solution.py:1053
  84.7 10.1 %all_to_all.44.got.got_one_back = f32[32,8,1,128]{3,2,1,0:T(1,128)S(1)} all-to-all(f32[32,8,1,128]{3,2,1,0:T(1,128)S(1)} %get-tuple-element.109), channel_id=1, replica_groups=mesh['row'=8,'col'=4] {'row','col'}, dimensions={0} | all-to-all | bytes 262144 | tf_op jit(solution)/shard_map/all_to_all | solution.py:1066
  94.8 3.5 %summed_back.1 = (f32[32,13,1,128]{3,2,1,0:T(1,128)}, f32[8,128]{1,0:T(8,128)S(1)}) custom-call(s32[3]{0:T(128)S(1)} %pad_add_fusion.place, f32[32,8,1,128]{3,2,1,0:T(1,128)S(1)} %all_to_all.44.got.got_one_back, f32[32,3,1,128]{3,2,1,0:T(1,128)S(1)} %all_to_all.42.got.got_style, f32[32,8,1,128]{3,2,1,0:T(1,128)S(1)} %all_to_all.43.got.got_head, ...), custom_call_target="tpu_custom_call" | custom-call | tf_op jit(solution)/shard_map/summed_back/pallas_call | solution.py:1053
  98.3 2.6 %all-to-all-start.7 = ((f32[32,13,1,128]{3,2,1,0:T(1,128)}), f32[32,13,1,128]{3,2,1,0:T(1,128)S(1)}, u32[]{:S(2)}, u32[]{:S(2)}) async-start(f32[32,13,1,128]{3,2,1,0:T(1,128)} %get-tuple-element.116.pay), calls=%async_computation.7 | async-start | bytes 425984 | tf_op jit(solution)/shard_map/all_to_all | solution.py:1066
  100.9 1.0 update_early.1
  101.9 8.3 %all-to-all-done.7.got = f32[32,13,1,128]{3,2,1,0:T(1,128)S(1)} async-done(((f32[32,13,1,128]{3,2,1,0:T(1,128)}), f32[32,13,1,128]{3,2,1,0:T(1,128)S(1)}, u32[]{:S(2)}, u32[]{:S(2)}) %all-to-all-start.7) | async-done | bytes 213024 | tf_op jit(solution)/shard_map/all_to_all | solution.py:1066
  110.3 1.7 %update_late.1 = (f32[10,2,32]{2,1,0:T(2,128)}, f32[10,2,32]{2,1,0:T(2,128)}, f32[10,2,32]{2,1,0:T(2,128)}, bf16[10,2,32]{2,1,0:T(2,128)(2,1)}, f32[3,9,32,32]{3...) custom-call(f32[32,13,1,128]{3,2,1,0:T(1,128)S(1)} %all-to-all-done., ...), custom_call_target="tpu_custom_call" | custom-call | tf_op jit(solution)/shard_map/update_late/pallas_call | solution.py:1053
  (36 shorter events, 0.1 us)
Async XLA Ops:
  0.7 29.1 %copy-start.6 = (f32[2,4,32]{2,1,0:T(4,128)S(1)}, f32[2,4,32]{2,1,0:T(4,128)}, u32[]{:S(2)}) copy-start(f32[2,4,32]{2,1,0:T(4,128)} %table.13) | copy-start | bytes 3076
  2.7 15.5 %all-to-all-start = ((bf16[32,16,128]{2,1,0:T(8,128)(2,1)}), bf16[32,16,128]{2,1,0:T(8,128)(2,1)S(1)}, u32[]{:S(2)}, u32[]{:S(2)}) async-start(bf16[32,16,128]{2,1,0:T(8,128)(2,1)} %pack.1), calls=%async_computation | async-start | bytes 262144 | tf_op jit(solution)/shard_map/all_to_all | solution.py:1066
  40.8 11.8 %copy-start = (f32[3,9,32,32]{3,2,1,0:T(8,128)S(1)}, f32[3,9,32,32]{3,2,1,0:T(8,128)}, u32[]{:S(2)}) copy-start(f32[3,9,32,32]{3,2,1,0:T(8,128)} %w_convs.1) | copy-start | bytes 331780
  40.8 11.8 %copy-start.5 = (f32[2,32,32]{2,1,0:T(8,128)S(1)}, f32[2,32,32]{2,1,0:T(8,128)}, u32[]{:S(2)}) copy-start(f32[2,32,32]{2,1,0:T(8,128)} %w_style.5) | copy-start | bytes 24580
  56.9 9.9 %all-to-all-start.4 = ((f32[32,3,1,128]{3,2,1,0:T(1,128)}), f32[32,3,1,128]{3,2,1,0:T(1,128)S(1)}, u32[]{:S(2)}, u32[]{:S(2)}) async-start(f32[32,3,1,128]{3,2,1,0:T(1,128)} %get-tuple-element.95.pay), calls=%async_computation.4 | async-start | bytes 98304 | tf_op jit(solution)/shard_map/all_to_all | solution.py:1066
  59.5 7.3 %copy-start.1 = (bf16[1152,256]{1,0:T(8,128)(2,1)S(1)}, bf16[1152,256]{1,0:T(8,128)(2,1)}, u32[]{:S(2)}) copy-start(bf16[1152,256]{1,0:T(8,128)(2,1)} %get-tuple-element.103.back.back_two) | copy-start | bytes 1769476
  59.5 7.3 %copy-start.7 = (bf16[256,128]{1,0:T(8,128)(2,1)S(1)}, bf16[256,128]{1,0:T(8,128)(2,1)}, u32[]{:S(2)}) copy-start(bf16[256,128]{1,0:T(8,128)(2,1)} %get-tuple-element.97.head_mat) | copy-start | bytes 196612
  59.5 7.3 %copy-start.11 = (f32[33,3]{0,1:T(4,128)S(1)}, f32[33,3]{0,1:T(4,128)}, u32[]{:S(2)}) copy-start(f32[33,3]{0,1:T(4,128)} %param.26) | copy-start | bytes 1192
  79.9 14.9 %copy-start.2 = (bf16[1152,256]{1,0:T(8,128)(2,1)S(1)}, bf16[1152,256]{1,0:T(8,128)(2,1)}, u32[]{:S(2)}) copy-start(bf16[1152,256]{1,0:T(8,128)(2,1)} %get-tuple-element.115.back) | copy-start | bytes 1769476
  84.6 16.3 %copy-start.9 = (f32[2,32,32]{2,1,0:T(8,128)S(1)}, f32[2,32,32]{2,1,0:T(8,128)}, u32[]{:S(2)}) copy-start(f32[2,32,32]{2,1,0:T(8,128)} %m_style.1) | copy-start | bytes 24580
  84.6 16.3 %copy-start.10 = (f32[2,32,32]{2,1,0:T(8,128)S(1)}, f32[2,32,32]{2,1,0:T(8,128)}, u32[]{:S(2)}) copy-start(f32[2,32,32]{2,1,0:T(8,128)} %s_style.1) | copy-start | bytes 24580
  84.6 16.3 %copy-start.16 = (f32[33,3]{0,1:T(4,128)S(1)}, f32[33,3]{0,1:T(4,128)}, u32[]{:S(2)}) copy-start(f32[33,3]{0,1:T(4,128)} %param.31) | copy-start | bytes 1192
  84.6 16.3 %copy-start.17 = (f32[33,3]{0,1:T(4,128)S(1)}, f32[33,3]{0,1:T(4,128)}, u32[]{:S(2)}) copy-start(f32[33,3]{0,1:T(4,128)} %param.36) | copy-start | bytes 1192
  84.6 25.6 %copy-start.3 = (f32[3,9,32,32]{3,2,1,0:T(8,128)S(1)}, f32[3,9,32,32]{3,2,1,0:T(8,128)}, u32[]{:S(2)}) copy-start(f32[3,9,32,32]{3,2,1,0:T(8,128)} %m_convs.1) | copy-start | bytes 331780
  84.6 25.6 %copy-start.4 = (f32[3,9,32,32]{3,2,1,0:T(8,128)S(1)}, f32[3,9,32,32]{3,2,1,0:T(8,128)}, u32[]{:S(2)}) copy-start(f32[3,9,32,32]{3,2,1,0:T(8,128)} %s_convs.1) | copy-start | bytes 331780
  84.6 25.6 %copy-start.8 = (f32[10,2,32]{2,1,0:T(2,128)S(1)}, f32[10,2,32]{2,1,0:T(2,128)}, u32[]{:S(2)}) copy-start(f32[10,2,32]{2,1,0:T(2,128)} %w_first.1) | copy-start | bytes 7684
  84.7 25.6 %copy-start.12 = (f32[10,2,32]{2,1,0:T(2,128)S(1)}, f32[10,2,32]{2,1,0:T(2,128)}, u32[]{:S(2)}) copy-start(f32[10,2,32]{2,1,0:T(2,128)} %m_first.1) | copy-start | bytes 7684
  84.7 25.6 %copy-start.13 = (f32[10,2,32]{2,1,0:T(2,128)S(1)}, f32[10,2,32]{2,1,0:T(2,128)}, u32[]{:S(2)}) copy-start(f32[10,2,32]{2,1,0:T(2,128)} %s_first.1) | copy-start | bytes 7684
  84.7 25.6 %copy-start.14 = (f32[2,4,32]{2,1,0:T(4,128)S(1)}, f32[2,4,32]{2,1,0:T(4,128)}, u32[]{:S(2)}) copy-start(f32[2,4,32]{2,1,0:T(4,128)} %m_norms.1) | copy-start | bytes 3076
  84.7 25.6 %copy-start.15 = (f32[2,4,32]{2,1,0:T(4,128)S(1)}, f32[2,4,32]{2,1,0:T(4,128)}, u32[]{:S(2)}) copy-start(f32[2,4,32]{2,1,0:T(4,128)} %s_norms.1) | copy-start | bytes 3076
  98.3 12.0 %all-to-all-start.7 = ((f32[32,13,1,128]{3,2,1,0:T(1,128)}), f32[32,13,1,128]{3,2,1,0:T(1,128)S(1)}, u32[]{:S(2)}, u32[]{:S(2)}) async-start(f32[32,13,1,128]{3,2,1,0:T(1,128)} %get-tuple-element.116.pay), calls=%async_computation.7 | async-start | bytes 425984 | tf_op jit(solution)/shard_map/all_to_all | solution.py:1066

commit v9 on v8

--- a/solution.py
+++ b/solution.py
@@ -520,7 +520,8 @@
     mean, inverse = merge_stats(row_of_each(got, 0) + one, row_of_each(got, 1), local_count, pixel_count)
     notes(vec, inverse)
     gain, bias = affine(table, 2)
-    rows = raw.shape[0]
+    rows, kept = raw.shape[0], resid.shape[0]
+    off, skipped, mine = place[0], place[3], place[4]
     me = place[2]
     shift = mine_of(one, me) - mean
     two = mine_of(two, me)
@@ -543,13 +544,12 @@
 
     @pl.when(place[0] >= 0)
     def _():
-        for k, y in enumerate(blocks_of(conv(hidden, taps, 0, rows), rows)):
-            resid[:, k] = y + two + merged[1 : rows + 1, k].astype(F32)
+        for k, y in enumerate(blocks_of(conv(hidden, taps, skipped, kept), kept)):
+            resid[:, k] = y + two + merged[pl.ds(skipped + 1, kept), k].astype(F32)
 
     wait(fetched + stored)
-    off = place[0]
-    means, squares = local_stats(resid, off, height, local_count)
-    centre = fold(means) / GRP
+    hidden[kept + 1 : kept + 2] = jnp.zeros((1,) + hidden.shape[1:], BF16)
+    centre = fold(col_sum(resid[mine, 0] + resid[mine, 1])) / (SEG * raw.shape[2])
     at = pl.ds(off, height)
     probe = [slopes[at, k] for k in range(2)]
     probe += [slopes[at, k] * xhat[at, k] for k in range(2)]
@@ -559,9 +559,9 @@
         at = pl.ds(4 * i, 4)
         put_low(hidden, 4 * i, resid[at, 0] - centre, resid[at, 1] - centre, True)
 
-    loop(rows // 4, centred)
-    send(pay, means, squares)
-    links = norm_links(hidden, probe, off, height, w_conv, centre)
+    loop(kept // 4, centred)
+    links = norm_links(hidden, probe, mine, height, w_conv, centre)
+    send(pay, *local_stats(resid, mine, height, local_count))
     send_parts(pay, 2, 1)[:, 0, :] = links
 
 
@@ -618,7 +618,7 @@
         (spots(fields, "xhat_zero").at[own], below_x),
         (spots(fields, "xhat_one").at[own], xhat),
         (spots(fields, "shared").at[own], shared),
-        (spots(lows, "hidden_one"), field),
+        (spots(lows, "hidden_one").at[pl.ds(off, height + 2)], field),
     )
     wait(fetched[:1])
     at = pl.ds(0, height)
@@ -633,7 +633,7 @@
     wait(fetched[1:])
     centres = [fold(v) / local_count for v in row_sums(0, height, lambda at, k: (xhat[at, k], shared[at, k]))]
     probe = [flat(v[at, k] - c).astype(BF16) for v, c in zip((xhat, shared), centres) for k in range(2)]
-    wide = jnp.concatenate(views(field, off, height), axis=1)
+    wide = jnp.concatenate(views(field, 0, height), axis=1)
     found = lax.dot_general(
         jnp.concatenate(probe, axis=1), wide, (((0,), (0,)), ((), ())), preferred_element_type=F32
     )
@@ -668,7 +668,7 @@
     notes(vec, inverse, mean)
     gain, bias = affine(table, 3)
     rows, segments = resid.shape[0], resid.shape[2]
-    off = place[0]
+    all_off, skipped, off = place[0], place[3], place[4]
 
     def norm_rows(i):
         at = pl.ds(4 * i, 4)
@@ -688,7 +688,7 @@
         mine = (lane_of((1, LANES)) >> 3) == FLOW // 8 + k
         bias_row = jnp.where(mine, low(w_head[k : k + 1, CH : CH + 1]), bias_row)
     out = jnp.dot(wide, head, preferred_element_type=F32) + bias_row
-    given = flat(sides[1 : rows + 1]).astype(F32)
+    given = flat(sides[pl.ds(skipped + 1, rows)]).astype(F32)
     lane = lane_of(given.shape)
     is_flow = lane < LABEL
     near = [pltpu.roll(given, LANES - MASK + first, axis=1) for first in (FLOW, FLOW + 8, LABEL)]
@@ -725,7 +725,7 @@
     gain, bias = affine(table, 2)
 
     def links(at, k):
-        x = below_x[pl.ds(off + at.start, at.size), k]
+        x = below_x[pl.ds(all_off + at.start, at.size), k]
         g = slopes[at, k] * slope_at(x, gain, bias)
         return g, g * x
 
@@ -806,19 +806,21 @@
     return jnp.sum(jnp.where(lane_of(v.shape) == k, v, 0.0), axis=1, keepdims=True)
 
 
-def decoder_back_kernel(place, got, grad, xhat, mid_x, vec, vec_two, sums, table, back_two, weights, fields, lows, below, below_x, shared, pay, more, kept_grad, mid, low_two, low_one, field_two, field_one, field_zero, back_one, sems, *, spots, local_count, pixel_count, height):
+def decoder_back_kernel(place, got, grad, xhat, mid_x, vec, vec_two, sums, table, back_two, weights, fields, lows, below, below_x, shared, pay, more, kept_grad, mid, low_two, low_one, field_two, field_one, field_zero, back_one, sems, *, spots, local_count, pixel_count):
+    all_off, skipped, off = place[0], place[3], place[4]
+    height = field_two.shape[0] - 2
+    far_rows, near_rows = pl.ds(skipped, grad.shape[0]), pl.ds(all_off, height + 2)
     fetched = copies(
         sems,
         (back_at(weights), back_one),
-        (spots(fields, "xhat_one"), below_x),
-        (spots(fields, "shared"), shared),
-        (spots(lows, "hidden_three"), field_two),
-        (spots(lows, "merged"), field_one),
-        (spots(lows, "hidden_one"), field_zero),
+        (spots(fields, "xhat_one").at[far_rows], below_x),
+        (spots(fields, "shared").at[far_rows], shared),
+        (spots(lows, "hidden_three").at[near_rows], field_two),
+        (spots(lows, "merged").at[near_rows], field_one),
+        (spots(lows, "hidden_one").at[near_rows], field_zero),
     )
     devices = got.shape[0]
     rows = grad.shape[0]
-    off = place[0]
     total = total_of(got, 0)
     shift, scale = spread(total, 0) / pixel_count, spread(total, 1) / pixel_count
     inverse, mean = vec[0:1], vec[1:2]
@@ -854,7 +856,7 @@
     shift, scale = shift_two / pixel_count, scale_two / pixel_count
 
     def value_two(at, k):
-        x = mid_x[at, k]
+        x = mid_x[pl.ds(skipped + at.start, at.size), k]
         return norm_back(mid[at, k] * slope_at(x, gain, bias), x, factor, shift, scale)
 
     back_rows(low_one, rows, value_two)
@@ -874,17 +876,17 @@
     entry = spread(entry, 0)
     pay[:, 1, 0, :] = jnp.broadcast_to(entry, (devices, LANES))
     at = pl.ds(off + 1, height)
-    last_two = tap_sums(field_two, own_lanes(low_two, at), off, height, send_parts(pay, 2, 2))
-    last_one = tap_sums(field_one, own_lanes(low_one, at), off, height, send_parts(pay, 4, 2))
+    last_two = tap_sums(field_two, own_lanes(low_two, at), 0, height, send_parts(pay, 2, 2))
+    last_one = tap_sums(field_one, own_lanes(low_one, at), 0, height, send_parts(pay, 4, 2))
     centre = shift_sum / local_count
     at = pl.ds(off, height)
     grad = jnp.concatenate([flat(below[at, k] - centre).astype(BF16) for k in range(2)], axis=1)
-    last_zero = tap_sums(field_zero, grad, off, height, send_parts(pay, 6, 2), (centre, sums))
+    last_zero = tap_sums(field_zero, grad, 0, height, send_parts(pay, 6, 2), (centre, sums))
     pay[0:CH, 1, 0, :] = groups(last_two, last_one, last_zero, jnp.broadcast_to(entry, (CH, LANES)))
 
 
 def summed_kernel(place, got, got_style, got_head, grad, xhat, shared, vec, more_two, table, w_style, sides, back, fields, pay, more, below, below_x, grad_low, sems, *, spots, pixel_count, pool_cells, parts):
-    off = place[0]
+    off, mine = place[0], place[4]
     height = below.shape[0]
     fetched = copies(sems, (spots(fields, "xhat_zero").at[pl.ds(off, height)], below_x))
     devices = got.shape[0]
@@ -898,16 +900,16 @@
     total = col_sum(first)
     shift = spread(total, 0) + col_sum(each * by_image(spread(row_of_each(got_style, 2), 1), parts))
     scale = spread(total, 1) + col_sum(each * by_image(spread(row_of_each(got_style, 2), 2), parts))
-    mine = col_sum(jnp.where(row_of(each.shape) // parts == place[2] // parts, each, 0.0))
+    style_grad = col_sum(jnp.where(row_of(each.shape) // parts == place[2] // parts, each, 0.0))
     factor = affine(table, 1)[0] * vec[0:1]
     shift_mean, scale_mean = shift / pixel_count, scale / pixel_count
     def value(at, k):
-        return norm_back(grad[at, k] + shared[at, k] * mine, xhat[at, k], factor, shift_mean, scale_mean)
+        return norm_back(grad[at, k] + shared[at, k] * style_grad, xhat[at, k], factor, shift_mean, scale_mean)
 
     back_rows(grad_low, rows, value)
     gain, bias = affine(table, 0)
     wait(fetched)
-    for k, y in enumerate(blocks_of(conv(grad_low, back, off, height), height)):
+    for k, y in enumerate(blocks_of(conv(grad_low, back, mine, height), height)):
         below[:, k] = y * slope_at(below_x[:, k], gain, bias)
     me = place[2]
     weights = at_lane(by_image(each, parts), me)
@@ -921,7 +923,7 @@
         val = direct[q] + col_sum(weights * shares[q])
         val = val - at_lane(shift_mean, me) * hidden[q] - at_lane(scale_mean, me) * more_two[2 + q : 3 + q]
         shard.append(at_lane(factor, me) * val)
-    at = pl.ds(off + 1, height)
+    at = pl.ds(mine + 1, height)
     side = pixel_taps(sides, off + 1, height, own_lanes(grad_low, at), (0,))[0]
     low_below = own_lanes(below, pl.ds(0, height))
     taps = []
@@ -1092,11 +1094,18 @@
     me = lax.axis_index("row") * col_count + lax.axis_index("col")
     first_row = (me % parts) * height
     start = jnp.clip(first_row - RIM, 0, image_rows - rows)
-    place = jnp.stack([first_row - start, start // block_rows, me]).astype(jnp.int32)
+    off = first_row - start
+    back_rim = RIM // 2
+    rows_back = min(rows, height + back_rim * min(2, parts - 1))
+    skipped = jnp.clip(off - back_rim, 0, rows - rows_back)
+    place = jnp.stack([off, start // block_rows, me, skipped, off - skipped]).astype(jnp.int32)
 
     field = ((rows, 2, segments, LANES), F32)
     own_field = ((height,) + field[0][1:], F32)
+    back_field = ((rows_back,) + field[0][1:], F32)
     low_field = ((rows + 2, 3, segments, LANES), BF16)
+    own_low = ((height + 2,) + low_field[0][1:], BF16)
+    back_low = ((rows_back + 2,) + low_field[0][1:], BF16)
     vec = ((8, LANES), F32)
 
     def payload(count):
@@ -1170,7 +1179,7 @@
 
     resid, pay, inv_two, style, xhat_two, lows = call(
         part(style_kernel, spots=spots, **styled, **counts),
-        [field, payload(3), vec, ((devices, LANES), F32), field, store_of(low_field)],
+        [back_field, payload(3), vec, ((devices, LANES), F32), field, store_of(low_field)],
         place, got_style, raw, merged, batch_norm_table, w_style, far(w_convs), taps, far(lows),
         scalars=1, scratch=[low_field, field, (w_convs.shape[1:], F32)], sems=2,
         aliases={8: 5}, name="decoder",
@@ -1180,23 +1189,23 @@
         part(ahead_kernel, spots=spots, local_count=local_count),
         [((CH, 5, 1, LANES), F32), vec],
         place, far(pay), sides, far(fields), far(lows),
-        scalars=1, scratch=[own_field, own_field, own_field, low_field], sems=4, name="ahead",
+        scalars=1, scratch=[own_field, own_field, own_field, own_low], sems=4, name="ahead",
     )
 
     grad_three, xhat_three, pay, inv_three = call(
         part(head_kernel, **counts),
-        [field, field, payload(8), vec],
+        [back_field, back_field, payload(8), vec],
         place, got_three, got_style, resid, sides, head_mat, head_rows, xhat_two, ahead, hidden_sums, batch_norm_table, back_two,
-        scalars=1, scratch=[((rows, 2, segments, LANES), BF16), field, low_field], name="head",
+        scalars=1, scratch=[((rows_back, 2, segments, LANES), BF16), back_field, back_low], name="head",
     )
     got_head = exchange(pay)
 
     grad_one, xhat_one, shared, pay, more_two = call(
-        part(decoder_back_kernel, spots=spots, **counts),
-        [field, field, field, payload(8), vec],
+        part(decoder_back_kernel, spots=spots, local_count=local_count, pixel_count=pixel_count),
+        [back_field, back_field, back_field, payload(8), vec],
         place, got_head, grad_three, xhat_three, xhat_two, inv_three, inv_two, hidden_sums, batch_norm_table, back_two, far(weights),
         far(fields), far(lows),
-        scalars=1, scratch=[field, field, low_field, low_field, low_field, low_field, low_field, nine], sems=6,
+        scalars=1, scratch=[back_field, back_field, back_low, back_low, own_low, own_low, own_low, nine], sems=6,
         name="decoder_back",
     )
     got_one_back = exchange(pay)
@@ -1206,7 +1215,7 @@
         [payload(13), vec],
         place, got_one_back, got_style, got_head, grad_one, xhat_one, shared, inv_one, more_two, batch_norm_table, w_style,
         sides, back_zero, far(fields),
-        scalars=1, scratch=[own_field, own_field, low_field], sems=1, name="summed_back",
+        scalars=1, scratch=[own_field, own_field, back_low], sems=1, name="summed_back",
     )
     got_last = exchange(pay)
 

time: 113 us -> 112 us (level)
  no operation moved by 1% of the time
where the time goes in v9:
time: 112 us
  blocking collectives  47.8 us (43%)
  Pallas kernels  34.8 us (31%)
  waiting for transfers between devices  15.4 us (14%)
  starting transfers between devices  12.5 us (11%)
    all_to_all x5, blocking collectives, exchange(): return lax.all_to_all(pay, ('row', 'col'), 0, 0)  47.8 us
    pallas_call x12, Pallas kernels, call(): pl.pallas_call(kernel, out_shape=[jax.ShapeDtypeStruct(*plain(x)) for x i...  34.8 us
    all_to_all x3, waiting for transfers between devices, exchange(): return lax.all_to_all(pay, ('row', 'col'), 0, 0)  15.4 us
    all_to_all x3, starting transfers between devices, exchange(): return lax.all_to_all(pay, ('row', 'col'), 0, 0)  12.5 us
  transfers between devices with their start and end apart: 3, of which 3 were waited for; matrix products, arithmetic and copies ran while one was open for 0% of the time, Pallas kernels for 8%

profile of v9, /device:TPU:0, one launch (start us, length us, event | category | flops | bytes accessed | tf_op | source)
XLA Modules:
  0.0 111.7 jit_solution(3731493662488540476)
XLA Ops:
  0.7 2.0 %pack.1 = bf16[32,16,128]{2,1,0:T(8,128)(2,1)} custom-call(bf16[16,8,2,32]{3,2,1,0:T(2,128)(2,1)} %bitcast.22, s32[16,8,2,32]{3,2,1,0:T(2,128)} %bitcast.21, s32[16,8,32]{2,1,0:T(8,128)} %labels_in.1, s32[16,8,32]{2,1,0:T(8,128)} %valid_in.1), custom_call_target="tpu_custom_call" | custom-call | tf_op jit(solution)/shard_map/pack/pallas_call | solution.py:1055
  2.7 7.3 %all-to-all-start = ((bf16[32,16,128]{2,1,0:T(8,128)(2,1)}), bf16[32,16,128]{2,1,0:T(8,128)(2,1)S(1)}, u32[]{:S(2)}, u32[]{:S(2)}) async-start(bf16[32,16,128]{2,1,0:T(8,128)(2,1)} %pack.1), calls=%async_computation | async-start | bytes 262144 | tf_op jit(solution)/shard_map/all_to_all | solution.py:1068
  10.1 4.7 %prepare.1 = (bf16[65536,256]{1,0:T(8,128)(2,1)}, bf16[1152,256]{1,0:T(8,128)(2,1)}, bf16[1152,256]{1,0:T(8,128)(2,1)}, bf16[256,128]{1,0:T(8,128)(2,1)}) custom-call(f32[10,2,32]{2,1,0:T(2,128)} %w_first.1, f32[3,9,32,32]{3,2,1,0:T(8,128)} %w_convs.1, f32[3,33]{1,0:T(4,128)} %bitcast.16), custom_call_target="tpu_custom_call" | custom-call | tf_op jit(solution)/shard_map/prepare/pallas_call | solution.py:1055
  14.8 0.1 stack.23.place
  14.9 3.4 %all-to-all-done.got = bf16[32,16,128]{2,1,0:T(8,128)(2,1)S(1)} async-done(((bf16[32,16,128]{2,1,0:T(8,128)(2,1)}), bf16[32,16,128]{2,1,0:T(8,128)(2,1)S(1)}, u32[]{:S(2)}, u32[]{:S(2)}) %all-to-all-start) | async-done | bytes 131104 | tf_op jit(solution)/shard_map/all_to_all | solution.py:1068
  18.3 2.0 %image_conv.1 = (bf16[42,16,128]{2,1,0:T(8,128)(2,1)S(1)}, f32[40,2,16,128]{3,2,1,0:T(8,128)S(1)}, f32[32,2,1,128]{3,2,1,0:T(1,128)S(1)}, f32[8,128]{1,0:T(8,128)S(1)}, bf16[1280,256]{1,0:T(8,128)(2,1)S(1)}) custom-call(s32[5]{0:T(128)S(1)} %stack.23.place, bf16[32,16,128]{2,1,0:T(8,128)(2,1)S(1)} %all-to-all-done.got, ...), custom_call_target="tpu_custom_call" | custom-call | tf_op jit(solution)/shard_map/image_conv/pallas_call | solution.py:1055
  20.3 9.5 %all_to_all.40.got = f32[32,2,1,128]{3,2,1,0:T(1,128)S(1)} all-to-all(f32[32,2,1,128]{3,2,1,0:T(1,128)S(1)} %get-tuple-element.81), channel_id=1, replica_groups=mesh['row'=8,'col'=4] {'row','col'}, dimensions={0} | all-to-all | bytes 65536 | tf_op jit(solution)/shard_map/all_to_all | solution.py:1068
  29.8 2.0 %first_block.1 = (f32[40,2,16,128]{3,2,1,0:T(8,128)S(1)}, f32[32,2,1,128]{3,2,1,0:T(1,128)S(1)}, f32[8,128]{1,0:T(8,128)S(1)}, f32[2048,2,16,128]{3,2,1,0:T(8,128)}, bf16[2731,3,16,128]{3,2,1,0:T(8,128)(2,1)}) custom-call(s32[5]{0:T(128)S(1)} %stack.23.place, f32[32,2,1,128]{3,2,1,0:T(1,128)S(1)} %all_to_all.40.got, ...), custom_call_target="tpu_custom_call" | custom-call | tf_op jit(solution)/shard_map/first_block/pallas_call | solution.py:1055
  31.8 8.9 %all_to_all.41.got = f32[32,2,1,128]{3,2,1,0:T(1,128)S(1)} all-to-all(f32[32,2,1,128]{3,2,1,0:T(1,128)S(1)} %get-tuple-element.85), channel_id=1, replica_groups=mesh['row'=8,'col'=4] {'row','col'}, dimensions={0} | all-to-all | bytes 65536 | tf_op jit(solution)/shard_map/all_to_all | solution.py:1068
  40.8 2.8 %pool_and_merge.1 = (f32[40,2,16,128]{3,2,1,0:T(8,128)S(1)}, f32[32,3,1,128]{3,2,1,0:T(1,128)S(1)}, f32[8,128]{1,0:T(8,128)S(1)}, bf16[42,3,16,128]{3,2,1,0:T(8,...) custom-call(s32[5]{0:T(128)S(1)} %stack.23.place, ...), custom_call_target="tpu_custom_call", output_to_operand_aliasing={{5}: (6, {}), {6}: (7, {})} | custom-call | tf_op jit(solution)/shard_map/pool_and_merge/pallas_call | solution.py:1055
  43.6 9.0 %all_to_all.42.got.got_style = f32[32,3,1,128]{3,2,1,0:T(1,128)S(1)} all-to-all(f32[32,3,1,128]{3,2,1,0:T(1,128)S(1)} %get-tuple-element.90), channel_id=1, replica_groups=mesh['row'=8,'col'=4] {'row','col'}, dimensions={0} | all-to-all | bytes 98304 | tf_op jit(solution)/shard_map/all_to_all | solution.py:1068
  52.6 4.3 %decoder.1 = (f32[36,2,16,128]{3,2,1,0:T(8,128)S(1)}, f32[32,3,1,128]{3,2,1,0:T(1,128)}, f32[8,128]{1,0:T(8,128)S(1)}, f32[32,128]{1,0:T(8,128)S(1)}, f32[40,2,1...) custom-call(s32[5]{0:T(128)S(1)} %stack.23.place, ...), custom_call_target="tpu_custom_call", output_to_operand_aliasing={{5}: (8, {})} | custom-call | tf_op jit(solution)/shard_map/decoder/pallas_call | solution.py:1055
  56.9 2.6 %all-to-all-start.4 = ((f32[32,3,1,128]{3,2,1,0:T(1,128)}), f32[32,3,1,128]{3,2,1,0:T(1,128)S(1)}, u32[]{:S(2)}, u32[]{:S(2)}) async-start(f32[32,3,1,128]{3,2,1,0:T(1,128)} %get-tuple-element.95.pay), calls=%async_computation.4 | async-start | bytes 98304 | tf_op jit(solution)/shard_map/all_to_all | solution.py:1068
  59.5 3.6 %ahead.1 = (f32[32,5,1,128]{3,2,1,0:T(1,128)S(1)}, f32[8,128]{1,0:T(8,128)S(1)}) custom-call(s32[5]{0:T(128)S(1)} %stack.23.place, f32[32,3,1,128]{3,2,1,0:T(1,128)} %get-tuple-element.95.pay, bf16[42,16,128]{2,1,0:T(8,128)(2,1)S(1)} %get-tuple-element.83.sides, f32[2048,2,16,128]{3,2,1,0:T(8,128)} %get-tuple-element.99.fields, ...), custom_call_target="tpu_custom_call" | custom-call | tf_op jit(solution)/shard_map/ahead/pallas_call | solution.py:1055
  63.1 3.7 %all-to-all-done.4.got = f32[32,3,1,128]{3,2,1,0:T(1,128)S(1)} async-done(((f32[32,3,1,128]{3,2,1,0:T(1,128)}), f32[32,3,1,128]{3,2,1,0:T(1,128)S(1)}, u32[]{:S(2)}, u32[]{:S(2)}) %all-to-all-start.4) | async-done | bytes 49184 | tf_op jit(solution)/shard_map/all_to_all | solution.py:1068
  66.8 2.7 %head.1 = (f32[36,2,16,128]{3,2,1,0:T(8,128)S(1)}, f32[36,2,16,128]{3,2,1,0:T(8,128)S(1)}, f32[32,8,1,128]{3,2,1,0:T(1,128)S(1)}, f32[8,128]{1,0:T(8,128)S(1)}) custom-call(s32[5]{0:T(128)S(1)} %stack.23.place, f32[32,3,1,128]{3,2,1,0:T(1,128)S(1)} %all-to-all-done.4.got, f32[32,3,1,128]{3,2,1,0:T(1,128)S(1)} %all_to_all.42.got.got_style, ...), custom_call_target="tpu_custom_call" | custom-call | tf_op jit(solution)/shard_map/head/pallas_call | solution.py:1055
  69.6 10.2 %all_to_all.43.got.got_head = f32[32,8,1,128]{3,2,1,0:T(1,128)S(1)} all-to-all(f32[32,8,1,128]{3,2,1,0:T(1,128)S(1)} %get-tuple-element.104), channel_id=1, replica_groups=mesh['row'=8,'col'=4] {'row','col'}, dimensions={0} | all-to-all | bytes 262144 | tf_op jit(solution)/shard_map/all_to_all | solution.py:1068
  79.7 4.5 %decoder_back.1 = (f32[36,2,16,128]{3,2,1,0:T(8,128)S(1)}, f32[36,2,16,128]{3,2,1,0:T(8,128)S(1)}, f32[36,2,16,128]{3,2,1,0:T(8,128)S(1)}, f32[32,8,1,128]{3,2,1,0:T(1,128)S(1)}, f32[8,128]{1,0:T(8,128)S(1)}) custom-call(s32[5]{0:T(128)S(1)} %stack.23.place, f32[32,8,1,128]{3,2,1,0:T(1,128)S(1)} %all_to_all.43.got.got_head, ...), custom_call_target="tpu_custom_call" | custom-call | tf_op jit(solution)/shard_map/decoder_back/pallas_call | solution.py:1055
  84.4 10.1 %all_to_all.44.got.got_one_back = f32[32,8,1,128]{3,2,1,0:T(1,128)S(1)} all-to-all(f32[32,8,1,128]{3,2,1,0:T(1,128)S(1)} %get-tuple-element.109), channel_id=1, replica_groups=mesh['row'=8,'col'=4] {'row','col'}, dimensions={0} | all-to-all | bytes 262144 | tf_op jit(solution)/shard_map/all_to_all | solution.py:1068
  94.5 3.5 %summed_back.1 = (f32[32,13,1,128]{3,2,1,0:T(1,128)}, f32[8,128]{1,0:T(8,128)S(1)}) custom-call(s32[5]{0:T(128)S(1)} %stack.23.place, f32[32,8,1,128]{3,2,1,0:T(1,128)S(1)} %all_to_all.44.got.got_one_back, f32[32,3,1,128]{3,2,1,0:T(1,128)S(1)} %all_to_all.42.got.got_style, f32[32,8,1,128]{3,2,1,0:T(1,128)S(1)} %all_to_all.43.got.got_head, ...), custom_call_target="tpu_custom_call" | custom-call | tf_op jit(solution)/shard_map/summed_back/pallas_call | solution.py:1055
  97.9 2.6 %all-to-all-start.7 = ((f32[32,13,1,128]{3,2,1,0:T(1,128)}), f32[32,13,1,128]{3,2,1,0:T(1,128)S(1)}, u32[]{:S(2)}, u32[]{:S(2)}) async-start(f32[32,13,1,128]{3,2,1,0:T(1,128)} %get-tuple-element.116.pay), calls=%async_computation.7 | async-start | bytes 425984 | tf_op jit(solution)/shard_map/all_to_all | solution.py:1068
  100.6 1.0 update_early.1
  101.6 8.3 %all-to-all-done.7.got = f32[32,13,1,128]{3,2,1,0:T(1,128)S(1)} async-done(((f32[32,13,1,128]{3,2,1,0:T(1,128)}), f32[32,13,1,128]{3,2,1,0:T(1,128)S(1)}, u32[]{:S(2)}, u32[]{:S(2)}) %all-to-all-start.7) | async-done | bytes 213024 | tf_op jit(solution)/shard_map/all_to_all | solution.py:1068
  110.0 1.7 %update_late.1 = (f32[10,2,32]{2,1,0:T(2,128)}, f32[10,2,32]{2,1,0:T(2,128)}, f32[10,2,32]{2,1,0:T(2,128)}, bf16[10,2,32]{2,1,0:T(2,128)(2,1)}, f32[3,9,32,32]{3...) custom-call(f32[32,13,1,128]{3,2,1,0:T(1,128)S(1)} %all-to-all-done., ...), custom_call_target="tpu_custom_call" | custom-call | tf_op jit(solution)/shard_map/update_late/pallas_call | solution.py:1055
  (36 shorter events, 0.1 us)
Async XLA Ops:
  0.7 29.2 %copy-start.6 = (f32[2,4,32]{2,1,0:T(4,128)S(1)}, f32[2,4,32]{2,1,0:T(4,128)}, u32[]{:S(2)}) copy-start(f32[2,4,32]{2,1,0:T(4,128)} %table.13) | copy-start | bytes 3076
  2.7 15.5 %all-to-all-start = ((bf16[32,16,128]{2,1,0:T(8,128)(2,1)}), bf16[32,16,128]{2,1,0:T(8,128)(2,1)S(1)}, u32[]{:S(2)}, u32[]{:S(2)}) async-start(bf16[32,16,128]{2,1,0:T(8,128)(2,1)} %pack.1), calls=%async_computation | async-start | bytes 262144 | tf_op jit(solution)/shard_map/all_to_all | solution.py:1068
  40.8 11.8 %copy-start = (f32[3,9,32,32]{3,2,1,0:T(8,128)S(1)}, f32[3,9,32,32]{3,2,1,0:T(8,128)}, u32[]{:S(2)}) copy-start(f32[3,9,32,32]{3,2,1,0:T(8,128)} %w_convs.1) | copy-start | bytes 331780
  40.8 11.8 %copy-start.5 = (f32[2,32,32]{2,1,0:T(8,128)S(1)}, f32[2,32,32]{2,1,0:T(8,128)}, u32[]{:S(2)}) copy-start(f32[2,32,32]{2,1,0:T(8,128)} %w_style.5) | copy-start | bytes 24580
  56.9 9.9 %all-to-all-start.4 = ((f32[32,3,1,128]{3,2,1,0:T(1,128)}), f32[32,3,1,128]{3,2,1,0:T(1,128)S(1)}, u32[]{:S(2)}, u32[]{:S(2)}) async-start(f32[32,3,1,128]{3,2,1,0:T(1,128)} %get-tuple-element.95.pay), calls=%async_computation.4 | async-start | bytes 98304 | tf_op jit(solution)/shard_map/all_to_all | solution.py:1068
  59.5 7.3 %copy-start.1 = (bf16[1152,256]{1,0:T(8,128)(2,1)S(1)}, bf16[1152,256]{1,0:T(8,128)(2,1)}, u32[]{:S(2)}) copy-start(bf16[1152,256]{1,0:T(8,128)(2,1)} %get-tuple-element.103.back.back_two) | copy-start | bytes 1769476
  59.5 7.3 %copy-start.7 = (bf16[256,128]{1,0:T(8,128)(2,1)S(1)}, bf16[256,128]{1,0:T(8,128)(2,1)}, u32[]{:S(2)}) copy-start(bf16[256,128]{1,0:T(8,128)(2,1)} %get-tuple-element.97.head_mat) | copy-start | bytes 196612
  59.5 7.3 %copy-start.11 = (f32[33,3]{0,1:T(4,128)S(1)}, f32[33,3]{0,1:T(4,128)}, u32[]{:S(2)}) copy-start(f32[33,3]{0,1:T(4,128)} %param.26) | copy-start | bytes 1192
  79.7 14.7 %copy-start.2 = (bf16[1152,256]{1,0:T(8,128)(2,1)S(1)}, bf16[1152,256]{1,0:T(8,128)(2,1)}, u32[]{:S(2)}) copy-start(bf16[1152,256]{1,0:T(8,128)(2,1)} %get-tuple-element.115.back) | copy-start | bytes 1769476
  84.2 16.3 %copy-start.9 = (f32[2,32,32]{2,1,0:T(8,128)S(1)}, f32[2,32,32]{2,1,0:T(8,128)}, u32[]{:S(2)}) copy-start(f32[2,32,32]{2,1,0:T(8,128)} %m_style.1) | copy-start | bytes 24580
  84.3 16.3 %copy-start.10 = (f32[2,32,32]{2,1,0:T(8,128)S(1)}, f32[2,32,32]{2,1,0:T(8,128)}, u32[]{:S(2)}) copy-start(f32[2,32,32]{2,1,0:T(8,128)} %s_style.1) | copy-start | bytes 24580
  84.3 16.3 %copy-start.16 = (f32[33,3]{0,1:T(4,128)S(1)}, f32[33,3]{0,1:T(4,128)}, u32[]{:S(2)}) copy-start(f32[33,3]{0,1:T(4,128)} %param.31) | copy-start | bytes 1192
  84.3 16.3 %copy-start.17 = (f32[33,3]{0,1:T(4,128)S(1)}, f32[33,3]{0,1:T(4,128)}, u32[]{:S(2)}) copy-start(f32[33,3]{0,1:T(4,128)} %param.36) | copy-start | bytes 1192
  84.3 25.6 %copy-start.3 = (f32[3,9,32,32]{3,2,1,0:T(8,128)S(1)}, f32[3,9,32,32]{3,2,1,0:T(8,128)}, u32[]{:S(2)}) copy-start(f32[3,9,32,32]{3,2,1,0:T(8,128)} %m_convs.1) | copy-start | bytes 331780
  84.3 25.6 %copy-start.4 = (f32[3,9,32,32]{3,2,1,0:T(8,128)S(1)}, f32[3,9,32,32]{3,2,1,0:T(8,128)}, u32[]{:S(2)}) copy-start(f32[3,9,32,32]{3,2,1,0:T(8,128)} %s_convs.1) | copy-start | bytes 331780
  84.3 25.6 %copy-start.8 = (f32[10,2,32]{2,1,0:T(2,128)S(1)}, f32[10,2,32]{2,1,0:T(2,128)}, u32[]{:S(2)}) copy-start(f32[10,2,32]{2,1,0:T(2,128)} %w_first.1) | copy-start | bytes 7684
  84.3 25.6 %copy-start.12 = (f32[10,2,32]{2,1,0:T(2,128)S(1)}, f32[10,2,32]{2,1,0:T(2,128)}, u32[]{:S(2)}) copy-start(f32[10,2,32]{2,1,0:T(2,128)} %m_first.1) | copy-start | bytes 7684
  84.3 25.6 %copy-start.13 = (f32[10,2,32]{2,1,0:T(2,128)S(1)}, f32[10,2,32]{2,1,0:T(2,128)}, u32[]{:S(2)}) copy-start(f32[10,2,32]{2,1,0:T(2,128)} %s_first.1) | copy-start | bytes 7684
  84.4 25.6 %copy-start.14 = (f32[2,4,32]{2,1,0:T(4,128)S(1)}, f32[2,4,32]{2,1,0:T(4,128)}, u32[]{:S(2)}) copy-start(f32[2,4,32]{2,1,0:T(4,128)} %m_norms.1) | copy-start | bytes 3076
  84.4 25.6 %copy-start.15 = (f32[2,4,32]{2,1,0:T(4,128)S(1)}, f32[2,4,32]{2,1,0:T(4,128)}, u32[]{:S(2)}) copy-start(f32[2,4,32]{2,1,0:T(4,128)} %s_norms.1) | copy-start | bytes 3076
  97.9 12.0 %all-to-all-start.7 = ((f32[32,13,1,128]{3,2,1,0:T(1,128)}), f32[32,13,1,128]{3,2,1,0:T(1,128)S(1)}, u32[]{:S(2)}, u32[]{:S(2)}) async-start(f32[32,13,1,128]{3,2,1,0:T(1,128)} %get-tuple-element.116.pay), calls=%async_computation.7 | async-start | bytes 425984 | tf_op jit(solution)/shard_map/all_to_all | solution.py:1068

commit v10 on v9

--- a/solution.py
+++ b/solution.py
@@ -332,24 +332,30 @@
     return val.astype(BF16)
 
 
-def prepare(w_first_in, w_convs_in, w_head_in, store, back_zero, back_two, head_mat, w_first, w_convs, w_head, mats, sems):
+def prepare(w_first_in, w_convs_in, w_head_in, store, back_zero_out, back_two_out, head_out, w_first, w_convs, w_head, mats, back_zero, back_two, head_mat, sems):
     wait(copies(sems, (w_first_in, w_first), (w_convs_in, w_convs), (w_head_in, w_head)))
+    stored = []
+
+    def keep(source, target):
+        stored.extend(copies(sems.at[len(stored) :], (source, target)))
+
+    for i, back, out in ((2, back_two, back_two_out), (0, back_zero, back_zero_out)):
+        conv_matrix(w_convs.at[i], back, 0, True)
+        keep(back, out)
+    conv_matrix(w_convs.at[1], mats, BACK_AT, True)
+    keep(back_at(mats), back_at(store))
     shape = (LANES, 2 * LANES)
     inside, channel, here = image_lanes(shape)
     val = jnp.zeros(shape, F32)
     for c, tap in enumerate(first_taps(w_first, 9)):
         val = jnp.where((row_of(shape) < 16) & (channel == c) & (here == group_of(shape)), tap, val)
     mats[BACK:FORWARD, :] = val.astype(BF16)
+    for i in range(3):
+        conv_matrix(w_convs.at[i], mats, FORWARD * i, False)
+        keep(taps_at(mats, i), taps_at(store, i))
     for r in range(3):
         mats[IMAGE_AT + LANES * r : IMAGE_AT + LANES * (r + 1), :] = image_matrix(w_first, r)
-    stored = copies(sems, (image_at(mats), image_at(store)))
-    for i in range(3):
-        conv_matrix(w_convs.at[i], mats, FORWARD * i, False)
-        stored += copies(sems.at[1 + i :], (taps_at(mats, i), taps_at(store, i)))
-    conv_matrix(w_convs.at[1], mats, BACK_AT, True)
-    stored += copies(sems.at[4:], (back_at(mats), back_at(store)))
-    conv_matrix(w_convs.at[2], back_two, 0, True)
-    conv_matrix(w_convs.at[0], back_zero, 0, True)
+    keep(image_at(mats), image_at(store))
     lane = lane_of((CH, LANES))
     head = jnp.zeros((CH, LANES), F32)
     diagonal = row_of((CH, CH)) == lane_of((CH, CH))
@@ -358,6 +364,7 @@
         head = jnp.where((lane >> 3) == FLOW // 8 + k, column, head)
     for y in range(SEG):
         head_mat[CH * y : CH * (y + 1), :] = jnp.where((lane & 7) == y, head, 0.0).astype(BF16)
+    keep(head_mat, head_out)
     wait(stored)
 
 
@@ -806,7 +813,7 @@
     return jnp.sum(jnp.where(lane_of(v.shape) == k, v, 0.0), axis=1, keepdims=True)
 
 
-def decoder_back_kernel(place, got, grad, xhat, mid_x, vec, vec_two, sums, table, back_two, weights, fields, lows, below, below_x, shared, pay, more, kept_grad, mid, low_two, low_one, field_two, field_one, field_zero, back_one, sems, *, spots, local_count, pixel_count):
+def decoder_back_kernel(place, got, grad, xhat, mid_x, vec, vec_two, sums, table, back_two, weights, fields, lows, below, below_x, shared, pay, more, first_x, kept_grad, mid, low_two, low_one, field_two, field_one, field_zero, back_one, sems, *, spots, local_count, pixel_count):
     all_off, skipped, off = place[0], place[3], place[4]
     height = field_two.shape[0] - 2
     far_rows, near_rows = pl.ds(skipped, grad.shape[0]), pl.ds(all_off, height + 2)
@@ -819,6 +826,7 @@
         (spots(lows, "merged").at[near_rows], field_one),
         (spots(lows, "hidden_one").at[near_rows], field_zero),
     )
+    handed = copies(sems.at[6:], (spots(fields, "xhat_zero").at[pl.ds(all_off, height)], first_x))
     devices = got.shape[0]
     rows = grad.shape[0]
     total = total_of(got, 0)
@@ -883,12 +891,12 @@
     grad = jnp.concatenate([flat(below[at, k] - centre).astype(BF16) for k in range(2)], axis=1)
     last_zero = tap_sums(field_zero, grad, 0, height, send_parts(pay, 6, 2), (centre, sums))
     pay[0:CH, 1, 0, :] = groups(last_two, last_one, last_zero, jnp.broadcast_to(entry, (CH, LANES)))
-
-
-def summed_kernel(place, got, got_style, got_head, grad, xhat, shared, vec, more_two, table, w_style, sides, back, fields, pay, more, below, below_x, grad_low, sems, *, spots, pixel_count, pool_cells, parts):
+    wait(handed)
+
+
+def summed_kernel(place, got, got_style, got_head, grad, xhat, shared, vec, more_two, table, w_style, sides, back, below_x, pay, more, below, grad_low, *, pixel_count, pool_cells, parts):
     off, mine = place[0], place[4]
     height = below.shape[0]
-    fetched = copies(sems, (spots(fields, "xhat_zero").at[pl.ds(off, height)], below_x))
     devices = got.shape[0]
     rows = grad.shape[0]
     dims = (((1,), (1,)), ((), ()))
@@ -908,7 +916,6 @@
 
     back_rows(grad_low, rows, value)
     gain, bias = affine(table, 0)
-    wait(fetched)
     for k, y in enumerate(blocks_of(conv(grad_low, back, mine, height), height)):
         below[:, k] = y * slope_at(below_x[:, k], gain, bias)
     me = place[2]
@@ -1145,12 +1152,13 @@
     head_rows = w_head.T
     weights, back_zero, back_two, head_mat = call(
         prepare,
-        [far(((STORE_BYTES // (4 * LANES), 2 * LANES), BF16)), nine, nine, ((2 * LANES, LANES), BF16)],
+        [far(((STORE_BYTES // (4 * LANES), 2 * LANES), BF16)), far(nine), far(nine), far(((2 * LANES, LANES), BF16))],
         far(w_first), far(w_convs), far(head_rows),
         scratch=[
-            (w_first.shape, F32), (w_convs.shape, F32), (head_rows.shape, F32), ((BACK_AT + BACK, 2 * LANES), BF16)
+            (w_first.shape, F32), (w_convs.shape, F32), (head_rows.shape, F32), ((BACK_AT + BACK, 2 * LANES), BF16),
+            nine, nine, ((2 * LANES, LANES), BF16),
         ],
-        sems=5, limit=WHOLE_VMEM, name="prepare",
+        sems=8, limit=WHOLE_VMEM, name="prepare",
     )
 
     sides, raw, pay, count, taps = call(
@@ -1200,22 +1208,22 @@
     )
     got_head = exchange(pay)
 
-    grad_one, xhat_one, shared, pay, more_two = call(
+    grad_one, xhat_one, shared, pay, more_two, xhat_zero = call(
         part(decoder_back_kernel, spots=spots, local_count=local_count, pixel_count=pixel_count),
-        [back_field, back_field, back_field, payload(8), vec],
+        [back_field, back_field, back_field, payload(8), vec, own_field],
         place, got_head, grad_three, xhat_three, xhat_two, inv_three, inv_two, hidden_sums, batch_norm_table, back_two, far(weights),
         far(fields), far(lows),
-        scalars=1, scratch=[back_field, back_field, back_low, back_low, own_low, own_low, own_low, nine], sems=6,
+        scalars=1, scratch=[back_field, back_field, back_low, back_low, own_low, own_low, own_low, nine], sems=7,
         name="decoder_back",
     )
     got_one_back = exchange(pay)
 
     pay, more = call(
-        part(summed_kernel, spots=spots, pixel_count=pixel_count, **styled),
+        part(summed_kernel, pixel_count=pixel_count, **styled),
         [payload(13), vec],
         place, got_one_back, got_style, got_head, grad_one, xhat_one, shared, inv_one, more_two, batch_norm_table, w_style,
-        sides, back_zero, far(fields),
-        scalars=1, scratch=[own_field, own_field, back_low], sems=1, name="summed_back",
+        sides, back_zero, xhat_zero,
+        scalars=1, scratch=[own_field, back_low], name="summed_back",
     )
     got_last = exchange(pay)
 

time: 112 us -> 111 us (level)
  Pallas kernels: 34.8 us -> 33 us
    pallas_call x12, Pallas kernels: 34.8 us -> 33 us  [call(): pl.pallas_call(kernel, out_shape=[jax.ShapeDtypeStruct(*plain(x)) for x i...]
    all_to_all x3, waiting for transfers between devices: 15.4 us -> 16.5 us  [exchange(): return lax.all_to_all(pay, ('row', 'col'), 0, 0)]
  transfers between devices with their start and end apart: 3 -> 3, of which waited for: 3 -> 3; matrix products, arithmetic and copies ran while one was open for 0% -> 0% of each run, Pallas kernels for 8% -> 7%
where the time goes in v10:
time: 111 us; the launch traced here: 110 us
  blocking collectives  47.2 us (43%)
  Pallas kernels  33 us (30%)
  waiting for transfers between devices  16.5 us (15%)
  starting transfers between devices  12.5 us (11%)
    all_to_all x5, blocking collectives, exchange(): return lax.all_to_all(pay, ('row', 'col'), 0, 0)  47.2 us
    pallas_call x12, Pallas kernels, call(): pl.pallas_call(kernel, out_shape=[jax.ShapeDtypeStruct(*plain(x)) for x i...  33 us
    all_to_all x3, waiting for transfers between devices, exchange(): return lax.all_to_all(pay, ('row', 'col'), 0, 0)  16.5 us
    all_to_all x3, starting transfers between devices, exchange(): return lax.all_to_all(pay, ('row', 'col'), 0, 0)  12.5 us
  transfers between devices with their start and end apart: 3, of which 3 were waited for; matrix products, arithmetic and copies ran while one was open for 0% of the time, Pallas kernels for 7%

profile of v10, /device:TPU:0, one launch (start us, length us, event | category | flops | bytes accessed | tf_op | source)
XLA Modules:
  0.0 110.3 jit_solution(7430710826117236791)
XLA Ops:
  0.7 2.0 %pack.1 = bf16[32,16,128]{2,1,0:T(8,128)(2,1)} custom-call(bf16[16,8,2,32]{3,2,1,0:T(2,128)(2,1)} %bitcast.22, s32[16,8,2,32]{3,2,1,0:T(2,128)} %bitcast.21, s32[16,8,32]{2,1,0:T(8,128)} %labels_in.1, s32[16,8,32]{2,1,0:T(8,128)} %valid_in.1), custom_call_target="tpu_custom_call" | custom-call | tf_op jit(solution)/shard_map/pack/pallas_call | solution.py:1062
  2.7 7.3 %all-to-all-start = ((bf16[32,16,128]{2,1,0:T(8,128)(2,1)}), bf16[32,16,128]{2,1,0:T(8,128)(2,1)S(1)}, u32[]{:S(2)}, u32[]{:S(2)}) async-start(bf16[32,16,128]{2,1,0:T(8,128)(2,1)} %pack.1), calls=%async_computation | async-start | bytes 262144 | tf_op jit(solution)/shard_map/all_to_all | solution.py:1075
  10.1 3.6 %prepare.1 = (bf16[65536,256]{1,0:T(8,128)(2,1)}, bf16[1152,256]{1,0:T(8,128)(2,1)}, bf16[1152,256]{1,0:T(8,128)(2,1)}, bf16[256,128]{1,0:T(8,128)(2,1)}) custom-call(f32[10,2,32]{2,1,0:T(2,128)} %w_first.1, f32[3,9,32,32]{3,2,1,0:T(8,128)} %w_convs.1, f32[3,33]{1,0:T(4,128)} %bitcast.16), custom_call_target="tpu_custom_call" | custom-call | tf_op jit(solution)/shard_map/prepare/pallas_call | solution.py:1062
  13.7 0.1 stack.23.place
  13.8 4.5 %all-to-all-done.got = bf16[32,16,128]{2,1,0:T(8,128)(2,1)S(1)} async-done(((bf16[32,16,128]{2,1,0:T(8,128)(2,1)}), bf16[32,16,128]{2,1,0:T(8,128)(2,1)S(1)}, u32[]{:S(2)}, u32[]{:S(2)}) %all-to-all-start) | async-done | bytes 131104 | tf_op jit(solution)/shard_map/all_to_all | solution.py:1075
  18.3 2.0 %image_conv.1 = (bf16[42,16,128]{2,1,0:T(8,128)(2,1)S(1)}, f32[40,2,16,128]{3,2,1,0:T(8,128)S(1)}, f32[32,2,1,128]{3,2,1,0:T(1,128)S(1)}, f32[8,128]{1,0:T(8,128)S(1)}, bf16[1280,256]{1,0:T(8,128)(2,1)S(1)}) custom-call(s32[5]{0:T(128)S(1)} %stack.23.place, bf16[32,16,128]{2,1,0:T(8,128)(2,1)S(1)} %all-to-all-done.got, ...), custom_call_target="tpu_custom_call" | custom-call | tf_op jit(solution)/shard_map/image_conv/pallas_call | solution.py:1062
  20.3 9.0 %all_to_all.40.got = f32[32,2,1,128]{3,2,1,0:T(1,128)S(1)} all-to-all(f32[32,2,1,128]{3,2,1,0:T(1,128)S(1)} %get-tuple-element.82), channel_id=1, replica_groups=mesh['row'=8,'col'=4] {'row','col'}, dimensions={0} | all-to-all | bytes 65536 | tf_op jit(solution)/shard_map/all_to_all | solution.py:1075
  29.3 2.0 %first_block.1 = (f32[40,2,16,128]{3,2,1,0:T(8,128)S(1)}, f32[32,2,1,128]{3,2,1,0:T(1,128)S(1)}, f32[8,128]{1,0:T(8,128)S(1)}, f32[2048,2,16,128]{3,2,1,0:T(8,128)}, bf16[2731,3,16,128]{3,2,1,0:T(8,128)(2,1)}) custom-call(s32[5]{0:T(128)S(1)} %stack.23.place, f32[32,2,1,128]{3,2,1,0:T(1,128)S(1)} %all_to_all.40.got, ...), custom_call_target="tpu_custom_call" | custom-call | tf_op jit(solution)/shard_map/first_block/pallas_call | solution.py:1062
  31.3 8.9 %all_to_all.41.got = f32[32,2,1,128]{3,2,1,0:T(1,128)S(1)} all-to-all(f32[32,2,1,128]{3,2,1,0:T(1,128)S(1)} %get-tuple-element.86), channel_id=1, replica_groups=mesh['row'=8,'col'=4] {'row','col'}, dimensions={0} | all-to-all | bytes 65536 | tf_op jit(solution)/shard_map/all_to_all | solution.py:1075
  40.2 2.7 %pool_and_merge.1 = (f32[40,2,16,128]{3,2,1,0:T(8,128)S(1)}, f32[32,3,1,128]{3,2,1,0:T(1,128)S(1)}, f32[8,128]{1,0:T(8,128)S(1)}, bf16[42,3,16,128]{3,2,1,0:T(8,...) custom-call(s32[5]{0:T(128)S(1)} %stack.23.place, ...), custom_call_target="tpu_custom_call", output_to_operand_aliasing={{5}: (6, {}), {6}: (7, {})} | custom-call | tf_op jit(solution)/shard_map/pool_and_merge/pallas_call | solution.py:1062
  43.0 9.0 %all_to_all.42.got.got_style = f32[32,3,1,128]{3,2,1,0:T(1,128)S(1)} all-to-all(f32[32,3,1,128]{3,2,1,0:T(1,128)S(1)} %get-tuple-element.91), channel_id=1, replica_groups=mesh['row'=8,'col'=4] {'row','col'}, dimensions={0} | all-to-all | bytes 98304 | tf_op jit(solution)/shard_map/all_to_all | solution.py:1075
  52.0 4.3 %decoder.1 = (f32[36,2,16,128]{3,2,1,0:T(8,128)S(1)}, f32[32,3,1,128]{3,2,1,0:T(1,128)}, f32[8,128]{1,0:T(8,128)S(1)}, f32[32,128]{1,0:T(8,128)S(1)}, f32[40,2,1...) custom-call(s32[5]{0:T(128)S(1)} %stack.23.place, ...), custom_call_target="tpu_custom_call", output_to_operand_aliasing={{5}: (8, {})} | custom-call | tf_op jit(solution)/shard_map/decoder/pallas_call | solution.py:1062
  56.3 2.6 %all-to-all-start.4 = ((f32[32,3,1,128]{3,2,1,0:T(1,128)}), f32[32,3,1,128]{3,2,1,0:T(1,128)S(1)}, u32[]{:S(2)}, u32[]{:S(2)}) async-start(f32[32,3,1,128]{3,2,1,0:T(1,128)} %get-tuple-element.96.pay), calls=%async_computation.4 | async-start | bytes 98304 | tf_op jit(solution)/shard_map/all_to_all | solution.py:1075
  58.9 3.6 %ahead.1 = (f32[32,5,1,128]{3,2,1,0:T(1,128)S(1)}, f32[8,128]{1,0:T(8,128)S(1)}) custom-call(s32[5]{0:T(128)S(1)} %stack.23.place, f32[32,3,1,128]{3,2,1,0:T(1,128)} %get-tuple-element.96.pay, bf16[42,16,128]{2,1,0:T(8,128)(2,1)S(1)} %get-tuple-element.84.sides, f32[2048,2,16,128]{3,2,1,0:T(8,128)} %get-tuple-element.100.fields, ...), custom_call_target="tpu_custom_call" | custom-call | tf_op jit(solution)/shard_map/ahead/pallas_call | solution.py:1062
  62.5 3.7 %all-to-all-done.4.got = f32[32,3,1,128]{3,2,1,0:T(1,128)S(1)} async-done(((f32[32,3,1,128]{3,2,1,0:T(1,128)}), f32[32,3,1,128]{3,2,1,0:T(1,128)S(1)}, u32[]{:S(2)}, u32[]{:S(2)}) %all-to-all-start.4) | async-done | bytes 49184 | tf_op jit(solution)/shard_map/all_to_all | solution.py:1075
  66.2 2.8 %head.1 = (f32[36,2,16,128]{3,2,1,0:T(8,128)S(1)}, f32[36,2,16,128]{3,2,1,0:T(8,128)S(1)}, f32[32,8,1,128]{3,2,1,0:T(1,128)S(1)}, f32[8,128]{1,0:T(8,128)S(1)}) custom-call(s32[5]{0:T(128)S(1)} %stack.23.place, f32[32,3,1,128]{3,2,1,0:T(1,128)S(1)} %all-to-all-done.4.got, f32[32,3,1,128]{3,2,1,0:T(1,128)S(1)} %all_to_all.42.got.got_style, ...), custom_call_target="tpu_custom_call" | custom-call | tf_op jit(solution)/shard_map/head/pallas_call | solution.py:1062
  69.0 10.2 %all_to_all.43.got.got_head = f32[32,8,1,128]{3,2,1,0:T(1,128)S(1)} all-to-all(f32[32,8,1,128]{3,2,1,0:T(1,128)S(1)} %get-tuple-element.105), channel_id=1, replica_groups=mesh['row'=8,'col'=4] {'row','col'}, dimensions={0} | all-to-all | bytes 262144 | tf_op jit(solution)/shard_map/all_to_all | solution.py:1075
  79.2 4.4 %decoder_back.1 = (f32[36,2,16,128]{3,2,1,0:T(8,128)S(1)}, f32[36,2,16,128]{3,2,1,0:T(8,128)S(1)}, f32[36,2,16,128]{3,2,1,0:T(8,128)S(1)}, f32[32,8,1,128]{3,2,1...) custom-call(s32[5]{0:T(128)S(1)} %stack.23.place, f32[32,8,1,128]{3,2,1,0:T(1,128)S(1)} %all_to_all.43.got.got_head, ...), custom_call_target="tpu_custom_call" | custom-call | tf_op jit(solution)/shard_map/decoder_back/pallas_call | solution.py:1062
  83.7 10.0 %all_to_all.44.got.got_one_back = f32[32,8,1,128]{3,2,1,0:T(1,128)S(1)} all-to-all(f32[32,8,1,128]{3,2,1,0:T(1,128)S(1)} %get-tuple-element.110), channel_id=1, replica_groups=mesh['row'=8,'col'=4] {'row','col'}, dimensions={0} | all-to-all | bytes 262144 | tf_op jit(solution)/shard_map/all_to_all | solution.py:1075
  93.7 2.9 %summed_back.1 = (f32[32,13,1,128]{3,2,1,0:T(1,128)}, f32[8,128]{1,0:T(8,128)S(1)}) custom-call(s32[5]{0:T(128)S(1)} %stack.23.place, f32[32,8,1,128]{3,2,1,0:T(1,128)S(1)} %all_to_all.44.got.got_one_back, f32[32,3,1,128]{3,2,1,0:T(1,128)S(1)} %all_to_all.42.got.got_style, f32[32,8,1,128]{3,2,1,0:T(1,128)S(1)} %all_to_all.43.got.got_head, ...), custom_call_target="tpu_custom_call" | custom-call | tf_op jit(solution)/shard_map/summed_back/pallas_call | solution.py:1062
  96.6 2.6 %all-to-all-start.7 = ((f32[32,13,1,128]{3,2,1,0:T(1,128)}), f32[32,13,1,128]{3,2,1,0:T(1,128)S(1)}, u32[]{:S(2)}, u32[]{:S(2)}) async-start(f32[32,13,1,128]{3,2,1,0:T(1,128)} %get-tuple-element.118.pay), calls=%async_computation.7 | async-start | bytes 425984 | tf_op jit(solution)/shard_map/all_to_all | solution.py:1075
  99.3 1.0 update_early.1
  100.3 8.3 %all-to-all-done.7.got = f32[32,13,1,128]{3,2,1,0:T(1,128)S(1)} async-done(((f32[32,13,1,128]{3,2,1,0:T(1,128)}), f32[32,13,1,128]{3,2,1,0:T(1,128)S(1)}, u32[]{:S(2)}, u32[]{:S(2)}) %all-to-all-start.7) | async-done | bytes 213024 | tf_op jit(solution)/shard_map/all_to_all | solution.py:1075
  108.6 1.7 %update_late.1 = (f32[10,2,32]{2,1,0:T(2,128)}, f32[10,2,32]{2,1,0:T(2,128)}, f32[10,2,32]{2,1,0:T(2,128)}, bf16[10,2,32]{2,1,0:T(2,128)(2,1)}, f32[3,9,32,32]{3...) custom-call(f32[32,13,1,128]{3,2,1,0:T(1,128)S(1)} %all-to-all-done., ...), custom_call_target="tpu_custom_call" | custom-call | tf_op jit(solution)/shard_map/update_late/pallas_call | solution.py:1062
  (36 shorter events, 0.1 us)
Async XLA Ops:
  0.7 28.6 %copy-start.6 = (f32[2,4,32]{2,1,0:T(4,128)S(1)}, f32[2,4,32]{2,1,0:T(4,128)}, u32[]{:S(2)}) copy-start(f32[2,4,32]{2,1,0:T(4,128)} %table.13) | copy-start | bytes 3076
  2.7 15.5 %all-to-all-start = ((bf16[32,16,128]{2,1,0:T(8,128)(2,1)}), bf16[32,16,128]{2,1,0:T(8,128)(2,1)S(1)}, u32[]{:S(2)}, u32[]{:S(2)}) async-start(bf16[32,16,128]{2,1,0:T(8,128)(2,1)} %pack.1), calls=%async_computation | async-start | bytes 262144 | tf_op jit(solution)/shard_map/all_to_all | solution.py:1075
  40.2 11.8 %copy-start = (f32[3,9,32,32]{3,2,1,0:T(8,128)S(1)}, f32[3,9,32,32]{3,2,1,0:T(8,128)}, u32[]{:S(2)}) copy-start(f32[3,9,32,32]{3,2,1,0:T(8,128)} %w_convs.1) | copy-start | bytes 331780
  40.2 11.8 %copy-start.5 = (f32[2,32,32]{2,1,0:T(8,128)S(1)}, f32[2,32,32]{2,1,0:T(8,128)}, u32[]{:S(2)}) copy-start(f32[2,32,32]{2,1,0:T(8,128)} %w_style.5) | copy-start | bytes 24580
  56.3 9.9 %all-to-all-start.4 = ((f32[32,3,1,128]{3,2,1,0:T(1,128)}), f32[32,3,1,128]{3,2,1,0:T(1,128)S(1)}, u32[]{:S(2)}, u32[]{:S(2)}) async-start(f32[32,3,1,128]{3,2,1,0:T(1,128)} %get-tuple-element.96.pay), calls=%async_computation.4 | async-start | bytes 98304 | tf_op jit(solution)/shard_map/all_to_all | solution.py:1075
  58.9 7.3 %copy-start.1 = (bf16[1152,256]{1,0:T(8,128)(2,1)S(1)}, bf16[1152,256]{1,0:T(8,128)(2,1)}, u32[]{:S(2)}) copy-start(bf16[1152,256]{1,0:T(8,128)(2,1)} %get-tuple-element.104.back.back_two) | copy-start | bytes 1769476
  58.9 7.3 %copy-start.7 = (bf16[256,128]{1,0:T(8,128)(2,1)S(1)}, bf16[256,128]{1,0:T(8,128)(2,1)}, u32[]{:S(2)}) copy-start(bf16[256,128]{1,0:T(8,128)(2,1)} %get-tuple-element.98.head_mat) | copy-start | bytes 196612
  58.9 7.3 %copy-start.11 = (f32[33,3]{0,1:T(4,128)S(1)}, f32[33,3]{0,1:T(4,128)}, u32[]{:S(2)}) copy-start(f32[33,3]{0,1:T(4,128)} %param.26) | copy-start | bytes 1192
  79.1 14.6 %copy-start.2 = (bf16[1152,256]{1,0:T(8,128)(2,1)S(1)}, bf16[1152,256]{1,0:T(8,128)(2,1)}, u32[]{:S(2)}) copy-start(bf16[1152,256]{1,0:T(8,128)(2,1)} %get-tuple-element.116.back) | copy-start | bytes 1769476
  79.1 20.1 %copy-start.9 = (f32[2,32,32]{2,1,0:T(8,128)S(1)}, f32[2,32,32]{2,1,0:T(8,128)}, u32[]{:S(2)}) copy-start(f32[2,32,32]{2,1,0:T(8,128)} %m_style.1) | copy-start | bytes 24580
  79.1 20.1 %copy-start.10 = (f32[2,32,32]{2,1,0:T(8,128)S(1)}, f32[2,32,32]{2,1,0:T(8,128)}, u32[]{:S(2)}) copy-start(f32[2,32,32]{2,1,0:T(8,128)} %s_style.1) | copy-start | bytes 24580
  79.1 20.1 %copy-start.16 = (f32[33,3]{0,1:T(4,128)S(1)}, f32[33,3]{0,1:T(4,128)}, u32[]{:S(2)}) copy-start(f32[33,3]{0,1:T(4,128)} %param.31) | copy-start | bytes 1192
  79.2 20.1 %copy-start.17 = (f32[33,3]{0,1:T(4,128)S(1)}, f32[33,3]{0,1:T(4,128)}, u32[]{:S(2)}) copy-start(f32[33,3]{0,1:T(4,128)} %param.36) | copy-start | bytes 1192
  79.2 29.4 %copy-start.3 = (f32[3,9,32,32]{3,2,1,0:T(8,128)S(1)}, f32[3,9,32,32]{3,2,1,0:T(8,128)}, u32[]{:S(2)}) copy-start(f32[3,9,32,32]{3,2,1,0:T(8,128)} %m_convs.1) | copy-start | bytes 331780
  79.2 29.4 %copy-start.4 = (f32[3,9,32,32]{3,2,1,0:T(8,128)S(1)}, f32[3,9,32,32]{3,2,1,0:T(8,128)}, u32[]{:S(2)}) copy-start(f32[3,9,32,32]{3,2,1,0:T(8,128)} %s_convs.1) | copy-start | bytes 331780
  79.2 29.4 %copy-start.8 = (f32[10,2,32]{2,1,0:T(2,128)S(1)}, f32[10,2,32]{2,1,0:T(2,128)}, u32[]{:S(2)}) copy-start(f32[10,2,32]{2,1,0:T(2,128)} %w_first.1) | copy-start | bytes 7684
  79.2 29.4 %copy-start.12 = (f32[10,2,32]{2,1,0:T(2,128)S(1)}, f32[10,2,32]{2,1,0:T(2,128)}, u32[]{:S(2)}) copy-start(f32[10,2,32]{2,1,0:T(2,128)} %m_first.1) | copy-start | bytes 7684
  79.2 29.4 %copy-start.13 = (f32[10,2,32]{2,1,0:T(2,128)S(1)}, f32[10,2,32]{2,1,0:T(2,128)}, u32[]{:S(2)}) copy-start(f32[10,2,32]{2,1,0:T(2,128)} %s_first.1) | copy-start | bytes 7684
  79.2 29.4 %copy-start.14 = (f32[2,4,32]{2,1,0:T(4,128)S(1)}, f32[2,4,32]{2,1,0:T(4,128)}, u32[]{:S(2)}) copy-start(f32[2,4,32]{2,1,0:T(4,128)} %m_norms.1) | copy-start | bytes 3076
  79.2 29.4 %copy-start.15 = (f32[2,4,32]{2,1,0:T(4,128)S(1)}, f32[2,4,32]{2,1,0:T(4,128)}, u32[]{:S(2)}) copy-start(f32[2,4,32]{2,1,0:T(4,128)} %s_norms.1) | copy-start | bytes 3076
  96.6 12.0 %all-to-all-start.7 = ((f32[32,13,1,128]{3,2,1,0:T(1,128)}), f32[32,13,1,128]{3,2,1,0:T(1,128)S(1)}, u32[]{:S(2)}, u32[]{:S(2)}) async-start(f32[32,13,1,128]{3,2,1,0:T(1,128)} %get-tuple-element.118.pay), calls=%async_computation.7 | async-start | bytes 425984 | tf_op jit(solution)/shard_map/all_to_all | solution.py:1075

commit v11 on v10

--- a/solution.py
+++ b/solution.py
@@ -517,8 +517,16 @@
     return col_sum(jnp.where(row_of(v.shape) == me, v, 0.0))
 
 
-def style_kernel(place, got, raw, merged, table, w_style, w_convs_in, taps, lows_in, resid, pay, vec, style_out, xhat, lows, hidden, slopes, w_conv, sems, *, spots, local_count, pixel_count, pool_cells, height, parts):
-    fetched = copies(sems, (w_convs_in.at[2], w_conv))
+def style_kernel(place, got, raw, merged, table, w_style, w_convs_in, taps, sides, fields, lows_in, resid, pay, vec, style_out, xhat, ahead, sums, lows, hidden, slopes, w_conv, zero_x, one_x, shared, field, sems, *, spots, local_count, pixel_count, pool_cells, height, parts):
+    own = pl.ds(place[0], height)
+    fetched = copies(
+        sems,
+        (w_convs_in.at[2], w_conv),
+        (spots(fields, "xhat_zero").at[own], zero_x),
+        (spots(fields, "xhat_one").at[own], one_x),
+        (spots(fields, "shared").at[own], shared),
+        (spots(lows_in, "hidden_one").at[pl.ds(place[0], height + 2)], field),
+    )
     style = by_image(spread(row_of_each(got, 2), 0), parts) / pool_cells
     style_out[...] = style
     one, two = [
@@ -547,7 +555,7 @@
 
     blank(hidden)
     loop(rows // 4, norm_rows)
-    stored = copies(sems.at[1:], (hidden, spots(lows, "hidden_three")))
+    stored = copies(sems.at[5:], (hidden, spots(lows, "hidden_three")))
 
     @pl.when(place[0] >= 0)
     def _():
@@ -570,6 +578,7 @@
     links = norm_links(hidden, probe, mine, height, w_conv, centre)
     send(pay, *local_stats(resid, mine, height, local_count))
     send_parts(pay, 2, 1)[:, 0, :] = links
+    put_ahead(off, sides, ahead, sums, zero_x, one_x, shared, field, local_count)
 
 
 def norm_links(field, probe, first, rows, taps, centre):
@@ -616,18 +625,8 @@
     return 1 + x // GRP, x % GRP
 
 
-def ahead_kernel(place, pay, sides, fields, lows, out, sums, below_x, xhat, shared, field, sems, *, spots, local_count):
-    off = place[0]
+def put_ahead(off, sides, out, sums, below_x, xhat, shared, field, local_count):
     height = xhat.shape[0]
-    own = pl.ds(off, height)
-    fetched = copies(
-        sems,
-        (spots(fields, "xhat_zero").at[own], below_x),
-        (spots(fields, "xhat_one").at[own], xhat),
-        (spots(fields, "shared").at[own], shared),
-        (spots(lows, "hidden_one").at[pl.ds(off, height + 2)], field),
-    )
-    wait(fetched[:1])
     at = pl.ds(0, height)
     low_x = jnp.concatenate([own_lanes(below_x, at), jnp.ones((height * field.shape[2], LANES), BF16)], axis=1)
     entries, alone = [], zero_row()
@@ -637,7 +636,6 @@
             for v, b in zip(tap, bare):
                 alone = jnp.where(lane == ALONE + len(entries), b, alone)
                 entries.append(v)
-    wait(fetched[1:])
     centres = [fold(v) / local_count for v in row_sums(0, height, lambda at, k: (xhat[at, k], shared[at, k]))]
     probe = [flat(v[at, k] - c).astype(BF16) for v, c in zip((xhat, shared), centres) for k in range(2)]
     wide = jnp.concatenate(views(field, 0, height), axis=1)
@@ -1044,6 +1042,13 @@
         put(i, (table, m_norms, s_norms), grad, rate_table[4], (norms_master, norms_moment, norms_square))
 
 
+def update_kernel(*refs, pixel_count):
+    ins, outs = refs[:23], refs[23:]
+    late, early = ins[:15], ins[15:]
+    update_late(*late, *outs[:11], pixel_count=pixel_count)
+    update_early(late[1], late[2], early[0], None, *early[1:], *outs[11:])
+
+
 def far(x):
     return ("far", x)
 
@@ -1185,20 +1190,15 @@
     )
     got_style = exchange(pay)
 
-    resid, pay, inv_two, style, xhat_two, lows = call(
+    resid, pay, inv_two, style, xhat_two, ahead, hidden_sums, lows = call(
         part(style_kernel, spots=spots, **styled, **counts),
-        [back_field, payload(3), vec, ((devices, LANES), F32), field, store_of(low_field)],
-        place, got_style, raw, merged, batch_norm_table, w_style, far(w_convs), taps, far(lows),
-        scalars=1, scratch=[low_field, field, (w_convs.shape[1:], F32)], sems=2,
-        aliases={8: 5}, name="decoder",
+        [back_field, payload(3), vec, ((devices, LANES), F32), field, ((CH, 5, 1, LANES), F32), vec, store_of(low_field)],
+        place, got_style, raw, merged, batch_norm_table, w_style, far(w_convs), taps, sides, far(fields),
+        far(lows),
+        scalars=1, scratch=[low_field, field, (w_convs.shape[1:], F32), own_field, own_field, own_field, own_low], sems=6,
+        aliases={10: 7}, name="decoder",
     )
     got_three = exchange(pay)
-    ahead, hidden_sums = call(
-        part(ahead_kernel, spots=spots, local_count=local_count),
-        [((CH, 5, 1, LANES), F32), vec],
-        place, far(pay), sides, far(fields), far(lows),
-        scalars=1, scratch=[own_field, own_field, own_field, own_low], sems=4, name="ahead",
-    )
 
     grad_three, xhat_three, pay, inv_three = call(
         part(head_kernel, **counts),
@@ -1230,20 +1230,20 @@
     def results(param, copy):
         return [(param.shape, F32)] * 3 + [(param.shape, BF16)] * copy
 
-    early = call(
-        update_early,
-        [((1, 1), F32), ((1, 1), F32)] + results(w_style, 0) + results(head_rows, 1),
-        got_one_back, got_head, got_style, far(pay), style,
-        w_style, head_rows, mom_style, mom_head.T, sqr_style, sqr_head.T,
-        scalar_outs=(0, 1), name="update_early",
-    )
-    late = call(
-        part(update_late, pixel_count=pixel_count),
-        results(w_first, 1) + results(w_convs, 1) + results(batch_norm_table, 0),
+    found = call(
+        part(update_kernel, pixel_count=pixel_count),
+        results(w_first, 1)
+        + results(w_convs, 1)
+        + results(batch_norm_table, 0)
+        + [((1, 1), F32), ((1, 1), F32)]
+        + results(w_style, 0)
+        + results(head_rows, 1),
         got_last, got_one_back, got_head, more, more_two, inv_zero,
         w_first, w_convs, batch_norm_table, mom_first, mom_convs, mom_norms, sqr_first, sqr_convs, sqr_norms,
-        name="update_late",
-    )
+        got_style, style, w_style, head_rows, mom_style, mom_head.T, sqr_style, sqr_head.T,
+        scalar_outs=(11, 12), name="update",
+    )
+    late, early = found[:11], found[11:]
     loss, count = early[0].reshape(()), early[1].reshape(())
     head = tuple(value.T for value in early[5:9])
     return (loss, count, *late[0:8], *early[2:5], *head, *late[8:11])

time: 111 us -> 109 us (0.982)
  blocking collectives: 47.2 us -> 67 us
  waiting for transfers between devices: 16.5 us -> 4.47 us
  starting transfers between devices: 12.5 us -> 7.3 us
  Pallas kernels: 33 us -> 28.8 us
    all_to_all x5 -> x7, blocking collectives: 47.2 us -> 67 us  [exchange(): return lax.all_to_all(pay, ('row', 'col'), 0, 0)]
    all_to_all x3 -> x1, waiting for transfers between devices: 16.5 us -> 4.47 us  [exchange(): return lax.all_to_all(pay, ('row', 'col'), 0, 0)]
    all_to_all x3 -> x1, starting transfers between devices: 12.5 us -> 7.3 us  [exchange(): return lax.all_to_all(pay, ('row', 'col'), 0, 0)]
    pallas_call x12 -> x10, Pallas kernels: 33 us -> 28.8 us  [call(): pl.pallas_call(kernel, out_shape=[jax.ShapeDtypeStruct(*plain(x)) for x i...]
  transfers between devices with their start and end apart: 3 -> 1, of which waited for: 3 -> 1; matrix products, arithmetic and copies ran while one was open for 0% -> 0% of each run, Pallas kernels for 7% -> 3%
where the time goes in v11:
time: 109 us
  blocking collectives  67 us (61%)
  Pallas kernels  28.8 us (26%)
  starting transfers between devices  7.3 us (7%)
  waiting for transfers between devices  4.47 us (4%)
  between operations  1.1 us (1%)
    all_to_all x7, blocking collectives, exchange(): return lax.all_to_all(pay, ('row', 'col'), 0, 0)  67 us
    pallas_call x10, Pallas kernels, call(): pl.pallas_call(kernel, out_shape=[jax.ShapeDtypeStruct(*plain(x)) for x i...  28.8 us
    all_to_all x1, starting transfers between devices, exchange(): return lax.all_to_all(pay, ('row', 'col'), 0, 0)  7.3 us
    all_to_all x1, waiting for transfers between devices, exchange(): return lax.all_to_all(pay, ('row', 'col'), 0, 0)  4.47 us
  transfers between devices with their start and end apart: 1, of which 1 were waited for; matrix products, arithmetic and copies ran while one was open for 0% of the time, Pallas kernels for 3%

profile of v11, /device:TPU:0, one launch (start us, length us, event | category | flops | bytes accessed | tf_op | source)
XLA Modules:
  0.0 108.9 jit_solution(14035438952812590374)
XLA Ops:
  0.7 2.0 %pack.1 = bf16[32,16,128]{2,1,0:T(8,128)(2,1)} custom-call(bf16[16,8,2,32]{3,2,1,0:T(2,128)(2,1)} %bitcast.22, s32[16,8,2,32]{3,2,1,0:T(2,128)} %bitcast.21, s32[16,8,32]{2,1,0:T(8,128)} %labels_in.1, s32[16,8,32]{2,1,0:T(8,128)} %valid_in.1), custom_call_target="tpu_custom_call" | custom-call | tf_op jit(solution)/shard_map/pack/pallas_call | solution.py:1067
  2.7 7.3 %all-to-all-start = ((bf16[32,16,128]{2,1,0:T(8,128)(2,1)}), bf16[32,16,128]{2,1,0:T(8,128)(2,1)S(1)}, u32[]{:S(2)}, u32[]{:S(2)}) async-start(bf16[32,16,128]{2,1,0:T(8,128)(2,1)} %pack.1), calls=%async_computation | async-start | bytes 262144 | tf_op jit(solution)/shard_map/all_to_all | solution.py:1080
  10.1 3.6 %prepare.1 = (bf16[65536,256]{1,0:T(8,128)(2,1)}, bf16[1152,256]{1,0:T(8,128)(2,1)}, bf16[1152,256]{1,0:T(8,128)(2,1)}, bf16[256,128]{1,0:T(8,128)(2,1)}) custom-call(f32[10,2,32]{2,1,0:T(2,128)} %refs_6_.1, f32[3,9,32,32]{3,2,1,0:T(8,128)} %refs_7_.1, f32[3,33]{1,0:T(4,128)} %bitcast.16), custom_call_target="tpu_custom_call" | custom-call | tf_op jit(solution)/shard_map/prepare/pallas_call | solution.py:1067
  13.7 0.1 stack.23.place
  13.8 4.5 %all-to-all-done.got = bf16[32,16,128]{2,1,0:T(8,128)(2,1)S(1)} async-done(((bf16[32,16,128]{2,1,0:T(8,128)(2,1)}), bf16[32,16,128]{2,1,0:T(8,128)(2,1)S(1)}, u32[]{:S(2)}, u32[]{:S(2)}) %all-to-all-start) | async-done | bytes 131104 | tf_op jit(solution)/shard_map/all_to_all | solution.py:1080
  18.3 2.0 %image_conv.1 = (bf16[42,16,128]{2,1,0:T(8,128)(2,1)S(1)}, f32[40,2,16,128]{3,2,1,0:T(8,128)S(1)}, f32[32,2,1,128]{3,2,1,0:T(1,128)S(1)}, f32[8,128]{1,0:T(8,128)S(1)}, bf16[1280,256]{1,0:T(8,128)(2,1)S(1)}) custom-call(s32[5]{0:T(128)S(1)} %stack.23.place, bf16[32,16,128]{2,1,0:T(8,128)(2,1)S(1)} %all-to-all-done.got, ...), custom_call_target="tpu_custom_call" | custom-call | tf_op jit(solution)/shard_map/image_conv/pallas_call | solution.py:1067
  20.3 9.0 %all_to_all.40.got = f32[32,2,1,128]{3,2,1,0:T(1,128)S(1)} all-to-all(f32[32,2,1,128]{3,2,1,0:T(1,128)S(1)} %get-tuple-element.82), channel_id=1, replica_groups=mesh['row'=8,'col'=4] {'row','col'}, dimensions={0} | all-to-all | bytes 65536 | tf_op jit(solution)/shard_map/all_to_all | solution.py:1080
  29.3 2.0 %first_block.1 = (f32[40,2,16,128]{3,2,1,0:T(8,128)S(1)}, f32[32,2,1,128]{3,2,1,0:T(1,128)S(1)}, f32[8,128]{1,0:T(8,128)S(1)}, f32[2048,2,16,128]{3,2,1,0:T(8,128)}, bf16[2731,3,16,128]{3,2,1,0:T(8,128)(2,1)}) custom-call(s32[5]{0:T(128)S(1)} %stack.23.place, f32[32,2,1,128]{3,2,1,0:T(1,128)S(1)} %all_to_all.40.got, ...), custom_call_target="tpu_custom_call" | custom-call | tf_op jit(solution)/shard_map/first_block/pallas_call | solution.py:1067
  31.3 8.9 %all_to_all.41.got = f32[32,2,1,128]{3,2,1,0:T(1,128)S(1)} all-to-all(f32[32,2,1,128]{3,2,1,0:T(1,128)S(1)} %get-tuple-element.86), channel_id=1, replica_groups=mesh['row'=8,'col'=4] {'row','col'}, dimensions={0} | all-to-all | bytes 65536 | tf_op jit(solution)/shard_map/all_to_all | solution.py:1080
  40.3 2.7 %pool_and_merge.1 = (f32[40,2,16,128]{3,2,1,0:T(8,128)S(1)}, f32[32,3,1,128]{3,2,1,0:T(1,128)S(1)}, f32[8,128]{1,0:T(8,128)S(1)}, bf16[42,3,16,128]{3,2,1,0:T(8,...) custom-call(s32[5]{0:T(128)S(1)} %stack.23.place, ...), custom_call_target="tpu_custom_call", output_to_operand_aliasing={{5}: (6, {}), {6}: (7, {})} | custom-call | tf_op jit(solution)/shard_map/pool_and_merge/pallas_call | solution.py:1067
  43.0 9.0 %all_to_all.42.got.got_style.refs_15_ = f32[32,3,1,128]{3,2,1,0:T(1,128)S(1)} all-to-all(f32[32,3,1,128]{3,2,1,0:T(1,128)S(1)} %get-tuple-element.91), channel_id=1, replica_groups=mesh['row'=8,'col'=4] {'row','col'}, dimensions={0} | all-to-all | bytes 98304 | tf_op jit(solution)/shard_map/all_to_all | solution.py:1080
  52.1 5.0 %decoder.1 = (f32[36,2,16,128]{3,2,1,0:T(8,128)S(1)}, f32[32,3,1,128]{3,2,1,0:T(1,128)S(1)}, f32[8,128]{1,0:T(8,128)S(1)}, f32[32,128]{1,0:T(8,128)S(1)}, f32[40...) custom-call(s32[5]{0:T(128)S(1)} %stack.23.place, ...), custom_call_target="tpu_custom_call", output_to_operand_aliasing={{7}: (10, {})} | custom-call | tf_op jit(solution)/shard_map/decoder/pallas_call | solution.py:1067
  57.1 9.0 %all_to_all.43.got = f32[32,3,1,128]{3,2,1,0:T(1,128)S(1)} all-to-all(f32[32,3,1,128]{3,2,1,0:T(1,128)S(1)} %get-tuple-element.97), channel_id=1, replica_groups=mesh['row'=8,'col'=4] {'row','col'}, dimensions={0} | all-to-all | bytes 98304 | tf_op jit(solution)/shard_map/all_to_all | solution.py:1080
  66.1 2.7 %head.1 = (f32[36,2,16,128]{3,2,1,0:T(8,128)S(1)}, f32[36,2,16,128]{3,2,1,0:T(8,128)S(1)}, f32[32,8,1,128]{3,2,1,0:T(1,128)S(1)}, f32[8,128]{1,0:T(8,128)S(1)}) custom-call(s32[5]{0:T(128)S(1)} %stack.23.place, f32[32,3,1,128]{3,2,1,0:T(1,128)S(1)} %all_to_all.43.got, f32[32,3,1,128]{3,2,1,0:T(1,128)S(1)} %all_to_all.42.got.got_style.refs_15_, ...), custom_call_target="tpu_custom_call" | custom-call | tf_op jit(solution)/shard_map/head/pallas_call | solution.py:1067
  68.9 9.9 %all_to_all.44.got.got_head.refs_2_ = f32[32,8,1,128]{3,2,1,0:T(1,128)S(1)} all-to-all(f32[32,8,1,128]{3,2,1,0:T(1,128)S(1)} %get-tuple-element.104), channel_id=1, replica_groups=mesh['row'=8,'col'=4] {'row','col'}, dimensions={0} | all-to-all | bytes 262144 | tf_op jit(solution)/shard_map/all_to_all | solution.py:1080
  78.8 0.0 copy-start.9
  78.8 0.0 copy-start.10
  78.9 0.0 copy-start.14
  78.9 0.0 copy-start.15
  78.9 4.4 %decoder_back.1 = (f32[36,2,16,128]{3,2,1,0:T(8,128)S(1)}, f32[36,2,16,128]{3,2,1,0:T(8,128)S(1)}, f32[36,2,16,128]{3,2,1,0:T(8,128)S(1)}, f32[32,8,1,128]{3,2,1...) custom-call(s32[5]{0:T(128)S(1)} %stack.23.place, ...), custom_call_target="tpu_custom_call" | custom-call | tf_op jit(solution)/shard_map/decoder_back/pallas_call | solution.py:1067
  83.4 9.9 %all_to_all.45.got.refs_1_ = f32[32,8,1,128]{3,2,1,0:T(1,128)S(1)} all-to-all(f32[32,8,1,128]{3,2,1,0:T(1,128)S(1)} %get-tuple-element.110), channel_id=1, replica_groups=mesh['row'=8,'col'=4] {'row','col'}, dimensions={0} | all-to-all | bytes 262144 | tf_op jit(solution)/shard_map/all_to_all | solution.py:1080
  93.3 2.2 %summed_back.1 = (f32[32,13,1,128]{3,2,1,0:T(1,128)S(1)}, f32[8,128]{1,0:T(8,128)S(1)}) custom-call(s32[5]{0:T(128)S(1)} %stack.23.place, f32[32,8,1,128]{3,2,1,0:T(1,128)S(1)} %all_to_all.45.got.refs_1_, f32[32,3,1,128]{3,2,1,0:T(1,128)S(1)} %all_to_all.42.got.got_style.refs_15_, f32[32,8,1,128]{3,2,1,0:T(1,128)S(1)} %all_to_all.44.got.got_head.refs_2_, ...), custom_call_target="tpu_custom_call" | custom-call | tf_op jit(solution)/shard_map/summed_back/pallas_call | solution.py:1067
  95.6 11.1 %all_to_all.46.refs_0_ = f32[32,13,1,128]{3,2,1,0:T(1,128)S(1)} all-to-all(f32[32,13,1,128]{3,2,1,0:T(1,128)S(1)} %get-tuple-element.118), channel_id=1, replica_groups=mesh['row'=8,'col'=4] {'row','col'}, dimensions={0} | all-to-all | bytes 425984 | tf_op jit(solution)/shard_map/all_to_all | solution.py:1080
  106.8 1.9 %update.1 = (f32[10,2,32]{2,1,0:T(2,128)}, f32[10,2,32]{2,1,0:T(2,128)}, f32[10,2,32]{2,1,0:T(2,128)}, bf16[10,2,32]{2,1,0:T(2,128)(2,1)}, f32[3,9,32,32]{3,2,1,...) custom-call(f32[32,13,1,128]{3,2,1,0:T(1,128)S(1)} %all_to_all.46.re, ...), custom_call_target="tpu_custom_call" | custom-call | tf_op jit(solution)/shard_map/update/pallas_call | solution.py:1067
  (32 shorter events, 0.1 us)
Async XLA Ops:
  0.7 28.6 %copy-start.6 = (f32[2,4,32]{2,1,0:T(4,128)S(1)}, f32[2,4,32]{2,1,0:T(4,128)}, u32[]{:S(2)}) copy-start(f32[2,4,32]{2,1,0:T(4,128)} %refs_8_.1) | copy-start | bytes 3076
  2.7 15.5 %all-to-all-start = ((bf16[32,16,128]{2,1,0:T(8,128)(2,1)}), bf16[32,16,128]{2,1,0:T(8,128)(2,1)S(1)}, u32[]{:S(2)}, u32[]{:S(2)}) async-start(bf16[32,16,128]{2,1,0:T(8,128)(2,1)} %pack.1), calls=%async_computation | async-start | bytes 262144 | tf_op jit(solution)/shard_map/all_to_all | solution.py:1080
  40.3 11.8 %copy-start = (f32[3,9,32,32]{3,2,1,0:T(8,128)S(1)}, f32[3,9,32,32]{3,2,1,0:T(8,128)}, u32[]{:S(2)}) copy-start(f32[3,9,32,32]{3,2,1,0:T(8,128)} %refs_7_.1) | copy-start | bytes 331780
  40.3 11.8 %copy-start.5 = (f32[2,32,32]{2,1,0:T(8,128)S(1)}, f32[2,32,32]{2,1,0:T(8,128)}, u32[]{:S(2)}) copy-start(f32[2,32,32]{2,1,0:T(8,128)} %refs_17_.1) | copy-start | bytes 24580
  52.0 14.1 %copy-start.1 = (bf16[1152,256]{1,0:T(8,128)(2,1)S(1)}, bf16[1152,256]{1,0:T(8,128)(2,1)}, u32[]{:S(2)}) copy-start(bf16[1152,256]{1,0:T(8,128)(2,1)} %get-tuple-element.103.back.back_two) | copy-start | bytes 1769476
  52.0 14.1 %copy-start.7 = (bf16[256,128]{1,0:T(8,128)(2,1)S(1)}, bf16[256,128]{1,0:T(8,128)(2,1)}, u32[]{:S(2)}) copy-start(bf16[256,128]{1,0:T(8,128)(2,1)} %get-tuple-element.99.head_mat) | copy-start | bytes 196612
  52.0 14.1 %copy-start.11 = (f32[33,3]{0,1:T(4,128)S(1)}, f32[33,3]{0,1:T(4,128)}, u32[]{:S(2)}) copy-start(f32[33,3]{0,1:T(4,128)} %param.26) | copy-start | bytes 1192
  78.8 14.5 %copy-start.2 = (bf16[1152,256]{1,0:T(8,128)(2,1)S(1)}, bf16[1152,256]{1,0:T(8,128)(2,1)}, u32[]{:S(2)}) copy-start(bf16[1152,256]{1,0:T(8,128)(2,1)} %get-tuple-element.116.back) | copy-start | bytes 1769476
  78.8 27.9 %copy-start.3 = (f32[3,9,32,32]{3,2,1,0:T(8,128)S(1)}, f32[3,9,32,32]{3,2,1,0:T(8,128)}, u32[]{:S(2)}) copy-start(f32[3,9,32,32]{3,2,1,0:T(8,128)} %refs_10_.1) | copy-start | bytes 331780
  78.8 27.9 %copy-start.4 = (f32[3,9,32,32]{3,2,1,0:T(8,128)S(1)}, f32[3,9,32,32]{3,2,1,0:T(8,128)}, u32[]{:S(2)}) copy-start(f32[3,9,32,32]{3,2,1,0:T(8,128)} %refs_13_.1) | copy-start | bytes 331780
  78.8 27.9 %copy-start.8 = (f32[10,2,32]{2,1,0:T(2,128)S(1)}, f32[10,2,32]{2,1,0:T(2,128)}, u32[]{:S(2)}) copy-start(f32[10,2,32]{2,1,0:T(2,128)} %refs_6_.1) | copy-start | bytes 7684
  78.8 27.9 %copy-start.9 = (f32[2,32,32]{2,1,0:T(8,128)S(1)}, f32[2,32,32]{2,1,0:T(8,128)}, u32[]{:S(2)}) copy-start(f32[2,32,32]{2,1,0:T(8,128)} %refs_19_.1) | copy-start | bytes 24580
  78.8 27.9 %copy-start.10 = (f32[2,32,32]{2,1,0:T(8,128)S(1)}, f32[2,32,32]{2,1,0:T(8,128)}, u32[]{:S(2)}) copy-start(f32[2,32,32]{2,1,0:T(8,128)} %refs_21_.1) | copy-start | bytes 24580
  78.8 27.9 %copy-start.12 = (f32[10,2,32]{2,1,0:T(2,128)S(1)}, f32[10,2,32]{2,1,0:T(2,128)}, u32[]{:S(2)}) copy-start(f32[10,2,32]{2,1,0:T(2,128)} %refs_9_.1) | copy-start | bytes 7684
  78.9 27.9 %copy-start.13 = (f32[10,2,32]{2,1,0:T(2,128)S(1)}, f32[10,2,32]{2,1,0:T(2,128)}, u32[]{:S(2)}) copy-start(f32[10,2,32]{2,1,0:T(2,128)} %refs_12_.1) | copy-start | bytes 7684
  78.9 27.9 %copy-start.14 = (f32[2,4,32]{2,1,0:T(4,128)S(1)}, f32[2,4,32]{2,1,0:T(4,128)}, u32[]{:S(2)}) copy-start(f32[2,4,32]{2,1,0:T(4,128)} %refs_11_.1) | copy-start | bytes 3076
  78.9 27.9 %copy-start.15 = (f32[2,4,32]{2,1,0:T(4,128)S(1)}, f32[2,4,32]{2,1,0:T(4,128)}, u32[]{:S(2)}) copy-start(f32[2,4,32]{2,1,0:T(4,128)} %refs_14_.1) | copy-start | bytes 3076
  78.9 27.9 %copy-start.16 = (f32[33,3]{0,1:T(4,128)S(1)}, f32[33,3]{0,1:T(4,128)}, u32[]{:S(2)}) copy-start(f32[33,3]{0,1:T(4,128)} %param.31) | copy-start | bytes 1192
  78.9 27.9 %copy-start.17 = (f32[33,3]{0,1:T(4,128)S(1)}, f32[33,3]{0,1:T(4,128)}, u32[]{:S(2)}) copy-start(f32[33,3]{0,1:T(4,128)} %param.36) | copy-start | bytes 1192

commit v12 on v11

--- a/solution.py
+++ b/solution.py
@@ -935,14 +935,21 @@
     for r in range(3):
         for tap in pixel_taps(sides, off + r, height, low_below, (-1, 0, 1)):
             taps.extend(tap)
-    taps = [shard[2]] + taps + side
-    send(
-        pay,
-        groups(*own_sums(below, below_x, 0, height), spread(last, 0), spread(last, 1)),
+    sums = [in_parts(v, 3) for v in own_sums(below, below_x, 0, height)]
+    entries = [in_parts(v, 2) for v in taps + side]
+    tail = [shard[2]] + [v[0] for v in entries] + [v[1] for v in entries]
+    tail += [zero_row()] * (-len(tail) % 4)
+    values = [
+        groups(sums[0][0], sums[1][0], sums[0][1], sums[1][1]),
+        groups(sums[0][2], sums[1][2], spread(last, 0), spread(last, 1)),
         *[total_of(got, r) for r in range(2, 6)],
         *shard[0:2],
-        *[groups(*(taps[4 * q : 4 * q + 4] + [zero_row()])[0:4]) for q in range(6)],
-    )
+        *[groups(*tail[k : k + 4]) for k in range(0, len(tail), 4)],
+    ]
+    values += [zero_row()] * (len(values) % 2)
+    for k in range(len(values) // 2):
+        pair = jnp.concatenate(values[2 * k : 2 * k + 2], axis=0).astype(BF16)
+        pay[:, k] = jnp.broadcast_to(pair[None], (devices, 2, LANES))
     notes(more, scale, shift)
 
 
@@ -1010,15 +1017,16 @@
 ):
     refs = (w_convs, m_convs, s_convs)
     outs = (convs_master, convs_moment, convs_square, convs_copy)
-    packs = [[got[0:CH, k, 0, :].T for k in ks] for ks in ((5, 6, 7), (3, 4, 0), (1, 2, 0))]
+    pairs = [got[:, k].astype(F32) for k in range(got.shape[1])]
+    packs = [[pairs[k // 2][0:CH, k % 2, :].T for k in ks] for ks in ((6, 7, 8), (4, 5, 1), (2, 3, 1))]
     for i, pack in enumerate(packs):
         for t in range(9):
             b = t % 4 if t < 8 else (0, 3, 2)[i]
             put((i, t), refs, pack[t // 4][CH * b : CH * b + CH], rate_table[1], outs)
 
-    zero_sums = total_of(got, 0)
-    totals = [total_of(got, r) for r in range(7, 13)]
-    shift, scale = spread(zero_sums, 0), spread(zero_sums, 1)
+    totals = [jnp.sum(pair, axis=0) for pair in pairs]
+    totals = [pair[h : h + 1] for pair in totals for h in range(2)]
+    shift, scale = [spread(totals[0], k) + (spread(totals[0], 2 + k) + spread(totals[1], k)) for k in range(2)]
     factor = affine(table, 0)[0] * vec[0:1]
     by_x = spread(got_one_back[0:CH, 1, 0, :], 3)
     alone = total_of(got_head, 1)
@@ -1028,7 +1036,9 @@
         pair = []
         for e in (2 * t, 2 * t + 1):
             k, b = divmod(1 + e, 4)
-            v = spread(totals[k], b)
+            v = spread(totals[8 + k], b)
+            k, b = divmod(21 + e, 4)
+            v = v + spread(totals[8 + k], b)
             if t < 9:
                 v = factor * (v - (at_lane(alone, ALONE + e) * shift + by_x[e : e + 1] * scale) / pixel_count)
             pair.append(v[:, 0:CH])
@@ -1220,7 +1230,7 @@
 
     pay, more = call(
         part(summed_kernel, pixel_count=pixel_count, **styled),
-        [payload(13), vec],
+        [((devices, 10, 2, LANES), BF16), vec],
         place, got_one_back, got_style, got_head, grad_one, xhat_one, shared, inv_one, more_two, batch_norm_table, w_style,
         sides, back_zero, xhat_zero,
         scalars=1, scratch=[own_field, back_low], name="summed_back",

time: 109 us -> 109 us (level)
  no operation moved by 1% of the time
where the time goes in v12:
time: 109 us; the launch traced here: 108 us
  blocking collectives  66.2 us (61%)
  Pallas kernels  29 us (27%)
  starting transfers between devices  7.3 us (7%)
  waiting for transfers between devices  4.47 us (4%)
  between operations  1.1 us (1%)
    all_to_all x7, blocking collectives, exchange(): return lax.all_to_all(pay, ('row', 'col'), 0, 0)  66.2 us
    pallas_call x10, Pallas kernels, call(): pl.pallas_call(kernel, out_shape=[jax.ShapeDtypeStruct(*plain(x)) for x i...  29 us
    all_to_all x1, starting transfers between devices, exchange(): return lax.all_to_all(pay, ('row', 'col'), 0, 0)  7.3 us
    all_to_all x1, waiting for transfers between devices, exchange(): return lax.all_to_all(pay, ('row', 'col'), 0, 0)  4.47 us
  transfers between devices with their start and end apart: 1, of which 1 were waited for; matrix products, arithmetic and copies ran while one was open for 0% of the time, Pallas kernels for 3%

profile of v12, /device:TPU:0, one launch (start us, length us, event | category | flops | bytes accessed | tf_op | source)
XLA Modules:
  0.0 108.2 jit_solution(5896611501688286962)
XLA Ops:
  0.7 2.0 %pack.1 = bf16[32,16,128]{2,1,0:T(8,128)(2,1)} custom-call(bf16[16,8,2,32]{3,2,1,0:T(2,128)(2,1)} %bitcast.22, s32[16,8,2,32]{3,2,1,0:T(2,128)} %bitcast.21, s32[16,8,32]{2,1,0:T(8,128)} %labels_in.1, s32[16,8,32]{2,1,0:T(8,128)} %valid_in.1), custom_call_target="tpu_custom_call" | custom-call | tf_op jit(solution)/shard_map/pack/pallas_call | solution.py:1077
  2.7 7.3 %all-to-all-start = ((bf16[32,16,128]{2,1,0:T(8,128)(2,1)}), bf16[32,16,128]{2,1,0:T(8,128)(2,1)S(1)}, u32[]{:S(2)}, u32[]{:S(2)}) async-start(bf16[32,16,128]{2,1,0:T(8,128)(2,1)} %pack.1), calls=%async_computation | async-start | bytes 262144 | tf_op jit(solution)/shard_map/all_to_all | solution.py:1090
  10.1 3.6 %prepare.1 = (bf16[65536,256]{1,0:T(8,128)(2,1)}, bf16[1152,256]{1,0:T(8,128)(2,1)}, bf16[1152,256]{1,0:T(8,128)(2,1)}, bf16[256,128]{1,0:T(8,128)(2,1)}) custom-call(f32[10,2,32]{2,1,0:T(2,128)} %refs_6_.1, f32[3,9,32,32]{3,2,1,0:T(8,128)} %refs_7_.1, f32[3,33]{1,0:T(4,128)} %bitcast.16), custom_call_target="tpu_custom_call" | custom-call | tf_op jit(solution)/shard_map/prepare/pallas_call | solution.py:1077
  13.7 0.1 stack.23.place
  13.8 4.5 %all-to-all-done.got = bf16[32,16,128]{2,1,0:T(8,128)(2,1)S(1)} async-done(((bf16[32,16,128]{2,1,0:T(8,128)(2,1)}), bf16[32,16,128]{2,1,0:T(8,128)(2,1)S(1)}, u32[]{:S(2)}, u32[]{:S(2)}) %all-to-all-start) | async-done | bytes 131104 | tf_op jit(solution)/shard_map/all_to_all | solution.py:1090
  18.3 2.0 %image_conv.1 = (bf16[42,16,128]{2,1,0:T(8,128)(2,1)S(1)}, f32[40,2,16,128]{3,2,1,0:T(8,128)S(1)}, f32[32,2,1,128]{3,2,1,0:T(1,128)S(1)}, f32[8,128]{1,0:T(8,128)S(1)}, bf16[1280,256]{1,0:T(8,128)(2,1)S(1)}) custom-call(s32[5]{0:T(128)S(1)} %stack.23.place, bf16[32,16,128]{2,1,0:T(8,128)(2,1)S(1)} %all-to-all-done.got, ...), custom_call_target="tpu_custom_call" | custom-call | tf_op jit(solution)/shard_map/image_conv/pallas_call | solution.py:1077
  20.3 9.0 %all_to_all.40.got = f32[32,2,1,128]{3,2,1,0:T(1,128)S(1)} all-to-all(f32[32,2,1,128]{3,2,1,0:T(1,128)S(1)} %get-tuple-element.82), channel_id=1, replica_groups=mesh['row'=8,'col'=4] {'row','col'}, dimensions={0} | all-to-all | bytes 65536 | tf_op jit(solution)/shard_map/all_to_all | solution.py:1090
  29.3 2.0 %first_block.1 = (f32[40,2,16,128]{3,2,1,0:T(8,128)S(1)}, f32[32,2,1,128]{3,2,1,0:T(1,128)S(1)}, f32[8,128]{1,0:T(8,128)S(1)}, f32[2048,2,16,128]{3,2,1,0:T(8,128)}, bf16[2731,3,16,128]{3,2,1,0:T(8,128)(2,1)}) custom-call(s32[5]{0:T(128)S(1)} %stack.23.place, f32[32,2,1,128]{3,2,1,0:T(1,128)S(1)} %all_to_all.40.got, ...), custom_call_target="tpu_custom_call" | custom-call | tf_op jit(solution)/shard_map/first_block/pallas_call | solution.py:1077
  31.3 8.9 %all_to_all.41.got = f32[32,2,1,128]{3,2,1,0:T(1,128)S(1)} all-to-all(f32[32,2,1,128]{3,2,1,0:T(1,128)S(1)} %get-tuple-element.86), channel_id=1, replica_groups=mesh['row'=8,'col'=4] {'row','col'}, dimensions={0} | all-to-all | bytes 65536 | tf_op jit(solution)/shard_map/all_to_all | solution.py:1090
  40.3 2.7 %pool_and_merge.1 = (f32[40,2,16,128]{3,2,1,0:T(8,128)S(1)}, f32[32,3,1,128]{3,2,1,0:T(1,128)S(1)}, f32[8,128]{1,0:T(8,128)S(1)}, bf16[42,3,16,128]{3,2,1,0:T(8,...) custom-call(s32[5]{0:T(128)S(1)} %stack.23.place, ...), custom_call_target="tpu_custom_call", output_to_operand_aliasing={{5}: (6, {}), {6}: (7, {})} | custom-call | tf_op jit(solution)/shard_map/pool_and_merge/pallas_call | solution.py:1077
  43.0 9.0 %all_to_all.42.got.got_style.refs_15_ = f32[32,3,1,128]{3,2,1,0:T(1,128)S(1)} all-to-all(f32[32,3,1,128]{3,2,1,0:T(1,128)S(1)} %get-tuple-element.91), channel_id=1, replica_groups=mesh['row'=8,'col'=4] {'row','col'}, dimensions={0} | all-to-all | bytes 98304 | tf_op jit(solution)/shard_map/all_to_all | solution.py:1090
  52.1 5.0 %decoder.1 = (f32[36,2,16,128]{3,2,1,0:T(8,128)S(1)}, f32[32,3,1,128]{3,2,1,0:T(1,128)S(1)}, f32[8,128]{1,0:T(8,128)S(1)}, f32[32,128]{1,0:T(8,128)S(1)}, f32[40...) custom-call(s32[5]{0:T(128)S(1)} %stack.23.place, ...), custom_call_target="tpu_custom_call", output_to_operand_aliasing={{7}: (10, {})} | custom-call | tf_op jit(solution)/shard_map/decoder/pallas_call | solution.py:1077
  57.1 9.0 %all_to_all.43.got = f32[32,3,1,128]{3,2,1,0:T(1,128)S(1)} all-to-all(f32[32,3,1,128]{3,2,1,0:T(1,128)S(1)} %get-tuple-element.97), channel_id=1, replica_groups=mesh['row'=8,'col'=4] {'row','col'}, dimensions={0} | all-to-all | bytes 98304 | tf_op jit(solution)/shard_map/all_to_all | solution.py:1090
  66.1 2.7 %head.1 = (f32[36,2,16,128]{3,2,1,0:T(8,128)S(1)}, f32[36,2,16,128]{3,2,1,0:T(8,128)S(1)}, f32[32,8,1,128]{3,2,1,0:T(1,128)S(1)}, f32[8,128]{1,0:T(8,128)S(1)}) custom-call(s32[5]{0:T(128)S(1)} %stack.23.place, f32[32,3,1,128]{3,2,1,0:T(1,128)S(1)} %all_to_all.43.got, f32[32,3,1,128]{3,2,1,0:T(1,128)S(1)} %all_to_all.42.got.got_style.refs_15_, ...), custom_call_target="tpu_custom_call" | custom-call | tf_op jit(solution)/shard_map/head/pallas_call | solution.py:1077
  68.9 9.9 %all_to_all.44.got.got_head.refs_2_ = f32[32,8,1,128]{3,2,1,0:T(1,128)S(1)} all-to-all(f32[32,8,1,128]{3,2,1,0:T(1,128)S(1)} %get-tuple-element.104), channel_id=1, replica_groups=mesh['row'=8,'col'=4] {'row','col'}, dimensions={0} | all-to-all | bytes 262144 | tf_op jit(solution)/shard_map/all_to_all | solution.py:1090
  78.8 0.0 copy-start.9
  78.8 0.0 copy-start.10
  78.9 0.0 copy-start.14
  78.9 0.0 copy-start.15
  78.9 4.4 %decoder_back.1 = (f32[36,2,16,128]{3,2,1,0:T(8,128)S(1)}, f32[36,2,16,128]{3,2,1,0:T(8,128)S(1)}, f32[36,2,16,128]{3,2,1,0:T(8,128)S(1)}, f32[32,8,1,128]{3,2,1...) custom-call(s32[5]{0:T(128)S(1)} %stack.23.place, ...), custom_call_target="tpu_custom_call" | custom-call | tf_op jit(solution)/shard_map/decoder_back/pallas_call | solution.py:1077
  83.4 9.9 %all_to_all.45.got.refs_1_ = f32[32,8,1,128]{3,2,1,0:T(1,128)S(1)} all-to-all(f32[32,8,1,128]{3,2,1,0:T(1,128)S(1)} %get-tuple-element.110), channel_id=1, replica_groups=mesh['row'=8,'col'=4] {'row','col'}, dimensions={0} | all-to-all | bytes 262144 | tf_op jit(solution)/shard_map/all_to_all | solution.py:1090
  93.3 2.2 %summed_back.1 = (bf16[32,10,2,128]{3,2,1,0:T(2,128)(2,1)S(1)}, f32[8,128]{1,0:T(8,128)S(1)}) custom-call(s32[5]{0:T(128)S(1)} %stack.23.place, f32[32,8,1,128]{3,2,1,0:T(1,128)S(1)} %all_to_all.45.got.refs_1_, f32[32,3,1,128]{3,2,1,0:T(1,128)S(1)} %all_to_all.42.got.got_style.refs_15_, f32[32,8,1,128]{3,2,1,0:T(1,128)S(1)} %all_to_all.44.got.got_head.refs_2_, ...), custom_call_target="tpu_custom_call" | custom-call | tf_op jit(solution)/shard_map/summed_back/pallas_call | solution.py:1077
  95.6 10.3 %all_to_all.46.refs_0_ = bf16[32,10,2,128]{3,2,1,0:T(2,128)(2,1)S(1)} all-to-all(bf16[32,10,2,128]{3,2,1,0:T(2,128)(2,1)S(1)} %get-tuple-element.118), channel_id=1, replica_groups=mesh['row'=8,'col'=4] {'row','col'}, dimensions={0} | all-to-all | bytes 327680 | tf_op jit(solution)/shard_map/all_to_all | solution.py:1090
  106.0 2.1 %update.1 = (f32[10,2,32]{2,1,0:T(2,128)}, f32[10,2,32]{2,1,0:T(2,128)}, f32[10,2,32]{2,1,0:T(2,128)}, bf16[10,2,32]{2,1,0:T(2,128)(2,1)}, f32[3,9,32,32]{3,2,1,...) custom-call(bf16[32,10,2,128]{3,2,1,0:T(2,128)(2,1)S(1)} %all_to_all, ...), custom_call_target="tpu_custom_call" | custom-call | tf_op jit(solution)/shard_map/update/pallas_call | solution.py:1077
  (32 shorter events, 0.1 us)
Async XLA Ops:
  0.7 28.6 %copy-start.6 = (f32[2,4,32]{2,1,0:T(4,128)S(1)}, f32[2,4,32]{2,1,0:T(4,128)}, u32[]{:S(2)}) copy-start(f32[2,4,32]{2,1,0:T(4,128)} %refs_8_.1) | copy-start | bytes 3076
  2.7 15.5 %all-to-all-start = ((bf16[32,16,128]{2,1,0:T(8,128)(2,1)}), bf16[32,16,128]{2,1,0:T(8,128)(2,1)S(1)}, u32[]{:S(2)}, u32[]{:S(2)}) async-start(bf16[32,16,128]{2,1,0:T(8,128)(2,1)} %pack.1), calls=%async_computation | async-start | bytes 262144 | tf_op jit(solution)/shard_map/all_to_all | solution.py:1090
  40.3 11.8 %copy-start = (f32[3,9,32,32]{3,2,1,0:T(8,128)S(1)}, f32[3,9,32,32]{3,2,1,0:T(8,128)}, u32[]{:S(2)}) copy-start(f32[3,9,32,32]{3,2,1,0:T(8,128)} %refs_7_.1) | copy-start | bytes 331780
  40.3 11.8 %copy-start.5 = (f32[2,32,32]{2,1,0:T(8,128)S(1)}, f32[2,32,32]{2,1,0:T(8,128)}, u32[]{:S(2)}) copy-start(f32[2,32,32]{2,1,0:T(8,128)} %refs_17_.1) | copy-start | bytes 24580
  52.0 14.1 %copy-start.1 = (bf16[1152,256]{1,0:T(8,128)(2,1)S(1)}, bf16[1152,256]{1,0:T(8,128)(2,1)}, u32[]{:S(2)}) copy-start(bf16[1152,256]{1,0:T(8,128)(2,1)} %get-tuple-element.103.back.back_two) | copy-start | bytes 1769476
  52.0 14.1 %copy-start.7 = (bf16[256,128]{1,0:T(8,128)(2,1)S(1)}, bf16[256,128]{1,0:T(8,128)(2,1)}, u32[]{:S(2)}) copy-start(bf16[256,128]{1,0:T(8,128)(2,1)} %get-tuple-element.99.head_mat) | copy-start | bytes 196612
  52.0 14.1 %copy-start.11 = (f32[33,3]{0,1:T(4,128)S(1)}, f32[33,3]{0,1:T(4,128)}, u32[]{:S(2)}) copy-start(f32[33,3]{0,1:T(4,128)} %param.26) | copy-start | bytes 1192
  78.8 14.5 %copy-start.2 = (bf16[1152,256]{1,0:T(8,128)(2,1)S(1)}, bf16[1152,256]{1,0:T(8,128)(2,1)}, u32[]{:S(2)}) copy-start(bf16[1152,256]{1,0:T(8,128)(2,1)} %get-tuple-element.116.back) | copy-start | bytes 1769476
  78.8 27.1 %copy-start.3 = (f32[3,9,32,32]{3,2,1,0:T(8,128)S(1)}, f32[3,9,32,32]{3,2,1,0:T(8,128)}, u32[]{:S(2)}) copy-start(f32[3,9,32,32]{3,2,1,0:T(8,128)} %refs_10_.1) | copy-start | bytes 331780
  78.8 27.1 %copy-start.4 = (f32[3,9,32,32]{3,2,1,0:T(8,128)S(1)}, f32[3,9,32,32]{3,2,1,0:T(8,128)}, u32[]{:S(2)}) copy-start(f32[3,9,32,32]{3,2,1,0:T(8,128)} %refs_13_.1) | copy-start | bytes 331780
  78.8 27.1 %copy-start.8 = (f32[10,2,32]{2,1,0:T(2,128)S(1)}, f32[10,2,32]{2,1,0:T(2,128)}, u32[]{:S(2)}) copy-start(f32[10,2,32]{2,1,0:T(2,128)} %refs_6_.1) | copy-start | bytes 7684
  78.8 27.1 %copy-start.9 = (f32[2,32,32]{2,1,0:T(8,128)S(1)}, f32[2,32,32]{2,1,0:T(8,128)}, u32[]{:S(2)}) copy-start(f32[2,32,32]{2,1,0:T(8,128)} %refs_19_.1) | copy-start | bytes 24580
  78.8 27.1 %copy-start.10 = (f32[2,32,32]{2,1,0:T(8,128)S(1)}, f32[2,32,32]{2,1,0:T(8,128)}, u32[]{:S(2)}) copy-start(f32[2,32,32]{2,1,0:T(8,128)} %refs_21_.1) | copy-start | bytes 24580
  78.8 27.1 %copy-start.12 = (f32[10,2,32]{2,1,0:T(2,128)S(1)}, f32[10,2,32]{2,1,0:T(2,128)}, u32[]{:S(2)}) copy-start(f32[10,2,32]{2,1,0:T(2,128)} %refs_9_.1) | copy-start | bytes 7684
  78.9 27.1 %copy-start.13 = (f32[10,2,32]{2,1,0:T(2,128)S(1)}, f32[10,2,32]{2,1,0:T(2,128)}, u32[]{:S(2)}) copy-start(f32[10,2,32]{2,1,0:T(2,128)} %refs_12_.1) | copy-start | bytes 7684
  78.9 27.1 %copy-start.14 = (f32[2,4,32]{2,1,0:T(4,128)S(1)}, f32[2,4,32]{2,1,0:T(4,128)}, u32[]{:S(2)}) copy-start(f32[2,4,32]{2,1,0:T(4,128)} %refs_11_.1) | copy-start | bytes 3076
  78.9 27.1 %copy-start.15 = (f32[2,4,32]{2,1,0:T(4,128)S(1)}, f32[2,4,32]{2,1,0:T(4,128)}, u32[]{:S(2)}) copy-start(f32[2,4,32]{2,1,0:T(4,128)} %refs_14_.1) | copy-start | bytes 3076
  78.9 27.1 %copy-start.16 = (f32[33,3]{0,1:T(4,128)S(1)}, f32[33,3]{0,1:T(4,128)}, u32[]{:S(2)}) copy-start(f32[33,3]{0,1:T(4,128)} %param.31) | copy-start | bytes 1192
  78.9 27.0 %copy-start.17 = (f32[33,3]{0,1:T(4,128)S(1)}, f32[33,3]{0,1:T(4,128)}, u32[]{:S(2)}) copy-start(f32[33,3]{0,1:T(4,128)} %param.36) | copy-start | bytes 1192

commit v13 on v12

--- a/solution.py
+++ b/solution.py
@@ -368,8 +368,11 @@
     wait(stored)
 
 
-def start_kernel(place, got, weights, sides, raw, pay, vec, taps, first_mat, sems, *, local_count, height, sources):
-    fetched = copies(sems, (image_at(weights), first_mat), (taps_at(weights, 0), taps))
+def hand_kernel(weights, first_mat, taps, sems):
+    wait(copies(sems, (image_at(weights), first_mat), (taps_at(weights, 0), taps)))
+
+
+def start_kernel(place, got, first_mat, sides, raw, pay, vec, *, local_count, height, sources):
     rows, segments = raw.shape[0], raw.shape[2]
     off, block = place[0], place[1]
     blank(sides)
@@ -385,7 +388,6 @@
         sides[pl.ds(8 * t + 1, 8)] = v.astype(BF16)
 
     loop(rows // 8, eight)
-    wait(fetched[:1])
     y = None
     for r in range(3):
         part = jnp.dot(flat(sides[r : r + rows]), first_mat[LANES * r : LANES * (r + 1)], preferred_element_type=F32)
@@ -399,7 +401,6 @@
     count = jnp.sum(jnp.where((lane >= MASK) & (lane < MASK + 8), mask, 0.0))
     send(pay, mean, square)
     notes(vec, jnp.full((1, LANES), count, F32))
-    wait(fetched[1:])
 
 
 def first_kernel(place, got, raw, sides, table, taps, summed, pay, vec, fields, lows, hidden, xhat, sems, *, spots, local_count, pixel_count, height):
@@ -1176,11 +1177,14 @@
         sems=8, limit=WHOLE_VMEM, name="prepare",
     )
 
-    sides, raw, pay, count, taps = call(
+    first_mat, taps = call(
+        hand_kernel, [((3 * LANES, 2 * LANES), BF16), ten], far(weights), sems=2, name="hand"
+    )
+    sides, raw, pay, count = call(
         part(start_kernel, local_count=local_count, height=height, sources=col_count),
-        [((rows + 2, segments, LANES), BF16), field, payload(2), vec, ten],
-        place, got_inputs, far(weights),
-        scalars=1, scratch=[((3 * LANES, 2 * LANES), BF16)], sems=2, name="image_conv",
+        [((rows + 2, segments, LANES), BF16), field, payload(2), vec],
+        place, got_inputs, first_mat,
+        scalars=1, name="image_conv",
     )
     got_zero = exchange(pay)
     summed, pay, inv_zero, fields, lows = call(

time: 109 us -> 109 us (level)
  waiting for transfers between devices: 4.47 us -> 3.24 us
    all_to_all x1, waiting for transfers between devices: 4.47 us -> 3.24 us  [exchange(): return lax.all_to_all(pay, ('row', 'col'), 0, 0)]
    pallas_call x10 -> x11, Pallas kernels: 29 us -> 29.5 us  [call(): pl.pallas_call(kernel, out_shape=[jax.ShapeDtypeStruct(*plain(x)) for x i...]
  transfers between devices with their start and end apart: 1 -> 1, of which waited for: 1 -> 1; matrix products, arithmetic and copies ran while one was open for 0% -> 0% of each run, Pallas kernels for 3% -> 4%
where the time goes in v13:
time: 109 us; the launch traced here: 108 us
  blocking collectives  66.9 us (61%)
  Pallas kernels  29.5 us (27%)
  starting transfers between devices  7.3 us (7%)
  waiting for transfers between devices  3.24 us (3%)
  between operations  1.11 us (1%)
    all_to_all x7, blocking collectives, exchange(): return lax.all_to_all(pay, ('row', 'col'), 0, 0)  66.9 us
    pallas_call x11, Pallas kernels, call(): pl.pallas_call(kernel, out_shape=[jax.ShapeDtypeStruct(*plain(x)) for x i...  29.5 us
    all_to_all x1, starting transfers between devices, exchange(): return lax.all_to_all(pay, ('row', 'col'), 0, 0)  7.3 us
    all_to_all x1, waiting for transfers between devices, exchange(): return lax.all_to_all(pay, ('row', 'col'), 0, 0)  3.24 us
  transfers between devices with their start and end apart: 1, of which 1 were waited for; matrix products, arithmetic and copies ran while one was open for 0% of the time, Pallas kernels for 4%

profile of v13, /device:TPU:0, one launch (start us, length us, event | category | flops | bytes accessed | tf_op | source)
XLA Modules:
  0.0 108.2 jit_solution(13759543053123502510)
XLA Ops:
  0.7 2.0 %pack.1 = bf16[32,16,128]{2,1,0:T(8,128)(2,1)} custom-call(bf16[16,8,2,32]{3,2,1,0:T(2,128)(2,1)} %bitcast.22, s32[16,8,2,32]{3,2,1,0:T(2,128)} %bitcast.21, s32[16,8,32]{2,1,0:T(8,128)} %labels_in.1, s32[16,8,32]{2,1,0:T(8,128)} %valid_in.1), custom_call_target="tpu_custom_call" | custom-call | tf_op jit(solution)/shard_map/pack/pallas_call | solution.py:1078
  2.7 7.3 %all-to-all-start = ((bf16[32,16,128]{2,1,0:T(8,128)(2,1)}), bf16[32,16,128]{2,1,0:T(8,128)(2,1)S(1)}, u32[]{:S(2)}, u32[]{:S(2)}) async-start(bf16[32,16,128]{2,1,0:T(8,128)(2,1)} %pack.1), calls=%async_computation | async-start | bytes 262144 | tf_op jit(solution)/shard_map/all_to_all | solution.py:1091
  10.1 3.6 %prepare.1 = (bf16[65536,256]{1,0:T(8,128)(2,1)}, bf16[1152,256]{1,0:T(8,128)(2,1)}, bf16[1152,256]{1,0:T(8,128)(2,1)}, bf16[256,128]{1,0:T(8,128)(2,1)}) custom-call(f32[10,2,32]{2,1,0:T(2,128)} %refs_6_.1, f32[3,9,32,32]{3,2,1,0:T(8,128)} %refs_7_.1, f32[3,33]{1,0:T(4,128)} %bitcast.16), custom_call_target="tpu_custom_call" | custom-call | tf_op jit(solution)/shard_map/prepare/pallas_call | solution.py:1078
  13.7 1.2 %hand.1 = (bf16[384,256]{1,0:T(8,128)(2,1)S(1)}, bf16[1280,256]{1,0:T(8,128)(2,1)S(1)}) custom-call(bf16[65536,256]{1,0:T(8,128)(2,1)} %get-tuple-element.82.weights), custom_call_target="tpu_custom_call" | custom-call | tf_op jit(solution)/shard_map/hand/pallas_call | solution.py:1078
  14.9 0.1 stack.23.place
  15.0 3.2 %all-to-all-done.got = bf16[32,16,128]{2,1,0:T(8,128)(2,1)S(1)} async-done(((bf16[32,16,128]{2,1,0:T(8,128)(2,1)}), bf16[32,16,128]{2,1,0:T(8,128)(2,1)S(1)}, u32[]{:S(2)}, u32[]{:S(2)}) %all-to-all-start) | async-done | bytes 131104 | tf_op jit(solution)/shard_map/all_to_all | solution.py:1091
  18.3 1.3 %image_conv.1 = (bf16[42,16,128]{2,1,0:T(8,128)(2,1)S(1)}, f32[40,2,16,128]{3,2,1,0:T(8,128)S(1)}, f32[32,2,1,128]{3,2,1,0:T(1,128)S(1)}, f32[8,128]{1,0:T(8,128)S(1)}) custom-call(s32[5]{0:T(128)S(1)} %stack.23.place, bf16[32,16,128]{2,1,0:T(8,128)(2,1)S(1)} %all-to-all-done.got, bf16[384,256]{1,0:T(8,128)(2,1)S(1)} %get-tuple-element.83.first_mat), custom_call_target="tpu_custom_call" | custom-call | tf_op jit(solution)/shard_map/image_conv/pallas_call | solution.py:1078
  19.6 9.7 %all_to_all.40.got = f32[32,2,1,128]{3,2,1,0:T(1,128)S(1)} all-to-all(f32[32,2,1,128]{3,2,1,0:T(1,128)S(1)} %get-tuple-element.84), channel_id=1, replica_groups=mesh['row'=8,'col'=4] {'row','col'}, dimensions={0} | all-to-all | bytes 65536 | tf_op jit(solution)/shard_map/all_to_all | solution.py:1091
  29.3 2.0 %first_block.1 = (f32[40,2,16,128]{3,2,1,0:T(8,128)S(1)}, f32[32,2,1,128]{3,2,1,0:T(1,128)S(1)}, f32[8,128]{1,0:T(8,128)S(1)}, f32[2048,2,16,128]{3,2,1,0:T(8,128)}, bf16[2731,3,16,128]{3,2,1,0:T(8,128)(2,1)}) custom-call(s32[5]{0:T(128)S(1)} %stack.23.place, f32[32,2,1,128]{3,2,1,0:T(1,128)S(1)} %all_to_all.40.got, ...), custom_call_target="tpu_custom_call" | custom-call | tf_op jit(solution)/shard_map/first_block/pallas_call | solution.py:1078
  31.3 8.9 %all_to_all.41.got = f32[32,2,1,128]{3,2,1,0:T(1,128)S(1)} all-to-all(f32[32,2,1,128]{3,2,1,0:T(1,128)S(1)} %get-tuple-element.88), channel_id=1, replica_groups=mesh['row'=8,'col'=4] {'row','col'}, dimensions={0} | all-to-all | bytes 65536 | tf_op jit(solution)/shard_map/all_to_all | solution.py:1091
  40.2 2.7 %pool_and_merge.1 = (f32[40,2,16,128]{3,2,1,0:T(8,128)S(1)}, f32[32,3,1,128]{3,2,1,0:T(1,128)S(1)}, f32[8,128]{1,0:T(8,128)S(1)}, bf16[42,3,16,128]{3,2,1,0:T(8,...) custom-call(s32[5]{0:T(128)S(1)} %stack.23.place, ...), custom_call_target="tpu_custom_call", output_to_operand_aliasing={{5}: (6, {}), {6}: (7, {})} | custom-call | tf_op jit(solution)/shard_map/pool_and_merge/pallas_call | solution.py:1078
  43.0 9.0 %all_to_all.42.got.got_style.refs_15_ = f32[32,3,1,128]{3,2,1,0:T(1,128)S(1)} all-to-all(f32[32,3,1,128]{3,2,1,0:T(1,128)S(1)} %get-tuple-element.93), channel_id=1, replica_groups=mesh['row'=8,'col'=4] {'row','col'}, dimensions={0} | all-to-all | bytes 98304 | tf_op jit(solution)/shard_map/all_to_all | solution.py:1091
  52.0 5.0 %decoder.1 = (f32[36,2,16,128]{3,2,1,0:T(8,128)S(1)}, f32[32,3,1,128]{3,2,1,0:T(1,128)S(1)}, f32[8,128]{1,0:T(8,128)S(1)}, f32[32,128]{1,0:T(8,128)S(1)}, f32[40...) custom-call(s32[5]{0:T(128)S(1)} %stack.23.place, ...), custom_call_target="tpu_custom_call", output_to_operand_aliasing={{7}: (10, {})} | custom-call | tf_op jit(solution)/shard_map/decoder/pallas_call | solution.py:1078
  57.0 9.0 %all_to_all.43.got = f32[32,3,1,128]{3,2,1,0:T(1,128)S(1)} all-to-all(f32[32,3,1,128]{3,2,1,0:T(1,128)S(1)} %get-tuple-element.99), channel_id=1, replica_groups=mesh['row'=8,'col'=4] {'row','col'}, dimensions={0} | all-to-all | bytes 98304 | tf_op jit(solution)/shard_map/all_to_all | solution.py:1091
  66.1 2.7 %head.1 = (f32[36,2,16,128]{3,2,1,0:T(8,128)S(1)}, f32[36,2,16,128]{3,2,1,0:T(8,128)S(1)}, f32[32,8,1,128]{3,2,1,0:T(1,128)S(1)}, f32[8,128]{1,0:T(8,128)S(1)}) custom-call(s32[5]{0:T(128)S(1)} %stack.23.place, f32[32,3,1,128]{3,2,1,0:T(1,128)S(1)} %all_to_all.43.got, f32[32,3,1,128]{3,2,1,0:T(1,128)S(1)} %all_to_all.42.got.got_style.refs_15_, ...), custom_call_target="tpu_custom_call" | custom-call | tf_op jit(solution)/shard_map/head/pallas_call | solution.py:1078
  68.8 9.9 %all_to_all.44.got.got_head.refs_2_ = f32[32,8,1,128]{3,2,1,0:T(1,128)S(1)} all-to-all(f32[32,8,1,128]{3,2,1,0:T(1,128)S(1)} %get-tuple-element.106), channel_id=1, replica_groups=mesh['row'=8,'col'=4] {'row','col'}, dimensions={0} | all-to-all | bytes 262144 | tf_op jit(solution)/shard_map/all_to_all | solution.py:1091
  78.8 0.0 copy-start.12
  78.8 0.0 copy-start.13
  78.9 0.0 copy-start.16
  78.9 4.5 %decoder_back.1 = (f32[36,2,16,128]{3,2,1,0:T(8,128)S(1)}, f32[36,2,16,128]{3,2,1,0:T(8,128)S(1)}, f32[36,2,16,128]{3,2,1,0:T(8,128)S(1)}, f32[32,8,1,128]{3,2,1...) custom-call(s32[5]{0:T(128)S(1)} %stack.23.place, ...), custom_call_target="tpu_custom_call" | custom-call | tf_op jit(solution)/shard_map/decoder_back/pallas_call | solution.py:1078
  83.3 9.9 %all_to_all.45.got.refs_1_ = f32[32,8,1,128]{3,2,1,0:T(1,128)S(1)} all-to-all(f32[32,8,1,128]{3,2,1,0:T(1,128)S(1)} %get-tuple-element.112), channel_id=1, replica_groups=mesh['row'=8,'col'=4] {'row','col'}, dimensions={0} | all-to-all | bytes 262144 | tf_op jit(solution)/shard_map/all_to_all | solution.py:1091
  93.3 2.2 %summed_back.1 = (bf16[32,10,2,128]{3,2,1,0:T(2,128)(2,1)S(1)}, f32[8,128]{1,0:T(8,128)S(1)}) custom-call(s32[5]{0:T(128)S(1)} %stack.23.place, f32[32,8,1,128]{3,2,1,0:T(1,128)S(1)} %all_to_all.45.got.refs_1_, f32[32,3,1,128]{3,2,1,0:T(1,128)S(1)} %all_to_all.42.got.got_style.refs_15_, f32[32,8,1,128]{3,2,1,0:T(1,128)S(1)} %all_to_all.44.got.got_head.refs_2_, ...), custom_call_target="tpu_custom_call" | custom-call | tf_op jit(solution)/shard_map/summed_back/pallas_call | solution.py:1078
  95.5 10.3 %all_to_all.46.refs_0_ = bf16[32,10,2,128]{3,2,1,0:T(2,128)(2,1)S(1)} all-to-all(bf16[32,10,2,128]{3,2,1,0:T(2,128)(2,1)S(1)} %get-tuple-element.120), channel_id=1, replica_groups=mesh['row'=8,'col'=4] {'row','col'}, dimensions={0} | all-to-all | bytes 327680 | tf_op jit(solution)/shard_map/all_to_all | solution.py:1091
  105.9 2.1 %update.1 = (f32[10,2,32]{2,1,0:T(2,128)}, f32[10,2,32]{2,1,0:T(2,128)}, f32[10,2,32]{2,1,0:T(2,128)}, bf16[10,2,32]{2,1,0:T(2,128)(2,1)}, f32[3,9,32,32]{3,2,1,...) custom-call(bf16[32,10,2,128]{3,2,1,0:T(2,128)(2,1)S(1)} %all_to_all, ...), custom_call_target="tpu_custom_call" | custom-call | tf_op jit(solution)/shard_map/update/pallas_call | solution.py:1078
  (33 shorter events, 0.1 us)
Async XLA Ops:
  0.7 28.6 %copy-start.6 = (f32[2,4,32]{2,1,0:T(4,128)S(1)}, f32[2,4,32]{2,1,0:T(4,128)}, u32[]{:S(2)}) copy-start(f32[2,4,32]{2,1,0:T(4,128)} %refs_8_.1) | copy-start | bytes 3076
  2.7 15.5 %all-to-all-start = ((bf16[32,16,128]{2,1,0:T(8,128)(2,1)}), bf16[32,16,128]{2,1,0:T(8,128)(2,1)S(1)}, u32[]{:S(2)}, u32[]{:S(2)}) async-start(bf16[32,16,128]{2,1,0:T(8,128)(2,1)} %pack.1), calls=%async_computation | async-start | bytes 262144 | tf_op jit(solution)/shard_map/all_to_all | solution.py:1091
  40.2 11.8 %copy-start = (f32[3,9,32,32]{3,2,1,0:T(8,128)S(1)}, f32[3,9,32,32]{3,2,1,0:T(8,128)}, u32[]{:S(2)}) copy-start(f32[3,9,32,32]{3,2,1,0:T(8,128)} %refs_7_.1) | copy-start | bytes 331780
  40.2 11.8 %copy-start.5 = (f32[2,32,32]{2,1,0:T(8,128)S(1)}, f32[2,32,32]{2,1,0:T(8,128)}, u32[]{:S(2)}) copy-start(f32[2,32,32]{2,1,0:T(8,128)} %refs_17_.1) | copy-start | bytes 24580
  52.0 14.1 %copy-start.1 = (bf16[1152,256]{1,0:T(8,128)(2,1)S(1)}, bf16[1152,256]{1,0:T(8,128)(2,1)}, u32[]{:S(2)}) copy-start(bf16[1152,256]{1,0:T(8,128)(2,1)} %get-tuple-element.105.back.back_two) | copy-start | bytes 1769476
  52.0 14.1 %copy-start.7 = (bf16[256,128]{1,0:T(8,128)(2,1)S(1)}, bf16[256,128]{1,0:T(8,128)(2,1)}, u32[]{:S(2)}) copy-start(bf16[256,128]{1,0:T(8,128)(2,1)} %get-tuple-element.101.head_mat) | copy-start | bytes 196612
  52.0 14.1 %copy-start.11 = (f32[33,3]{0,1:T(4,128)S(1)}, f32[33,3]{0,1:T(4,128)}, u32[]{:S(2)}) copy-start(f32[33,3]{0,1:T(4,128)} %param.26) | copy-start | bytes 1192
  78.8 14.5 %copy-start.2 = (bf16[1152,256]{1,0:T(8,128)(2,1)S(1)}, bf16[1152,256]{1,0:T(8,128)(2,1)}, u32[]{:S(2)}) copy-start(bf16[1152,256]{1,0:T(8,128)(2,1)} %get-tuple-element.118.back) | copy-start | bytes 1769476
  78.8 27.1 %copy-start.3 = (f32[3,9,32,32]{3,2,1,0:T(8,128)S(1)}, f32[3,9,32,32]{3,2,1,0:T(8,128)}, u32[]{:S(2)}) copy-start(f32[3,9,32,32]{3,2,1,0:T(8,128)} %refs_10_.1) | copy-start | bytes 331780
  78.8 27.1 %copy-start.4 = (f32[3,9,32,32]{3,2,1,0:T(8,128)S(1)}, f32[3,9,32,32]{3,2,1,0:T(8,128)}, u32[]{:S(2)}) copy-start(f32[3,9,32,32]{3,2,1,0:T(8,128)} %refs_13_.1) | copy-start | bytes 331780
  78.8 27.1 %copy-start.8 = (f32[10,2,32]{2,1,0:T(2,128)S(1)}, f32[10,2,32]{2,1,0:T(2,128)}, u32[]{:S(2)}) copy-start(f32[10,2,32]{2,1,0:T(2,128)} %refs_6_.1) | copy-start | bytes 7684
  78.8 27.1 %copy-start.9 = (f32[2,32,32]{2,1,0:T(8,128)S(1)}, f32[2,32,32]{2,1,0:T(8,128)}, u32[]{:S(2)}) copy-start(f32[2,32,32]{2,1,0:T(8,128)} %refs_19_.1) | copy-start | bytes 24580
  78.8 27.1 %copy-start.10 = (f32[2,32,32]{2,1,0:T(8,128)S(1)}, f32[2,32,32]{2,1,0:T(8,128)}, u32[]{:S(2)}) copy-start(f32[2,32,32]{2,1,0:T(8,128)} %refs_21_.1) | copy-start | bytes 24580
  78.8 27.1 %copy-start.12 = (f32[10,2,32]{2,1,0:T(2,128)S(1)}, f32[10,2,32]{2,1,0:T(2,128)}, u32[]{:S(2)}) copy-start(f32[10,2,32]{2,1,0:T(2,128)} %refs_9_.1) | copy-start | bytes 7684
  78.8 27.1 %copy-start.13 = (f32[10,2,32]{2,1,0:T(2,128)S(1)}, f32[10,2,32]{2,1,0:T(2,128)}, u32[]{:S(2)}) copy-start(f32[10,2,32]{2,1,0:T(2,128)} %refs_12_.1) | copy-start | bytes 7684
  78.8 27.1 %copy-start.14 = (f32[2,4,32]{2,1,0:T(4,128)S(1)}, f32[2,4,32]{2,1,0:T(4,128)}, u32[]{:S(2)}) copy-start(f32[2,4,32]{2,1,0:T(4,128)} %refs_11_.1) | copy-start | bytes 3076
  78.8 27.1 %copy-start.15 = (f32[2,4,32]{2,1,0:T(4,128)S(1)}, f32[2,4,32]{2,1,0:T(4,128)}, u32[]{:S(2)}) copy-start(f32[2,4,32]{2,1,0:T(4,128)} %refs_14_.1) | copy-start | bytes 3076
  78.9 27.1 %copy-start.16 = (f32[33,3]{0,1:T(4,128)S(1)}, f32[33,3]{0,1:T(4,128)}, u32[]{:S(2)}) copy-start(f32[33,3]{0,1:T(4,128)} %param.31) | copy-start | bytes 1192
  78.9 27.1 %copy-start.17 = (f32[33,3]{0,1:T(4,128)S(1)}, f32[33,3]{0,1:T(4,128)}, u32[]{:S(2)}) copy-start(f32[33,3]{0,1:T(4,128)} %param.36) | copy-start | bytes 1192

commit v14 on v12

--- a/solution.py
+++ b/solution.py
@@ -368,8 +368,12 @@
     wait(stored)
 
 
-def start_kernel(place, got, weights, sides, raw, pay, vec, taps, first_mat, sems, *, local_count, height, sources):
-    fetched = copies(sems, (image_at(weights), first_mat), (taps_at(weights, 0), taps))
+def hand_kernel(weights, first_mat, sems):
+    wait(copies(sems, (image_at(weights), first_mat)))
+
+
+def start_kernel(place, got, first_mat, weights, sides, raw, pay, vec, taps, sems, *, local_count, height, sources):
+    fetched = copies(sems, (taps_at(weights, 0), taps))
     rows, segments = raw.shape[0], raw.shape[2]
     off, block = place[0], place[1]
     blank(sides)
@@ -385,7 +389,6 @@
         sides[pl.ds(8 * t + 1, 8)] = v.astype(BF16)
 
     loop(rows // 8, eight)
-    wait(fetched[:1])
     y = None
     for r in range(3):
         part = jnp.dot(flat(sides[r : r + rows]), first_mat[LANES * r : LANES * (r + 1)], preferred_element_type=F32)
@@ -399,7 +402,7 @@
     count = jnp.sum(jnp.where((lane >= MASK) & (lane < MASK + 8), mask, 0.0))
     send(pay, mean, square)
     notes(vec, jnp.full((1, LANES), count, F32))
-    wait(fetched[1:])
+    wait(fetched)
 
 
 def first_kernel(place, got, raw, sides, table, taps, summed, pay, vec, fields, lows, hidden, xhat, sems, *, spots, local_count, pixel_count, height):
@@ -1176,11 +1179,12 @@
         sems=8, limit=WHOLE_VMEM, name="prepare",
     )
 
+    (first_mat,) = call(hand_kernel, [((3 * LANES, 2 * LANES), BF16)], far(weights), sems=1, name="hand")
     sides, raw, pay, count, taps = call(
         part(start_kernel, local_count=local_count, height=height, sources=col_count),
         [((rows + 2, segments, LANES), BF16), field, payload(2), vec, ten],
-        place, got_inputs, far(weights),
-        scalars=1, scratch=[((3 * LANES, 2 * LANES), BF16)], sems=2, name="image_conv",
+        place, got_inputs, first_mat, far(weights),
+        scalars=1, sems=1, name="image_conv",
     )
     got_zero = exchange(pay)
     summed, pay, inv_zero, fields, lows = call(

time: 109 us -> 109 us (level)
    pallas_call x10 -> x11, Pallas kernels: 29 us -> 29.5 us  [call(): pl.pallas_call(kernel, out_shape=[jax.ShapeDtypeStruct(*plain(x)) for x i...]
  transfers between devices with their start and end apart: 1 -> 1, of which waited for: 1 -> 1; matrix products, arithmetic and copies ran while one was open for 0% -> 0% of each run, Pallas kernels for 3% -> 4%
where the time goes in v14:
time: 109 us; the launch traced here: 108 us
  blocking collectives  66.6 us (61%)
  Pallas kernels  29.5 us (27%)
  starting transfers between devices  7.3 us (7%)
  waiting for transfers between devices  3.5 us (3%)
  between operations  1.12 us (1%)
    all_to_all x7, blocking collectives, exchange(): return lax.all_to_all(pay, ('row', 'col'), 0, 0)  66.6 us
    pallas_call x11, Pallas kernels, call(): pl.pallas_call(kernel, out_shape=[jax.ShapeDtypeStruct(*plain(x)) for x i...  29.5 us
    all_to_all x1, starting transfers between devices, exchange(): return lax.all_to_all(pay, ('row', 'col'), 0, 0)  7.3 us
    all_to_all x1, waiting for transfers between devices, exchange(): return lax.all_to_all(pay, ('row', 'col'), 0, 0)  3.5 us
  transfers between devices with their start and end apart: 1, of which 1 were waited for; matrix products, arithmetic and copies ran while one was open for 0% of the time, Pallas kernels for 4%

profile of v14, /device:TPU:0, one launch (start us, length us, event | category | flops | bytes accessed | tf_op | source)
XLA Modules:
  0.0 108.2 jit_solution(6525076647224687697)
XLA Ops:
  0.7 2.0 %pack.1 = bf16[32,16,128]{2,1,0:T(8,128)(2,1)} custom-call(bf16[16,8,2,32]{3,2,1,0:T(2,128)(2,1)} %bitcast.22, s32[16,8,2,32]{3,2,1,0:T(2,128)} %bitcast.21, s32[16,8,32]{2,1,0:T(8,128)} %labels_in.1, s32[16,8,32]{2,1,0:T(8,128)} %valid_in.1), custom_call_target="tpu_custom_call" | custom-call | tf_op jit(solution)/shard_map/pack/pallas_call | solution.py:1080
  2.7 7.3 %all-to-all-start = ((bf16[32,16,128]{2,1,0:T(8,128)(2,1)}), bf16[32,16,128]{2,1,0:T(8,128)(2,1)S(1)}, u32[]{:S(2)}, u32[]{:S(2)}) async-start(bf16[32,16,128]{2,1,0:T(8,128)(2,1)} %pack.1), calls=%async_computation | async-start | bytes 262144 | tf_op jit(solution)/shard_map/all_to_all | solution.py:1093
  10.1 3.6 %prepare.1 = (bf16[65536,256]{1,0:T(8,128)(2,1)}, bf16[1152,256]{1,0:T(8,128)(2,1)}, bf16[1152,256]{1,0:T(8,128)(2,1)}, bf16[256,128]{1,0:T(8,128)(2,1)}) custom-call(f32[10,2,32]{2,1,0:T(2,128)} %refs_6_.1, f32[3,9,32,32]{3,2,1,0:T(8,128)} %refs_7_.1, f32[3,33]{1,0:T(4,128)} %bitcast.16), custom_call_target="tpu_custom_call" | custom-call | tf_op jit(solution)/shard_map/prepare/pallas_call | solution.py:1080
  13.7 0.9 hand.1.first_mat
  14.7 0.1 stack.23.place
  14.8 3.5 %all-to-all-done.got = bf16[32,16,128]{2,1,0:T(8,128)(2,1)S(1)} async-done(((bf16[32,16,128]{2,1,0:T(8,128)(2,1)}), bf16[32,16,128]{2,1,0:T(8,128)(2,1)S(1)}, u32[]{:S(2)}, u32[]{:S(2)}) %all-to-all-start) | async-done | bytes 131104 | tf_op jit(solution)/shard_map/all_to_all | solution.py:1093
  18.2 1.6 %image_conv.1 = (bf16[42,16,128]{2,1,0:T(8,128)(2,1)S(1)}, f32[40,2,16,128]{3,2,1,0:T(8,128)S(1)}, f32[32,2,1,128]{3,2,1,0:T(1,128)S(1)}, f32[8,128]{1,0:T(8,128)S(1)}, bf16[1280,256]{1,0:T(8,128)(2,1)S(1)}) custom-call(s32[5]{0:T(128)S(1)} %stack.23.place, bf16[32,16,128]{2,1,0:T(8,128)(2,1)S(1)} %all-to-all-done.got, bf16[384,256]{1,0:T(8,128)(2,1)S(1)} %hand.1.first_mat, ...), custom_call_target="tpu_custom_call" | custom-call | tf_op jit(solution)/shard_map/image_conv/pallas_call | solution.py:1080
  19.9 9.4 %all_to_all.40.got = f32[32,2,1,128]{3,2,1,0:T(1,128)S(1)} all-to-all(f32[32,2,1,128]{3,2,1,0:T(1,128)S(1)} %get-tuple-element.82), channel_id=1, replica_groups=mesh['row'=8,'col'=4] {'row','col'}, dimensions={0} | all-to-all | bytes 65536 | tf_op jit(solution)/shard_map/all_to_all | solution.py:1093
  29.3 2.0 %first_block.1 = (f32[40,2,16,128]{3,2,1,0:T(8,128)S(1)}, f32[32,2,1,128]{3,2,1,0:T(1,128)S(1)}, f32[8,128]{1,0:T(8,128)S(1)}, f32[2048,2,16,128]{3,2,1,0:T(8,128)}, bf16[2731,3,16,128]{3,2,1,0:T(8,128)(2,1)}) custom-call(s32[5]{0:T(128)S(1)} %stack.23.place, f32[32,2,1,128]{3,2,1,0:T(1,128)S(1)} %all_to_all.40.got, ...), custom_call_target="tpu_custom_call" | custom-call | tf_op jit(solution)/shard_map/first_block/pallas_call | solution.py:1080
  31.3 8.9 %all_to_all.41.got = f32[32,2,1,128]{3,2,1,0:T(1,128)S(1)} all-to-all(f32[32,2,1,128]{3,2,1,0:T(1,128)S(1)} %get-tuple-element.86), channel_id=1, replica_groups=mesh['row'=8,'col'=4] {'row','col'}, dimensions={0} | all-to-all | bytes 65536 | tf_op jit(solution)/shard_map/all_to_all | solution.py:1093
  40.3 2.7 %pool_and_merge.1 = (f32[40,2,16,128]{3,2,1,0:T(8,128)S(1)}, f32[32,3,1,128]{3,2,1,0:T(1,128)S(1)}, f32[8,128]{1,0:T(8,128)S(1)}, bf16[42,3,16,128]{3,2,1,0:T(8,...) custom-call(s32[5]{0:T(128)S(1)} %stack.23.place, ...), custom_call_target="tpu_custom_call", output_to_operand_aliasing={{5}: (6, {}), {6}: (7, {})} | custom-call | tf_op jit(solution)/shard_map/pool_and_merge/pallas_call | solution.py:1080
  43.0 9.0 %all_to_all.42.got.got_style.refs_15_ = f32[32,3,1,128]{3,2,1,0:T(1,128)S(1)} all-to-all(f32[32,3,1,128]{3,2,1,0:T(1,128)S(1)} %get-tuple-element.91), channel_id=1, replica_groups=mesh['row'=8,'col'=4] {'row','col'}, dimensions={0} | all-to-all | bytes 98304 | tf_op jit(solution)/shard_map/all_to_all | solution.py:1093
  52.0 0.0 copy-start.11
  52.0 5.0 %decoder.1 = (f32[36,2,16,128]{3,2,1,0:T(8,128)S(1)}, f32[32,3,1,128]{3,2,1,0:T(1,128)S(1)}, f32[8,128]{1,0:T(8,128)S(1)}, f32[32,128]{1,0:T(8,128)S(1)}, f32[40...) custom-call(s32[5]{0:T(128)S(1)} %stack.23.place, ...), custom_call_target="tpu_custom_call", output_to_operand_aliasing={{7}: (10, {})} | custom-call | tf_op jit(solution)/shard_map/decoder/pallas_call | solution.py:1080
  57.1 9.0 %all_to_all.43.got = f32[32,3,1,128]{3,2,1,0:T(1,128)S(1)} all-to-all(f32[32,3,1,128]{3,2,1,0:T(1,128)S(1)} %get-tuple-element.97), channel_id=1, replica_groups=mesh['row'=8,'col'=4] {'row','col'}, dimensions={0} | all-to-all | bytes 98304 | tf_op jit(solution)/shard_map/all_to_all | solution.py:1093
  66.1 2.7 %head.1 = (f32[36,2,16,128]{3,2,1,0:T(8,128)S(1)}, f32[36,2,16,128]{3,2,1,0:T(8,128)S(1)}, f32[32,8,1,128]{3,2,1,0:T(1,128)S(1)}, f32[8,128]{1,0:T(8,128)S(1)}) custom-call(s32[5]{0:T(128)S(1)} %stack.23.place, f32[32,3,1,128]{3,2,1,0:T(1,128)S(1)} %all_to_all.43.got, f32[32,3,1,128]{3,2,1,0:T(1,128)S(1)} %all_to_all.42.got.got_style.refs_15_, ...), custom_call_target="tpu_custom_call" | custom-call | tf_op jit(solution)/shard_map/head/pallas_call | solution.py:1080
  68.8 9.9 %all_to_all.44.got.got_head.refs_2_ = f32[32,8,1,128]{3,2,1,0:T(1,128)S(1)} all-to-all(f32[32,8,1,128]{3,2,1,0:T(1,128)S(1)} %get-tuple-element.104), channel_id=1, replica_groups=mesh['row'=8,'col'=4] {'row','col'}, dimensions={0} | all-to-all | bytes 262144 | tf_op jit(solution)/shard_map/all_to_all | solution.py:1093
  78.8 0.0 copy-start.10
  78.8 0.0 copy-start.12
  78.9 4.4 %decoder_back.1 = (f32[36,2,16,128]{3,2,1,0:T(8,128)S(1)}, f32[36,2,16,128]{3,2,1,0:T(8,128)S(1)}, f32[36,2,16,128]{3,2,1,0:T(8,128)S(1)}, f32[32,8,1,128]{3,2,1...) custom-call(s32[5]{0:T(128)S(1)} %stack.23.place, ...), custom_call_target="tpu_custom_call" | custom-call | tf_op jit(solution)/shard_map/decoder_back/pallas_call | solution.py:1080
  83.3 9.9 %all_to_all.45.got.refs_1_ = f32[32,8,1,128]{3,2,1,0:T(1,128)S(1)} all-to-all(f32[32,8,1,128]{3,2,1,0:T(1,128)S(1)} %get-tuple-element.110), channel_id=1, replica_groups=mesh['row'=8,'col'=4] {'row','col'}, dimensions={0} | all-to-all | bytes 262144 | tf_op jit(solution)/shard_map/all_to_all | solution.py:1093
  93.3 2.2 %summed_back.1 = (bf16[32,10,2,128]{3,2,1,0:T(2,128)(2,1)S(1)}, f32[8,128]{1,0:T(8,128)S(1)}) custom-call(s32[5]{0:T(128)S(1)} %stack.23.place, f32[32,8,1,128]{3,2,1,0:T(1,128)S(1)} %all_to_all.45.got.refs_1_, f32[32,3,1,128]{3,2,1,0:T(1,128)S(1)} %all_to_all.42.got.got_style.refs_15_, f32[32,8,1,128]{3,2,1,0:T(1,128)S(1)} %all_to_all.44.got.got_head.refs_2_, ...), custom_call_target="tpu_custom_call" | custom-call | tf_op jit(solution)/shard_map/summed_back/pallas_call | solution.py:1080
  95.5 10.3 %all_to_all.46.refs_0_ = bf16[32,10,2,128]{3,2,1,0:T(2,128)(2,1)S(1)} all-to-all(bf16[32,10,2,128]{3,2,1,0:T(2,128)(2,1)S(1)} %get-tuple-element.118), channel_id=1, replica_groups=mesh['row'=8,'col'=4] {'row','col'}, dimensions={0} | all-to-all | bytes 327680 | tf_op jit(solution)/shard_map/all_to_all | solution.py:1093
  105.9 2.1 %update.1 = (f32[10,2,32]{2,1,0:T(2,128)}, f32[10,2,32]{2,1,0:T(2,128)}, f32[10,2,32]{2,1,0:T(2,128)}, bf16[10,2,32]{2,1,0:T(2,128)(2,1)}, f32[3,9,32,32]{3,2,1,...) custom-call(bf16[32,10,2,128]{3,2,1,0:T(2,128)(2,1)S(1)} %all_to_all, ...), custom_call_target="tpu_custom_call" | custom-call | tf_op jit(solution)/shard_map/update/pallas_call | solution.py:1080
  (33 shorter events, 0.1 us)
Async XLA Ops:
  2.7 15.5 %all-to-all-start = ((bf16[32,16,128]{2,1,0:T(8,128)(2,1)}), bf16[32,16,128]{2,1,0:T(8,128)(2,1)S(1)}, u32[]{:S(2)}, u32[]{:S(2)}) async-start(bf16[32,16,128]{2,1,0:T(8,128)(2,1)} %pack.1), calls=%async_computation | async-start | bytes 262144 | tf_op jit(solution)/shard_map/all_to_all | solution.py:1093
  13.7 15.6 %copy-start.6 = (f32[2,4,32]{2,1,0:T(4,128)S(1)}, f32[2,4,32]{2,1,0:T(4,128)}, u32[]{:S(2)}) copy-start(f32[2,4,32]{2,1,0:T(4,128)} %refs_8_.1) | copy-start | bytes 3076
  40.3 11.8 %copy-start = (f32[3,9,32,32]{3,2,1,0:T(8,128)S(1)}, f32[3,9,32,32]{3,2,1,0:T(8,128)}, u32[]{:S(2)}) copy-start(f32[3,9,32,32]{3,2,1,0:T(8,128)} %refs_7_.1) | copy-start | bytes 331780
  40.3 11.8 %copy-start.5 = (f32[2,32,32]{2,1,0:T(8,128)S(1)}, f32[2,32,32]{2,1,0:T(8,128)}, u32[]{:S(2)}) copy-start(f32[2,32,32]{2,1,0:T(8,128)} %refs_17_.1) | copy-start | bytes 24580
  52.0 14.1 %copy-start.1 = (bf16[1152,256]{1,0:T(8,128)(2,1)S(1)}, bf16[1152,256]{1,0:T(8,128)(2,1)}, u32[]{:S(2)}) copy-start(bf16[1152,256]{1,0:T(8,128)(2,1)} %get-tuple-element.103.back.back_two) | copy-start | bytes 1769476
  52.0 14.1 %copy-start.7 = (bf16[256,128]{1,0:T(8,128)(2,1)S(1)}, bf16[256,128]{1,0:T(8,128)(2,1)}, u32[]{:S(2)}) copy-start(bf16[256,128]{1,0:T(8,128)(2,1)} %get-tuple-element.99.head_mat) | copy-start | bytes 196612
  52.0 14.1 %copy-start.11 = (f32[33,3]{0,1:T(4,128)S(1)}, f32[33,3]{0,1:T(4,128)}, u32[]{:S(2)}) copy-start(f32[33,3]{0,1:T(4,128)} %param.26) | copy-start | bytes 1192
  78.8 14.5 %copy-start.2 = (bf16[1152,256]{1,0:T(8,128)(2,1)S(1)}, bf16[1152,256]{1,0:T(8,128)(2,1)}, u32[]{:S(2)}) copy-start(bf16[1152,256]{1,0:T(8,128)(2,1)} %get-tuple-element.116.back) | copy-start | bytes 1769476
  78.8 27.1 %copy-start.3 = (f32[3,9,32,32]{3,2,1,0:T(8,128)S(1)}, f32[3,9,32,32]{3,2,1,0:T(8,128)}, u32[]{:S(2)}) copy-start(f32[3,9,32,32]{3,2,1,0:T(8,128)} %refs_10_.1) | copy-start | bytes 331780
  78.8 27.1 %copy-start.4 = (f32[3,9,32,32]{3,2,1,0:T(8,128)S(1)}, f32[3,9,32,32]{3,2,1,0:T(8,128)}, u32[]{:S(2)}) copy-start(f32[3,9,32,32]{3,2,1,0:T(8,128)} %refs_13_.1) | copy-start | bytes 331780
  78.8 27.1 %copy-start.8 = (f32[10,2,32]{2,1,0:T(2,128)S(1)}, f32[10,2,32]{2,1,0:T(2,128)}, u32[]{:S(2)}) copy-start(f32[10,2,32]{2,1,0:T(2,128)} %refs_6_.1) | copy-start | bytes 7684
  78.8 27.1 %copy-start.9 = (f32[2,32,32]{2,1,0:T(8,128)S(1)}, f32[2,32,32]{2,1,0:T(8,128)}, u32[]{:S(2)}) copy-start(f32[2,32,32]{2,1,0:T(8,128)} %refs_19_.1) | copy-start | bytes 24580
  78.8 27.1 %copy-start.10 = (f32[2,32,32]{2,1,0:T(8,128)S(1)}, f32[2,32,32]{2,1,0:T(8,128)}, u32[]{:S(2)}) copy-start(f32[2,32,32]{2,1,0:T(8,128)} %refs_21_.1) | copy-start | bytes 24580
  78.8 27.1 %copy-start.12 = (f32[10,2,32]{2,1,0:T(2,128)S(1)}, f32[10,2,32]{2,1,0:T(2,128)}, u32[]{:S(2)}) copy-start(f32[10,2,32]{2,1,0:T(2,128)} %refs_9_.1) | copy-start | bytes 7684
  78.8 27.1 %copy-start.13 = (f32[10,2,32]{2,1,0:T(2,128)S(1)}, f32[10,2,32]{2,1,0:T(2,128)}, u32[]{:S(2)}) copy-start(f32[10,2,32]{2,1,0:T(2,128)} %refs_12_.1) | copy-start | bytes 7684
  78.8 27.1 %copy-start.14 = (f32[2,4,32]{2,1,0:T(4,128)S(1)}, f32[2,4,32]{2,1,0:T(4,128)}, u32[]{:S(2)}) copy-start(f32[2,4,32]{2,1,0:T(4,128)} %refs_11_.1) | copy-start | bytes 3076
  78.9 27.1 %copy-start.15 = (f32[2,4,32]{2,1,0:T(4,128)S(1)}, f32[2,4,32]{2,1,0:T(4,128)}, u32[]{:S(2)}) copy-start(f32[2,4,32]{2,1,0:T(4,128)} %refs_14_.1) | copy-start | bytes 3076
  78.9 27.1 %copy-start.16 = (f32[33,3]{0,1:T(4,128)S(1)}, f32[33,3]{0,1:T(4,128)}, u32[]{:S(2)}) copy-start(f32[33,3]{0,1:T(4,128)} %param.31) | copy-start | bytes 1192
  78.9 27.0 %copy-start.17 = (f32[33,3]{0,1:T(4,128)S(1)}, f32[33,3]{0,1:T(4,128)}, u32[]{:S(2)}) copy-start(f32[33,3]{0,1:T(4,128)} %param.36) | copy-start | bytes 1192
